TPU v7x, 32 devices: a whole 2x2x4 slice. The times are simulated.
32 devices in a mesh: groups: 2 (over y), dev: 8 (over z, x), sub: 2 (over core).
Axes of the slice: x: 2, y: 2, z: 4, core: 2. Of those that a mesh axis runs over, the one named last changes fastest.
Arguments:
- tokens: bfloat16 [2048, 2048], P(('groups', 'dev')), parts along dimension 0, may hold values from -6 to 6
- query_key_value: bfloat16 [2048, 3, 2048], P(('groups', 'dev'), None, 'sub'), parts along dimension 0, may hold values from -6 to 6
- out_weight: bfloat16 [2048, 2048], P('dev', 'sub'), may hold values from -0.125 to 0.125
- modulation: float32 [8, 2048], P('groups'), parts along dimension 0, may hold values from -3 to 3
- router_weight: bfloat16 [2048, 64], replicated, may hold values from -0.125 to 0.125
- expert_ids: int32 [2048, 4], P(('groups', 'dev')), parts along dimension 0, may hold values from 0 to 63, all different within a row; in each aligned block of 128 rows (0 to 127, 128 to 255, ...) at most 12 rows name the same one
- gate_up_weight: bfloat16 [128, 2, 2048, 384], P('dev', None, None, 'sub'), may hold values from -0.125 to 0.125
- down_weight: bfloat16 [128, 384, 2048], P('dev', None, 'sub'), may hold values from -0.21875 to 0.21875
Outputs:
- block_out: bfloat16 [2048, 2048], P(('groups', 'dev'), 'sub'), parts along dimension 0
There are 2 independent parts, one for each index of `groups`. A program takes and returns all parts, laid end to end along the dimension named above; an argument that names none is the same for every part. Nothing has to cross between parts.
Inputs may be any that keep to these rules, and one draw needn't show every extreme that they name: `expert_ids`: each token names 4 different experts. Within each aligned block of 128 rows no expert is named by more than 12 rows, a bound that some block reaches.
All inputs are finite; a program needn't handle non-finite values.
Results may differ from a plain program's by a relative error of at most 0.008.
Values may be sent and summed in bfloat16 or wider, within the bound.
No kernel may reach another device: no remote copies, remote signals or barrier semaphores. Data moves between devices by JAX's collectives and lax.ppermute only.
A program may use at most 128 MiB of HBM per device.

v0:
```python
import math

import jax
import jax.numpy as jnp
from jax import lax
from jax.sharding import PartitionSpec as P

HEAD = 128
CAP = 12


EPS = 1e-06
NEG = -1e30


def extended(cells, sides, width):
    for axis, dim in sides:
        count = lax.axis_size(axis)
        ends = count - 1
        head = lax.slice_in_dim(cells, 0, width, axis=dim)
        tail = lax.slice_in_dim(cells, cells.shape[dim] - width, cells.shape[dim], axis=dim)
        cells = jnp.concatenate(
            [
                lax.ppermute(tail, axis, [(i, (i + 1) % count) for i in range(ends)]),
                cells,
                lax.ppermute(head, axis, [((i + 1) % count, i) for i in range(ends)]),
            ],
            axis=dim,
        )
    return cells


def window_attention(query, keys, values, index, total):
    count = query.shape[0]
    rows = jnp.arange(count, dtype=jnp.int32)[:, None]
    cols = jnp.arange(3 * count, dtype=jnp.int32)[None, :] - count
    place = index * count + cols
    allowed = (jnp.abs(cols - rows) <= count) & (place >= 0) & (place < total)
    scores = jnp.einsum(
        "qhd,khd->hqk", query, keys, preferred_element_type=jnp.float32
    ) / math.sqrt(query.shape[2])
    scores = jnp.where(allowed[None], scores, NEG)
    top = jnp.max(scores, -1, keepdims=True)
    weight = jnp.exp(scores - top)
    weight = (weight / jnp.sum(weight, -1, keepdims=True)).astype(jnp.bfloat16)
    mixed = jnp.einsum("hqk,khd->qhd", weight, values, preferred_element_type=jnp.float32)
    return mixed.astype(jnp.bfloat16)


def normalize(state, modulation):
    scale = lax.rsqrt(jnp.mean(state * state, -1, keepdims=True) + EPS)
    return (state * scale * (1.0 + modulation[2]) + modulation[1]).astype(jnp.bfloat16)


def route(normed, router_weight, expert_ids):
    logits = jnp.dot(normed, router_weight, preferred_element_type=jnp.float32)
    experts = router_weight.shape[1]
    match = expert_ids[:, :, None] == jnp.arange(experts, dtype=jnp.int32)[None, None, :]
    picked = jnp.sum(jnp.where(match, logits[:, None, :], 0.0), -1)
    lifted = jax.nn.sigmoid(picked)
    return lifted / jnp.sum(lifted, -1, keepdims=True)


def body(
    tokens,
    query_key_value,
    out_weight,
    modulation,
    router_weight,
    expert_ids,
    gate_up_weight,
    down_weight,
):
    count = tokens.shape[0]
    width = tokens.shape[1]
    parts = lax.axis_size("sub")
    part = lax.axis_index("sub")
    position = lax.axis_index("dev")
    devices = lax.axis_size("dev")
    total = count * devices
    local_width = query_key_value.shape[2]
    heads_here = local_width // HEAD
    query = query_key_value[:, 0].reshape(count, heads_here, HEAD)
    pair = query_key_value[:, 1:]
    near = extended(pair, (("dev", 0),), count)
    keys = near[:, 0].reshape(3 * count, heads_here, HEAD)
    values = near[:, 1].reshape(3 * count, heads_here, HEAD)
    mixed = window_attention(query, keys, values, position, total).reshape(count, local_width)
    partial_proj = lax.dot_general(
        mixed,
        lax.all_gather(out_weight, "dev", axis=0, tiled=True),
        (((1,), (1,)), ((), ())),
        preferred_element_type=jnp.float32,
    )
    proj = lax.psum(partial_proj, "sub")
    state = tokens.astype(jnp.float32) + (1.0 + modulation[0]) * proj
    normed = normalize(state, modulation)
    gates = route(normed, router_weight, expert_ids)
    experts = router_weight.shape[1]
    topk = expert_ids.shape[1]
    flat = expert_ids.reshape(-1)
    picks = flat.shape[0]
    onehot = (flat[:, None] == jnp.arange(experts, dtype=jnp.int32)[None, :]).astype(jnp.int32)
    rank = jnp.sum((jnp.cumsum(onehot, 0) - 1) * onehot, 1)
    target = flat * CAP + rank
    hit = target[None, :] == jnp.arange(experts * CAP, dtype=jnp.int32)[:, None]
    filled = jnp.any(hit, 1)
    anchor = jnp.sum(jnp.where(hit, jnp.arange(picks, dtype=jnp.int32)[None, :], 0), 1) // topk
    slice_width = width // parts
    sent = lax.dynamic_slice_in_dim(normed, part * slice_width, slice_width, 1)
    sent_width = sent.shape[1]
    rows_out = jnp.where(filled[:, None], sent[anchor], jnp.zeros((), jnp.bfloat16))
    halves_here = gate_up_weight.shape[0]
    doubled = jnp.broadcast_to(
        rows_out.reshape(experts, 1, CAP, sent_width), (experts, 2, CAP, sent_width)
    )
    outgoing = doubled.reshape(devices, halves_here, CAP, sent_width)
    up_form = "sxcd,xgdf->sxcgf"
    down_form = "sxcf,xfd->sxcd"
    incoming = lax.all_to_all(outgoing, "dev", split_axis=0, concat_axis=0, tiled=True)
    both = jnp.einsum(
        up_form,
        lax.all_gather(incoming, "sub", axis=3, tiled=True),
        gate_up_weight,
        preferred_element_type=jnp.float32,
    )
    hidden = (jax.nn.silu(both[..., 0, :]) * both[..., 1, :]).astype(jnp.bfloat16)
    gathered = lax.all_gather(hidden, "sub", axis=hidden.ndim - 1, tiled=True)
    result = jnp.einsum(down_form, gathered, down_weight, preferred_element_type=jnp.float32)
    returned = lax.all_to_all(
        result.astype(jnp.bfloat16), "dev", split_axis=0, concat_axis=0, tiled=True
    )
    own_width = returned.shape[-1]
    arranged = returned.reshape(experts, 2, CAP, own_width)
    answers = arranged[flat, :, rank, :].reshape(count, topk, 2, own_width).astype(jnp.float32)
    combined = answers[:, :, 0] + answers[:, :, 1]
    routed = jnp.einsum("tk,tkd->td", gates, combined)
    own = lax.dynamic_slice_in_dim(state, part * slice_width, slice_width, 1)
    lift = lax.dynamic_slice_in_dim(modulation[3], part * slice_width, slice_width, 0)
    return (own + (1.0 + lift) * routed).astype(jnp.bfloat16)


def solution(mesh):
    return jax.shard_map(
        body,
        mesh=mesh,
        in_specs=(
            P(("groups", "dev"), None),
            P(("groups", "dev"), None, "sub"),
            P("dev", "sub"),
            P("groups", None),
            P(),
            P(("groups", "dev"), None),
            P("dev", None, None, "sub"),
            P("dev", None, "sub"),
        ),
        out_specs=P(("groups", "dev"), "sub"),
        check_vma=False,
    )
```

profile of v0, /device:TPU:0, one launch (start us, length us, event | category | flops | bytes accessed | tf_op | source)
XLA Modules:
  0.0 427.1 jit_solution(14000772186241778304)
XLA Ops:
  6.5 0.7 all-gather.4.cloned.1.call-update
  7.3 0.0 all-reduce.2.cloned.1.call-start
  7.3 1.1 slice.43
  8.4 0.3 copy.77
  8.7 1.3 collective-permute-start.1
  10.0 5.5 %collective-permute-start = (bf16[128,2,1024]{0,2,1:T(8,128)(2,1)S(1)}, bf16[128,2,1024]{0,2,1:T(8,128)(2,1)S(1)}, u32[]{:S(2)}, u32[]{:S(2)}) collective-permute-start(bf16[128,2,1024]{0,2,1:T(8,128)(2,1)S(1)} %copy.77), channel_id=1, source_target_pairs={{0,2},{2,4},{4,6},{6,8},{8,10},{10,12},{12,14},{1,3},{3,5},{5,7},{... | collective-permute-start | bytes 1572872 | tf_op jit(solution)/shard_map/ppermute | solution.py:24
  15.5 0.1 copy.55
  15.6 0.1 reshape.238
  15.7 0.1 eq.55
  15.8 1.2 reduce-window.6
  17.1 0.2 slice_reduce_fusion
  17.3 0.2 copy.78
  17.5 0.1 fusion.26
  17.7 0.2 fusion.24
  17.9 10.7 %collective-permute-done.1 = bf16[128,2,1024]{0,2,1:T(8,128)(2,1)S(1)} collective-permute-done((bf16[128,2,1024]{0,2,1:T(8,128)(2,1)S(1)}, bf16[128,2,1024]{0,2,1:T(8,128)(2,1)S(1)}, u32[]{:S(2)}, u32[]{:S(2)}) %collective-permute-start.1) | collective-permute-done | bytes 524320 | tf_op jit(solution)/shard_map/ppermute | solution.py:26
  28.6 13.9 %collective-permute-done = bf16[128,2,1024]{0,2,1:T(8,128)(2,1)S(1)} collective-permute-done((bf16[128,2,1024]{0,2,1:T(8,128)(2,1)S(1)}, bf16[128,2,1024]{0,2,1:T(8,128)(2,1)S(1)}, u32[]{:S(2)}, u32[]{:S(2)}) %collective-permute-start) | collective-permute-done | bytes 524320 | tf_op jit(solution)/shard_map/ppermute | solution.py:24
  42.4 0.2 pad_maximum_fusion
  42.6 0.2 fusion.37
  42.8 1.9 fusion.39
  44.7 1.8 convolution_convert_fusion
  46.5 49.4 %all-gather.4.cloned.1.call-done = bf16[2048,1024]{1,0:T(8,128)(2,1)} async-done(((bf16[256,1024]{1,0:T(8,128)(2,1)}), bf16[2048,1024]{1,0:T(8,128)(2,1)}) %all-gather.4.cloned.1.call-update) | async-done | bytes 4194320 | tf_op jit(solution)/shard_map/all_gather | solution.py:91
  95.8 4.7 %fusion.40 = f32[128,2048]{1,0:T(8,128)} fusion(bf16[128,1024]{0,1:T(8,128)(2,1)S(1)} %bitcast.105, bf16[2048,1024]{1,0:T(8,128)(2,1)} %all-gather.4.cloned.1.call-done), kind=kOutput, calls=%fused_computation.79 | convolution fusion | flops 536870912 | bytes 5505024 | tf_op jit(solution)/shard_map/dot_general | solution.py:89
  100.6 0.0 all-reduce.2.cloned.1.call-update
  100.6 0.0 all-gather.6.cloned.1.call-start
  100.6 0.2 fusion.19
  100.9 0.1 broadcast_in_dim.80
  101.0 0.2 select_reduce_fusion
  101.3 17.3 %all-reduce.2.cloned.1.call-done = f32[128,2048]{1,0:T(8,128)} async-done(((f32[128,2048]{1,0:T(8,128)}), f32[128,2048]{1,0:T(8,128)}) %all-reduce.2.cloned.1.call-update) | async-done | bytes 1048592 | tf_op jit(solution)/shard_map/psum | solution.py:95
  118.6 1.5 multiply_reduce_fusion
  120.1 1.0 copy-done.1
  121.1 0.2 add_convert_fusion
  121.3 0.8 copy-done.3
  122.1 3.6 gather_fusion
  125.7 2.4 gather.9
  128.0 0.2 broadcast_select_fusion
  128.3 2.0 copy.58
  130.3 3.7 broadcast_in_dim.85
  134.0 3.3 reshape.240
  137.3 2.4 copy.59
  139.7 76.7 %all_to_all.10 = bf16[8,16,12,1024]{3,1,2,0:T(8,128)(2,1)S(1)} all-to-all(bf16[8,16,12,1024]{3,1,2,0:T(8,128)(2,1)S(1)} %copy.59), channel_id=1, replica_groups=mesh['groups'=2,'dev'=8,'sub'=2] {'dev'}, dimensions={0} | all-to-all | bytes 6291456 | tf_op jit(solution)/shard_map/all_to_all | solution.py:120
  216.4 3.8 copy.60
  220.2 0.2 all-gather.8.cloned.1.call-start
  220.5 18.8 %all-gather.6.cloned.1.call-done = bf16[8,16,12,2048]{3,2,0,1:T(8,128)(2,1)} async-done(((bf16[8,16,12,1024]{3,2,0,1:T(8,128)(2,1)}), bf16[8,16,12,2048]{3,2,0,1:T(8,128)(2,1)}) %all-gather.6.cloned.1.call-update) | async-done | bytes 6291472 | tf_op jit(solution)/shard_map/all_gather | solution.py:123
  239.3 15.0 %fusion.8 = f32[8,16,12,2,192]{4,2,3,0,1:T(8,128)S(1)} fusion(bf16[16,2,2048,192]{2,3,1,0:T(8,128)(2,1)} %param.14, bf16[8,16,12,2048]{3,2,0,1:T(8,128)(2,1)} %all-gather.6.cloned.1.call-done), kind=kOutput, calls=%fused_computation.9 | convolution fusion | flops 2415919104 | bytes 33816576 | tf_op jit(solution)/shard_map/sxcd,xgdf->sxcgf/dot_general | solution.py:121
  254.3 0.7 fusion.14
  255.0 11.8 %copy.62 = bf16[8,16,12,192]{1,0,2,3:T(8,128)(2,1)} copy(bf16[8,16,12,192]{3,2,0,1:T(8,128)(2,1)S(1)} %fusion.14) | data formatting | bytes 1179648 | tf_op jit(solution)/shard_map/convert_element_type | solution.py:127
  266.8 23.1 %all-gather.8.cloned.1.call-done = bf16[8,16,12,384]{1,0,2,3:T(8,128)(2,1)} async-done(((bf16[8,16,12,192]{1,0,2,3:T(8,128)(2,1)}), bf16[8,16,12,384]{1,0,2,3:T(8,128)(2,1)}) %all-gather.8.cloned.1.call-update) | async-done | bytes 1179664 | tf_op jit(solution)/shard_map/all_gather | solution.py:128
  289.9 17.8 %copy.63 = bf16[8,16,12,384]{3,2,0,1:T(8,128)(2,1)S(1)} copy(bf16[8,16,12,384]{1,0,2,3:T(8,128)(2,1)} %all-gather.8.cloned.1.call-done) | data formatting | bytes 2359296 | tf_op jit(solution)/shard_map/all_gather | solution.py:128
  307.7 6.9 %convert_bitcast_fusion = bf16[8,16,12,1024]{3,2,0,1:T(8,128)(2,1)S(1)} fusion(bf16[8,16,12,384]{3,2,0,1:T(8,128)(2,1)S(1)} %copy.63, bf16[16,384,1024]{2,1,0:T(8,128)(2,1)} %param.15), kind=kOutput, calls=%fused_computation.8 | convolution fusion | flops 1209532416 | bytes 16908288 | tf_op jit(solution)/shard_map/sxcf,xfd->sxcd/dot_general | solution.py:129
  314.7 3.5 copy.64
  318.2 5.8 %all-to-all-start.1 = ((bf16[8,16,12,1024]{3,1,2,0:T(8,128)(2,1)}), bf16[8,16,12,1024]{3,1,2,0:T(8,128)(2,1)S(1)}, u32[]{:S(2)}, u32[]{:S(2)}) async-start(bf16[8,16,12,1024]{3,1,2,0:T(8,128)(2,1)} %copy.64), calls=%async_computation.1 | async-start | bytes 6291456 | tf_op jit(solution)/shard_map/all_to_all | solution.py:130
  323.9 0.1 reshape.242
  324.1 1.3 fusion.41
  325.5 0.2 copy.74
  325.7 69.4 %all-to-all-done.1 = bf16[8,16,12,1024]{3,1,2,0:T(8,128)(2,1)S(1)} async-done(((bf16[8,16,12,1024]{3,1,2,0:T(8,128)(2,1)}), bf16[8,16,12,1024]{3,1,2,0:T(8,128)(2,1)S(1)}, u32[]{:S(2)}, u32[]{:S(2)}) %all-to-all-start.1) | async-done | bytes 3145760 | tf_op jit(solution)/shard_map/all_to_all | solution.py:130
  395.1 2.0 copy.65
  397.1 4.0 reshape.241
  401.1 5.2 %copy.67 = bf16[64,2,12,1024]{3,1,2,0:T(2,128)(2,1)} copy(bf16[64,2,12,1024]{3,1,0,2:T(2,128)(2,1)S(1)} %reshape.241) | data formatting | bytes 6291456 | tf_op jit(solution)/shard_map/reshape | solution.py:134
  406.3 7.5 %gather_fusion.1 = bf16[512,2,1024]{2,1,0:T(2,128)(2,1)S(1)} fusion(bf16[64,2,12,1024]{3,1,2,0:T(2,128)(2,1)} %copy.67, s32[512]{0:T(512)S(1)} %bitcast.100), kind=kCustom, calls=%fused_computation.1 | custom fusion | bytes 4198400 | tf_op jit(solution)/shard_map/gather | solution.py:135
  413.9 2.0 convert.1
  415.8 2.7 slice_add_fusion
  418.5 0.7 fusion.15
  419.2 0.5 copy-done.2
  419.7 0.8 fusion.22
  (32 shorter events, 0.3 us)
Async XLA Ops:
  6.5 317.5 %copy-start = (bf16[2048,64]{0,1:T(8,128)(2,1)S(1)}, bf16[2048,64]{0,1:T(8,128)(2,1)}, u32[]{:S(2)}) copy-start(bf16[2048,64]{0,1:T(8,128)(2,1)} %param.12) | copy-start | bytes 786436
  6.5 10.8 %slice-start = ((bf16[128,3,1024]{2,0,1:T(8,128)(2,1)}), bf16[128,1,1024]{2,0,1:T(8,128)(2,1)S(1)}, s32[]{:S(2)}) async-start(bf16[128,3,1024]{2,0,1:T(8,128)(2,1)} %param.9), calls=%async_computation.6 | async-start | bytes 524288 | tf_op jit(solution)/shard_map/slice | solution.py:83
  6.5 8.9 %copy-start.6 = (s32[128,4]{0,1:T(4,128)S(1)}, s32[128,4]{0,1:T(4,128)}, u32[]{:S(2)}) copy-start(s32[128,4]{0,1:T(4,128)} %param.13) | copy-start | bytes 6148
  6.5 89.3 %all-gather.4.cloned.1.call-start = ((), (), s32[]{:S(2)}) async-start(), calls=%async_computation.2 | async-start | bytes 4718592 | tf_op jit(solution)/shard_map/all_gather | solution.py:91
  7.3 111.3 %all-reduce.2.cloned.1.call-start = ((), (), s32[]{:S(2)}) async-start(), calls=%async_computation.3 | async-start | bytes 2097152 | tf_op jit(solution)/shard_map/psum | solution.py:95
  8.7 19.9 %collective-permute-start.1 = (bf16[128,2,1024]{0,2,1:T(8,128)(2,1)S(1)}, bf16[128,2,1024]{0,2,1:T(8,128)(2,1)S(1)}, u32[]{:S(2)}, u32[]{:S(2)}) collective-permute-start(bf16[128,2,1024]{0,2,1:T(8,128)(2,1)S(1)} %copy.77), channel_id=1, source_target_pairs={{2,0},{4,2},{6,4},{8,6},{10,8},{12,10},{14,12},{3,1},{5,3},{7,5},{... | collective-permute-start | bytes 1572872 | tf_op jit(solution)/shard_map/ppermute | solution.py:26
  10.0 32.5 %collective-permute-start = (bf16[128,2,1024]{0,2,1:T(8,128)(2,1)S(1)}, bf16[128,2,1024]{0,2,1:T(8,128)(2,1)S(1)}, u32[]{:S(2)}, u32[]{:S(2)}) collective-permute-start(bf16[128,2,1024]{0,2,1:T(8,128)(2,1)S(1)} %copy.77), channel_id=1, source_target_pairs={{0,2},{2,4},{4,6},{6,8},{8,10},{10,12},{12,14},{1,3},{3,5},{5,7},{... | collective-permute-start | bytes 1572872 | tf_op jit(solution)/shard_map/ppermute | solution.py:24
  95.8 5.5 %copy-start.5 = (f32[4,2048]{1,0:T(4,128)S(1)}, f32[4,2048]{1,0:T(4,128)}, u32[]{:S(2)}) copy-start(f32[4,2048]{1,0:T(4,128)} %param.11) | copy-start | bytes 98308
  95.8 22.8 %copy-start.4 = (bf16[128,2048]{1,0:T(8,128)(2,1)S(1)}, bf16[128,2048]{1,0:T(8,128)(2,1)}, u32[]{:S(2)}) copy-start(bf16[128,2048]{1,0:T(8,128)(2,1)} %param.8) | copy-start | bytes 1572868
  100.6 138.7 %all-gather.6.cloned.1.call-start = ((), (), s32[]{:S(2)}) async-start(), calls=%async_computation.4 | async-start | bytes 12582912 | tf_op jit(solution)/shard_map/all_gather | solution.py:123
  120.1 1.0 copy-start.1
  121.3 0.8 copy-start.3
  220.2 69.7 %all-gather.8.cloned.1.call-start = ((), (), s32[]{:S(2)}) async-start(), calls=%async_computation.5 | async-start | bytes 14155776 | tf_op jit(solution)/shard_map/all_gather | solution.py:128
  318.2 76.9 %all-to-all-start.1 = ((bf16[8,16,12,1024]{3,1,2,0:T(8,128)(2,1)}), bf16[8,16,12,1024]{3,1,2,0:T(8,128)(2,1)S(1)}, u32[]{:S(2)}, u32[]{:S(2)}) async-start(bf16[8,16,12,1024]{3,1,2,0:T(8,128)(2,1)} %copy.64), calls=%async_computation.1 | async-start | bytes 6291456 | tf_op jit(solution)/shard_map/all_to_all | solution.py:130
  418.5 1.2 copy-start.2
Sparse Core Ops, SparseCore 0:
  9.5 86.2 all-gather.3
  100.7 17.8 all-reduce.1
  220.3 18.8 all-gather.5
  267.0 22.9 all-gather.7
where the time goes:
time: 428 us; the launch traced here: 427 us
  waiting for transfers between devices  203 us (47%)
  local copies, waits for them, and re-layouts  77.9 us (18%)
  blocking collectives  76.7 us (18%)
  matrix products  32.4 us (8%)
  between operations  13.5 us (3%)
  starting transfers between devices  12.9 us (3%)
  other arithmetic  10.5 us (2%)
    all_to_all x1, blocking collectives, body(): lax.all_to_all(outgoing, 'dev', split_axis=0, concat_axis=0, tiled=True)  76.7 us
    all_to_all x1, waiting for transfers between devices, body(): lax.all_to_all(result.astype(jnp.bfloat16), 'dev', split_axis=0, concat_a...  69.4 us
    all_gather x1, waiting for transfers between devices, body(): lax.all_gather(out_weight, 'dev', axis=0, tiled=True)  49.4 us
    all_gather x1, waiting for transfers between devices, body(): gathered = lax.all_gather(hidden, 'sub', axis=hidden.ndim - 1, tiled=True)  23.1 us
    all_gather x1, waiting for transfers between devices, body(): lax.all_gather(incoming, 'sub', axis=3, tiled=True)  18.8 us
    all_gather x1, local copies, waits for them, and re-layouts, body(): gathered = lax.all_gather(hidden, 'sub', axis=hidden.ndim - 1, tiled=True)  17.8 us
    psum x1, waiting for transfers between devices, body(): proj = lax.psum(partial_proj, 'sub')  17.3 us
    dot_general x1, matrix products, body(): jnp.einsum(up_form, lax.all_gather(incoming, 'sub', axis=3, tiled=True),...  15 us
  transfers between devices with their start and end apart: 7, of which 7 were waited for; matrix products, arithmetic and copies ran while one was open for 2% of the time, Pallas kernels for 0%

commit v1 on v0

--- a/solution.py
+++ b/solution.py
@@ -1,16 +1,340 @@
+import functools
 import math
 
 import jax
 import jax.numpy as jnp
 from jax import lax
+from jax.experimental import pallas as pl
+from jax.experimental.pallas import tpu as pltpu
 from jax.sharding import PartitionSpec as P
 
 HEAD = 128
 CAP = 12
-
+SLOTS = 16
+TILE = 16
 
 EPS = 1e-06
 NEG = -1e30
+F32 = jnp.float32
+BF16 = jnp.bfloat16
+
+NT = (((1,), (1,)), ((), ()))
+
+
+def vmem(mib):
+    return pltpu.CompilerParams(vmem_limit_bytes=mib * 2**20)
+
+
+def whole():
+    return pl.BlockSpec(memory_space=pltpu.VMEM)
+
+
+def attention_kernel(q_ref, before_ref, own_ref, after_ref, mixed_ref):
+    count, width = q_ref.shape
+    place = lax.axis_index("dev")
+    last = lax.axis_size("dev") - 1
+    row = lax.broadcasted_iota(jnp.int32, (count, count), 0)
+    col = lax.broadcasted_iota(jnp.int32, (count, count), 1)
+    see_before = (col >= row) & (place > 0)
+    see_after = (col <= row) & (place < last)
+    scale = 1.0 / math.sqrt(HEAD)
+
+    def scored(q, ref, lanes):
+        return lax.dot_general(q, ref[:, lanes], NT, preferred_element_type=F32) * scale
+
+    for head in range(width // HEAD):
+        lanes = slice(head * HEAD, (head + 1) * HEAD)
+        vlanes = slice(width + head * HEAD, width + (head + 1) * HEAD)
+        q = q_ref[:, lanes]
+        sb = jnp.where(see_before, scored(q, before_ref, lanes), NEG)
+        so = scored(q, own_ref, lanes)
+        sa = jnp.where(see_after, scored(q, after_ref, lanes), NEG)
+        top = jnp.max(jnp.maximum(jnp.maximum(sb, so), sa), 1, keepdims=True)
+        wb, wo, wa = jnp.exp(sb - top), jnp.exp(so - top), jnp.exp(sa - top)
+        inv = 1.0 / jnp.sum(wb + wo + wa, 1, keepdims=True)
+        out = jnp.dot((wo * inv).astype(BF16), own_ref[:, vlanes], preferred_element_type=F32)
+        out += jnp.dot((wb * inv).astype(BF16), before_ref[:, vlanes], preferred_element_type=F32)
+        out += jnp.dot((wa * inv).astype(BF16), after_ref[:, vlanes], preferred_element_type=F32)
+        mixed_ref[:, lanes] = out.astype(BF16)
+
+
+def projection_kernel(steps, pieces, *refs):
+    mixed_ref, other_ref = refs[0], refs[1]
+    weight_refs = refs[2 : 2 + len(pieces)]
+    keep_ref, send_ref, both_ref = refs[2 + len(pieces) :]
+    count = mixed_ref.shape[0]
+    half = steps // 2
+    chunk = keep_ref.shape[1] // half
+    z = lax.axis_index("dev") // 2
+    part = lax.axis_index("sub")
+    group = lax.axis_index("groups")
+    for (hop, side), w_ref in zip(pieces, weight_refs):
+        rows = w_ref.shape[0]
+        target = jnp.bitwise_xor(z, hop)
+        away = jnp.where(target // half == part, 0, 1)
+        lane = (target % half) * chunk
+        if side is not None:
+            lane += (group if side == 0 else 1 - group) * rows
+        lane = pl.multiple_of(lane, 128)
+        for block, ref in enumerate((mixed_ref, other_ref)):
+            both_ref[away, block * count : (block + 1) * count, pl.ds(lane, rows)] = (
+                lax.dot_general(ref[...], w_ref[...], NT, preferred_element_type=F32)
+            )
+    keep_ref[...] = both_ref[0]
+    send_ref[...] = both_ref[1]
+
+
+def state_kernel(keep_ref, got_ref, near_ref, far_ref, ids_ref, mod_ref, out_ref):
+    count, lanes = near_ref.shape
+    chunk = mod_ref.shape[1] // lax.axis_size("dev")
+    side = lax.axis_index("dev") % 2
+    part = lax.axis_index("sub")
+    for i in range(lanes // chunk):
+        at = pl.multiple_of(part * 2 * lanes + (2 * i + side) * chunk, 128)
+        lift = 1.0 + mod_ref[0:1, pl.ds(at, chunk)]
+        cols = slice(i * chunk, (i + 1) * chunk)
+        for block, ref in enumerate((near_ref, far_ref)):
+            rows = slice(block * count, (block + 1) * count)
+            proj = keep_ref[rows, cols] + got_ref[rows, cols]
+            out_ref[rows, cols] = (ref[:, cols].astype(F32) + lift * proj).astype(BF16)
+    out_ref[2 * count :, :] = ids_ref[...]
+
+
+def hidden_kernel(steps, local, topk, *refs):
+    shard_refs = refs[: 4 * steps]
+    mod_ref, router_ref, w_ref = refs[4 * steps : 4 * steps + 3]
+    hidden_ref, state_ref, back_ref = refs[4 * steps + 3 : 4 * steps + 6]
+    full_ref, rows_ref, gate_ref = refs[4 * steps + 6 :]
+    step = pl.program_id(0)
+    count, width = full_ref.shape
+    lanes = shard_refs[0].shape[1]
+    device = lax.axis_index("dev")
+    side = device % 2
+    part = lax.axis_index("sub")
+    chunk = width // lax.axis_size("dev")
+    experts = router_ref.shape[0]
+    slots = local * SLOTS
+
+    @pl.when(step == 0)
+    def _():
+        before = lax.broadcasted_iota(jnp.int32, (count, count), 0)
+        after = lax.broadcasted_iota(jnp.int32, (count, count), 1)
+        earlier = (before < after).astype(F32).astype(BF16)
+        slot = lax.broadcasted_iota(jnp.int32, (slots, count), 0) % SLOTS
+        mine = lax.broadcasted_iota(jnp.int32, (local, count), 0) + device * local
+        every = lax.broadcasted_iota(jnp.int32, (experts, count), 0)
+        for source in range(2 * steps):
+            hop, cross = source // 2, source % 2
+            for far_half in range(2):
+                for far_side in range(2):
+                    ref = shard_refs[4 * hop + 2 * far_half + far_side]
+                    top = (cross ^ far_side) * count
+                    half = part if far_half == 0 else 1 - part
+                    parity = side if far_side == 0 else 1 - side
+                    for i in range(lanes // chunk):
+                        block = ref[top : top + count, i * chunk : (i + 1) * chunk]
+                        at = (2 * i + parity) * chunk
+                        full_ref[:, pl.ds(pl.multiple_of(half * 2 * lanes + at, 128), chunk)] = block
+                        if source == 0 and far_half == 0:
+                            state_ref[:, pl.ds(pl.multiple_of(at, 128), chunk)] = block
+            state = full_ref[...].astype(F32)
+            scale = lax.rsqrt(jnp.mean(state * state, 1, keepdims=True) + EPS)
+            normed = state * scale * (1.0 + mod_ref[2:3, :]) + mod_ref[1:2, :]
+            normed = normed.astype(BF16)
+            ids = shard_refs[4 * hop + cross][2 * count : 2 * count + TILE, :]
+            ids = ids.astype(F32)[0:1, :].astype(jnp.int32)
+            named = [ids[:, k * count : (k + 1) * count] for k in range(topk)]
+            hot = sum((mine == n).astype(F32) for n in named)
+            rank = jnp.dot(hot.astype(BF16), earlier, preferred_element_type=F32)
+            rank = jnp.where(hot > 0.0, rank, -1.0)
+            rank = jnp.concatenate(
+                [jnp.broadcast_to(rank[e : e + 1], (SLOTS, count)) for e in range(local)]
+            )
+            pick = rank == slot.astype(F32)
+            chosen = jnp.dot(
+                jnp.where(pick, 1.0, 0.0).astype(BF16), normed, preferred_element_type=F32
+            ).astype(BF16)
+            for e in range(local):
+                rows_ref[e, source * SLOTS : (source + 1) * SLOTS, :] = chosen[
+                    e * SLOTS : (e + 1) * SLOTS
+                ]
+            logits = lax.dot_general(router_ref[...], normed, NT, preferred_element_type=F32)
+            lifted = sum(jnp.where(every == n, 1.0, 0.0) for n in named) * jax.nn.sigmoid(logits)
+            gate_ref[...] = lifted / jnp.sum(lifted, 0, keepdims=True)
+            here = gate_ref[pl.ds(pl.multiple_of(device * local, local), local), :]
+            here = jnp.concatenate(
+                [jnp.broadcast_to(here[e : e + 1], (SLOTS, count)) for e in range(local)]
+            )
+            back_ref[source] = jnp.where(pick, here, 0.0).T.astype(BF16)
+
+    rows = rows_ref[step // 2]
+    gate = jnp.dot(rows, w_ref[0, 0], preferred_element_type=F32)
+    up = jnp.dot(rows, w_ref[0, 1], preferred_element_type=F32)
+    hidden_ref[0] = (jax.nn.silu(gate) * up).astype(BF16)
+
+
+def output_kernel(sources, near_ref, far_ref, w_ref, back_ref, *refs):
+    out_refs, held_ref = refs[:sources], refs[sources]
+    step = pl.program_id(0)
+    part = lax.axis_index("sub")
+    units = near_ref.shape[2]
+    total = None
+    for half in range(2):
+        for ref, who in ((near_ref, part), (far_ref, 1 - part)):
+            at = pl.multiple_of(who * units, 64)
+            piece = jnp.dot(ref[half], w_ref[half, pl.ds(at, units), :], preferred_element_type=F32)
+            total = piece if total is None else total + piece
+    total = total.astype(BF16)
+    row = pl.multiple_of(step * SLOTS, SLOTS)
+    for source in range(sources):
+        held_ref[source, pl.ds(row, SLOTS), :] = total[source * SLOTS : (source + 1) * SLOTS]
+
+    @pl.when(step == pl.num_programs(0) - 1)
+    def _():
+        for source in range(sources):
+            out_refs[source][...] = jnp.dot(
+                back_ref[source], held_ref[source], preferred_element_type=F32
+            ).astype(BF16)
+
+
+def gathered_body(
+    tokens,
+    query_key_value,
+    out_weight,
+    modulation,
+    router_weight,
+    expert_ids,
+    gate_up_weight,
+    down_weight,
+):
+    count, width = tokens.shape
+    devices = lax.axis_size("dev")
+    groups = lax.axis_size("groups")
+    steps = devices // 2
+    side = lax.axis_index("dev") % 2
+    part = lax.axis_index("sub")
+    group = lax.axis_index("groups")
+    local_width = query_key_value.shape[2]
+    chunk = width // devices
+    lanes = width // 4
+    halves_here = gate_up_weight.shape[0]
+    local = halves_here // 2
+    experts = router_weight.shape[1]
+    topk = expert_ids.shape[1]
+    struct = jax.ShapeDtypeStruct
+
+    def hop(x, flip):
+        return lax.ppermute(x, "dev", [(i, i ^ flip) for i in range(devices)])
+
+    def swap(x):
+        return lax.ppermute(x, "sub", [(0, 1), (1, 0)])
+
+    query = query_key_value[:, 0]
+    pair = jnp.concatenate([query_key_value[:, 1], query_key_value[:, 2]], 1)
+    before = lax.ppermute(pair, "dev", [(i, i + 1) for i in range(devices - 1)])
+    after = lax.ppermute(pair, "dev", [(i + 1, i) for i in range(devices - 1)])
+
+    cut = tokens.reshape(count, 2, devices // 4, 2, chunk)
+    cut = lax.dynamic_index_in_dim(cut, part, 1, keepdims=False)
+    near = lax.dynamic_index_in_dim(cut, side, 2, keepdims=False).reshape(count, lanes)
+    far = lax.dynamic_index_in_dim(cut, 1 - side, 2, keepdims=False).reshape(count, lanes)
+    far = hop(far, 1)
+
+    pieces, weights = [(0, None)], [out_weight]
+    if groups == 2:
+        rows = out_weight.shape[0] // 2
+        sent = lax.dynamic_slice_in_dim(out_weight, group * rows, rows, 0)
+        for flip in range(1, steps):
+            mine = hop(sent, 2 * flip)
+            theirs = lax.ppermute(mine, "groups", [(0, 1), (1, 0)])
+            pieces += [(flip, 0), (flip, 1)]
+            weights += [mine, theirs]
+    else:
+        for flip in range(1, steps):
+            pieces.append((flip, None))
+            weights.append(hop(out_weight, 2 * flip))
+
+    mixed = pl.pallas_call(
+        attention_kernel,
+        out_shape=struct((count, local_width), BF16),
+        in_specs=[whole()] * 4,
+        out_specs=whole(),
+        compiler_params=vmem(32),
+    )(query, before, pair, after)
+    keep, send = pl.pallas_call(
+        functools.partial(projection_kernel, steps, tuple(pieces)),
+        out_shape=[struct((2 * count, lanes), F32)] * 2,
+        in_specs=[whole()] * (2 + len(weights)),
+        out_specs=[whole()] * 2,
+        scratch_shapes=[pltpu.VMEM((2, 2 * count, lanes), F32)],
+        compiler_params=vmem(32),
+    )(mixed, hop(mixed, 1), *weights)
+    ids = expert_ids.T.reshape(1, topk * count).astype(BF16)
+    ids = jnp.pad(ids, ((0, TILE - 1), (0, lanes - topk * count)))
+    shard = pl.pallas_call(
+        state_kernel,
+        out_shape=struct((2 * count + TILE, lanes), BF16),
+        in_specs=[whole()] * 6,
+        out_specs=whole(),
+        compiler_params=vmem(32),
+    )(keep, swap(send), near, far, ids, modulation)
+
+    column = [shard] + [hop(shard, 2 * flip) for flip in range(1, steps)]
+    shards = []
+    for block in column:
+        crossed = hop(block, 1)
+        shards += [block, crossed, swap(block), swap(crossed)]
+
+    sources = 2 * steps
+    slots = local * SLOTS
+    room = sources * SLOTS
+    units = gate_up_weight.shape[3]
+    hidden, state, back = pl.pallas_call(
+        functools.partial(hidden_kernel, steps, local, topk),
+        grid=(halves_here,),
+        out_shape=[
+            struct((halves_here, room, units), BF16),
+            struct((count, 2 * lanes), BF16),
+            struct((sources, count, slots), BF16),
+        ],
+        in_specs=[whole()] * (4 * steps + 2)
+        + [pl.BlockSpec((1, 2, width, units), lambda i: (i, 0, 0, 0))],
+        out_specs=[
+            pl.BlockSpec((1, room, units), lambda i: (i, 0, 0)),
+            whole(),
+            whole(),
+        ],
+        scratch_shapes=[
+            pltpu.VMEM((count, width), BF16),
+            pltpu.VMEM((local, room, width), BF16),
+            pltpu.VMEM((experts, count), F32),
+        ],
+        compiler_params=vmem(48),
+    )(*shards, modulation, router_weight.T, gate_up_weight)
+
+    share = pl.pallas_call(
+        functools.partial(output_kernel, sources),
+        grid=(local,),
+        out_shape=[struct((count, 2 * lanes), BF16)] * sources,
+        in_specs=[
+            pl.BlockSpec((2, room, units), lambda i: (i, 0, 0)),
+            pl.BlockSpec((2, room, units), lambda i: (i, 0, 0)),
+            pl.BlockSpec((2, 2 * units, 2 * lanes), lambda i: (i, 0, 0)),
+            whole(),
+        ],
+        out_specs=[whole()] * sources,
+        scratch_shapes=[pltpu.VMEM((sources, slots, 2 * lanes), BF16)],
+        compiler_params=vmem(32),
+    )(hidden, swap(hidden), down_weight, back)
+
+    routed = None
+    for flip in range(steps - 1, -1, -1):
+        mine = share[2 * flip].astype(F32) + hop(share[2 * flip + 1], 1).astype(F32)
+        if flip:
+            mine = hop(mine.astype(BF16), 2 * flip).astype(F32)
+        routed = mine if routed is None else routed + mine
+    lift = lax.dynamic_slice_in_dim(modulation[3], part * 2 * lanes, 2 * lanes, 0)
+    return (state.astype(F32) + (1.0 + lift) * routed).astype(BF16)
 
 
 def extended(cells, sides, width):
@@ -61,7 +385,7 @@
     return lifted / jnp.sum(lifted, -1, keepdims=True)
 
 
-def body(
+def exchanged_body(
     tokens,
     query_key_value,
     out_weight,
@@ -100,16 +424,18 @@
     topk = expert_ids.shape[1]
     flat = expert_ids.reshape(-1)
     picks = flat.shape[0]
-    onehot = (flat[:, None] == jnp.arange(experts, dtype=jnp.int32)[None, :]).astype(jnp.int32)
-    rank = jnp.sum((jnp.cumsum(onehot, 0) - 1) * onehot, 1)
+    onehot = (flat[:, None] == jnp.arange(experts, dtype=jnp.int32)[None, :]).astype(BF16)
+    order = jnp.arange(picks, dtype=jnp.int32)
+    earlier = (order[None, :] < order[:, None]).astype(BF16)
+    ahead = jnp.dot(earlier, onehot, preferred_element_type=F32)
+    rank = jnp.sum(ahead * onehot.astype(F32), 1).astype(jnp.int32)
     target = flat * CAP + rank
     hit = target[None, :] == jnp.arange(experts * CAP, dtype=jnp.int32)[:, None]
-    filled = jnp.any(hit, 1)
-    anchor = jnp.sum(jnp.where(hit, jnp.arange(picks, dtype=jnp.int32)[None, :], 0), 1) // topk
+    owner = jnp.any(hit.reshape(experts * CAP, count, topk), 2).astype(BF16)
     slice_width = width // parts
     sent = lax.dynamic_slice_in_dim(normed, part * slice_width, slice_width, 1)
     sent_width = sent.shape[1]
-    rows_out = jnp.where(filled[:, None], sent[anchor], jnp.zeros((), jnp.bfloat16))
+    rows_out = jnp.dot(owner, sent, preferred_element_type=F32).astype(BF16)
     halves_here = gate_up_weight.shape[0]
     doubled = jnp.broadcast_to(
         rows_out.reshape(experts, 1, CAP, sent_width), (experts, 2, CAP, sent_width)
@@ -132,12 +458,40 @@
     )
     own_width = returned.shape[-1]
     arranged = returned.reshape(experts, 2, CAP, own_width)
-    answers = arranged[flat, :, rank, :].reshape(count, topk, 2, own_width).astype(jnp.float32)
-    combined = answers[:, :, 0] + answers[:, :, 1]
-    routed = jnp.einsum("tk,tkd->td", gates, combined)
+    combined = arranged[:, 0].astype(F32) + arranged[:, 1].astype(F32)
+    share = jnp.sum(
+        jnp.where(hit.reshape(experts * CAP, count, topk), gates[None], 0.0), 2
+    )
+    routed = lax.dot_general(
+        share,
+        combined.reshape(experts * CAP, own_width),
+        (((0,), (0,)), ((), ())),
+        precision=lax.Precision.HIGHEST,
+        preferred_element_type=F32,
+    )
     own = lax.dynamic_slice_in_dim(state, part * slice_width, slice_width, 1)
     lift = lax.dynamic_slice_in_dim(modulation[3], part * slice_width, slice_width, 0)
     return (own + (1.0 + lift) * routed).astype(jnp.bfloat16)
+
+
+def body(*arrays):
+    tokens, router_weight, expert_ids, gate_up_weight = arrays[0], arrays[4], arrays[5], arrays[6]
+    devices = lax.axis_size("dev")
+    count, width = tokens.shape
+    local = gate_up_weight.shape[0] // 2
+    fits = (
+        lax.axis_size("sub") == 2
+        and devices >= 4
+        and devices & (devices - 1) == 0
+        and gate_up_weight.shape[0] % 2 == 0
+        and width % (devices * 128) == 0
+        and count % HEAD == 0
+        and expert_ids.shape[1] * count <= width // 4
+        and router_weight.shape[1] <= 256
+    )
+    if fits and count * devices <= 2 * local * devices * CAP:
+        return gathered_body(*arrays)
+    return exchanged_body(*arrays)
 
 
 def solution(mesh):

time: 428 us -> 224 us (0.52)
  waiting for transfers between devices: 203 us -> 94.8 us
  blocking collectives: 76.7 us -> 0 us
  matrix products: 32.4 us -> 0 us
  Pallas kernels: 0 us -> 32.4 us
  starting transfers between devices: 12.9 us -> 32.8 us
  local copies, waits for them, and re-layouts: 77.9 us -> 58.6 us
  between operations: 13.5 us -> 0.3 us
  other arithmetic: 10.5 us -> 2.85 us
    all_gather x3 -> x0, waiting for transfers between devices: 91.3 us -> none  [the longest x1 49.4 us: body(): lax.all_gather(out_weight, 'dev', axis=0, tiled=True)]
    all_to_all x1 -> x0, blocking collectives: 76.7 us -> none  [body(): lax.all_to_all(outgoing, 'dev', split_axis=0, concat_axis=0, tiled=True)]
    ppermute x2 -> x34, waiting for transfers between devices: 24.6 us -> 94.8 us  [the longest x19 88.2 us: hop(): return lax.ppermute(x, 'dev', [(i, i ^ flip) for i in range(devices)])]
    all_to_all x1 -> x0, waiting for transfers between devices: 69.4 us -> none  [body(): lax.all_to_all(result.astype(jnp.bfloat16), 'dev', split_axis=0, concat_a...]
    unnamed x17 -> x22, local copies, waits for them, and re-layouts: 2.85 us -> 51.1 us
    pallas_call x0 -> x5, Pallas kernels: none -> 32.4 us  [the longest x1 23.5 us: gathered_body(): pl.pallas_call(functools.partial(hidden_kernel, steps, local, topk), grid...]
    dot_general x6 -> x0, matrix products: 30.5 us -> none  [the longest x1 15 us: body(): jnp.einsum(up_form, lax.all_gather(incoming, 'sub', axis=3, tiled=True),...]
    ppermute x2 -> x34, starting transfers between devices: 6.8 us -> 32.8 us  [the longest x19 21.5 us: hop(): return lax.ppermute(x, 'dev', [(i, i ^ flip) for i in range(devices)])]
  transfers between devices with their start and end apart: 7 -> 34, of which waited for: 7 -> 16; matrix products, arithmetic and copies ran while one was open for 2% -> 20% of each run, Pallas kernels for 0% -> 1%
where the time goes in v1:
time: 224 us; the launch traced here: 222 us
  waiting for transfers between devices  94.8 us (42%)
  local copies, waits for them, and re-layouts  58.6 us (26%)
  starting transfers between devices  32.8 us (15%)
  Pallas kernels  32.4 us (14%)
  other arithmetic  2.85 us (1%)
    ppermute x19, waiting for transfers between devices, hop(): return lax.ppermute(x, 'dev', [(i, i ^ flip) for i in range(devices)])  88.2 us
    unnamed x22, local copies, waits for them, and re-layouts  51.1 us
    pallas_call x1, Pallas kernels, gathered_body(): pl.pallas_call(functools.partial(hidden_kernel, steps, local, topk), grid...  23.5 us
    ppermute x19, starting transfers between devices, hop(): return lax.ppermute(x, 'dev', [(i, i ^ flip) for i in range(devices)])  21.5 us
    ppermute x1, starting transfers between devices, gathered_body(): before = lax.ppermute(pair, 'dev', [(i, i + 1) for i in range(devices - 1)])  4.88 us
    ppermute x3, waiting for transfers between devices, gathered_body(): theirs = lax.ppermute(mine, 'groups', [(0, 1), (1, 0)])  4.62 us
  transfers between devices with their start and end apart: 34, of which 16 were waited for; matrix products, arithmetic and copies ran while one was open for 20% of the time, Pallas kernels for 1%

profile of v1, /device:TPU:0, one launch (start us, length us, event | category | flops | bytes accessed | tf_op | source)
XLA Modules:
  0.0 221.8 jit_solution(16268266361773777265)
XLA Ops:
  0.0 1.2 slice_bitcast_fusion.1
  1.2 4.9 %collective-permute-start = (bf16[128,2048]{1,0:T(8,128)(2,1)S(1)}, bf16[128,2048]{1,0:T(8,128)(2,1)S(1)}, u32[]{:S(2)}, u32[]{:S(2)}) collective-permute-start(bf16[128,2048]{1,0:T(8,128)(2,1)S(1)} %pad_maximum_fusion.own_ref), channel_id=1, source_target_pairs={{0,2},{2,4},{4,6},{6,8},{8,10},{10,12},{12,14},{1,3},{3,5},{5,7},{... | collective-permute-start | bytes 1572872 | tf_op jit(solution)/shard_map/ppermute | solution.py:234
  6.1 1.3 collective-permute-start.1
  7.4 1.0 constant_dynamic-slice_fusion
  8.4 3.7 %collective-permute-start.3 = (bf16[128,1024]{1,0:T(8,128)(2,1)S(1)}, bf16[128,1024]{1,0:T(8,128)(2,1)S(1)}, u32[]{:S(2)}, u32[]{:S(2)}) collective-permute-start(bf16[128,1024]{1,0:T(8,128)(2,1)S(1)} %constant_dynamic-slice_fusion), channel_id=1, source_target_pairs={{0,4},{2,6},{4,0},{6,2},{8,12},{10,14},{12,8},{14,10},{1,5},{3,7},... | collective-permute-start | bytes 786440 | tf_op jit(solution)/shard_map/ppermute | solution.py:227
  12.0 2.6 %collective-permute-start.5 = (bf16[128,1024]{1,0:T(8,128)(2,1)S(1)}, bf16[128,1024]{1,0:T(8,128)(2,1)S(1)}, u32[]{:S(2)}, u32[]{:S(2)}) collective-permute-start(bf16[128,1024]{1,0:T(8,128)(2,1)S(1)} %constant_dynamic-slice_fusion), channel_id=1, source_target_pairs={{0,8},{2,10},{4,12},{6,14},{8,0},{10,2},{12,4},{14,6},{1,9},{3,11}... | collective-permute-start | bytes 786440 | tf_op jit(solution)/shard_map/ppermute | solution.py:227
  14.6 18.8 %collective-permute-done.3.refs_3_ = bf16[128,1024]{1,0:T(8,128)(2,1)S(1)} collective-permute-done((bf16[128,1024]{1,0:T(8,128)(2,1)S(1)}, bf16[128,1024]{1,0:T(8,128)(2,1)S(1)}, u32[]{:S(2)}, u32[]{:S(2)}) %collective-permute-start.3) | collective-permute-done | bytes 262176 | tf_op jit(solution)/shard_map/ppermute | solution.py:227
  33.4 1.5 collective-permute-start.4
  35.0 6.8 %collective-permute-done.5.refs_5_ = bf16[128,1024]{1,0:T(8,128)(2,1)S(1)} collective-permute-done((bf16[128,1024]{1,0:T(8,128)(2,1)S(1)}, bf16[128,1024]{1,0:T(8,128)(2,1)S(1)}, u32[]{:S(2)}, u32[]{:S(2)}) %collective-permute-start.5) | collective-permute-done | bytes 262176 | tf_op jit(solution)/shard_map/ppermute | solution.py:227
  41.7 1.5 collective-permute-start.6
  43.2 0.5 collective-permute-start.8
  43.7 3.1 %shard_map.82.refs_0_ = bf16[128,1024]{1,0:T(8,128)(2,1)S(1)} custom-call(bf16[128,1024]{1,0:T(8,128)(2,1)S(1)} %get-tuple-element.34.q_ref, bf16[128,2048]{1,0:T(8,128)(2,1)S(1)} %collective-permute-done.before_ref, bf16[128,2048]{1,0:T(8,128)(2,1)S(1)} %pad_maximum_fusion.own_ref, bf16[128,2048]{1,0:T(8,128)(2,1)S(1)} %collective-permute-done.1.after_ref), custom_call_target="tpu_custom_call" | custom-call | tf_op jit(solution)/shard_map/pallas_call | solution.py:257
  46.9 0.1 collective-permute-start.2
  47.0 1.8 collective-permute-done.6.refs_6_
  48.8 2.8 %collective-permute-done.8.refs_8_ = bf16[128,1024]{1,0:T(8,128)(2,1)S(1)} collective-permute-done((bf16[128,1024]{1,0:T(8,128)(2,1)S(1)}, bf16[128,1024]{1,0:T(8,128)(2,1)S(1)}, u32[]{:S(2)}, u32[]{:S(2)}) %collective-permute-start.8) | collective-permute-done | bytes 262176 | tf_op jit(solution)/shard_map/ppermute | solution.py:249
  51.6 1.7 collective-permute-done.2.refs_1_
  53.3 1.0 copy-done.2
  54.3 1.4 shard_map.83
  55.7 0.1 collective-permute-start.9
  55.8 1.4 reshape.30
  57.3 1.8 dynamic-slice_reduce_fusion
  59.1 0.1 collective-permute-start.10
  59.2 0.7 convert_bitcast_fusion
  59.9 5.1 %collective-permute-done.10.far_ref = bf16[128,512]{1,0:T(8,128)(2,1)S(1)} collective-permute-done((bf16[128,512]{1,0:T(8,128)(2,1)S(1)}, bf16[128,512]{1,0:T(8,128)(2,1)S(1)}, u32[]{:S(2)}, u32[]{:S(2)}) %collective-permute-start.10) | collective-permute-done | bytes 131104 | tf_op jit(solution)/shard_map/ppermute | solution.py:227
  65.0 0.8 copy-done.7
  65.8 0.1 shard_map.84.refs_0_
  65.9 4.6 %collective-permute-start.14 = (bf16[272,512]{1,0:T(8,128)(2,1)S(1)}, bf16[272,512]{1,0:T(8,128)(2,1)S(1)}, u32[]{:S(2)}, u32[]{:S(2)}) collective-permute-start(bf16[272,512]{1,0:T(8,128)(2,1)S(1)} %shard_map.84.refs_0_), channel_id=1, source_target_pairs={{0,4},{2,6},{4,0},{6,2},{8,12},{10,14},{12,8},{14,10},{1,5},{3,7},... | collective-permute-start | bytes 835592 | tf_op jit(solution)/shard_map/ppermute | solution.py:227
  70.5 2.4 %collective-permute-start.22 = (bf16[272,512]{1,0:T(8,128)(2,1)S(1)}, bf16[272,512]{1,0:T(8,128)(2,1)S(1)}, u32[]{:S(2)}, u32[]{:S(2)}) collective-permute-start(bf16[272,512]{1,0:T(8,128)(2,1)S(1)} %shard_map.84.refs_0_), channel_id=1, source_target_pairs={{0,12},{2,14},{4,8},{6,10},{8,4},{10,6},{12,0},{14,2},{1,13},{3,15... | collective-permute-start | bytes 835592 | tf_op jit(solution)/shard_map/ppermute | solution.py:227
  72.9 0.3 collective-permute-start.11
  73.2 7.6 %collective-permute-done.14.refs_4_ = bf16[272,512]{1,0:T(8,128)(2,1)S(1)} collective-permute-done((bf16[272,512]{1,0:T(8,128)(2,1)S(1)}, bf16[272,512]{1,0:T(8,128)(2,1)S(1)}, u32[]{:S(2)}, u32[]{:S(2)}) %collective-permute-start.14) | collective-permute-done | bytes 278560 | tf_op jit(solution)/shard_map/ppermute | solution.py:227
  80.8 0.3 collective-permute-start.15
  81.1 11.8 %collective-permute-done.18.refs_8_ = bf16[272,512]{1,0:T(8,128)(2,1)S(1)} collective-permute-done((bf16[272,512]{1,0:T(8,128)(2,1)S(1)}, bf16[272,512]{1,0:T(8,128)(2,1)S(1)}, u32[]{:S(2)}, u32[]{:S(2)}) %collective-permute-start.18) | collective-permute-done | bytes 278560 | tf_op jit(solution)/shard_map/ppermute | solution.py:227
  92.9 0.3 collective-permute-start.19
  93.2 1.7 collective-permute-start.23
  94.9 0.5 collective-permute-start.16
  95.5 5.9 %collective-permute-done.19.refs_9_ = bf16[272,512]{1,0:T(8,128)(2,1)S(1)} collective-permute-done((bf16[272,512]{1,0:T(8,128)(2,1)S(1)}, bf16[272,512]{1,0:T(8,128)(2,1)S(1)}, u32[]{:S(2)}, u32[]{:S(2)}) %collective-permute-start.19) | collective-permute-done | bytes 278560 | tf_op jit(solution)/shard_map/ppermute | solution.py:227
  101.4 3.0 %collective-permute-done.23.refs_13_ = bf16[272,512]{1,0:T(8,128)(2,1)S(1)} collective-permute-done((bf16[272,512]{1,0:T(8,128)(2,1)S(1)}, bf16[272,512]{1,0:T(8,128)(2,1)S(1)}, u32[]{:S(2)}, u32[]{:S(2)}) %collective-permute-start.23) | collective-permute-done | bytes 278560 | tf_op jit(solution)/shard_map/ppermute | solution.py:227
  104.4 0.5 collective-permute-start.21
  104.9 40.2 %copy.14.refs_18_ = bf16[16,2,2048,192]{3,2,1,0:T(8,128)(2,1)} copy(bf16[16,2,2048,192]{2,3,1,0:T(8,128)(2,1)} %param.14) | data formatting | bytes 50331648 | tf_op args[6]
  145.2 0.9 copy-done.3
  146.1 23.5 %shard_map.85 = (bf16[16,128,192]{2,1,0:T(8,128)(2,1)}, bf16[128,1024]{1,0:T(8,128)(2,1)S(1)}, bf16[8,128,128]{2,1,0:T(8,128)(2,1)S(1)}) custom-call(bf16[272,512]{1,0:T(8,128)(2,1)S(1)} %shard_map.84.refs_0_, bf16[272,512]{1,0:T(8,128)(2,1)S(1)} %collective-permute-done.11.refs_1_, bf16[272,512]{1,0:T(8,128)(2,1)S(1)} %collective-permute-done.12.refs_2_, ...), custom_call_target="tpu_custom_call" | custom-call | tf_op jit(solution)/shard_map/pallas_call | solution.py:292
  169.7 0.7 copy-done.4
  170.4 0.7 copy-done.6
  171.1 1.6 copy.15
  172.6 0.4 collective-permute-start.26
  173.0 2.0 collective-permute-done.26
  175.0 0.5 copy.16.far_ref
  175.5 4.6 %copy-done = bf16[16,384,1024]{2,1,0:T(8,128)(2,1)S(1)} copy-done((bf16[16,384,1024]{2,1,0:T(8,128)(2,1)S(1)}, bf16[16,384,1024]{2,1,0:T(8,128)(2,1)}, u32[]{:S(2)}) %copy-start) | copy-done | bytes 12582936
  180.1 1.2 copy-done.1
  181.3 0.9 copy-done.5
  182.3 4.3 %shard_map.86 = (bf16[128,1024]{1,0:T(8,128)(2,1)S(1)}, bf16[128,1024]{1,0:T(8,128)(2,1)S(1)}, bf16[128,1024]{1,0:T(8,128)(2,1)S(1)}, bf16[128,1024]{1,0:T(8,128...) custom-call(bf16[16,128,192]{2,1,0:T(8,128)(2,1)S(1)} %copy-done.1, ...), custom_call_target="tpu_custom_call" | custom-call | tf_op jit(solution)/shard_map/pallas_call | solution.py:315
  186.5 0.4 collective-permute-start.27
  186.9 1.7 collective-permute-start.29
  188.6 0.3 collective-permute-start.31
  188.9 1.7 collective-permute-start.33
  190.7 5.1 %collective-permute-done.27 = bf16[128,1024]{1,0:T(8,128)(2,1)S(1)} collective-permute-done((bf16[128,1024]{1,0:T(8,128)(2,1)S(1)}, bf16[128,1024]{1,0:T(8,128)(2,1)S(1)}, u32[]{:S(2)}, u32[]{:S(2)}) %collective-permute-start.27) | collective-permute-done | bytes 262176 | tf_op jit(solution)/shard_map/ppermute | solution.py:227
  195.8 0.1 collective-permute-start.28
  195.9 5.5 %collective-permute-done.29 = bf16[128,1024]{1,0:T(8,128)(2,1)S(1)} collective-permute-done((bf16[128,1024]{1,0:T(8,128)(2,1)S(1)}, bf16[128,1024]{1,0:T(8,128)(2,1)S(1)}, u32[]{:S(2)}, u32[]{:S(2)}) %collective-permute-start.29) | collective-permute-done | bytes 262176 | tf_op jit(solution)/shard_map/ppermute | solution.py:227
  201.4 0.7 collective-permute-start.30
  202.1 4.9 %collective-permute-done.31 = bf16[128,1024]{1,0:T(8,128)(2,1)S(1)} collective-permute-done((bf16[128,1024]{1,0:T(8,128)(2,1)S(1)}, bf16[128,1024]{1,0:T(8,128)(2,1)S(1)}, u32[]{:S(2)}, u32[]{:S(2)}) %collective-permute-start.31) | collective-permute-done | bytes 262176 | tf_op jit(solution)/shard_map/ppermute | solution.py:227
  207.0 0.6 collective-permute-start.32
  207.7 4.3 %collective-permute-done.33 = bf16[128,1024]{1,0:T(8,128)(2,1)S(1)} collective-permute-done((bf16[128,1024]{1,0:T(8,128)(2,1)S(1)}, bf16[128,1024]{1,0:T(8,128)(2,1)S(1)}, u32[]{:S(2)}, u32[]{:S(2)}) %collective-permute-start.33) | collective-permute-done | bytes 262176 | tf_op jit(solution)/shard_map/ppermute | solution.py:227
  212.0 7.9 %collective-permute-done.30 = bf16[128,1024]{1,0:T(8,128)(2,1)S(1)} collective-permute-done((bf16[128,1024]{1,0:T(8,128)(2,1)S(1)}, bf16[128,1024]{1,0:T(8,128)(2,1)S(1)}, u32[]{:S(2)}, u32[]{:S(2)}) %collective-permute-start.30) | collective-permute-done | bytes 262176 | tf_op jit(solution)/shard_map/ppermute | solution.py:227
  219.9 1.9 add_convert_fusion
  (46 shorter events, 0.5 us)
Async XLA Ops:
  1.2 42.5 %collective-permute-start = (bf16[128,2048]{1,0:T(8,128)(2,1)S(1)}, bf16[128,2048]{1,0:T(8,128)(2,1)S(1)}, u32[]{:S(2)}, u32[]{:S(2)}) collective-permute-start(bf16[128,2048]{1,0:T(8,128)(2,1)S(1)} %pad_maximum_fusion.own_ref), channel_id=1, source_target_pairs={{0,2},{2,4},{4,6},{6,8},{8,10},{10,12},{12,14},{1,3},{3,5},{5,7},{... | collective-permute-start | bytes 1572872 | tf_op jit(solution)/shard_map/ppermute | solution.py:234
  6.1 37.6 %collective-permute-start.1 = (bf16[128,2048]{1,0:T(8,128)(2,1)S(1)}, bf16[128,2048]{1,0:T(8,128)(2,1)S(1)}, u32[]{:S(2)}, u32[]{:S(2)}) collective-permute-start(bf16[128,2048]{1,0:T(8,128)(2,1)S(1)} %pad_maximum_fusion.own_ref), channel_id=1, source_target_pairs={{2,0},{4,2},{6,4},{8,6},{10,8},{12,10},{14,12},{3,1},{5,3},{7,5},{... | collective-permute-start | bytes 1572872 | tf_op jit(solution)/shard_map/ppermute | solution.py:235
  8.4 25.1 %collective-permute-start.3 = (bf16[128,1024]{1,0:T(8,128)(2,1)S(1)}, bf16[128,1024]{1,0:T(8,128)(2,1)S(1)}, u32[]{:S(2)}, u32[]{:S(2)}) collective-permute-start(bf16[128,1024]{1,0:T(8,128)(2,1)S(1)} %constant_dynamic-slice_fusion), channel_id=1, source_target_pairs={{0,4},{2,6},{4,0},{6,2},{8,12},{10,14},{12,8},{14,10},{1,5},{3,7},... | collective-permute-start | bytes 786440 | tf_op jit(solution)/shard_map/ppermute | solution.py:227
  12.0 29.7 %collective-permute-start.5 = (bf16[128,1024]{1,0:T(8,128)(2,1)S(1)}, bf16[128,1024]{1,0:T(8,128)(2,1)S(1)}, u32[]{:S(2)}, u32[]{:S(2)}) collective-permute-start(bf16[128,1024]{1,0:T(8,128)(2,1)S(1)} %constant_dynamic-slice_fusion), channel_id=1, source_target_pairs={{0,8},{2,10},{4,12},{6,14},{8,0},{10,2},{12,4},{14,6},{1,9},{3,11}... | collective-permute-start | bytes 786440 | tf_op jit(solution)/shard_map/ppermute | solution.py:227
  14.6 28.6 %collective-permute-start.7 = (bf16[128,1024]{1,0:T(8,128)(2,1)S(1)}, bf16[128,1024]{1,0:T(8,128)(2,1)S(1)}, u32[]{:S(2)}, u32[]{:S(2)}) collective-permute-start(bf16[128,1024]{1,0:T(8,128)(2,1)S(1)} %constant_dynamic-slice_fusion), channel_id=1, source_target_pairs={{0,12},{2,14},{4,8},{6,10},{8,4},{10,6},{12,0},{14,2},{1,13},{3,15... | collective-permute-start | bytes 786440 | tf_op jit(solution)/shard_map/ppermute | solution.py:227
  33.4 13.5 %collective-permute-start.4 = (bf16[128,1024]{1,0:T(8,128)(2,1)S(1)}, bf16[128,1024]{1,0:T(8,128)(2,1)S(1)}, u32[]{:S(2)}, u32[]{:S(2)}) collective-permute-start(bf16[128,1024]{1,0:T(8,128)(2,1)S(1)} %collective-permute-done.3.refs_3_), channel_id=1, source_target_pairs={{0,16},{16,0},{1,17},{17,1},{2,18},{18,2},{3,19},{19,3},{4,20},{20... | collective-permute-start | bytes 786440 | tf_op jit(solution)/shard_map/ppermute | solution.py:249
  41.7 7.1 %collective-permute-start.6 = (bf16[128,1024]{1,0:T(8,128)(2,1)S(1)}, bf16[128,1024]{1,0:T(8,128)(2,1)S(1)}, u32[]{:S(2)}, u32[]{:S(2)}) collective-permute-start(bf16[128,1024]{1,0:T(8,128)(2,1)S(1)} %collective-permute-done.5.refs_5_), channel_id=1, source_target_pairs={{0,16},{16,0},{1,17},{17,1},{2,18},{18,2},{3,19},{19,3},{4,20},{20... | collective-permute-start | bytes 786440 | tf_op jit(solution)/shard_map/ppermute | solution.py:249
  43.2 8.3 %collective-permute-start.8 = (bf16[128,1024]{1,0:T(8,128)(2,1)S(1)}, bf16[128,1024]{1,0:T(8,128)(2,1)S(1)}, u32[]{:S(2)}, u32[]{:S(2)}) collective-permute-start(bf16[128,1024]{1,0:T(8,128)(2,1)S(1)} %collective-permute-done.7.refs_7_), channel_id=1, source_target_pairs={{0,16},{16,0},{1,17},{17,1},{2,18},{18,2},{3,19},{19,3},{4,20},{20... | collective-permute-start | bytes 786440 | tf_op jit(solution)/shard_map/ppermute | solution.py:249
  46.9 6.4 %collective-permute-start.2 = (bf16[128,1024]{1,0:T(8,128)(2,1)S(1)}, bf16[128,1024]{1,0:T(8,128)(2,1)S(1)}, u32[]{:S(2)}, u32[]{:S(2)}) collective-permute-start(bf16[128,1024]{1,0:T(8,128)(2,1)S(1)} %shard_map.82.refs_0_), channel_id=1, source_target_pairs={{0,2},{2,0},{4,6},{6,4},{8,10},{10,8},{12,14},{14,12},{1,3},{3,1},... | collective-permute-start | bytes 786440 | tf_op jit(solution)/shard_map/ppermute | solution.py:227
  53.3 1.0 copy-start.2
  55.7 9.3 %collective-permute-start.9 = (f32[256,512]{1,0:T(8,128)S(1)}, f32[256,512]{1,0:T(8,128)S(1)}, u32[]{:S(2)}, u32[]{:S(2)}) collective-permute-start(f32[256,512]{1,0:T(8,128)S(1)} %get-tuple-element.19), channel_id=1, source_target_pairs={{0,1},{1,0},{2,3},{3,2},{4,5},{5,4},{6,7},{7,6},{8,9},{9,8},{10,11... | collective-permute-start | bytes 1572872 | tf_op jit(solution)/shard_map/ppermute | solution.py:230
  59.1 5.9 %collective-permute-start.10 = (bf16[128,512]{1,0:T(8,128)(2,1)S(1)}, bf16[128,512]{1,0:T(8,128)(2,1)S(1)}, u32[]{:S(2)}, u32[]{:S(2)}) collective-permute-start(bf16[128,512]{1,0:T(8,128)(2,1)S(1)} %bitcast.23), channel_id=1, source_target_pairs={{0,2},{2,0},{4,6},{6,4},{8,10},{10,8},{12,14},{14,12},{1,3},{3,1},... | collective-permute-start | bytes 393224 | tf_op jit(solution)/shard_map/ppermute | solution.py:227
  65.0 0.8 copy-start.7
  65.9 79.3 %copy-start.8 = (f32[4,2048]{1,0:T(4,128)S(1)}, f32[4,2048]{1,0:T(4,128)}, u32[]{:S(2)}) copy-start(f32[4,2048]{1,0:T(4,128)} %refs_16_.1) | copy-start | bytes 98308
  65.9 14.9 %collective-permute-start.14 = (bf16[272,512]{1,0:T(8,128)(2,1)S(1)}, bf16[272,512]{1,0:T(8,128)(2,1)S(1)}, u32[]{:S(2)}, u32[]{:S(2)}) collective-permute-start(bf16[272,512]{1,0:T(8,128)(2,1)S(1)} %shard_map.84.refs_0_), channel_id=1, source_target_pairs={{0,4},{2,6},{4,0},{6,2},{8,12},{10,14},{12,8},{14,10},{1,5},{3,7},... | collective-permute-start | bytes 835592 | tf_op jit(solution)/shard_map/ppermute | solution.py:227
  70.5 22.4 %collective-permute-start.18 = (bf16[272,512]{1,0:T(8,128)(2,1)S(1)}, bf16[272,512]{1,0:T(8,128)(2,1)S(1)}, u32[]{:S(2)}, u32[]{:S(2)}) collective-permute-start(bf16[272,512]{1,0:T(8,128)(2,1)S(1)} %shard_map.84.refs_0_), channel_id=1, source_target_pairs={{0,8},{2,10},{4,12},{6,14},{8,0},{10,2},{12,4},{14,6},{1,9},{3,11}... | collective-permute-start | bytes 835592 | tf_op jit(solution)/shard_map/ppermute | solution.py:227
  70.5 22.7 %collective-permute-start.22 = (bf16[272,512]{1,0:T(8,128)(2,1)S(1)}, bf16[272,512]{1,0:T(8,128)(2,1)S(1)}, u32[]{:S(2)}, u32[]{:S(2)}) collective-permute-start(bf16[272,512]{1,0:T(8,128)(2,1)S(1)} %shard_map.84.refs_0_), channel_id=1, source_target_pairs={{0,12},{2,14},{4,8},{6,10},{8,4},{10,6},{12,0},{14,2},{1,13},{3,15... | collective-permute-start | bytes 835592 | tf_op jit(solution)/shard_map/ppermute | solution.py:227
  72.9 22.0 %collective-permute-start.11 = (bf16[272,512]{1,0:T(8,128)(2,1)S(1)}, bf16[272,512]{1,0:T(8,128)(2,1)S(1)}, u32[]{:S(2)}, u32[]{:S(2)}) collective-permute-start(bf16[272,512]{1,0:T(8,128)(2,1)S(1)} %shard_map.84.refs_0_), channel_id=1, source_target_pairs={{0,2},{2,0},{4,6},{6,4},{8,10},{10,8},{12,14},{14,12},{1,3},{3,1},... | collective-permute-start | bytes 835592 | tf_op jit(solution)/shard_map/ppermute | solution.py:227
  73.2 21.7 %collective-permute-start.12 = (bf16[272,512]{1,0:T(8,128)(2,1)S(1)}, bf16[272,512]{1,0:T(8,128)(2,1)S(1)}, u32[]{:S(2)}, u32[]{:S(2)}) collective-permute-start(bf16[272,512]{1,0:T(8,128)(2,1)S(1)} %shard_map.84.refs_0_), channel_id=1, source_target_pairs={{0,1},{1,0},{2,3},{3,2},{4,5},{5,4},{6,7},{7,6},{8,9},{9,8},{10,11... | collective-permute-start | bytes 835592 | tf_op jit(solution)/shard_map/ppermute | solution.py:230
  80.8 14.7 %collective-permute-start.15 = (bf16[272,512]{1,0:T(8,128)(2,1)S(1)}, bf16[272,512]{1,0:T(8,128)(2,1)S(1)}, u32[]{:S(2)}, u32[]{:S(2)}) collective-permute-start(bf16[272,512]{1,0:T(8,128)(2,1)S(1)} %collective-permute-done.14.refs_4_), channel_id=1, source_target_pairs={{0,2},{2,0},{4,6},{6,4},{8,10},{10,8},{12,14},{14,12},{1,3},{3,1},... | collective-permute-start | bytes 835592 | tf_op jit(solution)/shard_map/ppermute | solution.py:227
  92.9 8.5 %collective-permute-start.19 = (bf16[272,512]{1,0:T(8,128)(2,1)S(1)}, bf16[272,512]{1,0:T(8,128)(2,1)S(1)}, u32[]{:S(2)}, u32[]{:S(2)}) collective-permute-start(bf16[272,512]{1,0:T(8,128)(2,1)S(1)} %collective-permute-done.18.refs_8_), channel_id=1, source_target_pairs={{0,2},{2,0},{4,6},{6,4},{8,10},{10,8},{12,14},{14,12},{1,3},{3,1},... | collective-permute-start | bytes 835592 | tf_op jit(solution)/shard_map/ppermute | solution.py:227
  93.2 11.2 %collective-permute-start.23 = (bf16[272,512]{1,0:T(8,128)(2,1)S(1)}, bf16[272,512]{1,0:T(8,128)(2,1)S(1)}, u32[]{:S(2)}, u32[]{:S(2)}) collective-permute-start(bf16[272,512]{1,0:T(8,128)(2,1)S(1)} %collective-permute-done.22.refs_12_), channel_id=1, source_target_pairs={{0,2},{2,0},{4,6},{6,4},{8,10},{10,8},{12,14},{14,12},{1,3},{3,1},... | collective-permute-start | bytes 835592 | tf_op jit(solution)/shard_map/ppermute | solution.py:227
  94.9 9.4 %collective-permute-start.13 = (bf16[272,512]{1,0:T(8,128)(2,1)S(1)}, bf16[272,512]{1,0:T(8,128)(2,1)S(1)}, u32[]{:S(2)}, u32[]{:S(2)}) collective-permute-start(bf16[272,512]{1,0:T(8,128)(2,1)S(1)} %collective-permute-done.11.refs_1_), channel_id=1, source_target_pairs={{0,1},{1,0},{2,3},{3,2},{4,5},{5,4},{6,7},{7,6},{8,9},{9,8},{10,11... | collective-permute-start | bytes 835592 | tf_op jit(solution)/shard_map/ppermute | solution.py:230
  94.9 9.9 %collective-permute-start.16 = (bf16[272,512]{1,0:T(8,128)(2,1)S(1)}, bf16[272,512]{1,0:T(8,128)(2,1)S(1)}, u32[]{:S(2)}, u32[]{:S(2)}) collective-permute-start(bf16[272,512]{1,0:T(8,128)(2,1)S(1)} %collective-permute-done.14.refs_4_), channel_id=1, source_target_pairs={{0,1},{1,0},{2,3},{3,2},{4,5},{5,4},{6,7},{7,6},{8,9},{9,8},{10,11... | collective-permute-start | bytes 835592 | tf_op jit(solution)/shard_map/ppermute | solution.py:230
  95.5 49.7 %collective-permute-start.20 = (bf16[272,512]{1,0:T(8,128)(2,1)S(1)}, bf16[272,512]{1,0:T(8,128)(2,1)S(1)}, u32[]{:S(2)}, u32[]{:S(2)}) collective-permute-start(bf16[272,512]{1,0:T(8,128)(2,1)S(1)} %collective-permute-done.18.refs_8_), channel_id=1, source_target_pairs={{0,1},{1,0},{2,3},{3,2},{4,5},{5,4},{6,7},{7,6},{8,9},{9,8},{10,11... | collective-permute-start | bytes 835592 | tf_op jit(solution)/shard_map/ppermute | solution.py:230
  101.4 43.8 %collective-permute-start.24 = (bf16[272,512]{1,0:T(8,128)(2,1)S(1)}, bf16[272,512]{1,0:T(8,128)(2,1)}, u32[]{:S(2)}, u32[]{:S(2)}) collective-permute-start(bf16[272,512]{1,0:T(8,128)(2,1)S(1)} %collective-permute-done.22.refs_12_), channel_id=1, source_target_pairs={{0,1},{1,0},{2,3},{3,2},{4,5},{5,4},{6,7},{7,6},{8,9},{9,8},{10,11... | collective-permute-start | bytes 835592 | tf_op jit(solution)/shard_map/ppermute | solution.py:230
  104.4 40.8 %collective-permute-start.17 = (bf16[272,512]{1,0:T(8,128)(2,1)S(1)}, bf16[272,512]{1,0:T(8,128)(2,1)}, u32[]{:S(2)}, u32[]{:S(2)}) collective-permute-start(bf16[272,512]{1,0:T(8,128)(2,1)S(1)} %collective-permute-done.15.refs_5_), channel_id=1, source_target_pairs={{0,1},{1,0},{2,3},{3,2},{4,5},{5,4},{6,7},{7,6},{8,9},{9,8},{10,11... | collective-permute-start | bytes 835592 | tf_op jit(solution)/shard_map/ppermute | solution.py:230
  104.4 40.8 %collective-permute-start.21 = (bf16[272,512]{1,0:T(8,128)(2,1)S(1)}, bf16[272,512]{1,0:T(8,128)(2,1)}, u32[]{:S(2)}, u32[]{:S(2)}) collective-permute-start(bf16[272,512]{1,0:T(8,128)(2,1)S(1)} %collective-permute-done.19.refs_9_), channel_id=1, source_target_pairs={{0,1},{1,0},{2,3},{3,2},{4,5},{5,4},{6,7},{7,6},{8,9},{9,8},{10,11... | collective-permute-start | bytes 835592 | tf_op jit(solution)/shard_map/ppermute | solution.py:230
  104.9 40.3 %collective-permute-start.25 = (bf16[272,512]{1,0:T(8,128)(2,1)S(1)}, bf16[272,512]{1,0:T(8,128)(2,1)}, u32[]{:S(2)}, u32[]{:S(2)}) collective-permute-start(bf16[272,512]{1,0:T(8,128)(2,1)S(1)} %collective-permute-done.23.refs_13_), channel_id=1, source_target_pairs={{0,1},{1,0},{2,3},{3,2},{4,5},{5,4},{6,7},{7,6},{8,9},{9,8},{10,11... | collective-permute-start | bytes 835592 | tf_op jit(solution)/shard_map/ppermute | solution.py:230
  145.2 1.0 copy-start.3
  169.7 0.7 copy-start.4
  170.4 0.7 copy-start.6
  172.6 2.4 %collective-permute-start.26 = (bf16[16,128,192]{1,2,0:T(8,128)(2,1)S(1)}, bf16[16,128,192]{1,2,0:T(8,128)(2,1)S(1)}, u32[]{:S(2)}, u32[]{:S(2)}) collective-permute-start(bf16[16,128,192]{1,2,0:T(8,128)(2,1)S(1)} %copy.15), channel_id=1, source_target_pairs={{0,1},{1,0},{2,3},{3,2},{4,5},{5,4},{6,7},{7,6},{8,9},{9,8},{10,11... | collective-permute-start | bytes 2359304 | tf_op jit(solution)/shard_map/ppermute | solution.py:230
  175.5 4.6 %copy-start = (bf16[16,384,1024]{2,1,0:T(8,128)(2,1)S(1)}, bf16[16,384,1024]{2,1,0:T(8,128)(2,1)}, u32[]{:S(2)}) copy-start(bf16[16,384,1024]{2,1,0:T(8,128)(2,1)} %w_ref.1) | copy-start | bytes 37748740
  180.1 1.2 copy-start.1
  181.3 0.9 copy-start.5
  186.5 9.2 %collective-permute-start.27 = (bf16[128,1024]{1,0:T(8,128)(2,1)S(1)}, bf16[128,1024]{1,0:T(8,128)(2,1)S(1)}, u32[]{:S(2)}, u32[]{:S(2)}) collective-permute-start(bf16[128,1024]{1,0:T(8,128)(2,1)S(1)} %get-tuple-element.24), channel_id=1, source_target_pairs={{0,2},{2,0},{4,6},{6,4},{8,10},{10,8},{12,14},{14,12},{1,3},{3,1},... | collective-permute-start | bytes 786440 | tf_op jit(solution)/shard_map/ppermute | solution.py:227
  186.9 14.5 %collective-permute-start.29 = (bf16[128,1024]{1,0:T(8,128)(2,1)S(1)}, bf16[128,1024]{1,0:T(8,128)(2,1)S(1)}, u32[]{:S(2)}, u32[]{:S(2)}) collective-permute-start(bf16[128,1024]{1,0:T(8,128)(2,1)S(1)} %get-tuple-element.26), channel_id=1, source_target_pairs={{0,2},{2,0},{4,6},{6,4},{8,10},{10,8},{12,14},{14,12},{1,3},{3,1},... | collective-permute-start | bytes 786440 | tf_op jit(solution)/shard_map/ppermute | solution.py:227
  188.6 18.3 %collective-permute-start.31 = (bf16[128,1024]{1,0:T(8,128)(2,1)S(1)}, bf16[128,1024]{1,0:T(8,128)(2,1)S(1)}, u32[]{:S(2)}, u32[]{:S(2)}) collective-permute-start(bf16[128,1024]{1,0:T(8,128)(2,1)S(1)} %get-tuple-element.28), channel_id=1, source_target_pairs={{0,2},{2,0},{4,6},{6,4},{8,10},{10,8},{12,14},{14,12},{1,3},{3,1},... | collective-permute-start | bytes 786440 | tf_op jit(solution)/shard_map/ppermute | solution.py:227
  188.9 23.1 %collective-permute-start.33 = (bf16[128,1024]{1,0:T(8,128)(2,1)S(1)}, bf16[128,1024]{1,0:T(8,128)(2,1)S(1)}, u32[]{:S(2)}, u32[]{:S(2)}) collective-permute-start(bf16[128,1024]{1,0:T(8,128)(2,1)S(1)} %get-tuple-element.30), channel_id=1, source_target_pairs={{0,2},{2,0},{4,6},{6,4},{8,10},{10,8},{12,14},{14,12},{1,3},{3,1},... | collective-permute-start | bytes 786440 | tf_op jit(solution)/shard_map/ppermute | solution.py:227
  195.8 16.2 %collective-permute-start.28 = (bf16[128,1024]{1,0:T(8,128)(2,1)S(1)}, bf16[128,1024]{1,0:T(8,128)(2,1)S(1)}, u32[]{:S(2)}, u32[]{:S(2)}) collective-permute-start(bf16[128,1024]{1,0:T(8,128)(2,1)S(1)} %add_convert_fusion.3), channel_id=1, source_target_pairs={{0,12},{2,14},{4,8},{6,10},{8,4},{10,6},{12,0},{14,2},{1,13},{3,15... | collective-permute-start | bytes 786440 | tf_op jit(solution)/shard_map/ppermute | solution.py:227
  201.4 18.4 %collective-permute-start.30 = (bf16[128,1024]{1,0:T(8,128)(2,1)S(1)}, bf16[128,1024]{1,0:T(8,128)(2,1)S(1)}, u32[]{:S(2)}, u32[]{:S(2)}) collective-permute-start(bf16[128,1024]{1,0:T(8,128)(2,1)S(1)} %add_convert_fusion.2), channel_id=1, source_target_pairs={{0,8},{2,10},{4,12},{6,14},{8,0},{10,2},{12,4},{14,6},{1,9},{3,11}... | collective-permute-start | bytes 786440 | tf_op jit(solution)/shard_map/ppermute | solution.py:227
  207.0 12.8 %collective-permute-start.32 = (bf16[128,1024]{1,0:T(8,128)(2,1)S(1)}, bf16[128,1024]{1,0:T(8,128)(2,1)S(1)}, u32[]{:S(2)}, u32[]{:S(2)}) collective-permute-start(bf16[128,1024]{1,0:T(8,128)(2,1)S(1)} %add_convert_fusion.1), channel_id=1, source_target_pairs={{0,4},{2,6},{4,0},{6,2},{8,12},{10,14},{12,8},{14,10},{1,5},{3,7},... | collective-permute-start | bytes 786440 | tf_op jit(solution)/shard_map/ppermute | solution.py:227

commit v2 on v1

--- a/solution.py
+++ b/solution.py
@@ -29,8 +29,30 @@
     return pl.BlockSpec(memory_space=pltpu.VMEM)
 
 
-def attention_kernel(q_ref, before_ref, own_ref, after_ref, mixed_ref):
-    count, width = q_ref.shape
+def cut_kernel(split, tokens_ref, weight_ref, ids_ref, near_ref, far_ref, sent_ref, row_ref):
+    lanes = near_ref.shape[1]
+    chunk = tokens_ref.shape[1] // lax.axis_size("dev")
+    side = lax.axis_index("dev") % 2
+    part = lax.axis_index("sub")
+    for ref, parity in ((near_ref, side), (far_ref, 1 - side)):
+        for i in range(lanes // chunk):
+            at = pl.multiple_of(part * 2 * lanes + (2 * i + parity) * chunk, 128)
+            ref[:, i * chunk : (i + 1) * chunk] = tokens_ref[:, pl.ds(at, chunk)]
+    if split:
+        rows = sent_ref.shape[0]
+        at = pl.multiple_of(lax.axis_index("groups") * rows, TILE)
+        sent_ref[...] = weight_ref[pl.ds(at, rows), :]
+    else:
+        sent_ref[...] = weight_ref[...]
+    topk, count = ids_ref.shape
+    row_ref[...] = jnp.zeros(row_ref.shape, BF16)
+    for k in range(topk):
+        named = jnp.broadcast_to(ids_ref[k : k + 1, :], (TILE, count))
+        row_ref[:, k * count : (k + 1) * count] = named.astype(F32).astype(BF16)
+
+
+def attention_kernel(own_ref, before_ref, after_ref, _, mixed_ref):
+    count, width = mixed_ref.shape
     place = lax.axis_index("dev")
     last = lax.axis_size("dev") - 1
     row = lax.broadcasted_iota(jnp.int32, (count, count), 0)
@@ -39,22 +61,25 @@
     see_after = (col <= row) & (place < last)
     scale = 1.0 / math.sqrt(HEAD)
 
-    def scored(q, ref, lanes):
-        return lax.dot_general(q, ref[:, lanes], NT, preferred_element_type=F32) * scale
+    def scored(q, k):
+        return lax.dot_general(q, k, NT, preferred_element_type=F32) * scale
 
     for head in range(width // HEAD):
         lanes = slice(head * HEAD, (head + 1) * HEAD)
-        vlanes = slice(width + head * HEAD, width + (head + 1) * HEAD)
-        q = q_ref[:, lanes]
-        sb = jnp.where(see_before, scored(q, before_ref, lanes), NEG)
-        so = scored(q, own_ref, lanes)
-        sa = jnp.where(see_after, scored(q, after_ref, lanes), NEG)
+        q = own_ref[0, :, lanes]
+        sb = jnp.where(see_before, scored(q, before_ref[0, :, lanes]), NEG)
+        so = scored(q, own_ref[1, :, lanes])
+        sa = jnp.where(see_after, scored(q, after_ref[0, :, lanes]), NEG)
         top = jnp.max(jnp.maximum(jnp.maximum(sb, so), sa), 1, keepdims=True)
         wb, wo, wa = jnp.exp(sb - top), jnp.exp(so - top), jnp.exp(sa - top)
         inv = 1.0 / jnp.sum(wb + wo + wa, 1, keepdims=True)
-        out = jnp.dot((wo * inv).astype(BF16), own_ref[:, vlanes], preferred_element_type=F32)
-        out += jnp.dot((wb * inv).astype(BF16), before_ref[:, vlanes], preferred_element_type=F32)
-        out += jnp.dot((wa * inv).astype(BF16), after_ref[:, vlanes], preferred_element_type=F32)
+        out = 0.0
+        for weight, value in (
+            (wo, own_ref[2, :, lanes]),
+            (wb, before_ref[1, :, lanes]),
+            (wa, after_ref[1, :, lanes]),
+        ):
+            out += jnp.dot((weight * inv).astype(BF16), value, preferred_element_type=F32)
         mixed_ref[:, lanes] = out.astype(BF16)
 
 
@@ -100,12 +125,10 @@
     out_ref[2 * count :, :] = ids_ref[...]
 
 
-def hidden_kernel(steps, local, topk, *refs):
-    shard_refs = refs[: 4 * steps]
-    mod_ref, router_ref, w_ref = refs[4 * steps : 4 * steps + 3]
-    hidden_ref, state_ref, back_ref = refs[4 * steps + 3 : 4 * steps + 6]
-    full_ref, rows_ref, gate_ref = refs[4 * steps + 6 :]
-    step = pl.program_id(0)
+def select_kernel(local, topk, own, *refs):
+    shard_refs, (mod_ref, router_ref, rows_ref, back_ref) = refs[:4], refs[4:8]
+    state_ref = refs[8] if own else None
+    full_ref, gate_ref = refs[-2:]
     count, width = full_ref.shape
     lanes = shard_refs[0].shape[1]
     device = lax.axis_index("dev")
@@ -114,87 +137,94 @@
     chunk = width // lax.axis_size("dev")
     experts = router_ref.shape[0]
     slots = local * SLOTS
-
-    @pl.when(step == 0)
-    def _():
-        before = lax.broadcasted_iota(jnp.int32, (count, count), 0)
-        after = lax.broadcasted_iota(jnp.int32, (count, count), 1)
-        earlier = (before < after).astype(F32).astype(BF16)
-        slot = lax.broadcasted_iota(jnp.int32, (slots, count), 0) % SLOTS
-        mine = lax.broadcasted_iota(jnp.int32, (local, count), 0) + device * local
-        every = lax.broadcasted_iota(jnp.int32, (experts, count), 0)
-        for source in range(2 * steps):
-            hop, cross = source // 2, source % 2
-            for far_half in range(2):
-                for far_side in range(2):
-                    ref = shard_refs[4 * hop + 2 * far_half + far_side]
-                    top = (cross ^ far_side) * count
-                    half = part if far_half == 0 else 1 - part
-                    parity = side if far_side == 0 else 1 - side
-                    for i in range(lanes // chunk):
-                        block = ref[top : top + count, i * chunk : (i + 1) * chunk]
-                        at = (2 * i + parity) * chunk
-                        full_ref[:, pl.ds(pl.multiple_of(half * 2 * lanes + at, 128), chunk)] = block
-                        if source == 0 and far_half == 0:
-                            state_ref[:, pl.ds(pl.multiple_of(at, 128), chunk)] = block
-            state = full_ref[...].astype(F32)
-            scale = lax.rsqrt(jnp.mean(state * state, 1, keepdims=True) + EPS)
-            normed = state * scale * (1.0 + mod_ref[2:3, :]) + mod_ref[1:2, :]
-            normed = normed.astype(BF16)
-            ids = shard_refs[4 * hop + cross][2 * count : 2 * count + TILE, :]
-            ids = ids.astype(F32)[0:1, :].astype(jnp.int32)
-            named = [ids[:, k * count : (k + 1) * count] for k in range(topk)]
-            hot = sum((mine == n).astype(F32) for n in named)
-            rank = jnp.dot(hot.astype(BF16), earlier, preferred_element_type=F32)
-            rank = jnp.where(hot > 0.0, rank, -1.0)
-            rank = jnp.concatenate(
-                [jnp.broadcast_to(rank[e : e + 1], (SLOTS, count)) for e in range(local)]
-            )
-            pick = rank == slot.astype(F32)
-            chosen = jnp.dot(
-                jnp.where(pick, 1.0, 0.0).astype(BF16), normed, preferred_element_type=F32
-            ).astype(BF16)
-            for e in range(local):
-                rows_ref[e, source * SLOTS : (source + 1) * SLOTS, :] = chosen[
-                    e * SLOTS : (e + 1) * SLOTS
-                ]
-            logits = lax.dot_general(router_ref[...], normed, NT, preferred_element_type=F32)
-            lifted = sum(jnp.where(every == n, 1.0, 0.0) for n in named) * jax.nn.sigmoid(logits)
-            gate_ref[...] = lifted / jnp.sum(lifted, 0, keepdims=True)
-            here = gate_ref[pl.ds(pl.multiple_of(device * local, local), local), :]
-            here = jnp.concatenate(
-                [jnp.broadcast_to(here[e : e + 1], (SLOTS, count)) for e in range(local)]
-            )
-            back_ref[source] = jnp.where(pick, here, 0.0).T.astype(BF16)
-
-    rows = rows_ref[step // 2]
-    gate = jnp.dot(rows, w_ref[0, 0], preferred_element_type=F32)
-    up = jnp.dot(rows, w_ref[0, 1], preferred_element_type=F32)
-    hidden_ref[0] = (jax.nn.silu(gate) * up).astype(BF16)
-
-
-def output_kernel(sources, near_ref, far_ref, w_ref, back_ref, *refs):
-    out_refs, held_ref = refs[:sources], refs[sources]
-    step = pl.program_id(0)
-    part = lax.axis_index("sub")
-    units = near_ref.shape[2]
-    total = None
-    for half in range(2):
+    before = lax.broadcasted_iota(jnp.int32, (count, count), 0)
+    after = lax.broadcasted_iota(jnp.int32, (count, count), 1)
+    earlier = (before < after).astype(F32).astype(BF16)
+    slot = lax.broadcasted_iota(jnp.int32, (slots, count), 0) % SLOTS
+    mine = lax.broadcasted_iota(jnp.int32, (local, count), 0) + device * local
+    every = lax.broadcasted_iota(jnp.int32, (experts, count), 0)
+    for cross in range(2):
+        for far_half in range(2):
+            for far_side in range(2):
+                ref = shard_refs[2 * far_half + far_side]
+                top = (cross ^ far_side) * count
+                half = part if far_half == 0 else 1 - part
+                parity = side if far_side == 0 else 1 - side
+                for i in range(lanes // chunk):
+                    block = ref[top : top + count, i * chunk : (i + 1) * chunk]
+                    at = (2 * i + parity) * chunk
+                    full_ref[:, pl.ds(pl.multiple_of(half * 2 * lanes + at, 128), chunk)] = block
+                    if own and cross == 0 and far_half == 0:
+                        state_ref[:, pl.ds(pl.multiple_of(at, 128), chunk)] = block
+        state = full_ref[...].astype(F32)
+        scale = lax.rsqrt(jnp.mean(state * state, 1, keepdims=True) + EPS)
+        normed = state * scale * (1.0 + mod_ref[2:3, :]) + mod_ref[1:2, :]
+        normed = normed.astype(BF16)
+        ids = shard_refs[cross][2 * count : 2 * count + TILE, :]
+        ids = ids.astype(F32)[0:1, :].astype(jnp.int32)
+        named = [ids[:, k * count : (k + 1) * count] for k in range(topk)]
+        hot = sum((mine == n).astype(F32) for n in named)
+        rank = jnp.dot(hot.astype(BF16), earlier, preferred_element_type=F32)
+        rank = jnp.where(hot > 0.0, rank, -1.0)
+        rank = jnp.concatenate(
+            [jnp.broadcast_to(rank[e : e + 1], (SLOTS, count)) for e in range(local)]
+        )
+        pick = rank == slot.astype(F32)
+        chosen = jnp.dot(
+            jnp.where(pick, 1.0, 0.0).astype(BF16), normed, preferred_element_type=F32
+        ).astype(BF16)
+        for e in range(local):
+            rows_ref[e, cross * SLOTS : (cross + 1) * SLOTS, :] = chosen[
+                e * SLOTS : (e + 1) * SLOTS
+            ]
+        logits = lax.dot_general(router_ref[...], normed, NT, preferred_element_type=F32)
+        lifted = sum(jnp.where(every == n, 1.0, 0.0) for n in named) * jax.nn.sigmoid(logits)
+        gate_ref[...] = lifted / jnp.sum(lifted, 0, keepdims=True)
+        here = gate_ref[pl.ds(pl.multiple_of(device * local, local), local), :]
+        here = jnp.concatenate(
+            [jnp.broadcast_to(here[e : e + 1], (SLOTS, count)) for e in range(local)]
+        )
+        back_ref[cross] = jnp.where(pick, here, 0.0).T.astype(BF16)
+
+
+def hidden_kernel(steps, *refs):
+    rows_refs, (w_ref, hidden_ref) = refs[:steps], refs[steps:]
+
+    def expert(e, _):
+        rows = jnp.concatenate([ref[e] for ref in rows_refs])
+
+        def product(member):
+            weight = jnp.concatenate([w_ref[2 * e, member], w_ref[2 * e + 1, member]])
+            return lax.dot_general(rows, weight, NT, preferred_element_type=F32)
+
+        hidden_ref[e] = (jax.nn.silu(product(0)) * product(1)).astype(BF16)
+        return 0
+
+    lax.fori_loop(0, hidden_ref.shape[0], expert, 0, unroll=2)
+
+
+def output_kernel(steps, near_ref, far_ref, w_ref, *refs):
+    back_refs, out_refs, held_ref = refs[:steps], refs[steps : 3 * steps], refs[3 * steps]
+    part = lax.axis_index("sub")
+    units = near_ref.shape[2] // 2
+
+    def expert(e, _):
+        total = 0.0
         for ref, who in ((near_ref, part), (far_ref, 1 - part)):
             at = pl.multiple_of(who * units, 64)
-            piece = jnp.dot(ref[half], w_ref[half, pl.ds(at, units), :], preferred_element_type=F32)
-            total = piece if total is None else total + piece
-    total = total.astype(BF16)
-    row = pl.multiple_of(step * SLOTS, SLOTS)
-    for source in range(sources):
-        held_ref[source, pl.ds(row, SLOTS), :] = total[source * SLOTS : (source + 1) * SLOTS]
-
-    @pl.when(step == pl.num_programs(0) - 1)
-    def _():
-        for source in range(sources):
-            out_refs[source][...] = jnp.dot(
-                back_ref[source], held_ref[source], preferred_element_type=F32
-            ).astype(BF16)
+            weight = jnp.concatenate([w_ref[2 * e + b, pl.ds(at, units), :] for b in range(2)])
+            total += jnp.dot(ref[e], weight, preferred_element_type=F32)
+        total = total.astype(BF16)
+        row = pl.multiple_of(e * SLOTS, SLOTS)
+        for source in range(2 * steps):
+            held_ref[source, pl.ds(row, SLOTS), :] = total[source * SLOTS : (source + 1) * SLOTS]
+        return 0
+
+    lax.fori_loop(0, near_ref.shape[0], expert, 0, unroll=2)
+    for source in range(2 * steps):
+        out_refs[source][...] = jnp.dot(
+            back_refs[source // 2][source % 2], held_ref[source], preferred_element_type=F32
+        ).astype(BF16)
 
 
 def gathered_body(
@@ -229,103 +259,104 @@
     def swap(x):
         return lax.ppermute(x, "sub", [(0, 1), (1, 0)])
 
-    query = query_key_value[:, 0]
-    pair = jnp.concatenate([query_key_value[:, 1], query_key_value[:, 2]], 1)
+    stacked = query_key_value.transpose(1, 0, 2)
+    pair = stacked[1:]
     before = lax.ppermute(pair, "dev", [(i, i + 1) for i in range(devices - 1)])
     after = lax.ppermute(pair, "dev", [(i + 1, i) for i in range(devices - 1)])
 
-    cut = tokens.reshape(count, 2, devices // 4, 2, chunk)
-    cut = lax.dynamic_index_in_dim(cut, part, 1, keepdims=False)
-    near = lax.dynamic_index_in_dim(cut, side, 2, keepdims=False).reshape(count, lanes)
-    far = lax.dynamic_index_in_dim(cut, 1 - side, 2, keepdims=False).reshape(count, lanes)
+    split = groups == 2
+    held = out_weight.shape[0] // (2 if split else 1)
+    near, far, sent, ids = pl.pallas_call(
+        functools.partial(cut_kernel, split),
+        out_shape=[
+            struct((count, lanes), BF16),
+            struct((count, lanes), BF16),
+            struct((held, local_width), BF16),
+            struct((TILE, lanes), BF16),
+        ],
+        in_specs=[whole()] * 3,
+        out_specs=[whole()] * 4,
+        compiler_params=vmem(8),
+    )(tokens, out_weight, expert_ids.T)
     far = hop(far, 1)
 
     pieces, weights = [(0, None)], [out_weight]
-    if groups == 2:
-        rows = out_weight.shape[0] // 2
-        sent = lax.dynamic_slice_in_dim(out_weight, group * rows, rows, 0)
-        for flip in range(1, steps):
-            mine = hop(sent, 2 * flip)
+    for flip in range(1, steps):
+        mine = hop(sent, 2 * flip)
+        if split:
             theirs = lax.ppermute(mine, "groups", [(0, 1), (1, 0)])
             pieces += [(flip, 0), (flip, 1)]
             weights += [mine, theirs]
-    else:
-        for flip in range(1, steps):
+        else:
             pieces.append((flip, None))
-            weights.append(hop(out_weight, 2 * flip))
+            weights.append(mine)
 
     mixed = pl.pallas_call(
         attention_kernel,
         out_shape=struct((count, local_width), BF16),
-        in_specs=[whole()] * 4,
+        in_specs=[whole()] * 3 + [pl.BlockSpec(memory_space=pl.ANY)],
         out_specs=whole(),
-        compiler_params=vmem(32),
-    )(query, before, pair, after)
+        compiler_params=vmem(8),
+    )(stacked, before, after, far)
     keep, send = pl.pallas_call(
         functools.partial(projection_kernel, steps, tuple(pieces)),
         out_shape=[struct((2 * count, lanes), F32)] * 2,
         in_specs=[whole()] * (2 + len(weights)),
         out_specs=[whole()] * 2,
         scratch_shapes=[pltpu.VMEM((2, 2 * count, lanes), F32)],
-        compiler_params=vmem(32),
+        compiler_params=vmem(10),
     )(mixed, hop(mixed, 1), *weights)
-    ids = expert_ids.T.reshape(1, topk * count).astype(BF16)
-    ids = jnp.pad(ids, ((0, TILE - 1), (0, lanes - topk * count)))
     shard = pl.pallas_call(
         state_kernel,
         out_shape=struct((2 * count + TILE, lanes), BF16),
         in_specs=[whole()] * 6,
         out_specs=whole(),
-        compiler_params=vmem(32),
+        compiler_params=vmem(10),
     )(keep, swap(send), near, far, ids, modulation)
 
-    column = [shard] + [hop(shard, 2 * flip) for flip in range(1, steps)]
-    shards = []
-    for block in column:
+    slots = local * SLOTS
+    router = router_weight.T
+    state = None
+    picked, backs = [], []
+    for flip in range(steps):
+        block = shard if flip == 0 else hop(shard, 2 * flip)
         crossed = hop(block, 1)
-        shards += [block, crossed, swap(block), swap(crossed)]
+        own = flip == 0
+        results = pl.pallas_call(
+            functools.partial(select_kernel, local, topk, own),
+            out_shape=[
+                struct((local, 2 * SLOTS, width), BF16),
+                struct((2, count, slots), BF16),
+            ]
+            + ([struct((count, 2 * lanes), BF16)] if own else []),
+            in_specs=[whole()] * 6,
+            out_specs=[whole()] * (3 if own else 2),
+            scratch_shapes=[pltpu.VMEM((count, width), BF16), pltpu.VMEM((experts, count), F32)],
+            compiler_params=vmem(12),
+        )(block, crossed, swap(block), swap(crossed), modulation, router)
+        picked.append(results[0])
+        backs.append(results[1])
+        if own:
+            state = results[2]
 
     sources = 2 * steps
-    slots = local * SLOTS
     room = sources * SLOTS
     units = gate_up_weight.shape[3]
-    hidden, state, back = pl.pallas_call(
-        functools.partial(hidden_kernel, steps, local, topk),
-        grid=(halves_here,),
-        out_shape=[
-            struct((halves_here, room, units), BF16),
-            struct((count, 2 * lanes), BF16),
-            struct((sources, count, slots), BF16),
-        ],
-        in_specs=[whole()] * (4 * steps + 2)
-        + [pl.BlockSpec((1, 2, width, units), lambda i: (i, 0, 0, 0))],
-        out_specs=[
-            pl.BlockSpec((1, room, units), lambda i: (i, 0, 0)),
-            whole(),
-            whole(),
-        ],
-        scratch_shapes=[
-            pltpu.VMEM((count, width), BF16),
-            pltpu.VMEM((local, room, width), BF16),
-            pltpu.VMEM((experts, count), F32),
-        ],
-        compiler_params=vmem(48),
-    )(*shards, modulation, router_weight.T, gate_up_weight)
-
+    hidden = pl.pallas_call(
+        functools.partial(hidden_kernel, steps),
+        out_shape=struct((local, room, 2 * units), BF16),
+        in_specs=[whole()] * (steps + 1),
+        out_specs=whole(),
+        compiler_params=vmem(12),
+    )(*picked, gate_up_weight.swapaxes(2, 3))
     share = pl.pallas_call(
-        functools.partial(output_kernel, sources),
-        grid=(local,),
+        functools.partial(output_kernel, steps),
         out_shape=[struct((count, 2 * lanes), BF16)] * sources,
-        in_specs=[
-            pl.BlockSpec((2, room, units), lambda i: (i, 0, 0)),
-            pl.BlockSpec((2, room, units), lambda i: (i, 0, 0)),
-            pl.BlockSpec((2, 2 * units, 2 * lanes), lambda i: (i, 0, 0)),
-            whole(),
-        ],
+        in_specs=[whole()] * (3 + steps),
         out_specs=[whole()] * sources,
         scratch_shapes=[pltpu.VMEM((sources, slots, 2 * lanes), BF16)],
-        compiler_params=vmem(32),
-    )(hidden, swap(hidden), down_weight, back)
+        compiler_params=vmem(8),
+    )(hidden, swap(hidden), down_weight, *backs)
 
     routed = None
     for flip in range(steps - 1, -1, -1):

time: 224 us -> 171 us (0.76)
  local copies, waits for them, and re-layouts: 58.6 us -> 18.5 us
  Pallas kernels: 32.4 us -> 21.4 us
  starting transfers between devices: 32.8 us -> 42.6 us
  waiting for transfers between devices: 94.8 us -> 86.1 us
    unnamed x22 -> x26, local copies, waits for them, and re-layouts: 51.1 us -> 16.5 us
    ppermute x19, waiting for transfers between devices: 88.2 us -> 75.2 us  [hop(): return lax.ppermute(x, 'dev', [(i, i ^ flip) for i in range(devices)])]
    pallas_call x2 -> x7, Pallas kernels: 27.8 us -> 16.8 us  [the longest x1 7.84 us: gathered_body(): pl.pallas_call(functools.partial(hidden_kernel, steps), out_shape=struct(...]
    ppermute x19, starting transfers between devices: 21.5 us -> 31.4 us  [hop(): return lax.ppermute(x, 'dev', [(i, i ^ flip) for i in range(devices)])]
    dynamic_slice x2 -> x0, local copies, waits for them, and re-layouts: 2.76 us -> none  [the longest x1 1.79 us: gathered_body(): lax.dynamic_index_in_dim(cut, 1 - side, 2, keepdims=False)]
  transfers between devices with their start and end apart: 34 -> 34, of which waited for: 16 -> 16; matrix products, arithmetic and copies ran while one was open for 20% -> 1% of each run, Pallas kernels for 1% -> 4%
where the time goes in v2:
time: 171 us; the launch traced here: 170 us
  waiting for transfers between devices  86.1 us (50%)
  starting transfers between devices  42.6 us (25%)
  Pallas kernels  21.4 us (13%)
  local copies, waits for them, and re-layouts  18.5 us (11%)
    ppermute x19, waiting for transfers between devices, hop(): return lax.ppermute(x, 'dev', [(i, i ^ flip) for i in range(devices)])  75.2 us
    ppermute x19, starting transfers between devices, hop(): return lax.ppermute(x, 'dev', [(i, i ^ flip) for i in range(devices)])  31.4 us
    unnamed x26, local copies, waits for them, and re-layouts  16.5 us
    pallas_call x1, Pallas kernels, gathered_body(): pl.pallas_call(functools.partial(hidden_kernel, steps), out_shape=struct(...  7.84 us
    ppermute x3, waiting for transfers between devices, gathered_body(): theirs = lax.ppermute(mine, 'groups', [(0, 1), (1, 0)])  6.73 us
    pallas_call x4, Pallas kernels, gathered_body(): pl.pallas_call(functools.partial(select_kernel, local, topk, own), out_sh...  5.3 us
    ppermute x1, starting transfers between devices, gathered_body(): before = lax.ppermute(pair, 'dev', [(i, i + 1) for i in range(devices - 1)])  5.01 us
    ppermute x10, waiting for transfers between devices, swap(): return lax.ppermute(x, 'sub', [(0, 1), (1, 0)])  4.19 us
  transfers between devices with their start and end apart: 34, of which 16 were waited for; matrix products, arithmetic and copies ran while one was open for 1% of the time, Pallas kernels for 4%

profile of v2, /device:TPU:0, one launch (start us, length us, event | category | flops | bytes accessed | tf_op | source)
XLA Modules:
  0.0 170.0 jit_solution(17891250502192664915)
XLA Ops:
  0.0 1.2 slice.8
  1.2 5.0 %collective-permute-start = (bf16[2,128,1024]{2,1,0:T(8,128)(2,1)S(1)}, bf16[2,128,1024]{2,1,0:T(8,128)(2,1)S(1)}, u32[]{:S(2)}, u32[]{:S(2)}) collective-permute-start(bf16[2,128,1024]{2,1,0:T(8,128)(2,1)S(1)} %slice.8), channel_id=1, source_target_pairs={{0,2},{2,4},{4,6},{6,8},{8,10},{10,12},{12,14},{1,3},{3,5},{5,7},{... | collective-permute-start | bytes 1572872 | tf_op jit(solution)/shard_map/ppermute | solution.py:264
  6.2 1.3 collective-permute-start.1
  7.6 1.0 copy-done.4
  8.6 1.0 copy-done.8
  9.6 0.7 copy-done.9
  10.4 2.7 %collective-permute-start.2 = (bf16[128,512]{1,0:T(8,128)(2,1)S(1)}, bf16[128,512]{1,0:T(8,128)(2,1)S(1)}, u32[]{:S(2)}, u32[]{:S(2)}) collective-permute-start(bf16[128,512]{1,0:T(8,128)(2,1)S(1)} %get-tuple-element.28), channel_id=1, source_target_pairs={{0,2},{2,0},{4,6},{6,4},{8,10},{10,8},{12,14},{14,12},{1,3},{3,1},... | collective-permute-start | bytes 393224 | tf_op jit(solution)/shard_map/ppermute | solution.py:257
  13.1 1.5 collective-permute-start.4
  14.6 2.6 %collective-permute-start.6 = (bf16[128,1024]{1,0:T(8,128)(2,1)S(1)}, bf16[128,1024]{1,0:T(8,128)(2,1)S(1)}, u32[]{:S(2)}, u32[]{:S(2)}) collective-permute-start(bf16[128,1024]{1,0:T(8,128)(2,1)S(1)} %get-tuple-element.29), channel_id=1, source_target_pairs={{0,8},{2,10},{4,12},{6,14},{8,0},{10,2},{12,4},{14,6},{1,9},{3,11}... | collective-permute-start | bytes 786440 | tf_op jit(solution)/shard_map/ppermute | solution.py:257
  17.2 14.2 %collective-permute-done.2._.far_ref = bf16[128,512]{1,0:T(8,128)(2,1)S(1)} collective-permute-done((bf16[128,512]{1,0:T(8,128)(2,1)S(1)}, bf16[128,512]{1,0:T(8,128)(2,1)S(1)}, u32[]{:S(2)}, u32[]{:S(2)}) %collective-permute-start.2) | collective-permute-done | bytes 131104 | tf_op jit(solution)/shard_map/ppermute | solution.py:257
  31.4 5.5 %collective-permute-start.8 = (bf16[128,1024]{1,0:T(8,128)(2,1)S(1)}, bf16[128,1024]{1,0:T(8,128)(2,1)S(1)}, u32[]{:S(2)}, u32[]{:S(2)}) collective-permute-start(bf16[128,1024]{1,0:T(8,128)(2,1)S(1)} %get-tuple-element.29), channel_id=1, source_target_pairs={{0,12},{2,14},{4,8},{6,10},{8,4},{10,6},{12,0},{14,2},{1,13},{3,15... | collective-permute-start | bytes 786440 | tf_op jit(solution)/shard_map/ppermute | solution.py:257
  36.9 1.5 collective-permute-start.5
  38.4 0.5 collective-permute-start.7
  38.9 4.6 %collective-permute-done.8.refs_7_ = bf16[128,1024]{1,0:T(8,128)(2,1)S(1)} collective-permute-done((bf16[128,1024]{1,0:T(8,128)(2,1)S(1)}, bf16[128,1024]{1,0:T(8,128)(2,1)S(1)}, u32[]{:S(2)}, u32[]{:S(2)}) %collective-permute-start.8) | collective-permute-done | bytes 262176 | tf_op jit(solution)/shard_map/ppermute | solution.py:257
  43.5 1.5 collective-permute-start.9
  45.0 1.1 copy-done.3
  46.2 3.1 %shard_map.83.refs_0_ = bf16[128,1024]{1,0:T(8,128)(2,1)S(1)} custom-call(bf16[3,128,1024]{2,1,0:T(8,128)(2,1)S(1)} %bitcast.13, bf16[2,128,1024]{2,1,0:T(8,128)(2,1)S(1)} %collective-permute-done.before_ref, bf16[2,128,1024]{2,1,0:T(8,128)(2,1)S(1)} %collective-permute-done.1.after_ref, bf16[128,512]{1,0:T(8,128)(2,1)S(1)} %collective-permute-done.2._.far_ref), custom_call_target="tpu_custom_call" | custom-call | tf_op jit(solution)/shard_map/pallas_call | solution.py:294
  49.3 0.1 collective-permute-start.3
  49.4 2.4 %collective-permute-done.7.refs_6_ = bf16[128,1024]{1,0:T(8,128)(2,1)S(1)} collective-permute-done((bf16[128,1024]{1,0:T(8,128)(2,1)S(1)}, bf16[128,1024]{1,0:T(8,128)(2,1)S(1)}, u32[]{:S(2)}, u32[]{:S(2)}) %collective-permute-start.7) | collective-permute-done | bytes 262176 | tf_op jit(solution)/shard_map/ppermute | solution.py:287
  51.7 4.4 %collective-permute-done.9.refs_8_ = bf16[128,1024]{1,0:T(8,128)(2,1)S(1)} collective-permute-done((bf16[128,1024]{1,0:T(8,128)(2,1)S(1)}, bf16[128,1024]{1,0:T(8,128)(2,1)S(1)}, u32[]{:S(2)}, u32[]{:S(2)}) %collective-permute-start.9) | collective-permute-done | bytes 262176 | tf_op jit(solution)/shard_map/ppermute | solution.py:287
  56.1 0.6 collective-permute-done.3.refs_1_
  56.7 1.0 copy-done.5
  57.8 1.4 shard_map.84
  59.2 1.9 %collective-permute-done.10.got_ref = f32[256,512]{1,0:T(8,128)S(1)} collective-permute-done((f32[256,512]{1,0:T(8,128)S(1)}, f32[256,512]{1,0:T(8,128)S(1)}, u32[]{:S(2)}, u32[]{:S(2)}) %collective-permute-start.10) | collective-permute-done | bytes 524320 | tf_op jit(solution)/shard_map/ppermute | solution.py:260
  61.1 0.8 copy-done.6
  61.9 0.1 shard_map.85.refs_0_
  62.0 3.3 %collective-permute-start.22 = (bf16[272,512]{1,0:T(8,128)(2,1)S(1)}, bf16[272,512]{1,0:T(8,128)(2,1)S(1)}, u32[]{:S(2)}, u32[]{:S(2)}) collective-permute-start(bf16[272,512]{1,0:T(8,128)(2,1)S(1)} %shard_map.85.refs_0_), channel_id=1, source_target_pairs={{0,12},{2,14},{4,8},{6,10},{8,4},{10,6},{12,0},{14,2},{1,13},{3,15... | collective-permute-start | bytes 835592 | tf_op jit(solution)/shard_map/ppermute | solution.py:257
  65.3 3.2 %collective-permute-start.18 = (bf16[272,512]{1,0:T(8,128)(2,1)S(1)}, bf16[272,512]{1,0:T(8,128)(2,1)S(1)}, u32[]{:S(2)}, u32[]{:S(2)}) collective-permute-start(bf16[272,512]{1,0:T(8,128)(2,1)S(1)} %shard_map.85.refs_0_), channel_id=1, source_target_pairs={{0,8},{2,10},{4,12},{6,14},{8,0},{10,2},{12,4},{14,6},{1,9},{3,11}... | collective-permute-start | bytes 835592 | tf_op jit(solution)/shard_map/ppermute | solution.py:257
  68.5 0.1 collective-permute-start.14
  68.6 0.3 collective-permute-start.11
  68.9 4.6 %collective-permute-done.22.refs_0_ = bf16[272,512]{1,0:T(8,128)(2,1)S(1)} collective-permute-done((bf16[272,512]{1,0:T(8,128)(2,1)S(1)}, bf16[272,512]{1,0:T(8,128)(2,1)S(1)}, u32[]{:S(2)}, u32[]{:S(2)}) %collective-permute-start.22) | collective-permute-done | bytes 278560 | tf_op jit(solution)/shard_map/ppermute | solution.py:257
  73.4 0.3 collective-permute-start.23
  73.7 16.7 %collective-permute-done.18.refs_0_ = bf16[272,512]{1,0:T(8,128)(2,1)S(1)} collective-permute-done((bf16[272,512]{1,0:T(8,128)(2,1)S(1)}, bf16[272,512]{1,0:T(8,128)(2,1)S(1)}, u32[]{:S(2)}, u32[]{:S(2)}) %collective-permute-start.18) | collective-permute-done | bytes 278560 | tf_op jit(solution)/shard_map/ppermute | solution.py:257
  90.5 0.3 collective-permute-start.19
  90.8 1.7 %collective-permute-start.15 = (bf16[272,512]{1,0:T(8,128)(2,1)S(1)}, bf16[272,512]{1,0:T(8,128)(2,1)S(1)}, u32[]{:S(2)}, u32[]{:S(2)}) collective-permute-start(bf16[272,512]{1,0:T(8,128)(2,1)S(1)} %collective-permute-done.14.refs_0_), channel_id=1, source_target_pairs={{0,2},{2,0},{4,6},{6,4},{8,10},{10,8},{12,14},{14,12},{1,3},{3,1},... | collective-permute-start | bytes 835592 | tf_op jit(solution)/shard_map/ppermute | solution.py:257
  92.5 0.5 collective-permute-start.20
  93.1 6.8 %collective-permute-done.19.refs_1_ = bf16[272,512]{1,0:T(8,128)(2,1)S(1)} collective-permute-done((bf16[272,512]{1,0:T(8,128)(2,1)S(1)}, bf16[272,512]{1,0:T(8,128)(2,1)S(1)}, u32[]{:S(2)}, u32[]{:S(2)}) %collective-permute-start.19) | collective-permute-done | bytes 278560 | tf_op jit(solution)/shard_map/ppermute | solution.py:257
  99.9 5.5 %collective-permute-done.15.refs_1_ = bf16[272,512]{1,0:T(8,128)(2,1)S(1)} collective-permute-done((bf16[272,512]{1,0:T(8,128)(2,1)S(1)}, bf16[272,512]{1,0:T(8,128)(2,1)S(1)}, u32[]{:S(2)}, u32[]{:S(2)}) %collective-permute-start.15) | collective-permute-done | bytes 278560 | tf_op jit(solution)/shard_map/ppermute | solution.py:257
  105.5 0.5 collective-permute-start.17
  106.0 0.9 copy-done.1
  107.0 0.8 copy-done.7
  107.7 1.3 shard_map.86
  109.1 0.9 copy-done.2
  110.0 1.3 shard_map.89
  111.4 1.3 shard_map.88
  112.7 1.3 shard_map.87
  114.1 8.1 %copy-done = bf16[16,2,2048,192]{2,3,1,0:T(8,128)(2,1)S(1)} copy-done((bf16[16,2,2048,192]{2,3,1,0:T(8,128)(2,1)S(1)}, bf16[16,2,2048,192]{2,3,1,0:T(8,128)(2,1)}, u32[]{:S(2)}) %copy-start) | copy-done | bytes 25165848
  122.2 7.8 %shard_map.90.near_ref = bf16[8,128,384]{2,1,0:T(8,128)(2,1)S(1)} custom-call(bf16[8,32,2048]{2,1,0:T(8,128)(2,1)S(1)} %get-tuple-element.35.refs_0_, bf16[8,32,2048]{2,1,0:T(8,128)(2,1)S(1)} %get-tuple-element.36.refs_1_, bf16[8,32,2048]{2,1,0:T(8,128)(2,1)S(1)} %get-tuple-element.37.refs_2_, bf16[8,32,2048]{2,1,0:T(8,128)(2,1)S(1)} %get-tuple-element.38.refs_3_, ...), custom_call_target="tpu_custom_call" | custom-call | tf_op jit(solution)/shard_map/pallas_call | solution.py:345
  130.1 2.3 %collective-permute-done.26.far_ref = bf16[8,128,384]{2,1,0:T(8,128)(2,1)S(1)} collective-permute-done((bf16[8,128,384]{2,1,0:T(8,128)(2,1)S(1)}, bf16[8,128,384]{2,1,0:T(8,128)(2,1)S(1)}, u32[]{:S(2)}, u32[]{:S(2)}) %collective-permute-start.26) | collective-permute-done | bytes 786464 | tf_op jit(solution)/shard_map/ppermute | solution.py:260
  132.4 3.6 %shard_map.91 = (bf16[128,1024]{1,0:T(8,128)(2,1)S(1)}, bf16[128,1024]{1,0:T(8,128)(2,1)S(1)}, bf16[128,1024]{1,0:T(8,128)(2,1)S(1)}, bf16[128,1024]{1,0:T(8,128...) custom-call(bf16[8,128,384]{2,1,0:T(8,128)(2,1)S(1)} %shard_map.90.n, ...), custom_call_target="tpu_custom_call" | custom-call | tf_op jit(solution)/shard_map/pallas_call | solution.py:352
  136.0 0.4 collective-permute-start.27
  136.4 1.7 %collective-permute-start.29 = (bf16[128,1024]{1,0:T(8,128)(2,1)S(1)}, bf16[128,1024]{1,0:T(8,128)(2,1)S(1)}, u32[]{:S(2)}, u32[]{:S(2)}) collective-permute-start(bf16[128,1024]{1,0:T(8,128)(2,1)S(1)} %get-tuple-element.46), channel_id=1, source_target_pairs={{0,2},{2,0},{4,6},{6,4},{8,10},{10,8},{12,14},{14,12},{1,3},{3,1},... | collective-permute-start | bytes 786440 | tf_op jit(solution)/shard_map/ppermute | solution.py:257
  138.1 0.3 collective-permute-start.31
  138.4 1.7 %collective-permute-start.33 = (bf16[128,1024]{1,0:T(8,128)(2,1)S(1)}, bf16[128,1024]{1,0:T(8,128)(2,1)S(1)}, u32[]{:S(2)}, u32[]{:S(2)}) collective-permute-start(bf16[128,1024]{1,0:T(8,128)(2,1)S(1)} %get-tuple-element.50), channel_id=1, source_target_pairs={{0,2},{2,0},{4,6},{6,4},{8,10},{10,8},{12,14},{14,12},{1,3},{3,1},... | collective-permute-start | bytes 786440 | tf_op jit(solution)/shard_map/ppermute | solution.py:257
  140.2 5.1 %collective-permute-done.27 = bf16[128,1024]{1,0:T(8,128)(2,1)S(1)} collective-permute-done((bf16[128,1024]{1,0:T(8,128)(2,1)S(1)}, bf16[128,1024]{1,0:T(8,128)(2,1)S(1)}, u32[]{:S(2)}, u32[]{:S(2)}) %collective-permute-start.27) | collective-permute-done | bytes 262176 | tf_op jit(solution)/shard_map/ppermute | solution.py:257
  145.3 3.3 %collective-permute-start.28 = (bf16[128,1024]{1,0:T(8,128)(2,1)S(1)}, bf16[128,1024]{1,0:T(8,128)(2,1)S(1)}, u32[]{:S(2)}, u32[]{:S(2)}) collective-permute-start(bf16[128,1024]{1,0:T(8,128)(2,1)S(1)} %add_convert_fusion.3), channel_id=1, source_target_pairs={{0,12},{2,14},{4,8},{6,10},{8,4},{10,6},{12,0},{14,2},{1,13},{3,15... | collective-permute-start | bytes 786440 | tf_op jit(solution)/shard_map/ppermute | solution.py:257
  148.6 2.3 %collective-permute-done.29 = bf16[128,1024]{1,0:T(8,128)(2,1)S(1)} collective-permute-done((bf16[128,1024]{1,0:T(8,128)(2,1)S(1)}, bf16[128,1024]{1,0:T(8,128)(2,1)S(1)}, u32[]{:S(2)}, u32[]{:S(2)}) %collective-permute-start.29) | collective-permute-done | bytes 262176 | tf_op jit(solution)/shard_map/ppermute | solution.py:257
  151.0 1.9 %collective-permute-start.30 = (bf16[128,1024]{1,0:T(8,128)(2,1)S(1)}, bf16[128,1024]{1,0:T(8,128)(2,1)S(1)}, u32[]{:S(2)}, u32[]{:S(2)}) collective-permute-start(bf16[128,1024]{1,0:T(8,128)(2,1)S(1)} %add_convert_fusion.2), channel_id=1, source_target_pairs={{0,8},{2,10},{4,12},{6,14},{8,0},{10,2},{12,4},{14,6},{1,9},{3,11}... | collective-permute-start | bytes 786440 | tf_op jit(solution)/shard_map/ppermute | solution.py:257
  152.9 3.6 %collective-permute-done.31 = bf16[128,1024]{1,0:T(8,128)(2,1)S(1)} collective-permute-done((bf16[128,1024]{1,0:T(8,128)(2,1)S(1)}, bf16[128,1024]{1,0:T(8,128)(2,1)S(1)}, u32[]{:S(2)}, u32[]{:S(2)}) %collective-permute-start.31) | collective-permute-done | bytes 262176 | tf_op jit(solution)/shard_map/ppermute | solution.py:257
  156.6 0.5 collective-permute-start.32
  157.1 0.8 slice.7
  157.8 3.4 %collective-permute-done.33 = bf16[128,1024]{1,0:T(8,128)(2,1)S(1)} collective-permute-done((bf16[128,1024]{1,0:T(8,128)(2,1)S(1)}, bf16[128,1024]{1,0:T(8,128)(2,1)S(1)}, u32[]{:S(2)}, u32[]{:S(2)}) %collective-permute-start.33) | collective-permute-done | bytes 262176 | tf_op jit(solution)/shard_map/ppermute | solution.py:257
  161.3 7.7 %collective-permute-done.30 = bf16[128,1024]{1,0:T(8,128)(2,1)S(1)} collective-permute-done((bf16[128,1024]{1,0:T(8,128)(2,1)S(1)}, bf16[128,1024]{1,0:T(8,128)(2,1)S(1)}, u32[]{:S(2)}, u32[]{:S(2)}) %collective-permute-start.30) | collective-permute-done | bytes 262176 | tf_op jit(solution)/shard_map/ppermute | solution.py:257
  169.0 1.0 add_convert_fusion
  (48 shorter events, 0.6 us)
Async XLA Ops:
  0.0 132.4 %slice-start = ((s8[12582912]{0:T(1024)(128)(4,1)}), s8[4194304]{0:T(1024)(128)(4,1)S(1)}, s32[]{:S(2)}) async-start(s8[12582912]{0:T(1024)(128)(4,1)} %bitcast.6), calls=%async_computation | async-start | bytes 8388608
  1.2 43.8 %collective-permute-start = (bf16[2,128,1024]{2,1,0:T(8,128)(2,1)S(1)}, bf16[2,128,1024]{2,1,0:T(8,128)(2,1)S(1)}, u32[]{:S(2)}, u32[]{:S(2)}) collective-permute-start(bf16[2,128,1024]{2,1,0:T(8,128)(2,1)S(1)} %slice.8), channel_id=1, source_target_pairs={{0,2},{2,4},{4,6},{6,8},{8,10},{10,12},{12,14},{1,3},{3,5},{5,7},{... | collective-permute-start | bytes 1572872 | tf_op jit(solution)/shard_map/ppermute | solution.py:264
  6.2 38.8 %collective-permute-start.1 = (bf16[2,128,1024]{2,1,0:T(8,128)(2,1)S(1)}, bf16[2,128,1024]{2,1,0:T(8,128)(2,1)S(1)}, u32[]{:S(2)}, u32[]{:S(2)}) collective-permute-start(bf16[2,128,1024]{2,1,0:T(8,128)(2,1)S(1)} %slice.8), channel_id=1, source_target_pairs={{2,0},{4,2},{6,4},{8,6},{10,8},{12,10},{14,12},{3,1},{5,3},{7,5},{... | collective-permute-start | bytes 1572872 | tf_op jit(solution)/shard_map/ppermute | solution.py:265
  7.5 1.0 copy-start.4
  8.6 1.0 copy-start.8
  9.6 0.7 copy-start.9
  10.4 21.0 %collective-permute-start.2 = (bf16[128,512]{1,0:T(8,128)(2,1)S(1)}, bf16[128,512]{1,0:T(8,128)(2,1)S(1)}, u32[]{:S(2)}, u32[]{:S(2)}) collective-permute-start(bf16[128,512]{1,0:T(8,128)(2,1)S(1)} %get-tuple-element.28), channel_id=1, source_target_pairs={{0,2},{2,0},{4,6},{6,4},{8,10},{10,8},{12,14},{14,12},{1,3},{3,1},... | collective-permute-start | bytes 393224 | tf_op jit(solution)/shard_map/ppermute | solution.py:257
  13.1 23.8 %collective-permute-start.4 = (bf16[128,1024]{1,0:T(8,128)(2,1)S(1)}, bf16[128,1024]{1,0:T(8,128)(2,1)S(1)}, u32[]{:S(2)}, u32[]{:S(2)}) collective-permute-start(bf16[128,1024]{1,0:T(8,128)(2,1)S(1)} %get-tuple-element.29), channel_id=1, source_target_pairs={{0,4},{2,6},{4,0},{6,2},{8,12},{10,14},{12,8},{14,10},{1,5},{3,7},... | collective-permute-start | bytes 786440 | tf_op jit(solution)/shard_map/ppermute | solution.py:257
  14.6 23.8 %collective-permute-start.6 = (bf16[128,1024]{1,0:T(8,128)(2,1)S(1)}, bf16[128,1024]{1,0:T(8,128)(2,1)S(1)}, u32[]{:S(2)}, u32[]{:S(2)}) collective-permute-start(bf16[128,1024]{1,0:T(8,128)(2,1)S(1)} %get-tuple-element.29), channel_id=1, source_target_pairs={{0,8},{2,10},{4,12},{6,14},{8,0},{10,2},{12,4},{14,6},{1,9},{3,11}... | collective-permute-start | bytes 786440 | tf_op jit(solution)/shard_map/ppermute | solution.py:257
  31.4 12.1 %collective-permute-start.8 = (bf16[128,1024]{1,0:T(8,128)(2,1)S(1)}, bf16[128,1024]{1,0:T(8,128)(2,1)S(1)}, u32[]{:S(2)}, u32[]{:S(2)}) collective-permute-start(bf16[128,1024]{1,0:T(8,128)(2,1)S(1)} %get-tuple-element.29), channel_id=1, source_target_pairs={{0,12},{2,14},{4,8},{6,10},{8,4},{10,6},{12,0},{14,2},{1,13},{3,15... | collective-permute-start | bytes 786440 | tf_op jit(solution)/shard_map/ppermute | solution.py:257
  36.9 12.4 %collective-permute-start.5 = (bf16[128,1024]{1,0:T(8,128)(2,1)S(1)}, bf16[128,1024]{1,0:T(8,128)(2,1)S(1)}, u32[]{:S(2)}, u32[]{:S(2)}) collective-permute-start(bf16[128,1024]{1,0:T(8,128)(2,1)S(1)} %collective-permute-done.4.refs_3_), channel_id=1, source_target_pairs={{0,16},{16,0},{1,17},{17,1},{2,18},{18,2},{3,19},{19,3},{4,20},{20... | collective-permute-start | bytes 786440 | tf_op jit(solution)/shard_map/ppermute | solution.py:287
  38.4 13.3 %collective-permute-start.7 = (bf16[128,1024]{1,0:T(8,128)(2,1)S(1)}, bf16[128,1024]{1,0:T(8,128)(2,1)S(1)}, u32[]{:S(2)}, u32[]{:S(2)}) collective-permute-start(bf16[128,1024]{1,0:T(8,128)(2,1)S(1)} %collective-permute-done.6.refs_5_), channel_id=1, source_target_pairs={{0,16},{16,0},{1,17},{17,1},{2,18},{18,2},{3,19},{19,3},{4,20},{20... | collective-permute-start | bytes 786440 | tf_op jit(solution)/shard_map/ppermute | solution.py:287
  43.5 12.6 %collective-permute-start.9 = (bf16[128,1024]{1,0:T(8,128)(2,1)S(1)}, bf16[128,1024]{1,0:T(8,128)(2,1)S(1)}, u32[]{:S(2)}, u32[]{:S(2)}) collective-permute-start(bf16[128,1024]{1,0:T(8,128)(2,1)S(1)} %collective-permute-done.8.refs_7_), channel_id=1, source_target_pairs={{0,16},{16,0},{1,17},{17,1},{2,18},{18,2},{3,19},{19,3},{4,20},{20... | collective-permute-start | bytes 786440 | tf_op jit(solution)/shard_map/ppermute | solution.py:287
  45.0 1.1 copy-start.3
  49.3 7.4 %collective-permute-start.3 = (bf16[128,1024]{1,0:T(8,128)(2,1)S(1)}, bf16[128,1024]{1,0:T(8,128)(2,1)S(1)}, u32[]{:S(2)}, u32[]{:S(2)}) collective-permute-start(bf16[128,1024]{1,0:T(8,128)(2,1)S(1)} %shard_map.83.refs_0_), channel_id=1, source_target_pairs={{0,2},{2,0},{4,6},{6,4},{8,10},{10,8},{12,14},{14,12},{1,3},{3,1},... | collective-permute-start | bytes 786440 | tf_op jit(solution)/shard_map/ppermute | solution.py:257
  56.7 1.0 copy-start.5
  59.1 2.0 %collective-permute-start.10 = (f32[256,512]{1,0:T(8,128)S(1)}, f32[256,512]{1,0:T(8,128)S(1)}, u32[]{:S(2)}, u32[]{:S(2)}) collective-permute-start(f32[256,512]{1,0:T(8,128)S(1)} %get-tuple-element.31), channel_id=1, source_target_pairs={{0,1},{1,0},{2,3},{3,2},{4,5},{5,4},{6,7},{7,6},{8,9},{9,8},{10,11... | collective-permute-start | bytes 1572872 | tf_op jit(solution)/shard_map/ppermute | solution.py:260
  61.1 0.8 copy-start.6
  62.0 11.5 %collective-permute-start.22 = (bf16[272,512]{1,0:T(8,128)(2,1)S(1)}, bf16[272,512]{1,0:T(8,128)(2,1)S(1)}, u32[]{:S(2)}, u32[]{:S(2)}) collective-permute-start(bf16[272,512]{1,0:T(8,128)(2,1)S(1)} %shard_map.85.refs_0_), channel_id=1, source_target_pairs={{0,12},{2,14},{4,8},{6,10},{8,4},{10,6},{12,0},{14,2},{1,13},{3,15... | collective-permute-start | bytes 835592 | tf_op jit(solution)/shard_map/ppermute | solution.py:257
  65.3 25.2 %collective-permute-start.18 = (bf16[272,512]{1,0:T(8,128)(2,1)S(1)}, bf16[272,512]{1,0:T(8,128)(2,1)S(1)}, u32[]{:S(2)}, u32[]{:S(2)}) collective-permute-start(bf16[272,512]{1,0:T(8,128)(2,1)S(1)} %shard_map.85.refs_0_), channel_id=1, source_target_pairs={{0,8},{2,10},{4,12},{6,14},{8,0},{10,2},{12,4},{14,6},{1,9},{3,11}... | collective-permute-start | bytes 835592 | tf_op jit(solution)/shard_map/ppermute | solution.py:257
  68.5 22.0 %collective-permute-start.14 = (bf16[272,512]{1,0:T(8,128)(2,1)S(1)}, bf16[272,512]{1,0:T(8,128)(2,1)S(1)}, u32[]{:S(2)}, u32[]{:S(2)}) collective-permute-start(bf16[272,512]{1,0:T(8,128)(2,1)S(1)} %shard_map.85.refs_0_), channel_id=1, source_target_pairs={{0,4},{2,6},{4,0},{6,2},{8,12},{10,14},{12,8},{14,10},{1,5},{3,7},... | collective-permute-start | bytes 835592 | tf_op jit(solution)/shard_map/ppermute | solution.py:257
  68.6 22.2 %collective-permute-start.11 = (bf16[272,512]{1,0:T(8,128)(2,1)S(1)}, bf16[272,512]{1,0:T(8,128)(2,1)S(1)}, u32[]{:S(2)}, u32[]{:S(2)}) collective-permute-start(bf16[272,512]{1,0:T(8,128)(2,1)S(1)} %shard_map.85.refs_0_), channel_id=1, source_target_pairs={{0,2},{2,0},{4,6},{6,4},{8,10},{10,8},{12,14},{14,12},{1,3},{3,1},... | collective-permute-start | bytes 835592 | tf_op jit(solution)/shard_map/ppermute | solution.py:257
  68.9 23.6 %collective-permute-start.12 = (bf16[272,512]{1,0:T(8,128)(2,1)S(1)}, bf16[272,512]{1,0:T(8,128)(2,1)S(1)}, u32[]{:S(2)}, u32[]{:S(2)}) collective-permute-start(bf16[272,512]{1,0:T(8,128)(2,1)S(1)} %shard_map.85.refs_0_), channel_id=1, source_target_pairs={{0,1},{1,0},{2,3},{3,2},{4,5},{5,4},{6,7},{7,6},{8,9},{9,8},{10,11... | collective-permute-start | bytes 835592 | tf_op jit(solution)/shard_map/ppermute | solution.py:260
  73.4 19.1 %collective-permute-start.23 = (bf16[272,512]{1,0:T(8,128)(2,1)S(1)}, bf16[272,512]{1,0:T(8,128)(2,1)S(1)}, u32[]{:S(2)}, u32[]{:S(2)}) collective-permute-start(bf16[272,512]{1,0:T(8,128)(2,1)S(1)} %collective-permute-done.22.refs_0_), channel_id=1, source_target_pairs={{0,2},{2,0},{4,6},{6,4},{8,10},{10,8},{12,14},{14,12},{1,3},{3,1},... | collective-permute-start | bytes 835592 | tf_op jit(solution)/shard_map/ppermute | solution.py:257
  90.4 2.6 %collective-permute-start.24 = (bf16[272,512]{1,0:T(8,128)(2,1)S(1)}, bf16[272,512]{1,0:T(8,128)(2,1)S(1)}, u32[]{:S(2)}, u32[]{:S(2)}) collective-permute-start(bf16[272,512]{1,0:T(8,128)(2,1)S(1)} %collective-permute-done.22.refs_0_), channel_id=1, source_target_pairs={{0,1},{1,0},{2,3},{3,2},{4,5},{5,4},{6,7},{7,6},{8,9},{9,8},{10,11... | collective-permute-start | bytes 835592 | tf_op jit(solution)/shard_map/ppermute | solution.py:260
  90.5 9.5 %collective-permute-start.19 = (bf16[272,512]{1,0:T(8,128)(2,1)S(1)}, bf16[272,512]{1,0:T(8,128)(2,1)S(1)}, u32[]{:S(2)}, u32[]{:S(2)}) collective-permute-start(bf16[272,512]{1,0:T(8,128)(2,1)S(1)} %collective-permute-done.18.refs_0_), channel_id=1, source_target_pairs={{0,2},{2,0},{4,6},{6,4},{8,10},{10,8},{12,14},{14,12},{1,3},{3,1},... | collective-permute-start | bytes 835592 | tf_op jit(solution)/shard_map/ppermute | solution.py:257
  90.8 14.7 %collective-permute-start.15 = (bf16[272,512]{1,0:T(8,128)(2,1)S(1)}, bf16[272,512]{1,0:T(8,128)(2,1)S(1)}, u32[]{:S(2)}, u32[]{:S(2)}) collective-permute-start(bf16[272,512]{1,0:T(8,128)(2,1)S(1)} %collective-permute-done.14.refs_0_), channel_id=1, source_target_pairs={{0,2},{2,0},{4,6},{6,4},{8,10},{10,8},{12,14},{14,12},{1,3},{3,1},... | collective-permute-start | bytes 835592 | tf_op jit(solution)/shard_map/ppermute | solution.py:257
  92.5 13.0 %collective-permute-start.13 = (bf16[272,512]{1,0:T(8,128)(2,1)S(1)}, bf16[272,512]{1,0:T(8,128)(2,1)S(1)}, u32[]{:S(2)}, u32[]{:S(2)}) collective-permute-start(bf16[272,512]{1,0:T(8,128)(2,1)S(1)} %collective-permute-done.11.refs_1_), channel_id=1, source_target_pairs={{0,1},{1,0},{2,3},{3,2},{4,5},{5,4},{6,7},{7,6},{8,9},{9,8},{10,11... | collective-permute-start | bytes 835592 | tf_op jit(solution)/shard_map/ppermute | solution.py:260
  92.5 18.8 %collective-permute-start.20 = (bf16[272,512]{1,0:T(8,128)(2,1)S(1)}, bf16[272,512]{1,0:T(8,128)(2,1)S(1)}, u32[]{:S(2)}, u32[]{:S(2)}) collective-permute-start(bf16[272,512]{1,0:T(8,128)(2,1)S(1)} %collective-permute-done.18.refs_0_), channel_id=1, source_target_pairs={{0,1},{1,0},{2,3},{3,2},{4,5},{5,4},{6,7},{7,6},{8,9},{9,8},{10,11... | collective-permute-start | bytes 835592 | tf_op jit(solution)/shard_map/ppermute | solution.py:260
  93.0 16.0 %collective-permute-start.25 = (bf16[272,512]{1,0:T(8,128)(2,1)S(1)}, bf16[272,512]{1,0:T(8,128)(2,1)S(1)}, u32[]{:S(2)}, u32[]{:S(2)}) collective-permute-start(bf16[272,512]{1,0:T(8,128)(2,1)S(1)} %collective-permute-done.23.refs_1_), channel_id=1, source_target_pairs={{0,1},{1,0},{2,3},{3,2},{4,5},{5,4},{6,7},{7,6},{8,9},{9,8},{10,11... | collective-permute-start | bytes 835592 | tf_op jit(solution)/shard_map/ppermute | solution.py:260
  99.9 11.4 %collective-permute-start.21 = (bf16[272,512]{1,0:T(8,128)(2,1)S(1)}, bf16[272,512]{1,0:T(8,128)(2,1)S(1)}, u32[]{:S(2)}, u32[]{:S(2)}) collective-permute-start(bf16[272,512]{1,0:T(8,128)(2,1)S(1)} %collective-permute-done.19.refs_1_), channel_id=1, source_target_pairs={{0,1},{1,0},{2,3},{3,2},{4,5},{5,4},{6,7},{7,6},{8,9},{9,8},{10,11... | collective-permute-start | bytes 835592 | tf_op jit(solution)/shard_map/ppermute | solution.py:260
  105.5 7.2 %collective-permute-start.16 = (bf16[272,512]{1,0:T(8,128)(2,1)S(1)}, bf16[272,512]{1,0:T(8,128)(2,1)S(1)}, u32[]{:S(2)}, u32[]{:S(2)}) collective-permute-start(bf16[272,512]{1,0:T(8,128)(2,1)S(1)} %collective-permute-done.14.refs_0_), channel_id=1, source_target_pairs={{0,1},{1,0},{2,3},{3,2},{4,5},{5,4},{6,7},{7,6},{8,9},{9,8},{10,11... | collective-permute-start | bytes 835592 | tf_op jit(solution)/shard_map/ppermute | solution.py:260
  105.5 7.2 %collective-permute-start.17 = (bf16[272,512]{1,0:T(8,128)(2,1)S(1)}, bf16[272,512]{1,0:T(8,128)(2,1)S(1)}, u32[]{:S(2)}, u32[]{:S(2)}) collective-permute-start(bf16[272,512]{1,0:T(8,128)(2,1)S(1)} %collective-permute-done.15.refs_1_), channel_id=1, source_target_pairs={{0,1},{1,0},{2,3},{3,2},{4,5},{5,4},{6,7},{7,6},{8,9},{9,8},{10,11... | collective-permute-start | bytes 835592 | tf_op jit(solution)/shard_map/ppermute | solution.py:260
  106.0 0.9 copy-start.1
  107.0 0.8 copy-start.7
  109.1 1.0 copy-start.2
  114.0 8.2 %copy-start = (bf16[16,2,2048,192]{2,3,1,0:T(8,128)(2,1)S(1)}, bf16[16,2,2048,192]{2,3,1,0:T(8,128)(2,1)}, u32[]{:S(2)}) copy-start(bf16[16,2,2048,192]{2,3,1,0:T(8,128)(2,1)} %param.14) | copy-start | bytes 75497472
  122.2 10.2 %slice-start.1 = ((s8[12582912]{0:T(1024)(128)(4,1)}), s8[4194304]{0:T(1024)(128)(4,1)S(1)}, s32[]{:S(2)}) async-start(s8[12582912]{0:T(1024)(128)(4,1)} %bitcast.6), calls=%async_computation.1 | async-start | bytes 8388608
  122.2 10.2 %slice-start.2 = ((s8[12582912]{0:T(1024)(128)(4,1)}), s8[4194304]{0:T(1024)(128)(4,1)S(1)}, s32[]{:S(2)}) async-start(s8[12582912]{0:T(1024)(128)(4,1)} %bitcast.6), calls=%async_computation.2 | async-start | bytes 8388608
  130.1 2.4 %collective-permute-start.26 = (bf16[8,128,384]{2,1,0:T(8,128)(2,1)S(1)}, bf16[8,128,384]{2,1,0:T(8,128)(2,1)S(1)}, u32[]{:S(2)}, u32[]{:S(2)}) collective-permute-start(bf16[8,128,384]{2,1,0:T(8,128)(2,1)S(1)} %shard_map.90.near_ref), channel_id=1, source_target_pairs={{0,1},{1,0},{2,3},{3,2},{4,5},{5,4},{6,7},{7,6},{8,9},{9,8},{10,11... | collective-permute-start | bytes 2359304 | tf_op jit(solution)/shard_map/ppermute | solution.py:260
  136.0 9.2 %collective-permute-start.27 = (bf16[128,1024]{1,0:T(8,128)(2,1)S(1)}, bf16[128,1024]{1,0:T(8,128)(2,1)S(1)}, u32[]{:S(2)}, u32[]{:S(2)}) collective-permute-start(bf16[128,1024]{1,0:T(8,128)(2,1)S(1)} %get-tuple-element.44), channel_id=1, source_target_pairs={{0,2},{2,0},{4,6},{6,4},{8,10},{10,8},{12,14},{14,12},{1,3},{3,1},... | collective-permute-start | bytes 786440 | tf_op jit(solution)/shard_map/ppermute | solution.py:257
  136.4 14.5 %collective-permute-start.29 = (bf16[128,1024]{1,0:T(8,128)(2,1)S(1)}, bf16[128,1024]{1,0:T(8,128)(2,1)S(1)}, u32[]{:S(2)}, u32[]{:S(2)}) collective-permute-start(bf16[128,1024]{1,0:T(8,128)(2,1)S(1)} %get-tuple-element.46), channel_id=1, source_target_pairs={{0,2},{2,0},{4,6},{6,4},{8,10},{10,8},{12,14},{14,12},{1,3},{3,1},... | collective-permute-start | bytes 786440 | tf_op jit(solution)/shard_map/ppermute | solution.py:257
  138.1 18.4 %collective-permute-start.31 = (bf16[128,1024]{1,0:T(8,128)(2,1)S(1)}, bf16[128,1024]{1,0:T(8,128)(2,1)S(1)}, u32[]{:S(2)}, u32[]{:S(2)}) collective-permute-start(bf16[128,1024]{1,0:T(8,128)(2,1)S(1)} %get-tuple-element.48), channel_id=1, source_target_pairs={{0,2},{2,0},{4,6},{6,4},{8,10},{10,8},{12,14},{14,12},{1,3},{3,1},... | collective-permute-start | bytes 786440 | tf_op jit(solution)/shard_map/ppermute | solution.py:257
  138.4 22.8 %collective-permute-start.33 = (bf16[128,1024]{1,0:T(8,128)(2,1)S(1)}, bf16[128,1024]{1,0:T(8,128)(2,1)S(1)}, u32[]{:S(2)}, u32[]{:S(2)}) collective-permute-start(bf16[128,1024]{1,0:T(8,128)(2,1)S(1)} %get-tuple-element.50), channel_id=1, source_target_pairs={{0,2},{2,0},{4,6},{6,4},{8,10},{10,8},{12,14},{14,12},{1,3},{3,1},... | collective-permute-start | bytes 786440 | tf_op jit(solution)/shard_map/ppermute | solution.py:257
  145.3 16.0 %collective-permute-start.28 = (bf16[128,1024]{1,0:T(8,128)(2,1)S(1)}, bf16[128,1024]{1,0:T(8,128)(2,1)S(1)}, u32[]{:S(2)}, u32[]{:S(2)}) collective-permute-start(bf16[128,1024]{1,0:T(8,128)(2,1)S(1)} %add_convert_fusion.3), channel_id=1, source_target_pairs={{0,12},{2,14},{4,8},{6,10},{8,4},{10,6},{12,0},{14,2},{1,13},{3,15... | collective-permute-start | bytes 786440 | tf_op jit(solution)/shard_map/ppermute | solution.py:257
  151.0 18.1 %collective-permute-start.30 = (bf16[128,1024]{1,0:T(8,128)(2,1)S(1)}, bf16[128,1024]{1,0:T(8,128)(2,1)S(1)}, u32[]{:S(2)}, u32[]{:S(2)}) collective-permute-start(bf16[128,1024]{1,0:T(8,128)(2,1)S(1)} %add_convert_fusion.2), channel_id=1, source_target_pairs={{0,8},{2,10},{4,12},{6,14},{8,0},{10,2},{12,4},{14,6},{1,9},{3,11}... | collective-permute-start | bytes 786440 | tf_op jit(solution)/shard_map/ppermute | solution.py:257
  156.6 12.5 %collective-permute-start.32 = (bf16[128,1024]{1,0:T(8,128)(2,1)S(1)}, bf16[128,1024]{1,0:T(8,128)(2,1)S(1)}, u32[]{:S(2)}, u32[]{:S(2)}) collective-permute-start(bf16[128,1024]{1,0:T(8,128)(2,1)S(1)} %add_convert_fusion.1), channel_id=1, source_target_pairs={{0,4},{2,6},{4,0},{6,2},{8,12},{10,14},{12,8},{14,10},{1,5},{3,7},... | collective-permute-start | bytes 786440 | tf_op jit(solution)/shard_map/ppermute | solution.py:257

commit v3 on v2

--- a/solution.py
+++ b/solution.py
@@ -29,36 +29,44 @@
     return pl.BlockSpec(memory_space=pltpu.VMEM)
 
 
-def cut_kernel(split, tokens_ref, weight_ref, ids_ref, near_ref, far_ref, sent_ref, row_ref):
-    lanes = near_ref.shape[1]
+def cut_kernel(split, tokens_ref, pair_ref, weight_ref, ids_ref, near_ref, cross_ref, sent_ref, row_ref):
+    count, lanes = near_ref.shape
     chunk = tokens_ref.shape[1] // lax.axis_size("dev")
     side = lax.axis_index("dev") % 2
     part = lax.axis_index("sub")
-    for ref, parity in ((near_ref, side), (far_ref, 1 - side)):
-        for i in range(lanes // chunk):
-            at = pl.multiple_of(part * 2 * lanes + (2 * i + parity) * chunk, 128)
-            ref[:, i * chunk : (i + 1) * chunk] = tokens_ref[:, pl.ds(at, chunk)]
+    half = count // 2
+    cross_ref[: 2 * count] = pair_ref[...]
+    for i in range(lanes // chunk):
+        cols = slice(i * chunk, (i + 1) * chunk)
+        at = pl.multiple_of(part * 2 * lanes + (2 * i + side) * chunk, 128)
+        near_ref[:, cols] = tokens_ref[:, pl.ds(at, chunk)]
+        at = pl.multiple_of(part * 2 * lanes + (2 * i + 1 - side) * chunk, 128)
+        for j in range(2):
+            cross_ref[2 * count :, j * lanes + i * chunk : j * lanes + (i + 1) * chunk] = (
+                tokens_ref[j * half : (j + 1) * half, pl.ds(at, chunk)]
+            )
     if split:
         rows = sent_ref.shape[0]
         at = pl.multiple_of(lax.axis_index("groups") * rows, TILE)
         sent_ref[...] = weight_ref[pl.ds(at, rows), :]
     else:
         sent_ref[...] = weight_ref[...]
-    topk, count = ids_ref.shape
+    topk = ids_ref.shape[0]
     row_ref[...] = jnp.zeros(row_ref.shape, BF16)
     for k in range(topk):
         named = jnp.broadcast_to(ids_ref[k : k + 1, :], (TILE, count))
         row_ref[:, k * count : (k + 1) * count] = named.astype(F32).astype(BF16)
 
 
-def attention_kernel(own_ref, before_ref, after_ref, _, mixed_ref):
+def attention_kernel(own_ref, cross_ref, next_ref, mixed_ref):
     count, width = mixed_ref.shape
     place = lax.axis_index("dev")
-    last = lax.axis_size("dev") - 1
+    even = place % 2 == 0
     row = lax.broadcasted_iota(jnp.int32, (count, count), 0)
     col = lax.broadcasted_iota(jnp.int32, (count, count), 1)
-    see_before = (col >= row) & (place > 0)
-    see_after = (col <= row) & (place < last)
+    alone = (place == 0) | (place == lax.axis_size("dev") - 1)
+    see_cross = jnp.where(even, col - row, row - col) <= 0
+    see_next = (jnp.where(even, row - col, col - row) <= 0) & jnp.logical_not(alone)
     scale = 1.0 / math.sqrt(HEAD)
 
     def scored(q, k):
@@ -67,17 +75,17 @@
     for head in range(width // HEAD):
         lanes = slice(head * HEAD, (head + 1) * HEAD)
         q = own_ref[0, :, lanes]
-        sb = jnp.where(see_before, scored(q, before_ref[0, :, lanes]), NEG)
+        sc = jnp.where(see_cross, scored(q, cross_ref[:count, lanes]), NEG)
         so = scored(q, own_ref[1, :, lanes])
-        sa = jnp.where(see_after, scored(q, after_ref[0, :, lanes]), NEG)
-        top = jnp.max(jnp.maximum(jnp.maximum(sb, so), sa), 1, keepdims=True)
-        wb, wo, wa = jnp.exp(sb - top), jnp.exp(so - top), jnp.exp(sa - top)
-        inv = 1.0 / jnp.sum(wb + wo + wa, 1, keepdims=True)
+        sn = jnp.where(see_next, scored(q, next_ref[:count, lanes]), NEG)
+        top = jnp.max(jnp.maximum(jnp.maximum(sc, so), sn), 1, keepdims=True)
+        wc, wo, wn = jnp.exp(sc - top), jnp.exp(so - top), jnp.exp(sn - top)
+        inv = 1.0 / jnp.sum(wc + wo + wn, 1, keepdims=True)
         out = 0.0
         for weight, value in (
             (wo, own_ref[2, :, lanes]),
-            (wb, before_ref[1, :, lanes]),
-            (wa, after_ref[1, :, lanes]),
+            (wc, cross_ref[count : 2 * count, lanes]),
+            (wn, next_ref[count:, lanes]),
         ):
             out += jnp.dot((weight * inv).astype(BF16), value, preferred_element_type=F32)
         mixed_ref[:, lanes] = out.astype(BF16)
@@ -109,8 +117,9 @@
     send_ref[...] = both_ref[1]
 
 
-def state_kernel(keep_ref, got_ref, near_ref, far_ref, ids_ref, mod_ref, out_ref):
+def state_kernel(keep_ref, got_ref, near_ref, cross_ref, ids_ref, mod_ref, out_ref):
     count, lanes = near_ref.shape
+    half = count // 2
     chunk = mod_ref.shape[1] // lax.axis_size("dev")
     side = lax.axis_index("dev") % 2
     part = lax.axis_index("sub")
@@ -118,16 +127,22 @@
         at = pl.multiple_of(part * 2 * lanes + (2 * i + side) * chunk, 128)
         lift = 1.0 + mod_ref[0:1, pl.ds(at, chunk)]
         cols = slice(i * chunk, (i + 1) * chunk)
-        for block, ref in enumerate((near_ref, far_ref)):
-            rows = slice(block * count, (block + 1) * count)
+        for j in range(4):
+            rows = slice(j * half, (j + 1) * half)
+            if j < 2:
+                token = near_ref[rows, cols]
+            else:
+                left = (j - 2) * lanes + i * chunk
+                token = cross_ref[2 * count :, left : left + chunk]
             proj = keep_ref[rows, cols] + got_ref[rows, cols]
-            out_ref[rows, cols] = (ref[:, cols].astype(F32) + lift * proj).astype(BF16)
+            out_ref[rows, cols] = (token.astype(F32) + lift * proj).astype(BF16)
     out_ref[2 * count :, :] = ids_ref[...]
 
 
-def select_kernel(local, topk, own, *refs):
-    shard_refs, (mod_ref, router_ref, rows_ref, back_ref) = refs[:4], refs[4:8]
-    state_ref = refs[8] if own else None
+def select_kernel(local, topk, own, carried, *refs):
+    shard_refs, (mod_ref, router_ref) = refs[:4], refs[4:6]
+    rows_ref, back_ref = refs[6 + carried : 8 + carried]
+    state_ref = refs[8 + carried] if own else None
     full_ref, gate_ref = refs[-2:]
     count, width = full_ref.shape
     lanes = shard_refs[0].shape[1]
@@ -189,18 +204,12 @@
 
 def hidden_kernel(steps, *refs):
     rows_refs, (w_ref, hidden_ref) = refs[:steps], refs[steps:]
-
-    def expert(e, _):
-        rows = jnp.concatenate([ref[e] for ref in rows_refs])
-
-        def product(member):
-            weight = jnp.concatenate([w_ref[2 * e, member], w_ref[2 * e + 1, member]])
-            return lax.dot_general(rows, weight, NT, preferred_element_type=F32)
-
-        hidden_ref[e] = (jax.nn.silu(product(0)) * product(1)).astype(BF16)
-        return 0
-
-    lax.fori_loop(0, hidden_ref.shape[0], expert, 0, unroll=2)
+    both = hidden_ref.shape[2]
+    e = pl.program_id(0)
+    rows = jnp.concatenate([ref[e] for ref in rows_refs])
+    weight = jnp.concatenate([w_ref[b, g] for g in range(2) for b in range(2)])
+    product = lax.dot_general(rows, weight, NT, preferred_element_type=F32)
+    hidden_ref[0] = (jax.nn.silu(product[:, :both]) * product[:, both:]).astype(BF16)
 
 
 def output_kernel(steps, near_ref, far_ref, w_ref, *refs):
@@ -260,28 +269,27 @@
         return lax.ppermute(x, "sub", [(0, 1), (1, 0)])
 
     stacked = query_key_value.transpose(1, 0, 2)
-    pair = stacked[1:]
-    before = lax.ppermute(pair, "dev", [(i, i + 1) for i in range(devices - 1)])
-    after = lax.ppermute(pair, "dev", [(i + 1, i) for i in range(devices - 1)])
-
+    pair = stacked[1:].reshape(2 * count, local_width)
+    odd = [(i, i + 1) for i in range(1, devices - 1, 2)]
+    after = lax.ppermute(pair, "dev", odd + [(j, i) for i, j in odd])
     split = groups == 2
     held = out_weight.shape[0] // (2 if split else 1)
-    near, far, sent, ids = pl.pallas_call(
+    near, cross, sent, ids = pl.pallas_call(
         functools.partial(cut_kernel, split),
         out_shape=[
             struct((count, lanes), BF16),
-            struct((count, lanes), BF16),
+            struct((2 * count + count // 2, local_width), BF16),
             struct((held, local_width), BF16),
             struct((TILE, lanes), BF16),
         ],
-        in_specs=[whole()] * 3,
+        in_specs=[whole()] * 4,
         out_specs=[whole()] * 4,
         compiler_params=vmem(8),
-    )(tokens, out_weight, expert_ids.T)
-    far = hop(far, 1)
-
-    pieces, weights = [(0, None)], [out_weight]
-    for flip in range(1, steps):
+    )(tokens, pair, out_weight, expert_ids.T)
+    cross = hop(cross, 1)
+
+    pieces, weights = [(0, None), (1, None)], [out_weight, hop(out_weight, 2)]
+    for flip in range(2, steps):
         mine = hop(sent, 2 * flip)
         if split:
             theirs = lax.ppermute(mine, "groups", [(0, 1), (1, 0)])
@@ -291,64 +299,88 @@
             pieces.append((flip, None))
             weights.append(mine)
 
+    gate_up = gate_up_weight.swapaxes(2, 3)
     mixed = pl.pallas_call(
         attention_kernel,
         out_shape=struct((count, local_width), BF16),
-        in_specs=[whole()] * 3 + [pl.BlockSpec(memory_space=pl.ANY)],
+        in_specs=[whole()] * 3,
         out_specs=whole(),
         compiler_params=vmem(8),
-    )(stacked, before, after, far)
+    )(stacked, cross, after)
     keep, send = pl.pallas_call(
         functools.partial(projection_kernel, steps, tuple(pieces)),
         out_shape=[struct((2 * count, lanes), F32)] * 2,
         in_specs=[whole()] * (2 + len(weights)),
         out_specs=[whole()] * 2,
         scratch_shapes=[pltpu.VMEM((2, 2 * count, lanes), F32)],
-        compiler_params=vmem(10),
+        compiler_params=vmem(6),
     )(mixed, hop(mixed, 1), *weights)
     shard = pl.pallas_call(
         state_kernel,
         out_shape=struct((2 * count + TILE, lanes), BF16),
         in_specs=[whole()] * 6,
         out_specs=whole(),
-        compiler_params=vmem(10),
-    )(keep, swap(send), near, far, ids, modulation)
+        compiler_params=vmem(6),
+    )(keep, swap(send), near, cross, ids, modulation)
 
     slots = local * SLOTS
     router = router_weight.T
     state = None
     picked, backs = [], []
+    column = {0: shard}
+    for flip in range(1, steps):
+        low = flip & -flip
+        column[flip] = hop(column[flip - low], 2 * low)
     for flip in range(steps):
-        block = shard if flip == 0 else hop(shard, 2 * flip)
+        block = column[flip]
         crossed = hop(block, 1)
         own = flip == 0
+        later = steps - 1 if flip == steps - 3 else None
+        out_shape = [
+            struct((local, 2 * SLOTS, width), BF16),
+            struct((2, count, slots), BF16),
+        ]
+        out_specs = [whole()] * 2
+        if own:
+            out_shape.append(struct((count, 2 * lanes), BF16))
+            out_specs.append(whole())
+        inputs = [block, crossed, swap(block), swap(crossed), modulation, router]
+        in_specs = [whole()] * 6
+        aliases = {}
+        if later is not None:
+            inputs.append(column[later])
+            in_specs.append(pl.BlockSpec(memory_space=pl.ANY))
+            aliases = {6: len(out_shape)}
+            out_shape.append(struct(shard.shape, BF16))
+            out_specs.append(pl.BlockSpec(memory_space=pl.ANY))
         results = pl.pallas_call(
-            functools.partial(select_kernel, local, topk, own),
-            out_shape=[
-                struct((local, 2 * SLOTS, width), BF16),
-                struct((2, count, slots), BF16),
-            ]
-            + ([struct((count, 2 * lanes), BF16)] if own else []),
-            in_specs=[whole()] * 6,
-            out_specs=[whole()] * (3 if own else 2),
+            functools.partial(select_kernel, local, topk, own, later is not None),
+            out_shape=out_shape,
+            in_specs=in_specs,
+            out_specs=out_specs,
             scratch_shapes=[pltpu.VMEM((count, width), BF16), pltpu.VMEM((experts, count), F32)],
-            compiler_params=vmem(12),
-        )(block, crossed, swap(block), swap(crossed), modulation, router)
+            input_output_aliases=aliases,
+            compiler_params=vmem(6),
+        )(*inputs)
         picked.append(results[0])
         backs.append(results[1])
         if own:
             state = results[2]
+        if later is not None:
+            column[later] = results[-1]
 
     sources = 2 * steps
     room = sources * SLOTS
     units = gate_up_weight.shape[3]
     hidden = pl.pallas_call(
         functools.partial(hidden_kernel, steps),
+        grid=(local,),
         out_shape=struct((local, room, 2 * units), BF16),
-        in_specs=[whole()] * (steps + 1),
-        out_specs=whole(),
-        compiler_params=vmem(12),
-    )(*picked, gate_up_weight.swapaxes(2, 3))
+        in_specs=[whole()] * steps
+        + [pl.BlockSpec((2, 2, units, width), lambda e: (e, 0, 0, 0))],
+        out_specs=pl.BlockSpec((1, room, 2 * units), lambda e: (e, 0, 0)),
+        compiler_params=vmem(40),
+    )(*picked, gate_up)
     share = pl.pallas_call(
         functools.partial(output_kernel, steps),
         out_shape=[struct((count, 2 * lanes), BF16)] * sources,
@@ -516,6 +548,7 @@
         and devices & (devices - 1) == 0
         and gate_up_weight.shape[0] % 2 == 0
         and width % (devices * 128) == 0
+        and arrays[1].shape[2] * 2 == width
         and count % HEAD == 0
         and expert_ids.shape[1] * count <= width // 4
         and router_weight.shape[1] <= 256

time: 171 us -> 168 us (0.982)
  starting transfers between devices: 42.6 us -> 28.6 us
  waiting for transfers between devices: 86.1 us -> 97.6 us
  local copies, waits for them, and re-layouts: 18.5 us -> 9.41 us
  Pallas kernels: 21.4 us -> 29.8 us
    ppermute x19, waiting for transfers between devices: 75.2 us -> 89 us  [hop(): return lax.ppermute(x, 'dev', [(i, i ^ flip) for i in range(devices)])]
    unnamed x26 -> x22, local copies, waits for them, and re-layouts: 16.5 us -> 7.41 us
    ppermute x19, starting transfers between devices: 31.4 us -> 24.5 us  [hop(): return lax.ppermute(x, 'dev', [(i, i ^ flip) for i in range(devices)])]
    pallas_call x5, Pallas kernels: 13.1 us -> 19.4 us  [the longest x1 14.1 us: gathered_body(): pl.pallas_call(functools.partial(hidden_kernel, steps), grid=(local,), ou...]
    ppermute x2 -> x1, starting transfers between devices: 6.3 us -> 0.68 us  [gathered_body(): after = lax.ppermute(pair, 'dev', odd + [(j, i) for i, j in odd])]
    ppermute x3 -> x2, waiting for transfers between devices: 6.73 us -> 4.73 us  [gathered_body(): theirs = lax.ppermute(mine, 'groups', [(0, 1), (1, 0)])]
    ppermute x3 -> x2, starting transfers between devices: 3.55 us -> 2.03 us  [gathered_body(): theirs = lax.ppermute(mine, 'groups', [(0, 1), (1, 0)])]
  transfers between devices with their start and end apart: 34 -> 32, of which waited for: 16 -> 18; matrix products, arithmetic and copies ran while one was open for 1% -> 1% of each run, Pallas kernels for 4% -> 4%
where the time goes in v3:
time: 168 us; the launch traced here: 167 us
  waiting for transfers between devices  97.6 us (58%)
  Pallas kernels  29.8 us (18%)
  starting transfers between devices  28.6 us (17%)
  local copies, waits for them, and re-layouts  9.41 us (6%)
    ppermute x19, waiting for transfers between devices, hop(): return lax.ppermute(x, 'dev', [(i, i ^ flip) for i in range(devices)])  89 us
    ppermute x19, starting transfers between devices, hop(): return lax.ppermute(x, 'dev', [(i, i ^ flip) for i in range(devices)])  24.5 us
    pallas_call x1, Pallas kernels, gathered_body(): pl.pallas_call(functools.partial(hidden_kernel, steps), grid=(local,), ou...  14.1 us
    unnamed x22, local copies, waits for them, and re-layouts  7.41 us
    pallas_call x4, Pallas kernels, gathered_body(): pl.pallas_call(functools.partial(select_kernel, local, topk, own, later i...  5.3 us
    ppermute x2, waiting for transfers between devices, gathered_body(): theirs = lax.ppermute(mine, 'groups', [(0, 1), (1, 0)])  4.73 us
    ppermute x10, waiting for transfers between devices, swap(): return lax.ppermute(x, 'sub', [(0, 1), (1, 0)])  3.83 us
    pallas_call x1, Pallas kernels, gathered_body(): pl.pallas_call(functools.partial(output_kernel, steps), out_shape=[struct...  3.61 us
  transfers between devices with their start and end apart: 32, of which 18 were waited for; matrix products, arithmetic and copies ran while one was open for 1% of the time, Pallas kernels for 4%

profile of v3, /device:TPU:0, one launch (start us, length us, event | category | flops | bytes accessed | tf_op | source)
XLA Modules:
  0.0 166.8 jit_solution(5370275310375114247)
XLA Ops:
  0.0 1.2 slice.8
  1.2 1.2 copy-done.6
  2.5 0.7 copy-done.7
  3.1 1.1 shard_map.82
  4.3 3.0 %collective-permute-start = (bf16[320,1024]{1,0:T(8,128)(2,1)S(1)}, bf16[320,1024]{1,0:T(8,128)(2,1)S(1)}, u32[]{:S(2)}, u32[]{:S(2)}) collective-permute-start(bf16[320,1024]{1,0:T(8,128)(2,1)S(1)} %get-tuple-element.29), channel_id=1, source_target_pairs={{0,2},{2,0},{4,6},{6,4},{8,10},{10,8},{12,14},{14,12},{1,3},{3,1},... | collective-permute-start | bytes 1966088 | tf_op jit(solution)/shard_map/ppermute | solution.py:266
  7.3 0.7 collective-permute-start.1
  8.0 4.3 %collective-permute-start.4 = (bf16[128,1024]{1,0:T(8,128)(2,1)S(1)}, bf16[128,1024]{1,0:T(8,128)(2,1)S(1)}, u32[]{:S(2)}, u32[]{:S(2)}) collective-permute-start(bf16[128,1024]{1,0:T(8,128)(2,1)S(1)} %get-tuple-element.30), channel_id=1, source_target_pairs={{0,8},{2,10},{4,12},{6,14},{8,0},{10,2},{12,4},{14,6},{1,9},{3,11}... | collective-permute-start | bytes 786440 | tf_op jit(solution)/shard_map/ppermute | solution.py:266
  12.3 1.1 collective-permute-start.6
  13.4 0.5 collective-permute-start.3
  13.8 28.1 %collective-permute-done.4.refs_4_ = bf16[128,1024]{1,0:T(8,128)(2,1)S(1)} collective-permute-done((bf16[128,1024]{1,0:T(8,128)(2,1)S(1)}, bf16[128,1024]{1,0:T(8,128)(2,1)S(1)}, u32[]{:S(2)}, u32[]{:S(2)}) %collective-permute-start.4) | collective-permute-done | bytes 262176 | tf_op jit(solution)/shard_map/ppermute | solution.py:266
  41.9 1.5 collective-permute-start.5
  43.4 0.5 collective-permute-start.7
  43.9 1.1 copy-done.3
  45.1 3.1 %shard_map.83.refs_0_ = bf16[128,1024]{1,0:T(8,128)(2,1)S(1)} custom-call(bf16[3,128,1024]{2,1,0:T(8,128)(2,1)S(1)} %bitcast.13, bf16[320,1024]{1,0:T(8,128)(2,1)S(1)} %collective-permute-done.cross_ref, bf16[256,1024]{1,0:T(8,128)(2,1)S(1)} %collective-permute-done.1.next_ref), custom_call_target="tpu_custom_call" | custom-call | tf_op jit(solution)/shard_map/pallas_call | solution.py:303
  48.2 0.1 collective-permute-start.2
  48.3 1.9 %collective-permute-done.5.refs_5_ = bf16[128,1024]{1,0:T(8,128)(2,1)S(1)} collective-permute-done((bf16[128,1024]{1,0:T(8,128)(2,1)S(1)}, bf16[128,1024]{1,0:T(8,128)(2,1)S(1)}, u32[]{:S(2)}, u32[]{:S(2)}) %collective-permute-start.5) | collective-permute-done | bytes 262176 | tf_op jit(solution)/shard_map/ppermute | solution.py:295
  50.2 2.8 %collective-permute-done.7.refs_7_ = bf16[128,1024]{1,0:T(8,128)(2,1)S(1)} collective-permute-done((bf16[128,1024]{1,0:T(8,128)(2,1)S(1)}, bf16[128,1024]{1,0:T(8,128)(2,1)S(1)}, u32[]{:S(2)}, u32[]{:S(2)}) %collective-permute-start.7) | collective-permute-done | bytes 262176 | tf_op jit(solution)/shard_map/ppermute | solution.py:295
  53.0 1.6 collective-permute-done.2.refs_1_
  54.6 2.5 %shard_map.84 = (f32[256,512]{1,0:T(8,128)S(1)}, f32[256,512]{1,0:T(8,128)S(1)}) custom-call(bf16[128,1024]{1,0:T(8,128)(2,1)S(1)} %shard_map.83.refs_0_, bf16[128,1024]{1,0:T(8,128)(2,1)S(1)} %collective-permute-done.2.refs_1_, bf16[256,1024]{1,0:T(8,128)(2,1)} %refs_2_.1, bf16[256,1024]{1,0:T(8,128)(2,1)S(1)} %collective-permute-done.3.refs_3_, ...), custom_call_target="tpu_custom_call" | custom-call | tf_op jit(solution)/shard_map/pallas_call | solution.py:310
  57.1 0.1 collective-permute-start.8
  57.2 1.9 %collective-permute-done.8.got_ref = f32[256,512]{1,0:T(8,128)S(1)} collective-permute-done((f32[256,512]{1,0:T(8,128)S(1)}, f32[256,512]{1,0:T(8,128)S(1)}, u32[]{:S(2)}, u32[]{:S(2)}) %collective-permute-start.8) | collective-permute-done | bytes 524320 | tf_op jit(solution)/shard_map/ppermute | solution.py:269
  59.1 0.8 copy-done.4
  59.8 0.1 shard_map.85.refs_0_
  60.0 4.6 %collective-permute-start.12 = (bf16[272,512]{1,0:T(8,128)(2,1)S(1)}, bf16[272,512]{1,0:T(8,128)(2,1)S(1)}, u32[]{:S(2)}, u32[]{:S(2)}) collective-permute-start(bf16[272,512]{1,0:T(8,128)(2,1)S(1)} %shard_map.85.refs_0_), channel_id=1, source_target_pairs={{0,4},{2,6},{4,0},{6,2},{8,12},{10,14},{12,8},{14,10},{1,5},{3,7},... | collective-permute-start | bytes 835592 | tf_op jit(solution)/shard_map/ppermute | solution.py:266
  64.5 0.8 collective-permute-start.16
  65.4 11.7 %collective-permute-done.12.refs_0_ = bf16[272,512]{1,0:T(8,128)(2,1)S(1)} collective-permute-done((bf16[272,512]{1,0:T(8,128)(2,1)S(1)}, bf16[272,512]{1,0:T(8,128)(2,1)S(1)}, u32[]{:S(2)}, u32[]{:S(2)}) %collective-permute-start.12) | collective-permute-done | bytes 278560 | tf_op jit(solution)/shard_map/ppermute | solution.py:266
  77.1 1.0 collective-permute-start.13
  78.0 1.8 %collective-permute-done.16.refs_0_ = bf16[272,512]{1,0:T(8,128)(2,1)S(1)} collective-permute-done((bf16[272,512]{1,0:T(8,128)(2,1)S(1)}, bf16[272,512]{1,0:T(8,128)(2,1)S(1)}, u32[]{:S(2)}, u32[]{:S(2)}) %collective-permute-start.16) | collective-permute-done | bytes 278560 | tf_op jit(solution)/shard_map/ppermute | solution.py:266
  79.9 0.2 collective-permute-start.17
  80.1 5.2 %collective-permute-done.13.refs_1_ = bf16[272,512]{1,0:T(8,128)(2,1)S(1)} collective-permute-done((bf16[272,512]{1,0:T(8,128)(2,1)S(1)}, bf16[272,512]{1,0:T(8,128)(2,1)S(1)}, u32[]{:S(2)}, u32[]{:S(2)}) %collective-permute-start.13) | collective-permute-done | bytes 278560 | tf_op jit(solution)/shard_map/ppermute | solution.py:266
  85.3 1.0 collective-permute-start.9
  86.2 0.2 collective-permute-start.10
  86.5 1.4 collective-permute-start.18
  87.8 0.9 copy-done
  88.8 0.8 copy-done.5
  89.5 1.3 shard_map.87
  90.9 0.7 collective-permute-start.21
  91.6 3.1 %collective-permute-done.9.refs_1_ = bf16[272,512]{1,0:T(8,128)(2,1)S(1)} collective-permute-done((bf16[272,512]{1,0:T(8,128)(2,1)S(1)}, bf16[272,512]{1,0:T(8,128)(2,1)S(1)}, u32[]{:S(2)}, u32[]{:S(2)}) %collective-permute-start.9) | collective-permute-done | bytes 278560 | tf_op jit(solution)/shard_map/ppermute | solution.py:266
  94.7 6.0 %collective-permute-done.18.refs_1_ = bf16[272,512]{1,0:T(8,128)(2,1)S(1)} collective-permute-done((bf16[272,512]{1,0:T(8,128)(2,1)S(1)}, bf16[272,512]{1,0:T(8,128)(2,1)S(1)}, u32[]{:S(2)}, u32[]{:S(2)}) %collective-permute-start.18) | collective-permute-done | bytes 278560 | tf_op jit(solution)/shard_map/ppermute | solution.py:266
  100.7 0.5 collective-permute-start.22
  101.2 5.1 %collective-permute-done.21.refs_1_ = bf16[272,512]{1,0:T(8,128)(2,1)S(1)} collective-permute-done((bf16[272,512]{1,0:T(8,128)(2,1)S(1)}, bf16[272,512]{1,0:T(8,128)(2,1)S(1)}, u32[]{:S(2)}, u32[]{:S(2)}) %collective-permute-start.21) | collective-permute-done | bytes 278560 | tf_op jit(solution)/shard_map/ppermute | solution.py:266
  106.3 0.9 copy-done.1
  107.2 1.3 shard_map.86
  108.6 0.9 copy-done.2
  109.6 1.3 shard_map.88
  110.9 1.3 shard_map.89
  112.3 14.1 %shard_map.90.near_ref = bf16[8,128,384]{2,1,0:T(8,128)(2,1)S(1)} custom-call(bf16[8,32,2048]{2,1,0:T(8,128)(2,1)S(1)} %get-tuple-element.36.refs_0_, bf16[8,32,2048]{2,1,0:T(8,128)(2,1)S(1)} %get-tuple-element.37.refs_1_, bf16[8,32,2048]{2,1,0:T(8,128)(2,1)S(1)} %get-tuple-element.38.refs_2_, bf16[8,32,2048]{2,1,0:T(8,128)(2,1)S(1)} %get-tuple-element.40.refs_3_, ...), custom_call_target="tpu_custom_call" | custom-call | tf_op jit(solution)/shard_map/pallas_call | solution.py:375
  126.3 0.6 collective-permute-start.24
  126.9 1.9 %collective-permute-done.24.far_ref = bf16[8,128,384]{2,1,0:T(8,128)(2,1)S(1)} collective-permute-done((bf16[8,128,384]{2,1,0:T(8,128)(2,1)S(1)}, bf16[8,128,384]{2,1,0:T(8,128)(2,1)S(1)}, u32[]{:S(2)}, u32[]{:S(2)}) %collective-permute-start.24) | collective-permute-done | bytes 786464 | tf_op jit(solution)/shard_map/ppermute | solution.py:269
  128.8 3.6 %shard_map.91 = (bf16[128,1024]{1,0:T(8,128)(2,1)S(1)}, bf16[128,1024]{1,0:T(8,128)(2,1)S(1)}, bf16[128,1024]{1,0:T(8,128)(2,1)S(1)}, bf16[128,1024]{1,0:T(8,128...) custom-call(bf16[8,128,384]{2,1,0:T(8,128)(2,1)S(1)} %shard_map.90.n, ...), custom_call_target="tpu_custom_call" | custom-call | tf_op jit(solution)/shard_map/pallas_call | solution.py:384
  132.4 1.0 collective-permute-start.25
  133.5 1.1 collective-permute-start.27
  134.5 0.9 collective-permute-start.29
  135.5 1.1 collective-permute-start.31
  136.6 5.1 %collective-permute-done.25 = bf16[128,1024]{1,0:T(8,128)(2,1)S(1)} collective-permute-done((bf16[128,1024]{1,0:T(8,128)(2,1)S(1)}, bf16[128,1024]{1,0:T(8,128)(2,1)S(1)}, u32[]{:S(2)}, u32[]{:S(2)}) %collective-permute-start.25) | collective-permute-done | bytes 262176 | tf_op jit(solution)/shard_map/ppermute | solution.py:266
  141.7 1.7 collective-permute-start.26
  143.4 3.9 %collective-permute-done.27 = bf16[128,1024]{1,0:T(8,128)(2,1)S(1)} collective-permute-done((bf16[128,1024]{1,0:T(8,128)(2,1)S(1)}, bf16[128,1024]{1,0:T(8,128)(2,1)S(1)}, u32[]{:S(2)}, u32[]{:S(2)}) %collective-permute-start.27) | collective-permute-done | bytes 262176 | tf_op jit(solution)/shard_map/ppermute | solution.py:266
  147.3 0.1 collective-permute-start.28
  147.4 5.5 %collective-permute-done.29 = bf16[128,1024]{1,0:T(8,128)(2,1)S(1)} collective-permute-done((bf16[128,1024]{1,0:T(8,128)(2,1)S(1)}, bf16[128,1024]{1,0:T(8,128)(2,1)S(1)}, u32[]{:S(2)}, u32[]{:S(2)}) %collective-permute-start.29) | collective-permute-done | bytes 262176 | tf_op jit(solution)/shard_map/ppermute | solution.py:266
  153.0 0.8 slice.7
  153.8 4.1 %collective-permute-done.31 = bf16[128,1024]{1,0:T(8,128)(2,1)S(1)} collective-permute-done((bf16[128,1024]{1,0:T(8,128)(2,1)S(1)}, bf16[128,1024]{1,0:T(8,128)(2,1)S(1)}, u32[]{:S(2)}, u32[]{:S(2)}) %collective-permute-start.31) | collective-permute-done | bytes 262176 | tf_op jit(solution)/shard_map/ppermute | solution.py:266
  157.9 7.0 %collective-permute-done.28 = bf16[128,1024]{1,0:T(8,128)(2,1)S(1)} collective-permute-done((bf16[128,1024]{1,0:T(8,128)(2,1)S(1)}, bf16[128,1024]{1,0:T(8,128)(2,1)S(1)}, u32[]{:S(2)}, u32[]{:S(2)}) %collective-permute-start.28) | collective-permute-done | bytes 262176 | tf_op jit(solution)/shard_map/ppermute | solution.py:266
  164.9 0.9 collective-permute-done.30
  165.8 1.0 add_convert_fusion
  (40 shorter events, 0.4 us)
Async XLA Ops:
  0.0 128.8 %slice-start = ((s8[12582912]{0:T(1024)(128)(4,1)}), s8[4194304]{0:T(1024)(128)(4,1)S(1)}, s32[]{:S(2)}) async-start(s8[12582912]{0:T(1024)(128)(4,1)} %bitcast.6), calls=%async_computation | async-start | bytes 8388608
  1.2 1.2 copy-start.6
  2.5 0.7 copy-start.7
  4.3 39.7 %collective-permute-start = (bf16[320,1024]{1,0:T(8,128)(2,1)S(1)}, bf16[320,1024]{1,0:T(8,128)(2,1)S(1)}, u32[]{:S(2)}, u32[]{:S(2)}) collective-permute-start(bf16[320,1024]{1,0:T(8,128)(2,1)S(1)} %get-tuple-element.29), channel_id=1, source_target_pairs={{0,2},{2,0},{4,6},{6,4},{8,10},{10,8},{12,14},{14,12},{1,3},{3,1},... | collective-permute-start | bytes 1966088 | tf_op jit(solution)/shard_map/ppermute | solution.py:266
  7.3 36.7 %collective-permute-start.1 = (bf16[256,1024]{1,0:T(8,128)(2,1)S(1)}, bf16[256,1024]{1,0:T(8,128)(2,1)S(1)}, u32[]{:S(2)}, u32[]{:S(2)}) collective-permute-start(bf16[256,1024]{1,0:T(8,128)(2,1)S(1)} %bitcast.15), channel_id=1, source_target_pairs={{2,4},{6,8},{10,12},{4,2},{8,6},{12,10},{3,5},{7,9},{11,13},{5,3},... | collective-permute-start | bytes 1572872 | tf_op jit(solution)/shard_map/ppermute | solution.py:274
  8.0 33.9 %collective-permute-start.4 = (bf16[128,1024]{1,0:T(8,128)(2,1)S(1)}, bf16[128,1024]{1,0:T(8,128)(2,1)S(1)}, u32[]{:S(2)}, u32[]{:S(2)}) collective-permute-start(bf16[128,1024]{1,0:T(8,128)(2,1)S(1)} %get-tuple-element.30), channel_id=1, source_target_pairs={{0,8},{2,10},{4,12},{6,14},{8,0},{10,2},{12,4},{14,6},{1,9},{3,11}... | collective-permute-start | bytes 786440 | tf_op jit(solution)/shard_map/ppermute | solution.py:266
  12.3 31.2 %collective-permute-start.6 = (bf16[128,1024]{1,0:T(8,128)(2,1)S(1)}, bf16[128,1024]{1,0:T(8,128)(2,1)S(1)}, u32[]{:S(2)}, u32[]{:S(2)}) collective-permute-start(bf16[128,1024]{1,0:T(8,128)(2,1)S(1)} %get-tuple-element.30), channel_id=1, source_target_pairs={{0,12},{2,14},{4,8},{6,10},{8,4},{10,6},{12,0},{14,2},{1,13},{3,15... | collective-permute-start | bytes 786440 | tf_op jit(solution)/shard_map/ppermute | solution.py:266
  13.4 39.6 %collective-permute-start.3 = (bf16[256,1024]{1,0:T(8,128)(2,1)}, bf16[256,1024]{1,0:T(8,128)(2,1)S(1)}, u32[]{:S(2)}, u32[]{:S(2)}) collective-permute-start(bf16[256,1024]{1,0:T(8,128)(2,1)} %refs_2_.1), channel_id=1, source_target_pairs={{0,4},{2,6},{4,0},{6,2},{8,12},{10,14},{12,8},{14,10},{1,5},{3,7},... | collective-permute-start | bytes 1572872 | tf_op jit(solution)/shard_map/ppermute | solution.py:266
  41.9 8.3 %collective-permute-start.5 = (bf16[128,1024]{1,0:T(8,128)(2,1)S(1)}, bf16[128,1024]{1,0:T(8,128)(2,1)S(1)}, u32[]{:S(2)}, u32[]{:S(2)}) collective-permute-start(bf16[128,1024]{1,0:T(8,128)(2,1)S(1)} %collective-permute-done.4.refs_4_), channel_id=1, source_target_pairs={{0,16},{16,0},{1,17},{17,1},{2,18},{18,2},{3,19},{19,3},{4,20},{20... | collective-permute-start | bytes 786440 | tf_op jit(solution)/shard_map/ppermute | solution.py:295
  43.4 9.6 %collective-permute-start.7 = (bf16[128,1024]{1,0:T(8,128)(2,1)S(1)}, bf16[128,1024]{1,0:T(8,128)(2,1)S(1)}, u32[]{:S(2)}, u32[]{:S(2)}) collective-permute-start(bf16[128,1024]{1,0:T(8,128)(2,1)S(1)} %collective-permute-done.6.refs_6_), channel_id=1, source_target_pairs={{0,16},{16,0},{1,17},{17,1},{2,18},{18,2},{3,19},{19,3},{4,20},{20... | collective-permute-start | bytes 786440 | tf_op jit(solution)/shard_map/ppermute | solution.py:295
  43.9 1.1 copy-start.3
  48.2 6.4 %collective-permute-start.2 = (bf16[128,1024]{1,0:T(8,128)(2,1)S(1)}, bf16[128,1024]{1,0:T(8,128)(2,1)S(1)}, u32[]{:S(2)}, u32[]{:S(2)}) collective-permute-start(bf16[128,1024]{1,0:T(8,128)(2,1)S(1)} %shard_map.83.refs_0_), channel_id=1, source_target_pairs={{0,2},{2,0},{4,6},{6,4},{8,10},{10,8},{12,14},{14,12},{1,3},{3,1},... | collective-permute-start | bytes 786440 | tf_op jit(solution)/shard_map/ppermute | solution.py:266
  57.1 2.0 %collective-permute-start.8 = (f32[256,512]{1,0:T(8,128)S(1)}, f32[256,512]{1,0:T(8,128)S(1)}, u32[]{:S(2)}, u32[]{:S(2)}) collective-permute-start(f32[256,512]{1,0:T(8,128)S(1)} %get-tuple-element.32), channel_id=1, source_target_pairs={{0,1},{1,0},{2,3},{3,2},{4,5},{5,4},{6,7},{7,6},{8,9},{9,8},{10,11... | collective-permute-start | bytes 1572872 | tf_op jit(solution)/shard_map/ppermute | solution.py:269
  59.1 0.8 copy-start.4
  60.0 17.1 %collective-permute-start.12 = (bf16[272,512]{1,0:T(8,128)(2,1)S(1)}, bf16[272,512]{1,0:T(8,128)(2,1)S(1)}, u32[]{:S(2)}, u32[]{:S(2)}) collective-permute-start(bf16[272,512]{1,0:T(8,128)(2,1)S(1)} %shard_map.85.refs_0_), channel_id=1, source_target_pairs={{0,4},{2,6},{4,0},{6,2},{8,12},{10,14},{12,8},{14,10},{1,5},{3,7},... | collective-permute-start | bytes 835592 | tf_op jit(solution)/shard_map/ppermute | solution.py:266
  64.5 15.3 %collective-permute-start.16 = (bf16[272,512]{1,0:T(8,128)(2,1)S(1)}, bf16[272,512]{1,0:T(8,128)(2,1)S(1)}, u32[]{:S(2)}, u32[]{:S(2)}) collective-permute-start(bf16[272,512]{1,0:T(8,128)(2,1)S(1)} %shard_map.85.refs_0_), channel_id=1, source_target_pairs={{0,8},{2,10},{4,12},{6,14},{8,0},{10,2},{12,4},{14,6},{1,9},{3,11}... | collective-permute-start | bytes 835592 | tf_op jit(solution)/shard_map/ppermute | solution.py:266
  77.1 8.2 %collective-permute-start.13 = (bf16[272,512]{1,0:T(8,128)(2,1)S(1)}, bf16[272,512]{1,0:T(8,128)(2,1)S(1)}, u32[]{:S(2)}, u32[]{:S(2)}) collective-permute-start(bf16[272,512]{1,0:T(8,128)(2,1)S(1)} %collective-permute-done.12.refs_0_), channel_id=1, source_target_pairs={{0,2},{2,0},{4,6},{6,4},{8,10},{10,8},{12,14},{14,12},{1,3},{3,1},... | collective-permute-start | bytes 835592 | tf_op jit(solution)/shard_map/ppermute | solution.py:266
  79.9 6.6 %collective-permute-start.17 = (bf16[272,512]{1,0:T(8,128)(2,1)S(1)}, bf16[272,512]{1,0:T(8,128)(2,1)S(1)}, u32[]{:S(2)}, u32[]{:S(2)}) collective-permute-start(bf16[272,512]{1,0:T(8,128)(2,1)S(1)} %collective-permute-done.16.refs_0_), channel_id=1, source_target_pairs={{0,4},{2,6},{4,0},{6,2},{8,12},{10,14},{12,8},{14,10},{1,5},{3,7},... | collective-permute-start | bytes 835592 | tf_op jit(solution)/shard_map/ppermute | solution.py:266
  80.1 7.8 %collective-permute-start.14 = (bf16[272,512]{1,0:T(8,128)(2,1)S(1)}, bf16[272,512]{1,0:T(8,128)(2,1)S(1)}, u32[]{:S(2)}, u32[]{:S(2)}) collective-permute-start(bf16[272,512]{1,0:T(8,128)(2,1)S(1)} %collective-permute-done.12.refs_0_), channel_id=1, source_target_pairs={{0,1},{1,0},{2,3},{3,2},{4,5},{5,4},{6,7},{7,6},{8,9},{9,8},{10,11... | collective-permute-start | bytes 835592 | tf_op jit(solution)/shard_map/ppermute | solution.py:269
  85.3 2.6 %collective-permute-start.15 = (bf16[272,512]{1,0:T(8,128)(2,1)S(1)}, bf16[272,512]{1,0:T(8,128)(2,1)S(1)}, u32[]{:S(2)}, u32[]{:S(2)}) collective-permute-start(bf16[272,512]{1,0:T(8,128)(2,1)S(1)} %collective-permute-done.13.refs_1_), channel_id=1, source_target_pairs={{0,1},{1,0},{2,3},{3,2},{4,5},{5,4},{6,7},{7,6},{8,9},{9,8},{10,11... | collective-permute-start | bytes 835592 | tf_op jit(solution)/shard_map/ppermute | solution.py:269
  85.3 9.5 %collective-permute-start.9 = (bf16[272,512]{1,0:T(8,128)(2,1)S(1)}, bf16[272,512]{1,0:T(8,128)(2,1)S(1)}, u32[]{:S(2)}, u32[]{:S(2)}) collective-permute-start(bf16[272,512]{1,0:T(8,128)(2,1)S(1)} %shard_map.85.refs_0_), channel_id=1, source_target_pairs={{0,2},{2,0},{4,6},{6,4},{8,10},{10,8},{12,14},{14,12},{1,3},{3,1},... | collective-permute-start | bytes 835592 | tf_op jit(solution)/shard_map/ppermute | solution.py:266
  86.2 14.5 %collective-permute-start.10 = (bf16[272,512]{1,0:T(8,128)(2,1)S(1)}, bf16[272,512]{1,0:T(8,128)(2,1)S(1)}, u32[]{:S(2)}, u32[]{:S(2)}) collective-permute-start(bf16[272,512]{1,0:T(8,128)(2,1)S(1)} %shard_map.85.refs_0_), channel_id=1, source_target_pairs={{0,1},{1,0},{2,3},{3,2},{4,5},{5,4},{6,7},{7,6},{8,9},{9,8},{10,11... | collective-permute-start | bytes 835592 | tf_op jit(solution)/shard_map/ppermute | solution.py:269
  86.5 14.2 %collective-permute-start.18 = (bf16[272,512]{1,0:T(8,128)(2,1)S(1)}, bf16[272,512]{1,0:T(8,128)(2,1)S(1)}, u32[]{:S(2)}, u32[]{:S(2)}) collective-permute-start(bf16[272,512]{1,0:T(8,128)(2,1)S(1)} %collective-permute-done.16.refs_0_), channel_id=1, source_target_pairs={{0,2},{2,0},{4,6},{6,4},{8,10},{10,8},{12,14},{14,12},{1,3},{3,1},... | collective-permute-start | bytes 835592 | tf_op jit(solution)/shard_map/ppermute | solution.py:266
  87.8 1.0 copy-start
  88.8 0.8 copy-start.5
  90.9 15.4 %collective-permute-start.21 = (bf16[272,512]{1,0:T(8,128)(2,1)S(1)}, bf16[272,512]{1,0:T(8,128)(2,1)S(1)}, u32[]{:S(2)}, u32[]{:S(2)}) collective-permute-start(bf16[272,512]{1,0:T(8,128)(2,1)S(1)} %get-tuple-element.39.refs_0_), channel_id=1, source_target_pairs={{0,2},{2,0},{4,6},{6,4},{8,10},{10,8},{12,14},{14,12},{1,3},{3,1},... | collective-permute-start | bytes 835592 | tf_op jit(solution)/shard_map/ppermute | solution.py:266
  91.6 17.0 %collective-permute-start.19 = (bf16[272,512]{1,0:T(8,128)(2,1)S(1)}, bf16[272,512]{1,0:T(8,128)(2,1)S(1)}, u32[]{:S(2)}, u32[]{:S(2)}) collective-permute-start(bf16[272,512]{1,0:T(8,128)(2,1)S(1)} %collective-permute-done.16.refs_0_), channel_id=1, source_target_pairs={{0,1},{1,0},{2,3},{3,2},{4,5},{5,4},{6,7},{7,6},{8,9},{9,8},{10,11... | collective-permute-start | bytes 835592 | tf_op jit(solution)/shard_map/ppermute | solution.py:269
  94.7 11.6 %collective-permute-start.11 = (bf16[272,512]{1,0:T(8,128)(2,1)S(1)}, bf16[272,512]{1,0:T(8,128)(2,1)S(1)}, u32[]{:S(2)}, u32[]{:S(2)}) collective-permute-start(bf16[272,512]{1,0:T(8,128)(2,1)S(1)} %collective-permute-done.9.refs_1_), channel_id=1, source_target_pairs={{0,1},{1,0},{2,3},{3,2},{4,5},{5,4},{6,7},{7,6},{8,9},{9,8},{10,11... | collective-permute-start | bytes 835592 | tf_op jit(solution)/shard_map/ppermute | solution.py:269
  100.7 7.9 %collective-permute-start.20 = (bf16[272,512]{1,0:T(8,128)(2,1)S(1)}, bf16[272,512]{1,0:T(8,128)(2,1)S(1)}, u32[]{:S(2)}, u32[]{:S(2)}) collective-permute-start(bf16[272,512]{1,0:T(8,128)(2,1)S(1)} %collective-permute-done.18.refs_1_), channel_id=1, source_target_pairs={{0,1},{1,0},{2,3},{3,2},{4,5},{5,4},{6,7},{7,6},{8,9},{9,8},{10,11... | collective-permute-start | bytes 835592 | tf_op jit(solution)/shard_map/ppermute | solution.py:269
  100.7 10.2 %collective-permute-start.22 = (bf16[272,512]{1,0:T(8,128)(2,1)S(1)}, bf16[272,512]{1,0:T(8,128)(2,1)S(1)}, u32[]{:S(2)}, u32[]{:S(2)}) collective-permute-start(bf16[272,512]{1,0:T(8,128)(2,1)S(1)} %get-tuple-element.39.refs_0_), channel_id=1, source_target_pairs={{0,1},{1,0},{2,3},{3,2},{4,5},{5,4},{6,7},{7,6},{8,9},{9,8},{10,11... | collective-permute-start | bytes 835592 | tf_op jit(solution)/shard_map/ppermute | solution.py:269
  106.3 4.6 %collective-permute-start.23 = (bf16[272,512]{1,0:T(8,128)(2,1)S(1)}, bf16[272,512]{1,0:T(8,128)(2,1)S(1)}, u32[]{:S(2)}, u32[]{:S(2)}) collective-permute-start(bf16[272,512]{1,0:T(8,128)(2,1)S(1)} %collective-permute-done.21.refs_1_), channel_id=1, source_target_pairs={{0,1},{1,0},{2,3},{3,2},{4,5},{5,4},{6,7},{7,6},{8,9},{9,8},{10,11... | collective-permute-start | bytes 835592 | tf_op jit(solution)/shard_map/ppermute | solution.py:269
  106.3 1.0 copy-start.1
  108.6 1.0 copy-start.2
  110.9 17.9 %slice-start.1 = ((s8[12582912]{0:T(1024)(128)(4,1)}), s8[4194304]{0:T(1024)(128)(4,1)S(1)}, s32[]{:S(2)}) async-start(s8[12582912]{0:T(1024)(128)(4,1)} %bitcast.6), calls=%async_computation.1 | async-start | bytes 8388608
  112.3 16.6 %slice-start.2 = ((s8[12582912]{0:T(1024)(128)(4,1)}), s8[4194304]{0:T(1024)(128)(4,1)S(1)}, s32[]{:S(2)}) async-start(s8[12582912]{0:T(1024)(128)(4,1)} %bitcast.6), calls=%async_computation.2 | async-start | bytes 8388608
  126.3 2.5 %collective-permute-start.24 = (bf16[8,128,384]{2,1,0:T(8,128)(2,1)S(1)}, bf16[8,128,384]{2,1,0:T(8,128)(2,1)S(1)}, u32[]{:S(2)}, u32[]{:S(2)}) collective-permute-start(bf16[8,128,384]{2,1,0:T(8,128)(2,1)S(1)} %shard_map.90.near_ref), channel_id=1, source_target_pairs={{0,1},{1,0},{2,3},{3,2},{4,5},{5,4},{6,7},{7,6},{8,9},{9,8},{10,11... | collective-permute-start | bytes 2359304 | tf_op jit(solution)/shard_map/ppermute | solution.py:269
  132.4 9.2 %collective-permute-start.25 = (bf16[128,1024]{1,0:T(8,128)(2,1)S(1)}, bf16[128,1024]{1,0:T(8,128)(2,1)S(1)}, u32[]{:S(2)}, u32[]{:S(2)}) collective-permute-start(bf16[128,1024]{1,0:T(8,128)(2,1)S(1)} %get-tuple-element.46), channel_id=1, source_target_pairs={{0,2},{2,0},{4,6},{6,4},{8,10},{10,8},{12,14},{14,12},{1,3},{3,1},... | collective-permute-start | bytes 786440 | tf_op jit(solution)/shard_map/ppermute | solution.py:266
  133.5 13.8 %collective-permute-start.27 = (bf16[128,1024]{1,0:T(8,128)(2,1)S(1)}, bf16[128,1024]{1,0:T(8,128)(2,1)S(1)}, u32[]{:S(2)}, u32[]{:S(2)}) collective-permute-start(bf16[128,1024]{1,0:T(8,128)(2,1)S(1)} %get-tuple-element.48), channel_id=1, source_target_pairs={{0,2},{2,0},{4,6},{6,4},{8,10},{10,8},{12,14},{14,12},{1,3},{3,1},... | collective-permute-start | bytes 786440 | tf_op jit(solution)/shard_map/ppermute | solution.py:266
  134.5 18.3 %collective-permute-start.29 = (bf16[128,1024]{1,0:T(8,128)(2,1)S(1)}, bf16[128,1024]{1,0:T(8,128)(2,1)S(1)}, u32[]{:S(2)}, u32[]{:S(2)}) collective-permute-start(bf16[128,1024]{1,0:T(8,128)(2,1)S(1)} %get-tuple-element.50), channel_id=1, source_target_pairs={{0,2},{2,0},{4,6},{6,4},{8,10},{10,8},{12,14},{14,12},{1,3},{3,1},... | collective-permute-start | bytes 786440 | tf_op jit(solution)/shard_map/ppermute | solution.py:266
  135.5 22.4 %collective-permute-start.31 = (bf16[128,1024]{1,0:T(8,128)(2,1)S(1)}, bf16[128,1024]{1,0:T(8,128)(2,1)S(1)}, u32[]{:S(2)}, u32[]{:S(2)}) collective-permute-start(bf16[128,1024]{1,0:T(8,128)(2,1)S(1)} %get-tuple-element.52), channel_id=1, source_target_pairs={{0,2},{2,0},{4,6},{6,4},{8,10},{10,8},{12,14},{14,12},{1,3},{3,1},... | collective-permute-start | bytes 786440 | tf_op jit(solution)/shard_map/ppermute | solution.py:266
  141.7 16.2 %collective-permute-start.26 = (bf16[128,1024]{1,0:T(8,128)(2,1)S(1)}, bf16[128,1024]{1,0:T(8,128)(2,1)S(1)}, u32[]{:S(2)}, u32[]{:S(2)}) collective-permute-start(bf16[128,1024]{1,0:T(8,128)(2,1)S(1)} %add_convert_fusion.3), channel_id=1, source_target_pairs={{0,12},{2,14},{4,8},{6,10},{8,4},{10,6},{12,0},{14,2},{1,13},{3,15... | collective-permute-start | bytes 786440 | tf_op jit(solution)/shard_map/ppermute | solution.py:266
  147.3 17.6 %collective-permute-start.28 = (bf16[128,1024]{1,0:T(8,128)(2,1)S(1)}, bf16[128,1024]{1,0:T(8,128)(2,1)S(1)}, u32[]{:S(2)}, u32[]{:S(2)}) collective-permute-start(bf16[128,1024]{1,0:T(8,128)(2,1)S(1)} %add_convert_fusion.2), channel_id=1, source_target_pairs={{0,8},{2,10},{4,12},{6,14},{8,0},{10,2},{12,4},{14,6},{1,9},{3,11}... | collective-permute-start | bytes 786440 | tf_op jit(solution)/shard_map/ppermute | solution.py:266
  152.9 12.9 %collective-permute-start.30 = (bf16[128,1024]{1,0:T(8,128)(2,1)S(1)}, bf16[128,1024]{1,0:T(8,128)(2,1)S(1)}, u32[]{:S(2)}, u32[]{:S(2)}) collective-permute-start(bf16[128,1024]{1,0:T(8,128)(2,1)S(1)} %add_convert_fusion.1), channel_id=1, source_target_pairs={{0,4},{2,6},{4,0},{6,2},{8,12},{10,14},{12,8},{14,10},{1,5},{3,7},... | collective-permute-start | bytes 786440 | tf_op jit(solution)/shard_map/ppermute | solution.py:266

commit v4 on v3

--- a/solution.py
+++ b/solution.py
@@ -29,36 +29,58 @@
     return pl.BlockSpec(memory_space=pltpu.VMEM)
 
 
-def cut_kernel(split, tokens_ref, pair_ref, weight_ref, ids_ref, near_ref, cross_ref, sent_ref, row_ref):
+def cut_kernel(split, tokens_ref, qkv_ref, weight_ref, *refs):
+    query_ref, pair_ref, near_ref, cross_ref, sent_ref, own_ref, sem_ref = refs
     count, lanes = near_ref.shape
     chunk = tokens_ref.shape[1] // lax.axis_size("dev")
     side = lax.axis_index("dev") % 2
     part = lax.axis_index("sub")
     half = count // 2
-    cross_ref[: 2 * count] = pair_ref[...]
+    moves = [
+        (qkv_ref.at[1], pair_ref.at[:count]),
+        (qkv_ref.at[2], pair_ref.at[count:]),
+        (qkv_ref.at[1], cross_ref.at[:count]),
+        (qkv_ref.at[2], cross_ref.at[count : 2 * count]),
+    ]
     for i in range(lanes // chunk):
-        cols = slice(i * chunk, (i + 1) * chunk)
-        at = pl.multiple_of(part * 2 * lanes + (2 * i + side) * chunk, 128)
-        near_ref[:, cols] = tokens_ref[:, pl.ds(at, chunk)]
         at = pl.multiple_of(part * 2 * lanes + (2 * i + 1 - side) * chunk, 128)
         for j in range(2):
-            cross_ref[2 * count :, j * lanes + i * chunk : j * lanes + (i + 1) * chunk] = (
-                tokens_ref[j * half : (j + 1) * half, pl.ds(at, chunk)]
+            left = j * lanes + i * chunk
+            moves.append(
+                (
+                    tokens_ref.at[j * half : (j + 1) * half, pl.ds(at, chunk)],
+                    cross_ref.at[2 * count :, left : left + chunk],
+                )
             )
-    if split:
-        rows = sent_ref.shape[0]
-        at = pl.multiple_of(lax.axis_index("groups") * rows, TILE)
-        sent_ref[...] = weight_ref[pl.ds(at, rows), :]
-    else:
-        sent_ref[...] = weight_ref[...]
-    topk = ids_ref.shape[0]
+        at = pl.multiple_of(part * 2 * lanes + (2 * i + side) * chunk, 128)
+        moves.append(
+            (tokens_ref.at[:, pl.ds(at, chunk)], near_ref.at[:, i * chunk : (i + 1) * chunk])
+        )
+    rows = sent_ref.shape[0]
+    at = pl.multiple_of(lax.axis_index("groups") * rows if split else 0, TILE)
+    moves += [
+        (weight_ref.at[pl.ds(at, rows)], sent_ref),
+        (qkv_ref.at[0], query_ref),
+        (weight_ref, own_ref),
+    ]
+    copies = [pltpu.make_async_copy(*move, sem_ref.at[n]) for n, move in enumerate(moves)]
+    for copy in copies:
+        copy.start()
+    for copy in copies:
+        copy.wait()
+
+
+def small_kernel(ids_ref, mod_ref, router_ref, _, row_ref, mod_to_ref, router_to_ref):
+    topk, count = ids_ref.shape
     row_ref[...] = jnp.zeros(row_ref.shape, BF16)
     for k in range(topk):
         named = jnp.broadcast_to(ids_ref[k : k + 1, :], (TILE, count))
         row_ref[:, k * count : (k + 1) * count] = named.astype(F32).astype(BF16)
-
-
-def attention_kernel(own_ref, cross_ref, next_ref, mixed_ref):
+    mod_to_ref[...] = mod_ref[...]
+    router_to_ref[...] = router_ref[...]
+
+
+def attention_kernel(query_ref, own_ref, cross_ref, next_ref, _, mixed_ref):
     count, width = mixed_ref.shape
     place = lax.axis_index("dev")
     even = place % 2 == 0
@@ -74,16 +96,16 @@
 
     for head in range(width // HEAD):
         lanes = slice(head * HEAD, (head + 1) * HEAD)
-        q = own_ref[0, :, lanes]
+        q = query_ref[:, lanes]
         sc = jnp.where(see_cross, scored(q, cross_ref[:count, lanes]), NEG)
-        so = scored(q, own_ref[1, :, lanes])
+        so = scored(q, own_ref[:count, lanes])
         sn = jnp.where(see_next, scored(q, next_ref[:count, lanes]), NEG)
         top = jnp.max(jnp.maximum(jnp.maximum(sc, so), sn), 1, keepdims=True)
         wc, wo, wn = jnp.exp(sc - top), jnp.exp(so - top), jnp.exp(sn - top)
         inv = 1.0 / jnp.sum(wc + wo + wn, 1, keepdims=True)
         out = 0.0
         for weight, value in (
-            (wo, own_ref[2, :, lanes]),
+            (wo, own_ref[count:, lanes]),
             (wc, cross_ref[count : 2 * count, lanes]),
             (wn, next_ref[count:, lanes]),
         ):
@@ -137,6 +159,22 @@
             proj = keep_ref[rows, cols] + got_ref[rows, cols]
             out_ref[rows, cols] = (token.astype(F32) + lift * proj).astype(BF16)
     out_ref[2 * count :, :] = ids_ref[...]
+
+
+def tie_kernel(*refs):
+    pass
+
+
+def tie(array, *others):
+    anywhere = pl.BlockSpec(memory_space=pl.ANY)
+    return pl.pallas_call(
+        tie_kernel,
+        out_shape=jax.ShapeDtypeStruct(array.shape, array.dtype),
+        in_specs=[anywhere] * (1 + len(others)),
+        out_specs=anywhere,
+        input_output_aliases={0: 0},
+        compiler_params=vmem(1),
+    )(array, *others)
 
 
 def select_kernel(local, topk, own, carried, *refs):
@@ -202,38 +240,60 @@
         back_ref[cross] = jnp.where(pick, here, 0.0).T.astype(BF16)
 
 
+def load_kernel(local, up_ref, down_ref, _, *refs):
+    to_refs, done_ref, sem_ref = refs[: 2 * local], refs[2 * local], refs[2 * local + 1]
+    copies = []
+    for n, ref in enumerate(to_refs):
+        e = n % local
+        whole_ref = up_ref if n < local else down_ref
+        copies.append(
+            pltpu.make_async_copy(whole_ref.at[2 * e : 2 * e + 2], ref, sem_ref.at[n])
+        )
+    for copy in copies:
+        copy.start()
+    done_ref[...] = jnp.zeros(done_ref.shape, F32)
+    for copy in copies:
+        copy.wait()
+
+
 def hidden_kernel(steps, *refs):
-    rows_refs, (w_ref, hidden_ref) = refs[:steps], refs[steps:]
+    rows_refs, w_refs, hidden_ref = refs[:steps], refs[steps:-1], refs[-1]
     both = hidden_ref.shape[2]
-    e = pl.program_id(0)
-    rows = jnp.concatenate([ref[e] for ref in rows_refs])
-    weight = jnp.concatenate([w_ref[b, g] for g in range(2) for b in range(2)])
-    product = lax.dot_general(rows, weight, NT, preferred_element_type=F32)
-    hidden_ref[0] = (jax.nn.silu(product[:, :both]) * product[:, both:]).astype(BF16)
-
-
-def output_kernel(steps, near_ref, far_ref, w_ref, *refs):
-    back_refs, out_refs, held_ref = refs[:steps], refs[steps : 3 * steps], refs[3 * steps]
+    for e, w_ref in enumerate(w_refs):
+        rows = jnp.concatenate([ref[e] for ref in rows_refs])
+        weight = jnp.concatenate([w_ref[b, g] for g in range(2) for b in range(2)])
+        product = lax.dot_general(rows, weight, NT, preferred_element_type=F32)
+        hidden_ref[e] = (jax.nn.silu(product[:, :both]) * product[:, both:]).astype(BF16)
+
+
+def output_kernel(steps, local, near_ref, far_ref, *refs):
+    w_refs, back_refs = refs[:local], refs[local : local + steps]
+    out_refs, held_ref = refs[local + steps : local + 3 * steps], refs[-1]
     part = lax.axis_index("sub")
     units = near_ref.shape[2] // 2
-
-    def expert(e, _):
+    for e, w_ref in enumerate(w_refs):
         total = 0.0
         for ref, who in ((near_ref, part), (far_ref, 1 - part)):
             at = pl.multiple_of(who * units, 64)
-            weight = jnp.concatenate([w_ref[2 * e + b, pl.ds(at, units), :] for b in range(2)])
+            weight = jnp.concatenate([w_ref[b, pl.ds(at, units), :] for b in range(2)])
             total += jnp.dot(ref[e], weight, preferred_element_type=F32)
         total = total.astype(BF16)
-        row = pl.multiple_of(e * SLOTS, SLOTS)
         for source in range(2 * steps):
-            held_ref[source, pl.ds(row, SLOTS), :] = total[source * SLOTS : (source + 1) * SLOTS]
-        return 0
-
-    lax.fori_loop(0, near_ref.shape[0], expert, 0, unroll=2)
+            held_ref[source, e * SLOTS : (e + 1) * SLOTS, :] = total[
+                source * SLOTS : (source + 1) * SLOTS
+            ]
     for source in range(2 * steps):
         out_refs[source][...] = jnp.dot(
             back_refs[source // 2][source % 2], held_ref[source], preferred_element_type=F32
         ).astype(BF16)
+
+
+def final_kernel(state_ref, mod_ref, *refs):
+    routed = sum(ref[...].astype(F32) for ref in refs[:-1])
+    lanes = state_ref.shape[1]
+    at = pl.multiple_of(lax.axis_index("sub") * lanes, 128)
+    lift = 1.0 + mod_ref[3:4, pl.ds(at, lanes)]
+    refs[-1][...] = (state_ref[...].astype(F32) + lift * routed).astype(BF16)
 
 
 def gathered_body(
@@ -250,9 +310,6 @@
     devices = lax.axis_size("dev")
     groups = lax.axis_size("groups")
     steps = devices // 2
-    side = lax.axis_index("dev") % 2
-    part = lax.axis_index("sub")
-    group = lax.axis_index("groups")
     local_width = query_key_value.shape[2]
     chunk = width // devices
     lanes = width // 4
@@ -268,45 +325,61 @@
     def swap(x):
         return lax.ppermute(x, "sub", [(0, 1), (1, 0)])
 
-    stacked = query_key_value.transpose(1, 0, 2)
-    pair = stacked[1:].reshape(2 * count, local_width)
-    odd = [(i, i + 1) for i in range(1, devices - 1, 2)]
-    after = lax.ppermute(pair, "dev", odd + [(j, i) for i, j in odd])
     split = groups == 2
     held = out_weight.shape[0] // (2 if split else 1)
-    near, cross, sent, ids = pl.pallas_call(
+    query, pair, near, cross, sent, own_weight = pl.pallas_call(
         functools.partial(cut_kernel, split),
         out_shape=[
+            struct((count, local_width), BF16),
+            struct((2 * count, local_width), BF16),
             struct((count, lanes), BF16),
             struct((2 * count + count // 2, local_width), BF16),
             struct((held, local_width), BF16),
+            struct(out_weight.shape, BF16),
+        ],
+        in_specs=[pl.BlockSpec(memory_space=pl.ANY)] * 3,
+        out_specs=[whole()] * 6,
+        scratch_shapes=[pltpu.SemaphoreType.DMA((7 + 3 * (lanes // chunk),))],
+        compiler_params=vmem(52),
+    )(tokens, query_key_value.transpose(1, 0, 2), out_weight)
+    ids, small, router = pl.pallas_call(
+        small_kernel,
+        out_shape=[
             struct((TILE, lanes), BF16),
+            struct(modulation.shape, F32),
+            struct((experts, width), BF16),
         ],
-        in_specs=[whole()] * 4,
-        out_specs=[whole()] * 4,
-        compiler_params=vmem(8),
-    )(tokens, pair, out_weight, expert_ids.T)
+        in_specs=[whole()] * 3 + [pl.BlockSpec(memory_space=pl.ANY)],
+        out_specs=[whole()] * 3,
+        compiler_params=vmem(4),
+    )(expert_ids.T, modulation, router_weight.T, query)
+    odd = [(i, i + 1) for i in range(1, devices - 1, 2)]
+    after = lax.ppermute(pair, "dev", odd + [(j, i) for i, j in odd])
     cross = hop(cross, 1)
 
-    pieces, weights = [(0, None), (1, None)], [out_weight, hop(out_weight, 2)]
+    pieces, weights = [(0, None), (1, None)], [own_weight, hop(own_weight, 2)]
+    mine = {0: sent}
     for flip in range(2, steps):
-        mine = hop(sent, 2 * flip)
+        low = flip & -flip
+        if flip > 2 and flip - low > 0:
+            mine[flip] = hop(mine[flip - low], 2 * low)
+        else:
+            mine[flip] = hop(sent, 2 * flip)
         if split:
-            theirs = lax.ppermute(mine, "groups", [(0, 1), (1, 0)])
+            theirs = lax.ppermute(mine[flip], "groups", [(0, 1), (1, 0)])
             pieces += [(flip, 0), (flip, 1)]
-            weights += [mine, theirs]
+            weights += [mine[flip], theirs]
         else:
             pieces.append((flip, None))
-            weights.append(mine)
-
-    gate_up = gate_up_weight.swapaxes(2, 3)
+            weights.append(mine[flip])
+
     mixed = pl.pallas_call(
         attention_kernel,
         out_shape=struct((count, local_width), BF16),
-        in_specs=[whole()] * 3,
+        in_specs=[whole()] * 4 + [pl.BlockSpec(memory_space=pl.ANY)],
         out_specs=whole(),
-        compiler_params=vmem(8),
-    )(stacked, cross, after)
+        compiler_params=vmem(6),
+    )(query, pair, cross, after, small)
     keep, send = pl.pallas_call(
         functools.partial(projection_kernel, steps, tuple(pieces)),
         out_shape=[struct((2 * count, lanes), F32)] * 2,
@@ -321,19 +394,32 @@
         in_specs=[whole()] * 6,
         out_specs=whole(),
         compiler_params=vmem(6),
-    )(keep, swap(send), near, cross, ids, modulation)
+    )(keep, swap(send), near, cross, ids, small)
+
+    units = gate_up_weight.shape[3]
+    *loaded, done = pl.pallas_call(
+        functools.partial(load_kernel, local),
+        out_shape=[struct((2, 2, units, width), BF16)] * local
+        + [struct((2, *down_weight.shape[1:]), BF16)] * local
+        + [struct((8, 128), F32)],
+        in_specs=[pl.BlockSpec(memory_space=pl.ANY)] * 3,
+        out_specs=[whole()] * (2 * local + 1),
+        scratch_shapes=[pltpu.SemaphoreType.DMA((2 * local,))],
+        compiler_params=vmem(14),
+    )(gate_up_weight.swapaxes(2, 3), down_weight, shard)
 
     slots = local * SLOTS
-    router = router_weight.T
     state = None
     picked, backs = [], []
     column = {0: shard}
     for flip in range(1, steps):
         low = flip & -flip
         column[flip] = hop(column[flip - low], 2 * low)
+    across = hop(shard, 1)
+    column[1] = tie(column[1], across, done)
     for flip in range(steps):
         block = column[flip]
-        crossed = hop(block, 1)
+        crossed = hop(block, 1) if flip else across
         own = flip == 0
         later = steps - 1 if flip == steps - 3 else None
         out_shape = [
@@ -344,7 +430,7 @@
         if own:
             out_shape.append(struct((count, 2 * lanes), BF16))
             out_specs.append(whole())
-        inputs = [block, crossed, swap(block), swap(crossed), modulation, router]
+        inputs = [block, crossed, swap(block), swap(crossed), small, router]
         in_specs = [whole()] * 6
         aliases = {}
         if later is not None:
@@ -371,33 +457,36 @@
 
     sources = 2 * steps
     room = sources * SLOTS
-    units = gate_up_weight.shape[3]
     hidden = pl.pallas_call(
         functools.partial(hidden_kernel, steps),
-        grid=(local,),
         out_shape=struct((local, room, 2 * units), BF16),
-        in_specs=[whole()] * steps
-        + [pl.BlockSpec((2, 2, units, width), lambda e: (e, 0, 0, 0))],
-        out_specs=pl.BlockSpec((1, room, 2 * units), lambda e: (e, 0, 0)),
-        compiler_params=vmem(40),
-    )(*picked, gate_up)
+        in_specs=[whole()] * (steps + local),
+        out_specs=whole(),
+        compiler_params=vmem(6),
+    )(*picked, *loaded[:local])
     share = pl.pallas_call(
-        functools.partial(output_kernel, steps),
+        functools.partial(output_kernel, steps, local),
         out_shape=[struct((count, 2 * lanes), BF16)] * sources,
-        in_specs=[whole()] * (3 + steps),
+        in_specs=[whole()] * (2 + local + steps),
         out_specs=[whole()] * sources,
         scratch_shapes=[pltpu.VMEM((sources, slots, 2 * lanes), BF16)],
         compiler_params=vmem(8),
-    )(hidden, swap(hidden), down_weight, *backs)
-
-    routed = None
+    )(hidden, swap(hidden), *loaded[local:], *backs)
+
+    terms = [share[0]]
     for flip in range(steps - 1, -1, -1):
-        mine = share[2 * flip].astype(F32) + hop(share[2 * flip + 1], 1).astype(F32)
+        crossed = hop(share[2 * flip + 1], 1)
         if flip:
-            mine = hop(mine.astype(BF16), 2 * flip).astype(F32)
-        routed = mine if routed is None else routed + mine
-    lift = lax.dynamic_slice_in_dim(modulation[3], part * 2 * lanes, 2 * lanes, 0)
-    return (state.astype(F32) + (1.0 + lift) * routed).astype(BF16)
+            crossed = (share[2 * flip].astype(F32) + crossed.astype(F32)).astype(BF16)
+            crossed = hop(crossed, 2 * flip)
+        terms.append(crossed)
+    return pl.pallas_call(
+        final_kernel,
+        out_shape=struct((count, 2 * lanes), BF16),
+        in_specs=[whole()] * (2 + len(terms)),
+        out_specs=whole(),
+        compiler_params=vmem(8),
+    )(state, small, *terms)
 
 
 def extended(cells, sides, width):

time: 168 us -> 142 us (0.85)
  waiting for transfers between devices: 97.6 us -> 76.4 us
  Pallas kernels: 29.8 us -> 36.9 us
  local copies, waits for them, and re-layouts: 9.41 us -> 2.39 us
  starting transfers between devices: 28.6 us -> 25.4 us
    ppermute x19, waiting for transfers between devices: 89 us -> 72.3 us  [hop(): return lax.ppermute(x, 'dev', [(i, i ^ flip) for i in range(devices)])]
    pallas_call x2 -> x6, Pallas kernels: 17.7 us -> 24.3 us  [the longest x1 11.9 us: gathered_body(): pl.pallas_call(functools.partial(load_kernel, local), out_shape=[struct((...]
    unnamed x22 -> x6, local copies, waits for them, and re-layouts: 7.41 us -> 2.39 us
    ppermute x19, starting transfers between devices: 24.5 us -> 19.5 us  [hop(): return lax.ppermute(x, 'dev', [(i, i ^ flip) for i in range(devices)])]
    ppermute x2, waiting for transfers between devices: 4.73 us -> 0.01 us  [gathered_body(): theirs = lax.ppermute(mine[flip], 'groups', [(0, 1), (1, 0)])]
    slice x2 -> x0, local copies, waits for them, and re-layouts: 2 us -> none  [the longest x1 1.23 us: gathered_body(): pair = stacked[1:].reshape(2 * count, local_width)]
  transfers between devices with their start and end apart: 32 -> 32, of which waited for: 18 -> 18; matrix products, arithmetic and copies ran while one was open for 1% -> 0% of each run, Pallas kernels for 4% -> 13%
where the time goes in v4:
time: 142 us; the launch traced here: 141 us
  waiting for transfers between devices  76.4 us (54%)
  Pallas kernels  36.9 us (26%)
  starting transfers between devices  25.4 us (18%)
  local copies, waits for them, and re-layouts  2.39 us (2%)
    ppermute x19, waiting for transfers between devices, hop(): return lax.ppermute(x, 'dev', [(i, i ^ flip) for i in range(devices)])  72.3 us
    ppermute x19, starting transfers between devices, hop(): return lax.ppermute(x, 'dev', [(i, i ^ flip) for i in range(devices)])  19.5 us
    pallas_call x1, Pallas kernels, gathered_body(): pl.pallas_call(functools.partial(load_kernel, local), out_shape=[struct((...  11.9 us
    pallas_call x1, Pallas kernels, gathered_body(): pl.pallas_call(functools.partial(hidden_kernel, steps), out_shape=struct(...  8.45 us
    pallas_call x4, Pallas kernels, gathered_body(): pl.pallas_call(functools.partial(select_kernel, local, topk, own, later i...  5.31 us
    ppermute x10, waiting for transfers between devices, swap(): return lax.ppermute(x, 'sub', [(0, 1), (1, 0)])  4.09 us
    pallas_call x1, Pallas kernels, gathered_body(): pl.pallas_call(attention_kernel, out_shape=struct((count, local_width), B...  3.11 us
    ppermute x2, starting transfers between devices, gathered_body(): theirs = lax.ppermute(mine[flip], 'groups', [(0, 1), (1, 0)])  2.99 us
  transfers between devices with their start and end apart: 32, of which 18 were waited for; matrix products, arithmetic and copies ran while one was open for 0% of the time, Pallas kernels for 13%

profile of v4, /device:TPU:0, one launch (start us, length us, event | category | flops | bytes accessed | tf_op | source)
XLA Modules:
  0.0 141.5 jit_solution(5986713762256625488)
XLA Ops:
  0.0 2.6 %shard_map.82 = (bf16[128,1024]{1,0:T(8,128)(2,1)S(1)}, bf16[256,1024]{1,0:T(8,128)(2,1)S(1)}, bf16[128,512]{1,0:T(8,128)(2,1)S(1)}, bf16[320,1024]{1,0:T(8,128)...) custom-call(bf16[128,2048]{1,0:T(8,128)(2,1)} %tokens_ref.1, bf16[3,128,1024]{2,1,0:T(8,128)(2,1)} %bitcast.7, ...), custom_call_target="tpu_custom_call" | custom-call | tf_op jit(solution)/shard_map/pallas_call | solution.py:330
  2.7 3.0 %collective-permute-start = (bf16[320,1024]{1,0:T(8,128)(2,1)}, bf16[320,1024]{1,0:T(8,128)(2,1)S(1)}, u32[]{:S(2)}, u32[]{:S(2)}) collective-permute-start(bf16[320,1024]{1,0:T(8,128)(2,1)} %get-tuple-element.53), channel_id=1, source_target_pairs={{0,2},{2,0},{4,6},{6,4},{8,10},{10,8},{12,14},{14,12},{1,3},{3,1},... | collective-permute-start | bytes 1966088 | tf_op jit(solution)/shard_map/ppermute | solution.py:323
  5.7 2.6 %collective-permute-start.4 = (bf16[128,1024]{1,0:T(8,128)(2,1)S(1)}, bf16[128,1024]{1,0:T(8,128)(2,1)S(1)}, u32[]{:S(2)}, u32[]{:S(2)}) collective-permute-start(bf16[128,1024]{1,0:T(8,128)(2,1)S(1)} %get-tuple-element.56), channel_id=1, source_target_pairs={{0,8},{2,10},{4,12},{6,14},{8,0},{10,2},{12,4},{14,6},{1,9},{3,11}... | collective-permute-start | bytes 786440 | tf_op jit(solution)/shard_map/ppermute | solution.py:323
  8.2 0.7 collective-permute-start.1
  8.9 12.2 %collective-permute-done.4.refs_4_ = bf16[128,1024]{1,0:T(8,128)(2,1)S(1)} collective-permute-done((bf16[128,1024]{1,0:T(8,128)(2,1)S(1)}, bf16[128,1024]{1,0:T(8,128)(2,1)S(1)}, u32[]{:S(2)}, u32[]{:S(2)}) %collective-permute-start.4) | collective-permute-done | bytes 262176 | tf_op jit(solution)/shard_map/ppermute | solution.py:323
  21.1 0.0 collective-permute-start.6
  21.1 2.0 %collective-permute-start.3 = (bf16[256,1024]{1,0:T(8,128)(2,1)S(1)}, bf16[256,1024]{1,0:T(8,128)(2,1)S(1)}, u32[]{:S(2)}, u32[]{:S(2)}) collective-permute-start(bf16[256,1024]{1,0:T(8,128)(2,1)S(1)} %get-tuple-element.55.refs_2_), channel_id=1, source_target_pairs={{0,4},{2,6},{4,0},{6,2},{8,12},{10,14},{12,8},{14,10},{1,5},{3,7},... | collective-permute-start | bytes 1572872 | tf_op jit(solution)/shard_map/ppermute | solution.py:323
  23.1 0.9 copy-done
  24.1 0.8 copy-done.1
  24.8 0.7 copy-done.2
  25.6 1.5 %collective-permute-start.5 = (bf16[128,1024]{1,0:T(8,128)(2,1)S(1)}, bf16[128,1024]{1,0:T(8,128)(2,1)S(1)}, u32[]{:S(2)}, u32[]{:S(2)}) collective-permute-start(bf16[128,1024]{1,0:T(8,128)(2,1)S(1)} %collective-permute-done.4.refs_4_), channel_id=1, source_target_pairs={{0,16},{16,0},{1,17},{17,1},{2,18},{18,2},{3,19},{19,3},{4,20},{20... | collective-permute-start | bytes 786440 | tf_op jit(solution)/shard_map/ppermute | solution.py:369
  27.1 8.0 %collective-permute-done.6.refs_6_ = bf16[128,1024]{1,0:T(8,128)(2,1)S(1)} collective-permute-done((bf16[128,1024]{1,0:T(8,128)(2,1)S(1)}, bf16[128,1024]{1,0:T(8,128)(2,1)S(1)}, u32[]{:S(2)}, u32[]{:S(2)}) %collective-permute-start.6) | collective-permute-done | bytes 262176 | tf_op jit(solution)/shard_map/ppermute | solution.py:323
  35.1 1.4 %collective-permute-start.7 = (bf16[128,1024]{1,0:T(8,128)(2,1)S(1)}, bf16[128,1024]{1,0:T(8,128)(2,1)S(1)}, u32[]{:S(2)}, u32[]{:S(2)}) collective-permute-start(bf16[128,1024]{1,0:T(8,128)(2,1)S(1)} %collective-permute-done.6.refs_6_), channel_id=1, source_target_pairs={{0,16},{16,0},{1,17},{17,1},{2,18},{18,2},{3,19},{19,3},{4,20},{20... | collective-permute-start | bytes 786440 | tf_op jit(solution)/shard_map/ppermute | solution.py:369
  36.6 0.0 collective-permute-done.1.next_ref
  36.6 3.1 %shard_map.84.refs_0_ = bf16[128,1024]{1,0:T(8,128)(2,1)S(1)} custom-call(bf16[128,1024]{1,0:T(8,128)(2,1)S(1)} %get-tuple-element.51._.query_ref, bf16[256,1024]{1,0:T(8,128)(2,1)S(1)} %get-tuple-element.52.own_ref, bf16[320,1024]{1,0:T(8,128)(2,1)S(1)} %collective-permute-done.cross_ref, bf16[256,1024]{1,0:T(8,128)(2,1)S(1)} %collective-permute-done.1.next_ref, ...), custom_call_target="tpu_custom_call" | custom-call | tf_op jit(solution)/shard_map/pallas_call | solution.py:376
  39.7 0.1 collective-permute-start.2
  39.8 4.8 %collective-permute-done.3.refs_3_ = bf16[256,1024]{1,0:T(8,128)(2,1)S(1)} collective-permute-done((bf16[256,1024]{1,0:T(8,128)(2,1)S(1)}, bf16[256,1024]{1,0:T(8,128)(2,1)S(1)}, u32[]{:S(2)}, u32[]{:S(2)}) %collective-permute-start.3) | collective-permute-done | bytes 524320 | tf_op jit(solution)/shard_map/ppermute | solution.py:323
  44.6 1.5 %collective-permute-done.2.refs_1_ = bf16[128,1024]{1,0:T(8,128)(2,1)S(1)} collective-permute-done((bf16[128,1024]{1,0:T(8,128)(2,1)S(1)}, bf16[128,1024]{1,0:T(8,128)(2,1)S(1)}, u32[]{:S(2)}, u32[]{:S(2)}) %collective-permute-start.2) | collective-permute-done | bytes 262176 | tf_op jit(solution)/shard_map/ppermute | solution.py:323
  46.1 1.4 %shard_map.85 = (f32[256,512]{1,0:T(8,128)S(1)}, f32[256,512]{1,0:T(8,128)S(1)}) custom-call(bf16[128,1024]{1,0:T(8,128)(2,1)S(1)} %shard_map.84.refs_0_, bf16[128,1024]{1,0:T(8,128)(2,1)S(1)} %collective-permute-done.2.refs_1_, bf16[256,1024]{1,0:T(8,128)(2,1)S(1)} %get-tuple-element.55.refs_2_, bf16[256,1024]{1,0:T(8,128)(2,1)S(1)} %collective-permute-done.3.refs_3_, ...), custom_call_target="tpu_custom_call" | custom-call | tf_op jit(solution)/shard_map/pallas_call | solution.py:383
  47.6 0.1 collective-permute-start.8
  47.7 1.9 %collective-permute-done.8.got_ref = f32[256,512]{1,0:T(8,128)S(1)} collective-permute-done((f32[256,512]{1,0:T(8,128)S(1)}, f32[256,512]{1,0:T(8,128)S(1)}, u32[]{:S(2)}, u32[]{:S(2)}) %collective-permute-start.8) | collective-permute-done | bytes 524320 | tf_op jit(solution)/shard_map/ppermute | solution.py:326
  49.6 0.1 shard_map.86.refs_0_._
  49.7 0.1 collective-permute-start.12
  49.7 0.1 collective-permute-start.9
  49.8 4.3 %collective-permute-start.16 = (bf16[272,512]{1,0:T(8,128)(2,1)S(1)}, bf16[272,512]{1,0:T(8,128)(2,1)S(1)}, u32[]{:S(2)}, u32[]{:S(2)}) collective-permute-start(bf16[272,512]{1,0:T(8,128)(2,1)S(1)} %shard_map.86.refs_0_._), channel_id=1, source_target_pairs={{0,8},{2,10},{4,12},{6,14},{8,0},{10,2},{12,4},{14,6},{1,9},{3,11}... | collective-permute-start | bytes 835592 | tf_op jit(solution)/shard_map/ppermute | solution.py:323
  54.1 11.9 %shard_map.88 = (bf16[2,2,192,2048]{3,2,1,0:T(8,128)(2,1)S(1)}, bf16[2,2,192,2048]{3,2,1,0:T(8,128)(2,1)S(1)}, bf16[2,2,192,2048]{3,2,1,0:T(8,128)(2,1)S(1)}, bf...) custom-call(bf16[16,2,192,2048]{3,2,1,0:T(8,128)(2,1)} %bitcast.6, ...), custom_call_target="tpu_custom_call" | custom-call | tf_op jit(solution)/shard_map/pallas_call | solution.py:400
  66.1 0.1 collective-permute-start.13
  66.2 0.1 collective-permute-start.14
  66.2 0.3 collective-permute-done.16.refs_0_
  66.6 7.5 %collective-permute-done.13.refs_1_ = bf16[272,512]{1,0:T(8,128)(2,1)S(1)} collective-permute-done((bf16[272,512]{1,0:T(8,128)(2,1)S(1)}, bf16[272,512]{1,0:T(8,128)(2,1)S(1)}, u32[]{:S(2)}, u32[]{:S(2)}) %collective-permute-start.13) | collective-permute-done | bytes 278560 | tf_op jit(solution)/shard_map/ppermute | solution.py:323
  74.0 0.5 collective-permute-start.10
  74.5 0.3 collective-permute-start.18
  74.8 0.5 collective-permute-done.17.refs_6_
  75.3 0.3 collective-permute-done.15.refs_3_
  75.6 1.3 shard_map.90
  76.9 1.8 %collective-permute-start.21 = (bf16[272,512]{1,0:T(8,128)(2,1)S(1)}, bf16[272,512]{1,0:T(8,128)(2,1)S(1)}, u32[]{:S(2)}, u32[]{:S(2)}) collective-permute-start(bf16[272,512]{1,0:T(8,128)(2,1)S(1)} %get-tuple-element.67.refs_0_), channel_id=1, source_target_pairs={{0,2},{2,0},{4,6},{6,4},{8,10},{10,8},{12,14},{14,12},{1,3},{3,1},... | collective-permute-start | bytes 835592 | tf_op jit(solution)/shard_map/ppermute | solution.py:323
  78.7 0.5 collective-permute-start.11
  79.2 4.9 %collective-permute-done.18.refs_1_ = bf16[272,512]{1,0:T(8,128)(2,1)S(1)} collective-permute-done((bf16[272,512]{1,0:T(8,128)(2,1)S(1)}, bf16[272,512]{1,0:T(8,128)(2,1)S(1)}, u32[]{:S(2)}, u32[]{:S(2)}) %collective-permute-start.18) | collective-permute-done | bytes 278560 | tf_op jit(solution)/shard_map/ppermute | solution.py:323
  84.1 0.5 collective-permute-start.22
  84.6 4.5 %collective-permute-done.21.refs_1_ = bf16[272,512]{1,0:T(8,128)(2,1)S(1)} collective-permute-done((bf16[272,512]{1,0:T(8,128)(2,1)S(1)}, bf16[272,512]{1,0:T(8,128)(2,1)S(1)}, u32[]{:S(2)}, u32[]{:S(2)}) %collective-permute-start.21) | collective-permute-done | bytes 278560 | tf_op jit(solution)/shard_map/ppermute | solution.py:323
  89.1 1.3 shard_map.87
  90.4 1.3 shard_map.91
  91.8 1.3 shard_map.92
  93.1 8.4 %shard_map.93.near_ref = bf16[8,128,384]{2,1,0:T(8,128)(2,1)S(1)} custom-call(bf16[8,32,2048]{2,1,0:T(8,128)(2,1)S(1)} %get-tuple-element.63.refs_0_, bf16[8,32,2048]{2,1,0:T(8,128)(2,1)S(1)} %get-tuple-element.65.refs_1_, bf16[8,32,2048]{2,1,0:T(8,128)(2,1)S(1)} %get-tuple-element.66.refs_2_, bf16[8,32,2048]{2,1,0:T(8,128)(2,1)S(1)} %get-tuple-element.68.refs_3_, ...), custom_call_target="tpu_custom_call" | custom-call | tf_op jit(solution)/shard_map/pallas_call | solution.py:460
  101.6 0.6 collective-permute-start.24
  102.2 1.9 %collective-permute-done.24.far_ref = bf16[8,128,384]{2,1,0:T(8,128)(2,1)S(1)} collective-permute-done((bf16[8,128,384]{2,1,0:T(8,128)(2,1)S(1)}, bf16[8,128,384]{2,1,0:T(8,128)(2,1)S(1)}, u32[]{:S(2)}, u32[]{:S(2)}) %collective-permute-start.24) | collective-permute-done | bytes 786464 | tf_op jit(solution)/shard_map/ppermute | solution.py:326
  104.1 3.0 %shard_map.94 = (bf16[128,1024]{1,0:T(8,128)(2,1)S(1)}, bf16[128,1024]{1,0:T(8,128)(2,1)S(1)}, bf16[128,1024]{1,0:T(8,128)(2,1)S(1)}, bf16[128,1024]{1,0:T(8,128...) custom-call(bf16[8,128,384]{2,1,0:T(8,128)(2,1)S(1)} %shard_map.93.n, ...), custom_call_target="tpu_custom_call" | custom-call | tf_op jit(solution)/shard_map/pallas_call | solution.py:467
  107.0 0.3 collective-permute-start.25
  107.4 1.7 %collective-permute-start.27 = (bf16[128,1024]{1,0:T(8,128)(2,1)S(1)}, bf16[128,1024]{1,0:T(8,128)(2,1)S(1)}, u32[]{:S(2)}, u32[]{:S(2)}) collective-permute-start(bf16[128,1024]{1,0:T(8,128)(2,1)S(1)} %get-tuple-element.93), channel_id=1, source_target_pairs={{0,2},{2,0},{4,6},{6,4},{8,10},{10,8},{12,14},{14,12},{1,3},{3,1},... | collective-permute-start | bytes 786440 | tf_op jit(solution)/shard_map/ppermute | solution.py:323
  109.1 0.3 collective-permute-start.29
  109.4 1.7 %collective-permute-start.31 = (bf16[128,1024]{1,0:T(8,128)(2,1)S(1)}, bf16[128,1024]{1,0:T(8,128)(2,1)S(1)}, u32[]{:S(2)}, u32[]{:S(2)}) collective-permute-start(bf16[128,1024]{1,0:T(8,128)(2,1)S(1)} %get-tuple-element.96), channel_id=1, source_target_pairs={{0,2},{2,0},{4,6},{6,4},{8,10},{10,8},{12,14},{14,12},{1,3},{3,1},... | collective-permute-start | bytes 786440 | tf_op jit(solution)/shard_map/ppermute | solution.py:323
  111.2 5.1 %collective-permute-done.25 = bf16[128,1024]{1,0:T(8,128)(2,1)S(1)} collective-permute-done((bf16[128,1024]{1,0:T(8,128)(2,1)S(1)}, bf16[128,1024]{1,0:T(8,128)(2,1)S(1)}, u32[]{:S(2)}, u32[]{:S(2)}) %collective-permute-start.25) | collective-permute-done | bytes 262176 | tf_op jit(solution)/shard_map/ppermute | solution.py:323
  116.2 0.1 add_convert_fusion.2
  116.3 0.3 collective-permute-start.26
  116.6 5.2 %collective-permute-done.27 = bf16[128,1024]{1,0:T(8,128)(2,1)S(1)} collective-permute-done((bf16[128,1024]{1,0:T(8,128)(2,1)S(1)}, bf16[128,1024]{1,0:T(8,128)(2,1)S(1)}, u32[]{:S(2)}, u32[]{:S(2)}) %collective-permute-start.27) | collective-permute-done | bytes 262176 | tf_op jit(solution)/shard_map/ppermute | solution.py:323
  121.8 0.1 add_convert_fusion.1
  121.9 0.3 collective-permute-start.28
  122.2 5.2 %collective-permute-done.29 = bf16[128,1024]{1,0:T(8,128)(2,1)S(1)} collective-permute-done((bf16[128,1024]{1,0:T(8,128)(2,1)S(1)}, bf16[128,1024]{1,0:T(8,128)(2,1)S(1)}, u32[]{:S(2)}, u32[]{:S(2)}) %collective-permute-start.29) | collective-permute-done | bytes 262176 | tf_op jit(solution)/shard_map/ppermute | solution.py:323
  127.4 0.1 add_convert_fusion
  127.5 0.4 collective-permute-start.30
  127.9 4.7 %collective-permute-done.31.refs_4_ = bf16[128,1024]{1,0:T(8,128)(2,1)S(1)} collective-permute-done((bf16[128,1024]{1,0:T(8,128)(2,1)S(1)}, bf16[128,1024]{1,0:T(8,128)(2,1)S(1)}, u32[]{:S(2)}, u32[]{:S(2)}) %collective-permute-start.31) | collective-permute-done | bytes 262176 | tf_op jit(solution)/shard_map/ppermute | solution.py:323
  132.6 7.9 %collective-permute-done.28.refs_2_ = bf16[128,1024]{1,0:T(8,128)(2,1)S(1)} collective-permute-done((bf16[128,1024]{1,0:T(8,128)(2,1)S(1)}, bf16[128,1024]{1,0:T(8,128)(2,1)S(1)}, u32[]{:S(2)}, u32[]{:S(2)}) %collective-permute-start.28) | collective-permute-done | bytes 262176 | tf_op jit(solution)/shard_map/ppermute | solution.py:323
  140.5 0.1 collective-permute-done.30.refs_3_
  140.6 0.9 shard_map.95
  (23 shorter events, 0.1 us)
Async XLA Ops:
  2.7 33.9 %collective-permute-start = (bf16[320,1024]{1,0:T(8,128)(2,1)}, bf16[320,1024]{1,0:T(8,128)(2,1)S(1)}, u32[]{:S(2)}, u32[]{:S(2)}) collective-permute-start(bf16[320,1024]{1,0:T(8,128)(2,1)} %get-tuple-element.53), channel_id=1, source_target_pairs={{0,2},{2,0},{4,6},{6,4},{8,10},{10,8},{12,14},{14,12},{1,3},{3,1},... | collective-permute-start | bytes 1966088 | tf_op jit(solution)/shard_map/ppermute | solution.py:323
  5.7 15.4 %collective-permute-start.4 = (bf16[128,1024]{1,0:T(8,128)(2,1)S(1)}, bf16[128,1024]{1,0:T(8,128)(2,1)S(1)}, u32[]{:S(2)}, u32[]{:S(2)}) collective-permute-start(bf16[128,1024]{1,0:T(8,128)(2,1)S(1)} %get-tuple-element.56), channel_id=1, source_target_pairs={{0,8},{2,10},{4,12},{6,14},{8,0},{10,2},{12,4},{14,6},{1,9},{3,11}... | collective-permute-start | bytes 786440 | tf_op jit(solution)/shard_map/ppermute | solution.py:323
  8.2 28.3 %collective-permute-start.1 = (bf16[256,1024]{1,0:T(8,128)(2,1)S(1)}, bf16[256,1024]{1,0:T(8,128)(2,1)S(1)}, u32[]{:S(2)}, u32[]{:S(2)}) collective-permute-start(bf16[256,1024]{1,0:T(8,128)(2,1)S(1)} %get-tuple-element.52.own_ref), channel_id=1, source_target_pairs={{2,4},{6,8},{10,12},{4,2},{8,6},{12,10},{3,5},{7,9},{11,13},{5,3},... | collective-permute-start | bytes 1572872 | tf_op jit(solution)/shard_map/ppermute | solution.py:357
  21.1 14.0 %collective-permute-start.6 = (bf16[128,1024]{1,0:T(8,128)(2,1)S(1)}, bf16[128,1024]{1,0:T(8,128)(2,1)S(1)}, u32[]{:S(2)}, u32[]{:S(2)}) collective-permute-start(bf16[128,1024]{1,0:T(8,128)(2,1)S(1)} %collective-permute-done.4.refs_4_), channel_id=1, source_target_pairs={{0,4},{2,6},{4,0},{6,2},{8,12},{10,14},{12,8},{14,10},{1,5},{3,7},... | collective-permute-start | bytes 786440 | tf_op jit(solution)/shard_map/ppermute | solution.py:323
  21.1 23.5 %collective-permute-start.3 = (bf16[256,1024]{1,0:T(8,128)(2,1)S(1)}, bf16[256,1024]{1,0:T(8,128)(2,1)S(1)}, u32[]{:S(2)}, u32[]{:S(2)}) collective-permute-start(bf16[256,1024]{1,0:T(8,128)(2,1)S(1)} %get-tuple-element.55.refs_2_), channel_id=1, source_target_pairs={{0,4},{2,6},{4,0},{6,2},{8,12},{10,14},{12,8},{14,10},{1,5},{3,7},... | collective-permute-start | bytes 1572872 | tf_op jit(solution)/shard_map/ppermute | solution.py:323
  23.1 0.9 copy-start
  24.1 0.8 copy-start.1
  24.8 0.7 copy-start.2
  25.6 14.2 %collective-permute-start.5 = (bf16[128,1024]{1,0:T(8,128)(2,1)S(1)}, bf16[128,1024]{1,0:T(8,128)(2,1)S(1)}, u32[]{:S(2)}, u32[]{:S(2)}) collective-permute-start(bf16[128,1024]{1,0:T(8,128)(2,1)S(1)} %collective-permute-done.4.refs_4_), channel_id=1, source_target_pairs={{0,16},{16,0},{1,17},{17,1},{2,18},{18,2},{3,19},{19,3},{4,20},{20... | collective-permute-start | bytes 786440 | tf_op jit(solution)/shard_map/ppermute | solution.py:369
  35.1 9.5 %collective-permute-start.7 = (bf16[128,1024]{1,0:T(8,128)(2,1)S(1)}, bf16[128,1024]{1,0:T(8,128)(2,1)S(1)}, u32[]{:S(2)}, u32[]{:S(2)}) collective-permute-start(bf16[128,1024]{1,0:T(8,128)(2,1)S(1)} %collective-permute-done.6.refs_6_), channel_id=1, source_target_pairs={{0,16},{16,0},{1,17},{17,1},{2,18},{18,2},{3,19},{19,3},{4,20},{20... | collective-permute-start | bytes 786440 | tf_op jit(solution)/shard_map/ppermute | solution.py:369
  39.7 6.4 %collective-permute-start.2 = (bf16[128,1024]{1,0:T(8,128)(2,1)S(1)}, bf16[128,1024]{1,0:T(8,128)(2,1)S(1)}, u32[]{:S(2)}, u32[]{:S(2)}) collective-permute-start(bf16[128,1024]{1,0:T(8,128)(2,1)S(1)} %shard_map.84.refs_0_), channel_id=1, source_target_pairs={{0,2},{2,0},{4,6},{6,4},{8,10},{10,8},{12,14},{14,12},{1,3},{3,1},... | collective-permute-start | bytes 786440 | tf_op jit(solution)/shard_map/ppermute | solution.py:323
  47.6 2.0 %collective-permute-start.8 = (f32[256,512]{1,0:T(8,128)S(1)}, f32[256,512]{1,0:T(8,128)S(1)}, u32[]{:S(2)}, u32[]{:S(2)}) collective-permute-start(f32[256,512]{1,0:T(8,128)S(1)} %get-tuple-element.58), channel_id=1, source_target_pairs={{0,1},{1,0},{2,3},{3,2},{4,5},{5,4},{6,7},{7,6},{8,9},{9,8},{10,11... | collective-permute-start | bytes 1572872 | tf_op jit(solution)/shard_map/ppermute | solution.py:326
  49.7 16.4 %collective-permute-start.12 = (bf16[272,512]{1,0:T(8,128)(2,1)S(1)}, bf16[272,512]{1,0:T(8,128)(2,1)S(1)}, u32[]{:S(2)}, u32[]{:S(2)}) collective-permute-start(bf16[272,512]{1,0:T(8,128)(2,1)S(1)} %shard_map.86.refs_0_._), channel_id=1, source_target_pairs={{0,4},{2,6},{4,0},{6,2},{8,12},{10,14},{12,8},{14,10},{1,5},{3,7},... | collective-permute-start | bytes 835592 | tf_op jit(solution)/shard_map/ppermute | solution.py:323
  49.7 16.3 %collective-permute-start.9 = (bf16[272,512]{1,0:T(8,128)(2,1)S(1)}, bf16[272,512]{1,0:T(8,128)(2,1)S(1)}, u32[]{:S(2)}, u32[]{:S(2)}) collective-permute-start(bf16[272,512]{1,0:T(8,128)(2,1)S(1)} %shard_map.86.refs_0_._), channel_id=1, source_target_pairs={{0,2},{2,0},{4,6},{6,4},{8,10},{10,8},{12,14},{14,12},{1,3},{3,1},... | collective-permute-start | bytes 835592 | tf_op jit(solution)/shard_map/ppermute | solution.py:323
  49.8 16.7 %collective-permute-start.16 = (bf16[272,512]{1,0:T(8,128)(2,1)S(1)}, bf16[272,512]{1,0:T(8,128)(2,1)S(1)}, u32[]{:S(2)}, u32[]{:S(2)}) collective-permute-start(bf16[272,512]{1,0:T(8,128)(2,1)S(1)} %shard_map.86.refs_0_._), channel_id=1, source_target_pairs={{0,8},{2,10},{4,12},{6,14},{8,0},{10,2},{12,4},{14,6},{1,9},{3,11}... | collective-permute-start | bytes 835592 | tf_op jit(solution)/shard_map/ppermute | solution.py:323
  66.1 7.9 %collective-permute-start.13 = (bf16[272,512]{1,0:T(8,128)(2,1)S(1)}, bf16[272,512]{1,0:T(8,128)(2,1)S(1)}, u32[]{:S(2)}, u32[]{:S(2)}) collective-permute-start(bf16[272,512]{1,0:T(8,128)(2,1)S(1)} %shard_map.89.refs_0_), channel_id=1, source_target_pairs={{0,2},{2,0},{4,6},{6,4},{8,10},{10,8},{12,14},{14,12},{1,3},{3,1},... | collective-permute-start | bytes 835592 | tf_op jit(solution)/shard_map/ppermute | solution.py:323
  66.2 9.1 %collective-permute-start.14 = (bf16[272,512]{1,0:T(8,128)(2,1)S(1)}, bf16[272,512]{1,0:T(8,128)(2,1)S(1)}, u32[]{:S(2)}, u32[]{:S(2)}) collective-permute-start(bf16[272,512]{1,0:T(8,128)(2,1)S(1)} %shard_map.89.refs_0_), channel_id=1, source_target_pairs={{0,1},{1,0},{2,3},{3,2},{4,5},{5,4},{6,7},{7,6},{8,9},{9,8},{10,11... | collective-permute-start | bytes 835592 | tf_op jit(solution)/shard_map/ppermute | solution.py:326
  66.5 8.8 %collective-permute-start.17 = (bf16[272,512]{1,0:T(8,128)(2,1)S(1)}, bf16[272,512]{1,0:T(8,128)(2,1)S(1)}, u32[]{:S(2)}, u32[]{:S(2)}) collective-permute-start(bf16[272,512]{1,0:T(8,128)(2,1)S(1)} %collective-permute-done.16.refs_0_), channel_id=1, source_target_pairs={{0,4},{2,6},{4,0},{6,2},{8,12},{10,14},{12,8},{14,10},{1,5},{3,7},... | collective-permute-start | bytes 835592 | tf_op jit(solution)/shard_map/ppermute | solution.py:323
  74.0 1.6 %collective-permute-start.15 = (bf16[272,512]{1,0:T(8,128)(2,1)S(1)}, bf16[272,512]{1,0:T(8,128)(2,1)S(1)}, u32[]{:S(2)}, u32[]{:S(2)}) collective-permute-start(bf16[272,512]{1,0:T(8,128)(2,1)S(1)} %collective-permute-done.13.refs_1_), channel_id=1, source_target_pairs={{0,1},{1,0},{2,3},{3,2},{4,5},{5,4},{6,7},{7,6},{8,9},{9,8},{10,11... | collective-permute-start | bytes 835592 | tf_op jit(solution)/shard_map/ppermute | solution.py:326
  74.0 10.0 %collective-permute-start.10 = (bf16[272,512]{1,0:T(8,128)(2,1)S(1)}, bf16[272,512]{1,0:T(8,128)(2,1)S(1)}, u32[]{:S(2)}, u32[]{:S(2)}) collective-permute-start(bf16[272,512]{1,0:T(8,128)(2,1)S(1)} %shard_map.86.refs_0_._), channel_id=1, source_target_pairs={{0,1},{1,0},{2,3},{3,2},{4,5},{5,4},{6,7},{7,6},{8,9},{9,8},{10,11... | collective-permute-start | bytes 835592 | tf_op jit(solution)/shard_map/ppermute | solution.py:326
  74.5 9.5 %collective-permute-start.18 = (bf16[272,512]{1,0:T(8,128)(2,1)S(1)}, bf16[272,512]{1,0:T(8,128)(2,1)S(1)}, u32[]{:S(2)}, u32[]{:S(2)}) collective-permute-start(bf16[272,512]{1,0:T(8,128)(2,1)S(1)} %collective-permute-done.16.refs_0_), channel_id=1, source_target_pairs={{0,2},{2,0},{4,6},{6,4},{8,10},{10,8},{12,14},{14,12},{1,3},{3,1},... | collective-permute-start | bytes 835592 | tf_op jit(solution)/shard_map/ppermute | solution.py:323
  76.9 12.2 %collective-permute-start.21 = (bf16[272,512]{1,0:T(8,128)(2,1)S(1)}, bf16[272,512]{1,0:T(8,128)(2,1)S(1)}, u32[]{:S(2)}, u32[]{:S(2)}) collective-permute-start(bf16[272,512]{1,0:T(8,128)(2,1)S(1)} %get-tuple-element.67.refs_0_), channel_id=1, source_target_pairs={{0,2},{2,0},{4,6},{6,4},{8,10},{10,8},{12,14},{14,12},{1,3},{3,1},... | collective-permute-start | bytes 835592 | tf_op jit(solution)/shard_map/ppermute | solution.py:323
  78.7 11.8 %collective-permute-start.19 = (bf16[272,512]{1,0:T(8,128)(2,1)S(1)}, bf16[272,512]{1,0:T(8,128)(2,1)S(1)}, u32[]{:S(2)}, u32[]{:S(2)}) collective-permute-start(bf16[272,512]{1,0:T(8,128)(2,1)S(1)} %collective-permute-done.16.refs_0_), channel_id=1, source_target_pairs={{0,1},{1,0},{2,3},{3,2},{4,5},{5,4},{6,7},{7,6},{8,9},{9,8},{10,11... | collective-permute-start | bytes 835592 | tf_op jit(solution)/shard_map/ppermute | solution.py:326
  78.7 10.4 %collective-permute-start.11 = (bf16[272,512]{1,0:T(8,128)(2,1)S(1)}, bf16[272,512]{1,0:T(8,128)(2,1)S(1)}, u32[]{:S(2)}, u32[]{:S(2)}) collective-permute-start(bf16[272,512]{1,0:T(8,128)(2,1)S(1)} %collective-permute-done.9.refs_1_), channel_id=1, source_target_pairs={{0,1},{1,0},{2,3},{3,2},{4,5},{5,4},{6,7},{7,6},{8,9},{9,8},{10,11... | collective-permute-start | bytes 835592 | tf_op jit(solution)/shard_map/ppermute | solution.py:326
  84.0 6.4 %collective-permute-start.20 = (bf16[272,512]{1,0:T(8,128)(2,1)S(1)}, bf16[272,512]{1,0:T(8,128)(2,1)S(1)}, u32[]{:S(2)}, u32[]{:S(2)}) collective-permute-start(bf16[272,512]{1,0:T(8,128)(2,1)S(1)} %collective-permute-done.18.refs_1_), channel_id=1, source_target_pairs={{0,1},{1,0},{2,3},{3,2},{4,5},{5,4},{6,7},{7,6},{8,9},{9,8},{10,11... | collective-permute-start | bytes 835592 | tf_op jit(solution)/shard_map/ppermute | solution.py:326
  84.1 7.7 %collective-permute-start.22 = (bf16[272,512]{1,0:T(8,128)(2,1)S(1)}, bf16[272,512]{1,0:T(8,128)(2,1)S(1)}, u32[]{:S(2)}, u32[]{:S(2)}) collective-permute-start(bf16[272,512]{1,0:T(8,128)(2,1)S(1)} %get-tuple-element.67.refs_0_), channel_id=1, source_target_pairs={{0,1},{1,0},{2,3},{3,2},{4,5},{5,4},{6,7},{7,6},{8,9},{9,8},{10,11... | collective-permute-start | bytes 835592 | tf_op jit(solution)/shard_map/ppermute | solution.py:326
  89.1 2.7 %collective-permute-start.23 = (bf16[272,512]{1,0:T(8,128)(2,1)S(1)}, bf16[272,512]{1,0:T(8,128)(2,1)S(1)}, u32[]{:S(2)}, u32[]{:S(2)}) collective-permute-start(bf16[272,512]{1,0:T(8,128)(2,1)S(1)} %collective-permute-done.21.refs_1_), channel_id=1, source_target_pairs={{0,1},{1,0},{2,3},{3,2},{4,5},{5,4},{6,7},{7,6},{8,9},{9,8},{10,11... | collective-permute-start | bytes 835592 | tf_op jit(solution)/shard_map/ppermute | solution.py:326
  101.6 2.5 %collective-permute-start.24 = (bf16[8,128,384]{2,1,0:T(8,128)(2,1)S(1)}, bf16[8,128,384]{2,1,0:T(8,128)(2,1)S(1)}, u32[]{:S(2)}, u32[]{:S(2)}) collective-permute-start(bf16[8,128,384]{2,1,0:T(8,128)(2,1)S(1)} %shard_map.93.near_ref), channel_id=1, source_target_pairs={{0,1},{1,0},{2,3},{3,2},{4,5},{5,4},{6,7},{7,6},{8,9},{9,8},{10,11... | collective-permute-start | bytes 2359304 | tf_op jit(solution)/shard_map/ppermute | solution.py:326
  107.0 9.2 %collective-permute-start.25 = (bf16[128,1024]{1,0:T(8,128)(2,1)S(1)}, bf16[128,1024]{1,0:T(8,128)(2,1)S(1)}, u32[]{:S(2)}, u32[]{:S(2)}) collective-permute-start(bf16[128,1024]{1,0:T(8,128)(2,1)S(1)} %get-tuple-element.91), channel_id=1, source_target_pairs={{0,2},{2,0},{4,6},{6,4},{8,10},{10,8},{12,14},{14,12},{1,3},{3,1},... | collective-permute-start | bytes 786440 | tf_op jit(solution)/shard_map/ppermute | solution.py:323
  107.4 14.5 %collective-permute-start.27 = (bf16[128,1024]{1,0:T(8,128)(2,1)S(1)}, bf16[128,1024]{1,0:T(8,128)(2,1)S(1)}, u32[]{:S(2)}, u32[]{:S(2)}) collective-permute-start(bf16[128,1024]{1,0:T(8,128)(2,1)S(1)} %get-tuple-element.93), channel_id=1, source_target_pairs={{0,2},{2,0},{4,6},{6,4},{8,10},{10,8},{12,14},{14,12},{1,3},{3,1},... | collective-permute-start | bytes 786440 | tf_op jit(solution)/shard_map/ppermute | solution.py:323
  109.1 18.3 %collective-permute-start.29 = (bf16[128,1024]{1,0:T(8,128)(2,1)S(1)}, bf16[128,1024]{1,0:T(8,128)(2,1)S(1)}, u32[]{:S(2)}, u32[]{:S(2)}) collective-permute-start(bf16[128,1024]{1,0:T(8,128)(2,1)S(1)} %get-tuple-element.95), channel_id=1, source_target_pairs={{0,2},{2,0},{4,6},{6,4},{8,10},{10,8},{12,14},{14,12},{1,3},{3,1},... | collective-permute-start | bytes 786440 | tf_op jit(solution)/shard_map/ppermute | solution.py:323
  109.4 23.2 %collective-permute-start.31 = (bf16[128,1024]{1,0:T(8,128)(2,1)S(1)}, bf16[128,1024]{1,0:T(8,128)(2,1)S(1)}, u32[]{:S(2)}, u32[]{:S(2)}) collective-permute-start(bf16[128,1024]{1,0:T(8,128)(2,1)S(1)} %get-tuple-element.96), channel_id=1, source_target_pairs={{0,2},{2,0},{4,6},{6,4},{8,10},{10,8},{12,14},{14,12},{1,3},{3,1},... | collective-permute-start | bytes 786440 | tf_op jit(solution)/shard_map/ppermute | solution.py:323
  116.3 16.3 %collective-permute-start.26 = (bf16[128,1024]{1,0:T(8,128)(2,1)S(1)}, bf16[128,1024]{1,0:T(8,128)(2,1)S(1)}, u32[]{:S(2)}, u32[]{:S(2)}) collective-permute-start(bf16[128,1024]{1,0:T(8,128)(2,1)S(1)} %add_convert_fusion.2), channel_id=1, source_target_pairs={{0,12},{2,14},{4,8},{6,10},{8,4},{10,6},{12,0},{14,2},{1,13},{3,15... | collective-permute-start | bytes 786440 | tf_op jit(solution)/shard_map/ppermute | solution.py:323
  121.9 18.6 %collective-permute-start.28 = (bf16[128,1024]{1,0:T(8,128)(2,1)S(1)}, bf16[128,1024]{1,0:T(8,128)(2,1)S(1)}, u32[]{:S(2)}, u32[]{:S(2)}) collective-permute-start(bf16[128,1024]{1,0:T(8,128)(2,1)S(1)} %add_convert_fusion.1), channel_id=1, source_target_pairs={{0,8},{2,10},{4,12},{6,14},{8,0},{10,2},{12,4},{14,6},{1,9},{3,11}... | collective-permute-start | bytes 786440 | tf_op jit(solution)/shard_map/ppermute | solution.py:323
  127.5 13.1 %collective-permute-start.30 = (bf16[128,1024]{1,0:T(8,128)(2,1)S(1)}, bf16[128,1024]{1,0:T(8,128)(2,1)S(1)}, u32[]{:S(2)}, u32[]{:S(2)}) collective-permute-start(bf16[128,1024]{1,0:T(8,128)(2,1)S(1)} %add_convert_fusion), channel_id=1, source_target_pairs={{0,4},{2,6},{4,0},{6,2},{8,12},{10,14},{12,8},{14,10},{1,5},{3,7},... | collective-permute-start | bytes 786440 | tf_op jit(solution)/shard_map/ppermute | solution.py:323

commit v5 on v4

--- a/solution.py
+++ b/solution.py
@@ -80,7 +80,8 @@
     router_to_ref[...] = router_ref[...]
 
 
-def attention_kernel(query_ref, own_ref, cross_ref, next_ref, _, mixed_ref):
+def attention_kernel(query_ref, own_ref, cross_ref, next_ref, *refs):
+    mixed_ref = refs[-1]
     count, width = mixed_ref.shape
     place = lax.axis_index("dev")
     even = place % 2 == 0
@@ -177,10 +178,10 @@
     )(array, *others)
 
 
-def select_kernel(local, topk, own, carried, *refs):
+def select_kernel(local, topk, own, *refs):
     shard_refs, (mod_ref, router_ref) = refs[:4], refs[4:6]
-    rows_ref, back_ref = refs[6 + carried : 8 + carried]
-    state_ref = refs[8 + carried] if own else None
+    rows_ref, back_ref = refs[6:8]
+    state_ref = refs[8] if own else None
     full_ref, gate_ref = refs[-2:]
     count, width = full_ref.shape
     lanes = shard_refs[0].shape[1]
@@ -258,12 +259,14 @@
 
 def hidden_kernel(steps, *refs):
     rows_refs, w_refs, hidden_ref = refs[:steps], refs[steps:-1], refs[-1]
-    both = hidden_ref.shape[2]
     for e, w_ref in enumerate(w_refs):
         rows = jnp.concatenate([ref[e] for ref in rows_refs])
-        weight = jnp.concatenate([w_ref[b, g] for g in range(2) for b in range(2)])
-        product = lax.dot_general(rows, weight, NT, preferred_element_type=F32)
-        hidden_ref[e] = (jax.nn.silu(product[:, :both]) * product[:, both:]).astype(BF16)
+        halves = []
+        for b in range(2):
+            gate = lax.dot_general(w_ref[b, 0], rows, NT, preferred_element_type=F32)
+            up = lax.dot_general(w_ref[b, 1], rows, NT, preferred_element_type=F32)
+            halves.append(jax.nn.silu(gate) * up)
+        hidden_ref[e] = jnp.concatenate(halves).T.astype(BF16)
 
 
 def output_kernel(steps, local, near_ref, far_ref, *refs):
@@ -357,6 +360,18 @@
     after = lax.ppermute(pair, "dev", odd + [(j, i) for i, j in odd])
     cross = hop(cross, 1)
 
+    units = gate_up_weight.shape[3]
+    *loaded, done = pl.pallas_call(
+        functools.partial(load_kernel, local),
+        out_shape=[struct((2, 2, units, width), BF16)] * local
+        + [struct((2, *down_weight.shape[1:]), BF16)] * local
+        + [struct((8, 128), F32)],
+        in_specs=[pl.BlockSpec(memory_space=pl.ANY)] * 3,
+        out_specs=[whole()] * (2 * local + 1),
+        scratch_shapes=[pltpu.SemaphoreType.DMA((2 * local,))],
+        compiler_params=vmem(14),
+    )(gate_up_weight.swapaxes(2, 3), down_weight, query)
+
     pieces, weights = [(0, None), (1, None)], [own_weight, hop(own_weight, 2)]
     mine = {0: sent}
     for flip in range(2, steps):
@@ -364,22 +379,25 @@
         if flip > 2 and flip - low > 0:
             mine[flip] = hop(mine[flip - low], 2 * low)
         else:
-            mine[flip] = hop(sent, 2 * flip)
+            mine[flip] = tie(hop(sent, 2 * flip), done)
+
+    mixed = pl.pallas_call(
+        attention_kernel,
+        out_shape=struct((count, local_width), BF16),
+        in_specs=[whole()] * 4 + [pl.BlockSpec(memory_space=pl.ANY)] * 2,
+        out_specs=whole(),
+        compiler_params=vmem(6),
+    )(query, pair, cross, after, small, weights[1])
+    for flip in range(2, steps):
         if split:
+            if flip == steps - 1:
+                mine[flip] = tie(mine[flip], mixed)
             theirs = lax.ppermute(mine[flip], "groups", [(0, 1), (1, 0)])
             pieces += [(flip, 0), (flip, 1)]
             weights += [mine[flip], theirs]
         else:
             pieces.append((flip, None))
             weights.append(mine[flip])
-
-    mixed = pl.pallas_call(
-        attention_kernel,
-        out_shape=struct((count, local_width), BF16),
-        in_specs=[whole()] * 4 + [pl.BlockSpec(memory_space=pl.ANY)],
-        out_specs=whole(),
-        compiler_params=vmem(6),
-    )(query, pair, cross, after, small)
     keep, send = pl.pallas_call(
         functools.partial(projection_kernel, steps, tuple(pieces)),
         out_shape=[struct((2 * count, lanes), F32)] * 2,
@@ -396,18 +414,6 @@
         compiler_params=vmem(6),
     )(keep, swap(send), near, cross, ids, small)
 
-    units = gate_up_weight.shape[3]
-    *loaded, done = pl.pallas_call(
-        functools.partial(load_kernel, local),
-        out_shape=[struct((2, 2, units, width), BF16)] * local
-        + [struct((2, *down_weight.shape[1:]), BF16)] * local
-        + [struct((8, 128), F32)],
-        in_specs=[pl.BlockSpec(memory_space=pl.ANY)] * 3,
-        out_specs=[whole()] * (2 * local + 1),
-        scratch_shapes=[pltpu.SemaphoreType.DMA((2 * local,))],
-        compiler_params=vmem(14),
-    )(gate_up_weight.swapaxes(2, 3), down_weight, shard)
-
     slots = local * SLOTS
     state = None
     picked, backs = [], []
@@ -416,44 +422,31 @@
         low = flip & -flip
         column[flip] = hop(column[flip - low], 2 * low)
     across = hop(shard, 1)
-    column[1] = tie(column[1], across, done)
+    column[1] = tie(column[1], across)
     for flip in range(steps):
+        if flip == steps - 1:
+            column[flip] = tie(column[flip], picked[0])
         block = column[flip]
         crossed = hop(block, 1) if flip else across
+        if flip == steps - 1:
+            crossed = tie(crossed, *picked[1:])
         own = flip == 0
-        later = steps - 1 if flip == steps - 3 else None
-        out_shape = [
-            struct((local, 2 * SLOTS, width), BF16),
-            struct((2, count, slots), BF16),
-        ]
-        out_specs = [whole()] * 2
-        if own:
-            out_shape.append(struct((count, 2 * lanes), BF16))
-            out_specs.append(whole())
-        inputs = [block, crossed, swap(block), swap(crossed), small, router]
-        in_specs = [whole()] * 6
-        aliases = {}
-        if later is not None:
-            inputs.append(column[later])
-            in_specs.append(pl.BlockSpec(memory_space=pl.ANY))
-            aliases = {6: len(out_shape)}
-            out_shape.append(struct(shard.shape, BF16))
-            out_specs.append(pl.BlockSpec(memory_space=pl.ANY))
         results = pl.pallas_call(
-            functools.partial(select_kernel, local, topk, own, later is not None),
-            out_shape=out_shape,
-            in_specs=in_specs,
-            out_specs=out_specs,
+            functools.partial(select_kernel, local, topk, own),
+            out_shape=[
+                struct((local, 2 * SLOTS, width), BF16),
+                struct((2, count, slots), BF16),
+            ]
+            + ([struct((count, 2 * lanes), BF16)] if own else []),
+            in_specs=[whole()] * 6,
+            out_specs=[whole()] * (3 if own else 2),
             scratch_shapes=[pltpu.VMEM((count, width), BF16), pltpu.VMEM((experts, count), F32)],
-            input_output_aliases=aliases,
             compiler_params=vmem(6),
-        )(*inputs)
+        )(block, crossed, swap(block), swap(crossed), small, router)
         picked.append(results[0])
         backs.append(results[1])
         if own:
             state = results[2]
-        if later is not None:
-            column[later] = results[-1]
 
     sources = 2 * steps
     room = sources * SLOTS

time: 142 us -> 147 us (1.035)
  starting transfers between devices: 25.4 us -> 39.1 us
  waiting for transfers between devices: 76.4 us -> 71.6 us
  local copies, waits for them, and re-layouts: 2.39 us -> 0.01 us
  Pallas kernels: 36.9 us -> 35.4 us
    ppermute x19, starting transfers between devices: 19.5 us -> 34.6 us  [hop(): return lax.ppermute(x, 'dev', [(i, i ^ flip) for i in range(devices)])]
    ppermute x19, waiting for transfers between devices: 72.3 us -> 62.5 us  [hop(): return lax.ppermute(x, 'dev', [(i, i ^ flip) for i in range(devices)])]
    ppermute x2, waiting for transfers between devices: 0.01 us -> 3.46 us  [gathered_body(): theirs = lax.ppermute(mine[flip], 'groups', [(0, 1), (1, 0)])]
    unnamed x6, local copies, waits for them, and re-layouts: 2.39 us -> 0.01 us
    ppermute x10, waiting for transfers between devices: 4.09 us -> 5.61 us  [swap(): return lax.ppermute(x, 'sub', [(0, 1), (1, 0)])]
    pallas_call x1, Pallas kernels: 8.45 us -> 6.96 us  [gathered_body(): pl.pallas_call(functools.partial(hidden_kernel, steps), out_shape=struct(...]
  transfers between devices with their start and end apart: 32 -> 32, of which waited for: 18 -> 17; matrix products, arithmetic and copies ran while one was open for 0% -> 0% of each run, Pallas kernels for 13% -> 13%
where the time goes in v5:
time: 147 us; the launch traced here: 146 us
  waiting for transfers between devices  71.6 us (49%)
  starting transfers between devices  39.1 us (27%)
  Pallas kernels  35.4 us (24%)
    ppermute x19, waiting for transfers between devices, hop(): return lax.ppermute(x, 'dev', [(i, i ^ flip) for i in range(devices)])  62.5 us
    ppermute x19, starting transfers between devices, hop(): return lax.ppermute(x, 'dev', [(i, i ^ flip) for i in range(devices)])  34.6 us
    pallas_call x1, Pallas kernels, gathered_body(): pl.pallas_call(functools.partial(load_kernel, local), out_shape=[struct((...  11.9 us
    pallas_call x1, Pallas kernels, gathered_body(): pl.pallas_call(functools.partial(hidden_kernel, steps), out_shape=struct(...  6.96 us
    ppermute x10, waiting for transfers between devices, swap(): return lax.ppermute(x, 'sub', [(0, 1), (1, 0)])  5.61 us
    pallas_call x4, Pallas kernels, gathered_body(): pl.pallas_call(functools.partial(select_kernel, local, topk, own), out_sh...  5.3 us
    ppermute x2, waiting for transfers between devices, gathered_body(): theirs = lax.ppermute(mine[flip], 'groups', [(0, 1), (1, 0)])  3.46 us
    pallas_call x1, Pallas kernels, gathered_body(): pl.pallas_call(attention_kernel, out_shape=struct((count, local_width), B...  3.11 us
  transfers between devices with their start and end apart: 32, of which 17 were waited for; matrix products, arithmetic and copies ran while one was open for 0% of the time, Pallas kernels for 13%

profile of v5, /device:TPU:0, one launch (start us, length us, event | category | flops | bytes accessed | tf_op | source)
XLA Modules:
  0.0 146.5 jit_solution(9562814120754176455)
XLA Ops:
  0.0 2.6 %shard_map.82 = (bf16[128,1024]{1,0:T(8,128)(2,1)S(1)}, bf16[256,1024]{1,0:T(8,128)(2,1)S(1)}, bf16[128,512]{1,0:T(8,128)(2,1)S(1)}, bf16[320,1024]{1,0:T(8,128)...) custom-call(bf16[128,2048]{1,0:T(8,128)(2,1)} %tokens_ref.1, bf16[3,128,1024]{2,1,0:T(8,128)(2,1)} %bitcast.7, ...), custom_call_target="tpu_custom_call" | custom-call | tf_op jit(solution)/shard_map/pallas_call | solution.py:333
  2.7 3.0 %collective-permute-start = (bf16[320,1024]{1,0:T(8,128)(2,1)}, bf16[320,1024]{1,0:T(8,128)(2,1)S(1)}, u32[]{:S(2)}, u32[]{:S(2)}) collective-permute-start(bf16[320,1024]{1,0:T(8,128)(2,1)} %get-tuple-element.52), channel_id=1, source_target_pairs={{0,2},{2,0},{4,6},{6,4},{8,10},{10,8},{12,14},{14,12},{1,3},{3,1},... | collective-permute-start | bytes 1966088 | tf_op jit(solution)/shard_map/ppermute | solution.py:326
  5.7 0.7 collective-permute-start.1
  6.3 2.9 %collective-permute-start.2 = (bf16[256,1024]{1,0:T(8,128)(2,1)S(1)}, bf16[256,1024]{1,0:T(8,128)(2,1)S(1)}, u32[]{:S(2)}, u32[]{:S(2)}) collective-permute-start(bf16[256,1024]{1,0:T(8,128)(2,1)S(1)} %get-tuple-element.54.refs_2_), channel_id=1, source_target_pairs={{0,4},{2,6},{4,0},{6,2},{8,12},{10,14},{12,8},{14,10},{1,5},{3,7},... | collective-permute-start | bytes 1572872 | tf_op jit(solution)/shard_map/ppermute | solution.py:326
  9.2 3.0 %collective-permute-start.4 = (bf16[128,1024]{1,0:T(8,128)(2,1)S(1)}, bf16[128,1024]{1,0:T(8,128)(2,1)S(1)}, u32[]{:S(2)}, u32[]{:S(2)}) collective-permute-start(bf16[128,1024]{1,0:T(8,128)(2,1)S(1)} %get-tuple-element.55), channel_id=1, source_target_pairs={{0,8},{2,10},{4,12},{6,14},{8,0},{10,2},{12,4},{14,6},{1,9},{3,11}... | collective-permute-start | bytes 786440 | tf_op jit(solution)/shard_map/ppermute | solution.py:326
  12.2 11.9 %shard_map.85 = (bf16[2,2,192,2048]{3,2,1,0:T(8,128)(2,1)S(1)}, bf16[2,2,192,2048]{3,2,1,0:T(8,128)(2,1)S(1)}, bf16[2,2,192,2048]{3,2,1,0:T(8,128)(2,1)S(1)}, bf...) custom-call(bf16[16,2,192,2048]{3,2,1,0:T(8,128)(2,1)} %bitcast.6, ...), custom_call_target="tpu_custom_call" | custom-call | tf_op jit(solution)/shard_map/pallas_call | solution.py:364
  24.2 3.4 %collective-permute-done.4.refs_0_ = bf16[128,1024]{1,0:T(8,128)(2,1)S(1)} collective-permute-done((bf16[128,1024]{1,0:T(8,128)(2,1)S(1)}, bf16[128,1024]{1,0:T(8,128)(2,1)S(1)}, u32[]{:S(2)}, u32[]{:S(2)}) %collective-permute-start.4) | collective-permute-done | bytes 262176 | tf_op jit(solution)/shard_map/ppermute | solution.py:326
  27.6 13.6 %collective-permute-start.6 = (bf16[128,1024]{1,0:T(8,128)(2,1)S(1)}, bf16[128,1024]{1,0:T(8,128)(2,1)S(1)}, u32[]{:S(2)}, u32[]{:S(2)}) collective-permute-start(bf16[128,1024]{1,0:T(8,128)(2,1)S(1)} %shard_map.86.refs_4_), channel_id=1, source_target_pairs={{0,4},{2,6},{4,0},{6,2},{8,12},{10,14},{12,8},{14,10},{1,5},{3,7},... | collective-permute-start | bytes 786440 | tf_op jit(solution)/shard_map/ppermute | solution.py:326
  41.3 1.5 %collective-permute-start.5 = (bf16[128,1024]{1,0:T(8,128)(2,1)S(1)}, bf16[128,1024]{1,0:T(8,128)(2,1)S(1)}, u32[]{:S(2)}, u32[]{:S(2)}) collective-permute-start(bf16[128,1024]{1,0:T(8,128)(2,1)S(1)} %shard_map.86.refs_4_), channel_id=1, source_target_pairs={{0,16},{16,0},{1,17},{17,1},{2,18},{18,2},{3,19},{19,3},{4,20},{20... | collective-permute-start | bytes 786440 | tf_op jit(solution)/shard_map/ppermute | solution.py:395
  42.8 0.0 collective-permute-done.1.next_ref
  42.8 0.0 collective-permute-done.2.refs_1_.refs_3_
  42.8 0.0 collective-permute-done.cross_ref
  42.8 3.1 %shard_map.84.refs_1_.refs_0_ = bf16[128,1024]{1,0:T(8,128)(2,1)S(1)} custom-call(bf16[128,1024]{1,0:T(8,128)(2,1)S(1)} %get-tuple-element.50._.query_ref, bf16[256,1024]{1,0:T(8,128)(2,1)S(1)} %get-tuple-element.51.own_ref, bf16[320,1024]{1,0:T(8,128)(2,1)S(1)} %collective-permute-done.cross_ref, bf16[256,1024]{1,0:T(8,128)(2,1)S(1)} %collective-permute-done.1.next_ref, ...), custom_call_target="tpu_custom_call" | custom-call | tf_op jit(solution)/shard_map/pallas_call | solution.py:384
  45.9 0.1 collective-permute-start.3
  46.0 1.0 collective-permute-start.7
  47.0 2.5 %collective-permute-done.5.refs_5_ = bf16[128,1024]{1,0:T(8,128)(2,1)S(1)} collective-permute-done((bf16[128,1024]{1,0:T(8,128)(2,1)S(1)}, bf16[128,1024]{1,0:T(8,128)(2,1)S(1)}, u32[]{:S(2)}, u32[]{:S(2)}) %collective-permute-start.5) | collective-permute-done | bytes 262176 | tf_op jit(solution)/shard_map/ppermute | solution.py:395
  49.5 2.9 %collective-permute-done.3.refs_1_ = bf16[128,1024]{1,0:T(8,128)(2,1)S(1)} collective-permute-done((bf16[128,1024]{1,0:T(8,128)(2,1)S(1)}, bf16[128,1024]{1,0:T(8,128)(2,1)S(1)}, u32[]{:S(2)}, u32[]{:S(2)}) %collective-permute-start.3) | collective-permute-done | bytes 262176 | tf_op jit(solution)/shard_map/ppermute | solution.py:326
  52.3 1.0 collective-permute-done.7.refs_7_
  53.3 1.4 shard_map.88
  54.8 0.1 collective-permute-start.8
  54.9 1.9 %collective-permute-done.8.got_ref = f32[256,512]{1,0:T(8,128)S(1)} collective-permute-done((f32[256,512]{1,0:T(8,128)S(1)}, f32[256,512]{1,0:T(8,128)S(1)}, u32[]{:S(2)}, u32[]{:S(2)}) %collective-permute-start.8) | collective-permute-done | bytes 524320 | tf_op jit(solution)/shard_map/ppermute | solution.py:329
  56.8 0.1 shard_map.89.refs_0_
  56.9 0.5 collective-permute-start.16
  57.3 2.0 %collective-permute-start.12 = (bf16[272,512]{1,0:T(8,128)(2,1)S(1)}, bf16[272,512]{1,0:T(8,128)(2,1)S(1)}, u32[]{:S(2)}, u32[]{:S(2)}) collective-permute-start(bf16[272,512]{1,0:T(8,128)(2,1)S(1)} %shard_map.89.refs_0_), channel_id=1, source_target_pairs={{0,4},{2,6},{4,0},{6,2},{8,12},{10,14},{12,8},{14,10},{1,5},{3,7},... | collective-permute-start | bytes 835592 | tf_op jit(solution)/shard_map/ppermute | solution.py:326
  59.4 1.0 collective-permute-start.9
  60.3 12.2 %collective-permute-done.16.refs_0_ = bf16[272,512]{1,0:T(8,128)(2,1)S(1)} collective-permute-done((bf16[272,512]{1,0:T(8,128)(2,1)S(1)}, bf16[272,512]{1,0:T(8,128)(2,1)S(1)}, u32[]{:S(2)}, u32[]{:S(2)}) %collective-permute-start.16) | collective-permute-done | bytes 278560 | tf_op jit(solution)/shard_map/ppermute | solution.py:326
  72.5 0.6 collective-permute-start.17
  73.1 0.0 collective-permute-done.12.refs_0_
  73.1 0.0 collective-permute-done.9.refs_1_
  73.1 1.4 collective-permute-start.13
  74.5 0.0 collective-permute-start.11
  74.5 0.5 collective-permute-start.14
  75.1 7.0 %collective-permute-done.17.refs_1_ = bf16[272,512]{1,0:T(8,128)(2,1)S(1)} collective-permute-done((bf16[272,512]{1,0:T(8,128)(2,1)S(1)}, bf16[272,512]{1,0:T(8,128)(2,1)S(1)}, u32[]{:S(2)}, u32[]{:S(2)}) %collective-permute-start.17) | collective-permute-done | bytes 278560 | tf_op jit(solution)/shard_map/ppermute | solution.py:326
  82.0 0.0 collective-permute-start.18
  82.0 4.9 %collective-permute-done.13.refs_1_ = bf16[272,512]{1,0:T(8,128)(2,1)S(1)} collective-permute-done((bf16[272,512]{1,0:T(8,128)(2,1)S(1)}, bf16[272,512]{1,0:T(8,128)(2,1)S(1)}, u32[]{:S(2)}, u32[]{:S(2)}) %collective-permute-start.13) | collective-permute-done | bytes 278560 | tf_op jit(solution)/shard_map/ppermute | solution.py:326
  87.0 0.5 collective-permute-start.15
  87.5 1.3 shard_map.90
  88.8 0.7 collective-permute-start.21
  89.6 1.3 shard_map.93
  90.9 1.3 shard_map.92
  92.2 5.2 %collective-permute-done.21.refs_0_ = bf16[272,512]{1,0:T(8,128)(2,1)S(1)} collective-permute-done((bf16[272,512]{1,0:T(8,128)(2,1)S(1)}, bf16[272,512]{1,0:T(8,128)(2,1)S(1)}, u32[]{:S(2)}, u32[]{:S(2)}) %collective-permute-start.21) | collective-permute-done | bytes 278560 | tf_op jit(solution)/shard_map/ppermute | solution.py:326
  97.5 1.6 %collective-permute-done.23.refs_3_ = bf16[272,512]{1,0:T(8,128)(2,1)S(1)} collective-permute-done((bf16[272,512]{1,0:T(8,128)(2,1)S(1)}, bf16[272,512]{1,0:T(8,128)(2,1)S(1)}, u32[]{:S(2)}, u32[]{:S(2)}) %collective-permute-start.23) | collective-permute-done | bytes 278560 | tf_op jit(solution)/shard_map/ppermute | solution.py:329
  99.0 1.3 shard_map.96
  100.3 7.0 %shard_map.97.near_ref = bf16[8,128,384]{2,1,0:T(8,128)(2,1)S(1)} custom-call(bf16[8,32,2048]{2,1,0:T(8,128)(2,1)S(1)} %get-tuple-element.63.refs_1_.refs_0_, bf16[8,32,2048]{2,1,0:T(8,128)(2,1)S(1)} %get-tuple-element.64.refs_1_, bf16[8,32,2048]{2,1,0:T(8,128)(2,1)S(1)} %get-tuple-element.65.refs_2_, bf16[8,32,2048]{2,1,0:T(8,128)(2,1)S(1)} %get-tuple-element.66.refs_3_, ...), custom_call_target="tpu_custom_call" | custom-call | tf_op jit(solution)/shard_map/pallas_call | solution.py:453
  107.3 0.2 collective-permute-start.24
  107.5 2.1 %collective-permute-done.24.far_ref = bf16[8,128,384]{2,1,0:T(8,128)(2,1)S(1)} collective-permute-done((bf16[8,128,384]{2,1,0:T(8,128)(2,1)S(1)}, bf16[8,128,384]{2,1,0:T(8,128)(2,1)S(1)}, u32[]{:S(2)}, u32[]{:S(2)}) %collective-permute-start.24) | collective-permute-done | bytes 786464 | tf_op jit(solution)/shard_map/ppermute | solution.py:329
  109.7 3.0 %shard_map.98 = (bf16[128,1024]{1,0:T(8,128)(2,1)S(1)}, bf16[128,1024]{1,0:T(8,128)(2,1)S(1)}, bf16[128,1024]{1,0:T(8,128)(2,1)S(1)}, bf16[128,1024]{1,0:T(8,128...) custom-call(bf16[8,128,384]{2,1,0:T(8,128)(2,1)S(1)} %shard_map.97.n, ...), custom_call_target="tpu_custom_call" | custom-call | tf_op jit(solution)/shard_map/pallas_call | solution.py:460
  112.6 0.7 collective-permute-start.25
  113.4 1.4 collective-permute-start.27
  114.7 0.7 collective-permute-start.29
  115.4 1.4 collective-permute-start.31
  116.8 5.1 %collective-permute-done.25 = bf16[128,1024]{1,0:T(8,128)(2,1)S(1)} collective-permute-done((bf16[128,1024]{1,0:T(8,128)(2,1)S(1)}, bf16[128,1024]{1,0:T(8,128)(2,1)S(1)}, u32[]{:S(2)}, u32[]{:S(2)}) %collective-permute-start.25) | collective-permute-done | bytes 262176 | tf_op jit(solution)/shard_map/ppermute | solution.py:326
  121.8 0.1 add_convert_fusion.2
  121.9 1.5 %collective-permute-start.26 = (bf16[128,1024]{1,0:T(8,128)(2,1)S(1)}, bf16[128,1024]{1,0:T(8,128)(2,1)S(1)}, u32[]{:S(2)}, u32[]{:S(2)}) collective-permute-start(bf16[128,1024]{1,0:T(8,128)(2,1)S(1)} %add_convert_fusion.2), channel_id=1, source_target_pairs={{0,12},{2,14},{4,8},{6,10},{8,4},{10,6},{12,0},{14,2},{1,13},{3,15... | collective-permute-start | bytes 786440 | tf_op jit(solution)/shard_map/ppermute | solution.py:326
  123.5 4.0 %collective-permute-done.27 = bf16[128,1024]{1,0:T(8,128)(2,1)S(1)} collective-permute-done((bf16[128,1024]{1,0:T(8,128)(2,1)S(1)}, bf16[128,1024]{1,0:T(8,128)(2,1)S(1)}, u32[]{:S(2)}, u32[]{:S(2)}) %collective-permute-start.27) | collective-permute-done | bytes 262176 | tf_op jit(solution)/shard_map/ppermute | solution.py:326
  127.5 0.1 add_convert_fusion.1
  127.5 0.1 collective-permute-start.28
  127.6 5.5 %collective-permute-done.29 = bf16[128,1024]{1,0:T(8,128)(2,1)S(1)} collective-permute-done((bf16[128,1024]{1,0:T(8,128)(2,1)S(1)}, bf16[128,1024]{1,0:T(8,128)(2,1)S(1)}, u32[]{:S(2)}, u32[]{:S(2)}) %collective-permute-start.29) | collective-permute-done | bytes 262176 | tf_op jit(solution)/shard_map/ppermute | solution.py:326
  133.1 0.1 add_convert_fusion
  133.2 0.1 collective-permute-start.30
  133.2 4.7 %collective-permute-done.31.refs_4_ = bf16[128,1024]{1,0:T(8,128)(2,1)S(1)} collective-permute-done((bf16[128,1024]{1,0:T(8,128)(2,1)S(1)}, bf16[128,1024]{1,0:T(8,128)(2,1)S(1)}, u32[]{:S(2)}, u32[]{:S(2)}) %collective-permute-start.31) | collective-permute-done | bytes 262176 | tf_op jit(solution)/shard_map/ppermute | solution.py:326
  137.9 5.8 %collective-permute-done.28.refs_2_ = bf16[128,1024]{1,0:T(8,128)(2,1)S(1)} collective-permute-done((bf16[128,1024]{1,0:T(8,128)(2,1)S(1)}, bf16[128,1024]{1,0:T(8,128)(2,1)S(1)}, u32[]{:S(2)}, u32[]{:S(2)}) %collective-permute-start.28) | collective-permute-done | bytes 262176 | tf_op jit(solution)/shard_map/ppermute | solution.py:326
  143.8 1.8 %collective-permute-done.30.refs_3_ = bf16[128,1024]{1,0:T(8,128)(2,1)S(1)} collective-permute-done((bf16[128,1024]{1,0:T(8,128)(2,1)S(1)}, bf16[128,1024]{1,0:T(8,128)(2,1)S(1)}, u32[]{:S(2)}, u32[]{:S(2)}) %collective-permute-start.30) | collective-permute-done | bytes 262176 | tf_op jit(solution)/shard_map/ppermute | solution.py:326
  145.6 0.9 shard_map.99
  (27 shorter events, 0.1 us)
Async XLA Ops:
  2.7 40.1 %collective-permute-start = (bf16[320,1024]{1,0:T(8,128)(2,1)}, bf16[320,1024]{1,0:T(8,128)(2,1)S(1)}, u32[]{:S(2)}, u32[]{:S(2)}) collective-permute-start(bf16[320,1024]{1,0:T(8,128)(2,1)} %get-tuple-element.52), channel_id=1, source_target_pairs={{0,2},{2,0},{4,6},{6,4},{8,10},{10,8},{12,14},{14,12},{1,3},{3,1},... | collective-permute-start | bytes 1966088 | tf_op jit(solution)/shard_map/ppermute | solution.py:326
  5.7 37.1 %collective-permute-start.1 = (bf16[256,1024]{1,0:T(8,128)(2,1)S(1)}, bf16[256,1024]{1,0:T(8,128)(2,1)S(1)}, u32[]{:S(2)}, u32[]{:S(2)}) collective-permute-start(bf16[256,1024]{1,0:T(8,128)(2,1)S(1)} %get-tuple-element.51.own_ref), channel_id=1, source_target_pairs={{2,4},{6,8},{10,12},{4,2},{8,6},{12,10},{3,5},{7,9},{11,13},{5,3},... | collective-permute-start | bytes 1572872 | tf_op jit(solution)/shard_map/ppermute | solution.py:360
  6.3 36.4 %collective-permute-start.2 = (bf16[256,1024]{1,0:T(8,128)(2,1)S(1)}, bf16[256,1024]{1,0:T(8,128)(2,1)S(1)}, u32[]{:S(2)}, u32[]{:S(2)}) collective-permute-start(bf16[256,1024]{1,0:T(8,128)(2,1)S(1)} %get-tuple-element.54.refs_2_), channel_id=1, source_target_pairs={{0,4},{2,6},{4,0},{6,2},{8,12},{10,14},{12,8},{14,10},{1,5},{3,7},... | collective-permute-start | bytes 1572872 | tf_op jit(solution)/shard_map/ppermute | solution.py:326
  9.2 18.4 %collective-permute-start.4 = (bf16[128,1024]{1,0:T(8,128)(2,1)S(1)}, bf16[128,1024]{1,0:T(8,128)(2,1)S(1)}, u32[]{:S(2)}, u32[]{:S(2)}) collective-permute-start(bf16[128,1024]{1,0:T(8,128)(2,1)S(1)} %get-tuple-element.55), channel_id=1, source_target_pairs={{0,8},{2,10},{4,12},{6,14},{8,0},{10,2},{12,4},{14,6},{1,9},{3,11}... | collective-permute-start | bytes 786440 | tf_op jit(solution)/shard_map/ppermute | solution.py:326
  12.2 29.0 %copy-start = (bf16[2048,64]{0,1:T(8,128)(2,1)S(1)}, bf16[2048,64]{0,1:T(8,128)(2,1)}, u32[]{:S(2)}) copy-start(bf16[2048,64]{0,1:T(8,128)(2,1)} %param.12) | copy-start | bytes 786436
  12.2 29.0 %copy-start.1 = (f32[4,2048]{1,0:T(4,128)S(1)}, f32[4,2048]{1,0:T(4,128)}, u32[]{:S(2)}) copy-start(f32[4,2048]{1,0:T(4,128)} %mod_ref.1) | copy-start | bytes 98308
  12.2 29.0 %copy-start.2 = (s32[128,4]{0,1:T(4,128)S(1)}, s32[128,4]{0,1:T(4,128)}, u32[]{:S(2)}) copy-start(s32[128,4]{0,1:T(4,128)} %param.13) | copy-start | bytes 6148
  27.6 18.4 %collective-permute-start.6 = (bf16[128,1024]{1,0:T(8,128)(2,1)S(1)}, bf16[128,1024]{1,0:T(8,128)(2,1)S(1)}, u32[]{:S(2)}, u32[]{:S(2)}) collective-permute-start(bf16[128,1024]{1,0:T(8,128)(2,1)S(1)} %shard_map.86.refs_4_), channel_id=1, source_target_pairs={{0,4},{2,6},{4,0},{6,2},{8,12},{10,14},{12,8},{14,10},{1,5},{3,7},... | collective-permute-start | bytes 786440 | tf_op jit(solution)/shard_map/ppermute | solution.py:326
  41.3 8.2 %collective-permute-start.5 = (bf16[128,1024]{1,0:T(8,128)(2,1)S(1)}, bf16[128,1024]{1,0:T(8,128)(2,1)S(1)}, u32[]{:S(2)}, u32[]{:S(2)}) collective-permute-start(bf16[128,1024]{1,0:T(8,128)(2,1)S(1)} %shard_map.86.refs_4_), channel_id=1, source_target_pairs={{0,16},{16,0},{1,17},{17,1},{2,18},{18,2},{3,19},{19,3},{4,20},{20... | collective-permute-start | bytes 786440 | tf_op jit(solution)/shard_map/ppermute | solution.py:395
  45.9 6.4 %collective-permute-start.3 = (bf16[128,1024]{1,0:T(8,128)(2,1)S(1)}, bf16[128,1024]{1,0:T(8,128)(2,1)S(1)}, u32[]{:S(2)}, u32[]{:S(2)}) collective-permute-start(bf16[128,1024]{1,0:T(8,128)(2,1)S(1)} %shard_map.84.refs_1_.refs_0_), channel_id=1, source_target_pairs={{0,2},{2,0},{4,6},{6,4},{8,10},{10,8},{12,14},{14,12},{1,3},{3,1},... | collective-permute-start | bytes 786440 | tf_op jit(solution)/shard_map/ppermute | solution.py:326
  46.0 7.3 %collective-permute-start.7 = (bf16[128,1024]{1,0:T(8,128)(2,1)S(1)}, bf16[128,1024]{1,0:T(8,128)(2,1)S(1)}, u32[]{:S(2)}, u32[]{:S(2)}) collective-permute-start(bf16[128,1024]{1,0:T(8,128)(2,1)S(1)} %shard_map.87.refs_6_), channel_id=1, source_target_pairs={{0,16},{16,0},{1,17},{17,1},{2,18},{18,2},{3,19},{19,3},{4,20},{20... | collective-permute-start | bytes 786440 | tf_op jit(solution)/shard_map/ppermute | solution.py:395
  54.8 2.0 %collective-permute-start.8 = (f32[256,512]{1,0:T(8,128)S(1)}, f32[256,512]{1,0:T(8,128)S(1)}, u32[]{:S(2)}, u32[]{:S(2)}) collective-permute-start(f32[256,512]{1,0:T(8,128)S(1)} %get-tuple-element.58), channel_id=1, source_target_pairs={{0,1},{1,0},{2,3},{3,2},{4,5},{5,4},{6,7},{7,6},{8,9},{9,8},{10,11... | collective-permute-start | bytes 1572872 | tf_op jit(solution)/shard_map/ppermute | solution.py:329
  56.9 15.6 %collective-permute-start.16 = (bf16[272,512]{1,0:T(8,128)(2,1)S(1)}, bf16[272,512]{1,0:T(8,128)(2,1)S(1)}, u32[]{:S(2)}, u32[]{:S(2)}) collective-permute-start(bf16[272,512]{1,0:T(8,128)(2,1)S(1)} %shard_map.89.refs_0_), channel_id=1, source_target_pairs={{0,8},{2,10},{4,12},{6,14},{8,0},{10,2},{12,4},{14,6},{1,9},{3,11}... | collective-permute-start | bytes 835592 | tf_op jit(solution)/shard_map/ppermute | solution.py:326
  57.3 15.8 %collective-permute-start.12 = (bf16[272,512]{1,0:T(8,128)(2,1)S(1)}, bf16[272,512]{1,0:T(8,128)(2,1)S(1)}, u32[]{:S(2)}, u32[]{:S(2)}) collective-permute-start(bf16[272,512]{1,0:T(8,128)(2,1)S(1)} %shard_map.89.refs_0_), channel_id=1, source_target_pairs={{0,4},{2,6},{4,0},{6,2},{8,12},{10,14},{12,8},{14,10},{1,5},{3,7},... | collective-permute-start | bytes 835592 | tf_op jit(solution)/shard_map/ppermute | solution.py:326
  59.4 13.7 %collective-permute-start.9 = (bf16[272,512]{1,0:T(8,128)(2,1)S(1)}, bf16[272,512]{1,0:T(8,128)(2,1)S(1)}, u32[]{:S(2)}, u32[]{:S(2)}) collective-permute-start(bf16[272,512]{1,0:T(8,128)(2,1)S(1)} %shard_map.89.refs_0_), channel_id=1, source_target_pairs={{0,2},{2,0},{4,6},{6,4},{8,10},{10,8},{12,14},{14,12},{1,3},{3,1},... | collective-permute-start | bytes 835592 | tf_op jit(solution)/shard_map/ppermute | solution.py:326
  60.3 14.2 %collective-permute-start.10 = (bf16[272,512]{1,0:T(8,128)(2,1)S(1)}, bf16[272,512]{1,0:T(8,128)(2,1)S(1)}, u32[]{:S(2)}, u32[]{:S(2)}) collective-permute-start(bf16[272,512]{1,0:T(8,128)(2,1)S(1)} %shard_map.89.refs_0_), channel_id=1, source_target_pairs={{0,1},{1,0},{2,3},{3,2},{4,5},{5,4},{6,7},{7,6},{8,9},{9,8},{10,11... | collective-permute-start | bytes 835592 | tf_op jit(solution)/shard_map/ppermute | solution.py:329
  72.5 9.5 %collective-permute-start.17 = (bf16[272,512]{1,0:T(8,128)(2,1)S(1)}, bf16[272,512]{1,0:T(8,128)(2,1)S(1)}, u32[]{:S(2)}, u32[]{:S(2)}) collective-permute-start(bf16[272,512]{1,0:T(8,128)(2,1)S(1)} %collective-permute-done.16.refs_0_), channel_id=1, source_target_pairs={{0,2},{2,0},{4,6},{6,4},{8,10},{10,8},{12,14},{14,12},{1,3},{3,1},... | collective-permute-start | bytes 835592 | tf_op jit(solution)/shard_map/ppermute | solution.py:326
  73.1 13.8 %collective-permute-start.13 = (bf16[272,512]{1,0:T(8,128)(2,1)S(1)}, bf16[272,512]{1,0:T(8,128)(2,1)S(1)}, u32[]{:S(2)}, u32[]{:S(2)}) collective-permute-start(bf16[272,512]{1,0:T(8,128)(2,1)S(1)} %shard_map.91.refs_0_), channel_id=1, source_target_pairs={{0,2},{2,0},{4,6},{6,4},{8,10},{10,8},{12,14},{14,12},{1,3},{3,1},... | collective-permute-start | bytes 835592 | tf_op jit(solution)/shard_map/ppermute | solution.py:326
  74.5 12.4 %collective-permute-start.11 = (bf16[272,512]{1,0:T(8,128)(2,1)S(1)}, bf16[272,512]{1,0:T(8,128)(2,1)S(1)}, u32[]{:S(2)}, u32[]{:S(2)}) collective-permute-start(bf16[272,512]{1,0:T(8,128)(2,1)S(1)} %collective-permute-done.9.refs_1_), channel_id=1, source_target_pairs={{0,1},{1,0},{2,3},{3,2},{4,5},{5,4},{6,7},{7,6},{8,9},{9,8},{10,11... | collective-permute-start | bytes 835592 | tf_op jit(solution)/shard_map/ppermute | solution.py:329
  74.5 14.3 %collective-permute-start.20 = (bf16[272,512]{1,0:T(8,128)(2,1)S(1)}, bf16[272,512]{1,0:T(8,128)(2,1)S(1)}, u32[]{:S(2)}, u32[]{:S(2)}) collective-permute-start(bf16[272,512]{1,0:T(8,128)(2,1)S(1)} %collective-permute-done.16.refs_0_), channel_id=1, source_target_pairs={{0,4},{2,6},{4,0},{6,2},{8,12},{10,14},{12,8},{14,10},{1,5},{3,7},... | collective-permute-start | bytes 835592 | tf_op jit(solution)/shard_map/ppermute | solution.py:326
  74.5 16.3 %collective-permute-start.14 = (bf16[272,512]{1,0:T(8,128)(2,1)S(1)}, bf16[272,512]{1,0:T(8,128)(2,1)S(1)}, u32[]{:S(2)}, u32[]{:S(2)}) collective-permute-start(bf16[272,512]{1,0:T(8,128)(2,1)S(1)} %shard_map.91.refs_0_), channel_id=1, source_target_pairs={{0,1},{1,0},{2,3},{3,2},{4,5},{5,4},{6,7},{7,6},{8,9},{9,8},{10,11... | collective-permute-start | bytes 835592 | tf_op jit(solution)/shard_map/ppermute | solution.py:329
  82.0 7.5 %collective-permute-start.18 = (bf16[272,512]{1,0:T(8,128)(2,1)S(1)}, bf16[272,512]{1,0:T(8,128)(2,1)S(1)}, u32[]{:S(2)}, u32[]{:S(2)}) collective-permute-start(bf16[272,512]{1,0:T(8,128)(2,1)S(1)} %collective-permute-done.16.refs_0_), channel_id=1, source_target_pairs={{0,1},{1,0},{2,3},{3,2},{4,5},{5,4},{6,7},{7,6},{8,9},{9,8},{10,11... | collective-permute-start | bytes 835592 | tf_op jit(solution)/shard_map/ppermute | solution.py:329
  87.0 2.6 %collective-permute-start.19 = (bf16[272,512]{1,0:T(8,128)(2,1)S(1)}, bf16[272,512]{1,0:T(8,128)(2,1)S(1)}, u32[]{:S(2)}, u32[]{:S(2)}) collective-permute-start(bf16[272,512]{1,0:T(8,128)(2,1)S(1)} %collective-permute-done.17.refs_1_), channel_id=1, source_target_pairs={{0,1},{1,0},{2,3},{3,2},{4,5},{5,4},{6,7},{7,6},{8,9},{9,8},{10,11... | collective-permute-start | bytes 835592 | tf_op jit(solution)/shard_map/ppermute | solution.py:329
  87.0 3.9 %collective-permute-start.15 = (bf16[272,512]{1,0:T(8,128)(2,1)S(1)}, bf16[272,512]{1,0:T(8,128)(2,1)S(1)}, u32[]{:S(2)}, u32[]{:S(2)}) collective-permute-start(bf16[272,512]{1,0:T(8,128)(2,1)S(1)} %collective-permute-done.13.refs_1_), channel_id=1, source_target_pairs={{0,1},{1,0},{2,3},{3,2},{4,5},{5,4},{6,7},{7,6},{8,9},{9,8},{10,11... | collective-permute-start | bytes 835592 | tf_op jit(solution)/shard_map/ppermute | solution.py:329
  88.8 8.6 %collective-permute-start.21 = (bf16[272,512]{1,0:T(8,128)(2,1)S(1)}, bf16[272,512]{1,0:T(8,128)(2,1)S(1)}, u32[]{:S(2)}, u32[]{:S(2)}) collective-permute-start(bf16[272,512]{1,0:T(8,128)(2,1)S(1)} %shard_map.94.refs_0_), channel_id=1, source_target_pairs={{0,2},{2,0},{4,6},{6,4},{8,10},{10,8},{12,14},{14,12},{1,3},{3,1},... | collective-permute-start | bytes 835592 | tf_op jit(solution)/shard_map/ppermute | solution.py:326
  89.6 7.9 %collective-permute-start.22 = (bf16[272,512]{1,0:T(8,128)(2,1)S(1)}, bf16[272,512]{1,0:T(8,128)(2,1)S(1)}, u32[]{:S(2)}, u32[]{:S(2)}) collective-permute-start(bf16[272,512]{1,0:T(8,128)(2,1)S(1)} %shard_map.94.refs_0_), channel_id=1, source_target_pairs={{0,1},{1,0},{2,3},{3,2},{4,5},{5,4},{6,7},{7,6},{8,9},{9,8},{10,11... | collective-permute-start | bytes 835592 | tf_op jit(solution)/shard_map/ppermute | solution.py:329
  97.5 1.6 %collective-permute-start.23 = (bf16[272,512]{1,0:T(8,128)(2,1)S(1)}, bf16[272,512]{1,0:T(8,128)(2,1)S(1)}, u32[]{:S(2)}, u32[]{:S(2)}) collective-permute-start(bf16[272,512]{1,0:T(8,128)(2,1)S(1)} %shard_map.95.refs_1_), channel_id=1, source_target_pairs={{0,1},{1,0},{2,3},{3,2},{4,5},{5,4},{6,7},{7,6},{8,9},{9,8},{10,11... | collective-permute-start | bytes 835592 | tf_op jit(solution)/shard_map/ppermute | solution.py:329
  107.3 2.4 %collective-permute-start.24 = (bf16[8,128,384]{2,1,0:T(8,128)(2,1)S(1)}, bf16[8,128,384]{2,1,0:T(8,128)(2,1)S(1)}, u32[]{:S(2)}, u32[]{:S(2)}) collective-permute-start(bf16[8,128,384]{2,1,0:T(8,128)(2,1)S(1)} %shard_map.97.near_ref), channel_id=1, source_target_pairs={{0,1},{1,0},{2,3},{3,2},{4,5},{5,4},{6,7},{7,6},{8,9},{9,8},{10,11... | collective-permute-start | bytes 2359304 | tf_op jit(solution)/shard_map/ppermute | solution.py:329
  112.6 9.2 %collective-permute-start.25 = (bf16[128,1024]{1,0:T(8,128)(2,1)S(1)}, bf16[128,1024]{1,0:T(8,128)(2,1)S(1)}, u32[]{:S(2)}, u32[]{:S(2)}) collective-permute-start(bf16[128,1024]{1,0:T(8,128)(2,1)S(1)} %get-tuple-element.89), channel_id=1, source_target_pairs={{0,2},{2,0},{4,6},{6,4},{8,10},{10,8},{12,14},{14,12},{1,3},{3,1},... | collective-permute-start | bytes 786440 | tf_op jit(solution)/shard_map/ppermute | solution.py:326
  113.4 14.1 %collective-permute-start.27 = (bf16[128,1024]{1,0:T(8,128)(2,1)S(1)}, bf16[128,1024]{1,0:T(8,128)(2,1)S(1)}, u32[]{:S(2)}, u32[]{:S(2)}) collective-permute-start(bf16[128,1024]{1,0:T(8,128)(2,1)S(1)} %get-tuple-element.91), channel_id=1, source_target_pairs={{0,2},{2,0},{4,6},{6,4},{8,10},{10,8},{12,14},{14,12},{1,3},{3,1},... | collective-permute-start | bytes 786440 | tf_op jit(solution)/shard_map/ppermute | solution.py:326
  114.7 18.4 %collective-permute-start.29 = (bf16[128,1024]{1,0:T(8,128)(2,1)S(1)}, bf16[128,1024]{1,0:T(8,128)(2,1)S(1)}, u32[]{:S(2)}, u32[]{:S(2)}) collective-permute-start(bf16[128,1024]{1,0:T(8,128)(2,1)S(1)} %get-tuple-element.93), channel_id=1, source_target_pairs={{0,2},{2,0},{4,6},{6,4},{8,10},{10,8},{12,14},{14,12},{1,3},{3,1},... | collective-permute-start | bytes 786440 | tf_op jit(solution)/shard_map/ppermute | solution.py:326
  115.4 22.5 %collective-permute-start.31 = (bf16[128,1024]{1,0:T(8,128)(2,1)S(1)}, bf16[128,1024]{1,0:T(8,128)(2,1)S(1)}, u32[]{:S(2)}, u32[]{:S(2)}) collective-permute-start(bf16[128,1024]{1,0:T(8,128)(2,1)S(1)} %get-tuple-element.94), channel_id=1, source_target_pairs={{0,2},{2,0},{4,6},{6,4},{8,10},{10,8},{12,14},{14,12},{1,3},{3,1},... | collective-permute-start | bytes 786440 | tf_op jit(solution)/shard_map/ppermute | solution.py:326
  121.9 16.0 %collective-permute-start.26 = (bf16[128,1024]{1,0:T(8,128)(2,1)S(1)}, bf16[128,1024]{1,0:T(8,128)(2,1)S(1)}, u32[]{:S(2)}, u32[]{:S(2)}) collective-permute-start(bf16[128,1024]{1,0:T(8,128)(2,1)S(1)} %add_convert_fusion.2), channel_id=1, source_target_pairs={{0,12},{2,14},{4,8},{6,10},{8,4},{10,6},{12,0},{14,2},{1,13},{3,15... | collective-permute-start | bytes 786440 | tf_op jit(solution)/shard_map/ppermute | solution.py:326
  127.5 16.2 %collective-permute-start.28 = (bf16[128,1024]{1,0:T(8,128)(2,1)S(1)}, bf16[128,1024]{1,0:T(8,128)(2,1)S(1)}, u32[]{:S(2)}, u32[]{:S(2)}) collective-permute-start(bf16[128,1024]{1,0:T(8,128)(2,1)S(1)} %add_convert_fusion.1), channel_id=1, source_target_pairs={{0,8},{2,10},{4,12},{6,14},{8,0},{10,2},{12,4},{14,6},{1,9},{3,11}... | collective-permute-start | bytes 786440 | tf_op jit(solution)/shard_map/ppermute | solution.py:326
  133.2 12.4 %collective-permute-start.30 = (bf16[128,1024]{1,0:T(8,128)(2,1)S(1)}, bf16[128,1024]{1,0:T(8,128)(2,1)S(1)}, u32[]{:S(2)}, u32[]{:S(2)}) collective-permute-start(bf16[128,1024]{1,0:T(8,128)(2,1)S(1)} %add_convert_fusion), channel_id=1, source_target_pairs={{0,4},{2,6},{4,0},{6,2},{8,12},{10,14},{12,8},{14,10},{1,5},{3,7},... | collective-permute-start | bytes 786440 | tf_op jit(solution)/shard_map/ppermute | solution.py:326

commit v6 on v5

--- a/solution.py
+++ b/solution.py
@@ -372,7 +372,6 @@
         compiler_params=vmem(14),
     )(gate_up_weight.swapaxes(2, 3), down_weight, query)
 
-    pieces, weights = [(0, None), (1, None)], [own_weight, hop(own_weight, 2)]
     mine = {0: sent}
     for flip in range(2, steps):
         low = flip & -flip
@@ -380,14 +379,16 @@
             mine[flip] = hop(mine[flip - low], 2 * low)
         else:
             mine[flip] = tie(hop(sent, 2 * flip), done)
+    own_weight = tie(own_weight, mine[2])
+    pieces, weights = [(0, None), (1, None)], [own_weight, hop(own_weight, 2)]
 
     mixed = pl.pallas_call(
         attention_kernel,
         out_shape=struct((count, local_width), BF16),
-        in_specs=[whole()] * 4 + [pl.BlockSpec(memory_space=pl.ANY)] * 2,
+        in_specs=[whole()] * 4 + [pl.BlockSpec(memory_space=pl.ANY)],
         out_specs=whole(),
         compiler_params=vmem(6),
-    )(query, pair, cross, after, small, weights[1])
+    )(query, pair, cross, after, small)
     for flip in range(2, steps):
         if split:
             if flip == steps - 1:
@@ -417,17 +418,19 @@
     slots = local * SLOTS
     state = None
     picked, backs = [], []
-    column = {0: shard}
-    for flip in range(1, steps):
-        low = flip & -flip
-        column[flip] = hop(column[flip - low], 2 * low)
+    column = {0: shard, 1: hop(shard, 2)}
     across = hop(shard, 1)
     column[1] = tie(column[1], across)
+    crossing = {0: across, 1: hop(column[1], 1)}
+    column[2] = tie(hop(shard, 4), crossing[1])
+    for flip in range(3, steps):
+        low = flip & -flip
+        column[flip] = hop(column[flip - low] if flip > low else shard, 2 * low)
     for flip in range(steps):
         if flip == steps - 1:
             column[flip] = tie(column[flip], picked[0])
         block = column[flip]
-        crossed = hop(block, 1) if flip else across
+        crossed = crossing[flip] if flip in crossing else hop(block, 1)
         if flip == steps - 1:
             crossed = tie(crossed, *picked[1:])
         own = flip == 0
@@ -626,7 +629,7 @@
     local = gate_up_weight.shape[0] // 2
     fits = (
         lax.axis_size("sub") == 2
-        and devices >= 4
+        and devices >= 8
         and devices & (devices - 1) == 0
         and gate_up_weight.shape[0] % 2 == 0
         and width % (devices * 128) == 0

time: 147 us -> 135 us (0.918)
  starting transfers between devices: 39.1 us -> 27.9 us
    ppermute x19, starting transfers between devices: 34.6 us -> 22.8 us  [hop(): return lax.ppermute(x, 'dev', [(i, i ^ flip) for i in range(devices)])]
    ppermute x2, waiting for transfers between devices: 3.46 us -> 0.01 us  [gathered_body(): theirs = lax.ppermute(mine[flip], 'groups', [(0, 1), (1, 0)])]
    ppermute x19, waiting for transfers between devices: 62.5 us -> 65.3 us  [hop(): return lax.ppermute(x, 'dev', [(i, i ^ flip) for i in range(devices)])]
  transfers between devices with their start and end apart: 32 -> 32, of which waited for: 17 -> 18; matrix products, arithmetic and copies ran while one was open for 0% -> 0% of each run, Pallas kernels for 13% -> 14%
where the time goes in v6:
time: 135 us
  waiting for transfers between devices  70.9 us (53%)
  Pallas kernels  35.4 us (26%)
  starting transfers between devices  27.9 us (21%)
    ppermute x19, waiting for transfers between devices, hop(): return lax.ppermute(x, 'dev', [(i, i ^ flip) for i in range(devices)])  65.3 us
    ppermute x19, starting transfers between devices, hop(): return lax.ppermute(x, 'dev', [(i, i ^ flip) for i in range(devices)])  22.8 us
    pallas_call x1, Pallas kernels, gathered_body(): pl.pallas_call(functools.partial(load_kernel, local), out_shape=[struct((...  12 us
    pallas_call x1, Pallas kernels, gathered_body(): pl.pallas_call(functools.partial(hidden_kernel, steps), out_shape=struct(...  6.96 us
    ppermute x10, waiting for transfers between devices, swap(): return lax.ppermute(x, 'sub', [(0, 1), (1, 0)])  5.6 us
    pallas_call x4, Pallas kernels, gathered_body(): pl.pallas_call(functools.partial(select_kernel, local, topk, own), out_sh...  5.29 us
    pallas_call x1, Pallas kernels, gathered_body(): pl.pallas_call(attention_kernel, out_shape=struct((count, local_width), B...  3.11 us
    ppermute x2, starting transfers between devices, gathered_body(): theirs = lax.ppermute(mine[flip], 'groups', [(0, 1), (1, 0)])  3 us
  transfers between devices with their start and end apart: 32, of which 18 were waited for; matrix products, arithmetic and copies ran while one was open for 0% of the time, Pallas kernels for 14%

profile of v6, /device:TPU:0, one launch (start us, length us, event | category | flops | bytes accessed | tf_op | source)
XLA Modules:
  0.0 134.7 jit_solution(17429438637332605210)
XLA Ops:
  0.0 2.6 %shard_map.82 = (bf16[128,1024]{1,0:T(8,128)(2,1)S(1)}, bf16[256,1024]{1,0:T(8,128)(2,1)S(1)}, bf16[128,512]{1,0:T(8,128)(2,1)S(1)}, bf16[320,1024]{1,0:T(8,128)...) custom-call(bf16[128,2048]{1,0:T(8,128)(2,1)} %tokens_ref.1, bf16[3,128,1024]{2,1,0:T(8,128)(2,1)} %bitcast.7, ...), custom_call_target="tpu_custom_call" | custom-call | tf_op jit(solution)/shard_map/pallas_call | solution.py:333
  2.7 3.0 %collective-permute-start = (bf16[320,1024]{1,0:T(8,128)(2,1)}, bf16[320,1024]{1,0:T(8,128)(2,1)S(1)}, u32[]{:S(2)}, u32[]{:S(2)}) collective-permute-start(bf16[320,1024]{1,0:T(8,128)(2,1)} %get-tuple-element.52), channel_id=1, source_target_pairs={{0,2},{2,0},{4,6},{6,4},{8,10},{10,8},{12,14},{14,12},{1,3},{3,1},... | collective-permute-start | bytes 1966088 | tf_op jit(solution)/shard_map/ppermute | solution.py:326
  5.7 2.6 %collective-permute-start.3 = (bf16[128,1024]{1,0:T(8,128)(2,1)S(1)}, bf16[128,1024]{1,0:T(8,128)(2,1)S(1)}, u32[]{:S(2)}, u32[]{:S(2)}) collective-permute-start(bf16[128,1024]{1,0:T(8,128)(2,1)S(1)} %get-tuple-element.55), channel_id=1, source_target_pairs={{0,8},{2,10},{4,12},{6,14},{8,0},{10,2},{12,4},{14,6},{1,9},{3,11}... | collective-permute-start | bytes 786440 | tf_op jit(solution)/shard_map/ppermute | solution.py:326
  8.2 0.7 collective-permute-start.1
  8.9 0.0 copy-start
  8.9 0.0 copy-start.1
  9.0 0.0 copy-start.2
  9.0 12.0 %shard_map.85 = (bf16[2,2,192,2048]{3,2,1,0:T(8,128)(2,1)S(1)}, bf16[2,2,192,2048]{3,2,1,0:T(8,128)(2,1)S(1)}, bf16[2,2,192,2048]{3,2,1,0:T(8,128)(2,1)S(1)}, bf...) custom-call(bf16[16,2,192,2048]{3,2,1,0:T(8,128)(2,1)} %bitcast.6, ...), custom_call_target="tpu_custom_call" | custom-call | tf_op jit(solution)/shard_map/pallas_call | solution.py:364
  20.9 0.2 collective-permute-done.3.refs_0_
  21.1 3.1 %collective-permute-start.6 = (bf16[128,1024]{1,0:T(8,128)(2,1)S(1)}, bf16[128,1024]{1,0:T(8,128)(2,1)S(1)}, u32[]{:S(2)}, u32[]{:S(2)}) collective-permute-start(bf16[128,1024]{1,0:T(8,128)(2,1)S(1)} %shard_map.86.refs_1_.refs_4_), channel_id=1, source_target_pairs={{0,4},{2,6},{4,0},{6,2},{8,12},{10,14},{12,8},{14,10},{1,5},{3,7},... | collective-permute-start | bytes 786440 | tf_op jit(solution)/shard_map/ppermute | solution.py:326
  24.2 0.1 collective-permute-start.4
  24.4 1.5 %collective-permute-start.5 = (bf16[128,1024]{1,0:T(8,128)(2,1)S(1)}, bf16[128,1024]{1,0:T(8,128)(2,1)S(1)}, u32[]{:S(2)}, u32[]{:S(2)}) collective-permute-start(bf16[128,1024]{1,0:T(8,128)(2,1)S(1)} %shard_map.86.refs_1_.refs_4_), channel_id=1, source_target_pairs={{0,16},{16,0},{1,17},{17,1},{2,18},{18,2},{3,19},{19,3},{4,20},{20... | collective-permute-start | bytes 786440 | tf_op jit(solution)/shard_map/ppermute | solution.py:396
  25.9 5.3 %collective-permute-done.cross_ref = bf16[320,1024]{1,0:T(8,128)(2,1)S(1)} collective-permute-done((bf16[320,1024]{1,0:T(8,128)(2,1)}, bf16[320,1024]{1,0:T(8,128)(2,1)S(1)}, u32[]{:S(2)}, u32[]{:S(2)}) %collective-permute-start) | collective-permute-done | bytes 655392 | tf_op jit(solution)/shard_map/ppermute | solution.py:326
  31.1 3.1 %shard_map.84.refs_1_.refs_0_ = bf16[128,1024]{1,0:T(8,128)(2,1)S(1)} custom-call(bf16[128,1024]{1,0:T(8,128)(2,1)S(1)} %get-tuple-element.50._.query_ref, bf16[256,1024]{1,0:T(8,128)(2,1)S(1)} %get-tuple-element.51.own_ref, bf16[320,1024]{1,0:T(8,128)(2,1)S(1)} %collective-permute-done.cross_ref, bf16[256,1024]{1,0:T(8,128)(2,1)S(1)} %collective-permute-done.1.next_ref, ...), custom_call_target="tpu_custom_call" | custom-call | tf_op jit(solution)/shard_map/pallas_call | solution.py:385
  34.3 2.4 %collective-permute-start.2 = (bf16[128,1024]{1,0:T(8,128)(2,1)S(1)}, bf16[128,1024]{1,0:T(8,128)(2,1)S(1)}, u32[]{:S(2)}, u32[]{:S(2)}) collective-permute-start(bf16[128,1024]{1,0:T(8,128)(2,1)S(1)} %shard_map.84.refs_1_.refs_0_), channel_id=1, source_target_pairs={{0,2},{2,0},{4,6},{6,4},{8,10},{10,8},{12,14},{14,12},{1,3},{3,1},... | collective-permute-start | bytes 786440 | tf_op jit(solution)/shard_map/ppermute | solution.py:326
  36.7 0.0 collective-permute-done.6.refs_0_
  36.7 1.5 %collective-permute-start.7 = (bf16[128,1024]{1,0:T(8,128)(2,1)S(1)}, bf16[128,1024]{1,0:T(8,128)(2,1)S(1)}, u32[]{:S(2)}, u32[]{:S(2)}) collective-permute-start(bf16[128,1024]{1,0:T(8,128)(2,1)S(1)} %shard_map.88.refs_6_), channel_id=1, source_target_pairs={{0,16},{16,0},{1,17},{17,1},{2,18},{18,2},{3,19},{19,3},{4,20},{20... | collective-permute-start | bytes 786440 | tf_op jit(solution)/shard_map/ppermute | solution.py:396
  38.2 0.0 collective-permute-done.5.refs_5_
  38.2 6.4 %collective-permute-done.4.refs_3_ = bf16[256,1024]{1,0:T(8,128)(2,1)S(1)} collective-permute-done((bf16[256,1024]{1,0:T(8,128)(2,1)S(1)}, bf16[256,1024]{1,0:T(8,128)(2,1)S(1)}, u32[]{:S(2)}, u32[]{:S(2)}) %collective-permute-start.4) | collective-permute-done | bytes 524320 | tf_op jit(solution)/shard_map/ppermute | solution.py:326
  44.6 1.4 %shard_map.89 = (f32[256,512]{1,0:T(8,128)S(1)}, f32[256,512]{1,0:T(8,128)S(1)}) custom-call(bf16[128,1024]{1,0:T(8,128)(2,1)S(1)} %shard_map.84.refs_1_.refs_0_, bf16[128,1024]{1,0:T(8,128)(2,1)S(1)} %collective-permute-done.2.refs_1_, bf16[256,1024]{1,0:T(8,128)(2,1)S(1)} %shard_map.87.refs_2_, bf16[256,1024]{1,0:T(8,128)(2,1)S(1)} %collective-permute-done.4.refs_3_, ...), custom_call_target="tpu_custom_call" | custom-call | tf_op jit(solution)/shard_map/pallas_call | solution.py:402
  46.1 0.1 collective-permute-start.8
  46.1 1.9 %collective-permute-done.8.got_ref = f32[256,512]{1,0:T(8,128)S(1)} collective-permute-done((f32[256,512]{1,0:T(8,128)S(1)}, f32[256,512]{1,0:T(8,128)S(1)}, u32[]{:S(2)}, u32[]{:S(2)}) %collective-permute-start.8) | collective-permute-done | bytes 524320 | tf_op jit(solution)/shard_map/ppermute | solution.py:329
  48.0 0.1 shard_map.90.refs_0_
  48.1 0.6 collective-permute-start.12
  48.7 0.5 collective-permute-start.9
  49.3 3.4 %collective-permute-start.16 = (bf16[272,512]{1,0:T(8,128)(2,1)S(1)}, bf16[272,512]{1,0:T(8,128)(2,1)S(1)}, u32[]{:S(2)}, u32[]{:S(2)}) collective-permute-start(bf16[272,512]{1,0:T(8,128)(2,1)S(1)} %shard_map.90.refs_0_), channel_id=1, source_target_pairs={{0,8},{2,10},{4,12},{6,14},{8,0},{10,2},{12,4},{14,6},{1,9},{3,11}... | collective-permute-start | bytes 835592 | tf_op jit(solution)/shard_map/ppermute | solution.py:326
  52.6 9.2 %collective-permute-done.12.refs_0_ = bf16[272,512]{1,0:T(8,128)(2,1)S(1)} collective-permute-done((bf16[272,512]{1,0:T(8,128)(2,1)S(1)}, bf16[272,512]{1,0:T(8,128)(2,1)S(1)}, u32[]{:S(2)}, u32[]{:S(2)}) %collective-permute-start.12) | collective-permute-done | bytes 278560 | tf_op jit(solution)/shard_map/ppermute | solution.py:326
  61.8 0.1 collective-permute-start.10
  61.9 0.5 collective-permute-start.11
  62.4 2.7 %collective-permute-done.16.refs_0_ = bf16[272,512]{1,0:T(8,128)(2,1)S(1)} collective-permute-done((bf16[272,512]{1,0:T(8,128)(2,1)S(1)}, bf16[272,512]{1,0:T(8,128)(2,1)S(1)}, u32[]{:S(2)}, u32[]{:S(2)}) %collective-permute-start.16) | collective-permute-done | bytes 278560 | tf_op jit(solution)/shard_map/ppermute | solution.py:326
  65.0 4.6 %collective-permute-done.13.refs_1_ = bf16[272,512]{1,0:T(8,128)(2,1)S(1)} collective-permute-done((bf16[272,512]{1,0:T(8,128)(2,1)S(1)}, bf16[272,512]{1,0:T(8,128)(2,1)S(1)}, u32[]{:S(2)}, u32[]{:S(2)}) %collective-permute-start.13) | collective-permute-done | bytes 278560 | tf_op jit(solution)/shard_map/ppermute | solution.py:326
  69.7 0.3 collective-permute-start.17
  70.0 0.5 collective-permute-start.18
  70.5 0.1 collective-permute-start.15
  70.5 1.3 shard_map.91
  71.9 4.7 %collective-permute-done.17.refs_1_ = bf16[272,512]{1,0:T(8,128)(2,1)S(1)} collective-permute-done((bf16[272,512]{1,0:T(8,128)(2,1)S(1)}, bf16[272,512]{1,0:T(8,128)(2,1)S(1)}, u32[]{:S(2)}, u32[]{:S(2)}) %collective-permute-start.17) | collective-permute-done | bytes 278560 | tf_op jit(solution)/shard_map/ppermute | solution.py:326
  76.6 0.3 collective-permute-done.20.refs_0_
  76.9 1.4 %collective-permute-start.21 = (bf16[272,512]{1,0:T(8,128)(2,1)S(1)}, bf16[272,512]{1,0:T(8,128)(2,1)S(1)}, u32[]{:S(2)}, u32[]{:S(2)}) collective-permute-start(bf16[272,512]{1,0:T(8,128)(2,1)S(1)} %shard_map.96.refs_0_), channel_id=1, source_target_pairs={{0,2},{2,0},{4,6},{6,4},{8,10},{10,8},{12,14},{14,12},{1,3},{3,1},... | collective-permute-start | bytes 835592 | tf_op jit(solution)/shard_map/ppermute | solution.py:326
  78.4 1.3 shard_map.93
  79.7 1.3 shard_map.95
  81.1 4.6 %collective-permute-done.21.refs_0_ = bf16[272,512]{1,0:T(8,128)(2,1)S(1)} collective-permute-done((bf16[272,512]{1,0:T(8,128)(2,1)S(1)}, bf16[272,512]{1,0:T(8,128)(2,1)S(1)}, u32[]{:S(2)}, u32[]{:S(2)}) %collective-permute-start.21) | collective-permute-done | bytes 278560 | tf_op jit(solution)/shard_map/ppermute | solution.py:326
  85.7 1.6 %collective-permute-done.23.refs_3_ = bf16[272,512]{1,0:T(8,128)(2,1)S(1)} collective-permute-done((bf16[272,512]{1,0:T(8,128)(2,1)S(1)}, bf16[272,512]{1,0:T(8,128)(2,1)S(1)}, u32[]{:S(2)}, u32[]{:S(2)}) %collective-permute-start.23) | collective-permute-done | bytes 278560 | tf_op jit(solution)/shard_map/ppermute | solution.py:329
  87.3 1.3 shard_map.98
  88.6 7.0 %shard_map.99.near_ref = bf16[8,128,384]{2,1,0:T(8,128)(2,1)S(1)} custom-call(bf16[8,32,2048]{2,1,0:T(8,128)(2,1)S(1)} %get-tuple-element.63.refs_1_.refs_0_, bf16[8,32,2048]{2,1,0:T(8,128)(2,1)S(1)} %get-tuple-element.64.refs_1_, bf16[8,32,2048]{2,1,0:T(8,128)(2,1)S(1)} %get-tuple-element.65.refs_2_, bf16[8,32,2048]{2,1,0:T(8,128)(2,1)S(1)} %get-tuple-element.66.refs_3_, ...), custom_call_target="tpu_custom_call" | custom-call | tf_op jit(solution)/shard_map/pallas_call | solution.py:456
  95.5 0.2 collective-permute-start.24
  95.8 2.1 %collective-permute-done.24.far_ref = bf16[8,128,384]{2,1,0:T(8,128)(2,1)S(1)} collective-permute-done((bf16[8,128,384]{2,1,0:T(8,128)(2,1)S(1)}, bf16[8,128,384]{2,1,0:T(8,128)(2,1)S(1)}, u32[]{:S(2)}, u32[]{:S(2)}) %collective-permute-start.24) | collective-permute-done | bytes 786464 | tf_op jit(solution)/shard_map/ppermute | solution.py:329
  97.9 3.0 %shard_map.100 = (bf16[128,1024]{1,0:T(8,128)(2,1)S(1)}, bf16[128,1024]{1,0:T(8,128)(2,1)S(1)}, bf16[128,1024]{1,0:T(8,128)(2,1)S(1)}, bf16[128,1024]{1,0:T(8,12...) custom-call(bf16[8,128,384]{2,1,0:T(8,128)(2,1)S(1)} %shard_map.99.n, ...), custom_call_target="tpu_custom_call" | custom-call | tf_op jit(solution)/shard_map/pallas_call | solution.py:463
  100.9 0.6 collective-permute-start.25
  101.5 1.4 %collective-permute-start.27 = (bf16[128,1024]{1,0:T(8,128)(2,1)S(1)}, bf16[128,1024]{1,0:T(8,128)(2,1)S(1)}, u32[]{:S(2)}, u32[]{:S(2)}) collective-permute-start(bf16[128,1024]{1,0:T(8,128)(2,1)S(1)} %get-tuple-element.91), channel_id=1, source_target_pairs={{0,2},{2,0},{4,6},{6,4},{8,10},{10,8},{12,14},{14,12},{1,3},{3,1},... | collective-permute-start | bytes 786440 | tf_op jit(solution)/shard_map/ppermute | solution.py:326
  103.0 0.6 collective-permute-start.29
  103.5 1.4 %collective-permute-start.31 = (bf16[128,1024]{1,0:T(8,128)(2,1)S(1)}, bf16[128,1024]{1,0:T(8,128)(2,1)S(1)}, u32[]{:S(2)}, u32[]{:S(2)}) collective-permute-start(bf16[128,1024]{1,0:T(8,128)(2,1)S(1)} %get-tuple-element.94), channel_id=1, source_target_pairs={{0,2},{2,0},{4,6},{6,4},{8,10},{10,8},{12,14},{14,12},{1,3},{3,1},... | collective-permute-start | bytes 786440 | tf_op jit(solution)/shard_map/ppermute | solution.py:326
  105.0 5.1 %collective-permute-done.25 = bf16[128,1024]{1,0:T(8,128)(2,1)S(1)} collective-permute-done((bf16[128,1024]{1,0:T(8,128)(2,1)S(1)}, bf16[128,1024]{1,0:T(8,128)(2,1)S(1)}, u32[]{:S(2)}, u32[]{:S(2)}) %collective-permute-start.25) | collective-permute-done | bytes 262176 | tf_op jit(solution)/shard_map/ppermute | solution.py:326
  110.1 0.1 add_convert_fusion.2
  110.2 1.1 collective-permute-start.26
  111.3 4.4 %collective-permute-done.27 = bf16[128,1024]{1,0:T(8,128)(2,1)S(1)} collective-permute-done((bf16[128,1024]{1,0:T(8,128)(2,1)S(1)}, bf16[128,1024]{1,0:T(8,128)(2,1)S(1)}, u32[]{:S(2)}, u32[]{:S(2)}) %collective-permute-start.27) | collective-permute-done | bytes 262176 | tf_op jit(solution)/shard_map/ppermute | solution.py:326
  115.7 0.1 add_convert_fusion.1
  115.8 0.1 collective-permute-start.28
  115.9 5.5 %collective-permute-done.29 = bf16[128,1024]{1,0:T(8,128)(2,1)S(1)} collective-permute-done((bf16[128,1024]{1,0:T(8,128)(2,1)S(1)}, bf16[128,1024]{1,0:T(8,128)(2,1)S(1)}, u32[]{:S(2)}, u32[]{:S(2)}) %collective-permute-start.29) | collective-permute-done | bytes 262176 | tf_op jit(solution)/shard_map/ppermute | solution.py:326
  121.3 0.1 add_convert_fusion
  121.4 0.1 collective-permute-start.30
  121.5 4.7 %collective-permute-done.31.refs_4_ = bf16[128,1024]{1,0:T(8,128)(2,1)S(1)} collective-permute-done((bf16[128,1024]{1,0:T(8,128)(2,1)S(1)}, bf16[128,1024]{1,0:T(8,128)(2,1)S(1)}, u32[]{:S(2)}, u32[]{:S(2)}) %collective-permute-start.31) | collective-permute-done | bytes 262176 | tf_op jit(solution)/shard_map/ppermute | solution.py:326
  126.1 6.7 %collective-permute-done.28.refs_2_ = bf16[128,1024]{1,0:T(8,128)(2,1)S(1)} collective-permute-done((bf16[128,1024]{1,0:T(8,128)(2,1)S(1)}, bf16[128,1024]{1,0:T(8,128)(2,1)S(1)}, u32[]{:S(2)}, u32[]{:S(2)}) %collective-permute-start.28) | collective-permute-done | bytes 262176 | tf_op jit(solution)/shard_map/ppermute | solution.py:326
  132.9 0.9 collective-permute-done.30.refs_3_
  133.8 0.9 shard_map.101
  (29 shorter events, 0.1 us)
Async XLA Ops:
  2.7 28.5 %collective-permute-start = (bf16[320,1024]{1,0:T(8,128)(2,1)}, bf16[320,1024]{1,0:T(8,128)(2,1)S(1)}, u32[]{:S(2)}, u32[]{:S(2)}) collective-permute-start(bf16[320,1024]{1,0:T(8,128)(2,1)} %get-tuple-element.52), channel_id=1, source_target_pairs={{0,2},{2,0},{4,6},{6,4},{8,10},{10,8},{12,14},{14,12},{1,3},{3,1},... | collective-permute-start | bytes 1966088 | tf_op jit(solution)/shard_map/ppermute | solution.py:326
  5.7 15.4 %collective-permute-start.3 = (bf16[128,1024]{1,0:T(8,128)(2,1)S(1)}, bf16[128,1024]{1,0:T(8,128)(2,1)S(1)}, u32[]{:S(2)}, u32[]{:S(2)}) collective-permute-start(bf16[128,1024]{1,0:T(8,128)(2,1)S(1)} %get-tuple-element.55), channel_id=1, source_target_pairs={{0,8},{2,10},{4,12},{6,14},{8,0},{10,2},{12,4},{14,6},{1,9},{3,11}... | collective-permute-start | bytes 786440 | tf_op jit(solution)/shard_map/ppermute | solution.py:326
  8.2 17.6 %collective-permute-start.1 = (bf16[256,1024]{1,0:T(8,128)(2,1)S(1)}, bf16[256,1024]{1,0:T(8,128)(2,1)S(1)}, u32[]{:S(2)}, u32[]{:S(2)}) collective-permute-start(bf16[256,1024]{1,0:T(8,128)(2,1)S(1)} %get-tuple-element.51.own_ref), channel_id=1, source_target_pairs={{2,4},{6,8},{10,12},{4,2},{8,6},{12,10},{3,5},{7,9},{11,13},{5,3},... | collective-permute-start | bytes 1572872 | tf_op jit(solution)/shard_map/ppermute | solution.py:360
  8.9 15.4 %copy-start = (bf16[2048,64]{0,1:T(8,128)(2,1)S(1)}, bf16[2048,64]{0,1:T(8,128)(2,1)}, u32[]{:S(2)}) copy-start(bf16[2048,64]{0,1:T(8,128)(2,1)} %param.12) | copy-start | bytes 786436
  8.9 15.4 %copy-start.1 = (f32[4,2048]{1,0:T(4,128)S(1)}, f32[4,2048]{1,0:T(4,128)}, u32[]{:S(2)}) copy-start(f32[4,2048]{1,0:T(4,128)} %mod_ref.1) | copy-start | bytes 98308
  9.0 15.4 %copy-start.2 = (s32[128,4]{0,1:T(4,128)S(1)}, s32[128,4]{0,1:T(4,128)}, u32[]{:S(2)}) copy-start(s32[128,4]{0,1:T(4,128)} %param.13) | copy-start | bytes 6148
  21.1 15.6 %collective-permute-start.6 = (bf16[128,1024]{1,0:T(8,128)(2,1)S(1)}, bf16[128,1024]{1,0:T(8,128)(2,1)S(1)}, u32[]{:S(2)}, u32[]{:S(2)}) collective-permute-start(bf16[128,1024]{1,0:T(8,128)(2,1)S(1)} %shard_map.86.refs_1_.refs_4_), channel_id=1, source_target_pairs={{0,4},{2,6},{4,0},{6,2},{8,12},{10,14},{12,8},{14,10},{1,5},{3,7},... | collective-permute-start | bytes 786440 | tf_op jit(solution)/shard_map/ppermute | solution.py:326
  24.2 20.4 %collective-permute-start.4 = (bf16[256,1024]{1,0:T(8,128)(2,1)S(1)}, bf16[256,1024]{1,0:T(8,128)(2,1)S(1)}, u32[]{:S(2)}, u32[]{:S(2)}) collective-permute-start(bf16[256,1024]{1,0:T(8,128)(2,1)S(1)} %shard_map.87.refs_2_), channel_id=1, source_target_pairs={{0,4},{2,6},{4,0},{6,2},{8,12},{10,14},{12,8},{14,10},{1,5},{3,7},... | collective-permute-start | bytes 1572872 | tf_op jit(solution)/shard_map/ppermute | solution.py:326
  24.4 13.8 %collective-permute-start.5 = (bf16[128,1024]{1,0:T(8,128)(2,1)S(1)}, bf16[128,1024]{1,0:T(8,128)(2,1)S(1)}, u32[]{:S(2)}, u32[]{:S(2)}) collective-permute-start(bf16[128,1024]{1,0:T(8,128)(2,1)S(1)} %shard_map.86.refs_1_.refs_4_), channel_id=1, source_target_pairs={{0,16},{16,0},{1,17},{17,1},{2,18},{18,2},{3,19},{19,3},{4,20},{20... | collective-permute-start | bytes 786440 | tf_op jit(solution)/shard_map/ppermute | solution.py:396
  34.3 10.3 %collective-permute-start.2 = (bf16[128,1024]{1,0:T(8,128)(2,1)S(1)}, bf16[128,1024]{1,0:T(8,128)(2,1)S(1)}, u32[]{:S(2)}, u32[]{:S(2)}) collective-permute-start(bf16[128,1024]{1,0:T(8,128)(2,1)S(1)} %shard_map.84.refs_1_.refs_0_), channel_id=1, source_target_pairs={{0,2},{2,0},{4,6},{6,4},{8,10},{10,8},{12,14},{14,12},{1,3},{3,1},... | collective-permute-start | bytes 786440 | tf_op jit(solution)/shard_map/ppermute | solution.py:326
  36.7 7.9 %collective-permute-start.7 = (bf16[128,1024]{1,0:T(8,128)(2,1)S(1)}, bf16[128,1024]{1,0:T(8,128)(2,1)S(1)}, u32[]{:S(2)}, u32[]{:S(2)}) collective-permute-start(bf16[128,1024]{1,0:T(8,128)(2,1)S(1)} %shard_map.88.refs_6_), channel_id=1, source_target_pairs={{0,16},{16,0},{1,17},{17,1},{2,18},{18,2},{3,19},{19,3},{4,20},{20... | collective-permute-start | bytes 786440 | tf_op jit(solution)/shard_map/ppermute | solution.py:396
  46.1 2.0 %collective-permute-start.8 = (f32[256,512]{1,0:T(8,128)S(1)}, f32[256,512]{1,0:T(8,128)S(1)}, u32[]{:S(2)}, u32[]{:S(2)}) collective-permute-start(f32[256,512]{1,0:T(8,128)S(1)} %get-tuple-element.58), channel_id=1, source_target_pairs={{0,1},{1,0},{2,3},{3,2},{4,5},{5,4},{6,7},{7,6},{8,9},{9,8},{10,11... | collective-permute-start | bytes 1572872 | tf_op jit(solution)/shard_map/ppermute | solution.py:329
  48.1 13.6 %collective-permute-start.12 = (bf16[272,512]{1,0:T(8,128)(2,1)S(1)}, bf16[272,512]{1,0:T(8,128)(2,1)S(1)}, u32[]{:S(2)}, u32[]{:S(2)}) collective-permute-start(bf16[272,512]{1,0:T(8,128)(2,1)S(1)} %shard_map.90.refs_0_), channel_id=1, source_target_pairs={{0,4},{2,6},{4,0},{6,2},{8,12},{10,14},{12,8},{14,10},{1,5},{3,7},... | collective-permute-start | bytes 835592 | tf_op jit(solution)/shard_map/ppermute | solution.py:326
  48.7 13.1 %collective-permute-start.9 = (bf16[272,512]{1,0:T(8,128)(2,1)S(1)}, bf16[272,512]{1,0:T(8,128)(2,1)S(1)}, u32[]{:S(2)}, u32[]{:S(2)}) collective-permute-start(bf16[272,512]{1,0:T(8,128)(2,1)S(1)} %shard_map.90.refs_0_), channel_id=1, source_target_pairs={{0,2},{2,0},{4,6},{6,4},{8,10},{10,8},{12,14},{14,12},{1,3},{3,1},... | collective-permute-start | bytes 835592 | tf_op jit(solution)/shard_map/ppermute | solution.py:326
  49.3 15.8 %collective-permute-start.16 = (bf16[272,512]{1,0:T(8,128)(2,1)S(1)}, bf16[272,512]{1,0:T(8,128)(2,1)S(1)}, u32[]{:S(2)}, u32[]{:S(2)}) collective-permute-start(bf16[272,512]{1,0:T(8,128)(2,1)S(1)} %shard_map.90.refs_0_), channel_id=1, source_target_pairs={{0,8},{2,10},{4,12},{6,14},{8,0},{10,2},{12,4},{14,6},{1,9},{3,11}... | collective-permute-start | bytes 835592 | tf_op jit(solution)/shard_map/ppermute | solution.py:326
  61.8 7.9 %collective-permute-start.13 = (bf16[272,512]{1,0:T(8,128)(2,1)S(1)}, bf16[272,512]{1,0:T(8,128)(2,1)S(1)}, u32[]{:S(2)}, u32[]{:S(2)}) collective-permute-start(bf16[272,512]{1,0:T(8,128)(2,1)S(1)} %shard_map.92.refs_0_), channel_id=1, source_target_pairs={{0,2},{2,0},{4,6},{6,4},{8,10},{10,8},{12,14},{14,12},{1,3},{3,1},... | collective-permute-start | bytes 835592 | tf_op jit(solution)/shard_map/ppermute | solution.py:326
  61.8 8.2 %collective-permute-start.10 = (bf16[272,512]{1,0:T(8,128)(2,1)S(1)}, bf16[272,512]{1,0:T(8,128)(2,1)S(1)}, u32[]{:S(2)}, u32[]{:S(2)}) collective-permute-start(bf16[272,512]{1,0:T(8,128)(2,1)S(1)} %shard_map.90.refs_0_), channel_id=1, source_target_pairs={{0,1},{1,0},{2,3},{3,2},{4,5},{5,4},{6,7},{7,6},{8,9},{9,8},{10,11... | collective-permute-start | bytes 835592 | tf_op jit(solution)/shard_map/ppermute | solution.py:329
  61.9 8.6 %collective-permute-start.11 = (bf16[272,512]{1,0:T(8,128)(2,1)S(1)}, bf16[272,512]{1,0:T(8,128)(2,1)S(1)}, u32[]{:S(2)}, u32[]{:S(2)}) collective-permute-start(bf16[272,512]{1,0:T(8,128)(2,1)S(1)} %collective-permute-done.9.refs_1_), channel_id=1, source_target_pairs={{0,1},{1,0},{2,3},{3,2},{4,5},{5,4},{6,7},{7,6},{8,9},{9,8},{10,11... | collective-permute-start | bytes 835592 | tf_op jit(solution)/shard_map/ppermute | solution.py:329
  69.7 6.9 %collective-permute-start.17 = (bf16[272,512]{1,0:T(8,128)(2,1)S(1)}, bf16[272,512]{1,0:T(8,128)(2,1)S(1)}, u32[]{:S(2)}, u32[]{:S(2)}) collective-permute-start(bf16[272,512]{1,0:T(8,128)(2,1)S(1)} %shard_map.94.refs_0_), channel_id=1, source_target_pairs={{0,2},{2,0},{4,6},{6,4},{8,10},{10,8},{12,14},{14,12},{1,3},{3,1},... | collective-permute-start | bytes 835592 | tf_op jit(solution)/shard_map/ppermute | solution.py:326
  70.0 7.0 %collective-permute-start.20 = (bf16[272,512]{1,0:T(8,128)(2,1)S(1)}, bf16[272,512]{1,0:T(8,128)(2,1)S(1)}, u32[]{:S(2)}, u32[]{:S(2)}) collective-permute-start(bf16[272,512]{1,0:T(8,128)(2,1)S(1)} %shard_map.94.refs_0_), channel_id=1, source_target_pairs={{0,4},{2,6},{4,0},{6,2},{8,12},{10,14},{12,8},{14,10},{1,5},{3,7},... | collective-permute-start | bytes 835592 | tf_op jit(solution)/shard_map/ppermute | solution.py:326
  70.0 8.4 %collective-permute-start.14 = (bf16[272,512]{1,0:T(8,128)(2,1)S(1)}, bf16[272,512]{1,0:T(8,128)(2,1)S(1)}, u32[]{:S(2)}, u32[]{:S(2)}) collective-permute-start(bf16[272,512]{1,0:T(8,128)(2,1)S(1)} %shard_map.92.refs_0_), channel_id=1, source_target_pairs={{0,1},{1,0},{2,3},{3,2},{4,5},{5,4},{6,7},{7,6},{8,9},{9,8},{10,11... | collective-permute-start | bytes 835592 | tf_op jit(solution)/shard_map/ppermute | solution.py:329
  70.0 9.7 %collective-permute-start.18 = (bf16[272,512]{1,0:T(8,128)(2,1)S(1)}, bf16[272,512]{1,0:T(8,128)(2,1)S(1)}, u32[]{:S(2)}, u32[]{:S(2)}) collective-permute-start(bf16[272,512]{1,0:T(8,128)(2,1)S(1)} %shard_map.94.refs_0_), channel_id=1, source_target_pairs={{0,1},{1,0},{2,3},{3,2},{4,5},{5,4},{6,7},{7,6},{8,9},{9,8},{10,11... | collective-permute-start | bytes 835592 | tf_op jit(solution)/shard_map/ppermute | solution.py:329
  70.5 7.9 %collective-permute-start.15 = (bf16[272,512]{1,0:T(8,128)(2,1)S(1)}, bf16[272,512]{1,0:T(8,128)(2,1)S(1)}, u32[]{:S(2)}, u32[]{:S(2)}) collective-permute-start(bf16[272,512]{1,0:T(8,128)(2,1)S(1)} %collective-permute-done.13.refs_1_), channel_id=1, source_target_pairs={{0,1},{1,0},{2,3},{3,2},{4,5},{5,4},{6,7},{7,6},{8,9},{9,8},{10,11... | collective-permute-start | bytes 835592 | tf_op jit(solution)/shard_map/ppermute | solution.py:329
  76.6 3.1 %collective-permute-start.19 = (bf16[272,512]{1,0:T(8,128)(2,1)S(1)}, bf16[272,512]{1,0:T(8,128)(2,1)S(1)}, u32[]{:S(2)}, u32[]{:S(2)}) collective-permute-start(bf16[272,512]{1,0:T(8,128)(2,1)S(1)} %collective-permute-done.17.refs_1_), channel_id=1, source_target_pairs={{0,1},{1,0},{2,3},{3,2},{4,5},{5,4},{6,7},{7,6},{8,9},{9,8},{10,11... | collective-permute-start | bytes 835592 | tf_op jit(solution)/shard_map/ppermute | solution.py:329
  76.9 8.8 %collective-permute-start.21 = (bf16[272,512]{1,0:T(8,128)(2,1)S(1)}, bf16[272,512]{1,0:T(8,128)(2,1)S(1)}, u32[]{:S(2)}, u32[]{:S(2)}) collective-permute-start(bf16[272,512]{1,0:T(8,128)(2,1)S(1)} %shard_map.96.refs_0_), channel_id=1, source_target_pairs={{0,2},{2,0},{4,6},{6,4},{8,10},{10,8},{12,14},{14,12},{1,3},{3,1},... | collective-permute-start | bytes 835592 | tf_op jit(solution)/shard_map/ppermute | solution.py:326
  78.4 7.3 %collective-permute-start.22 = (bf16[272,512]{1,0:T(8,128)(2,1)S(1)}, bf16[272,512]{1,0:T(8,128)(2,1)S(1)}, u32[]{:S(2)}, u32[]{:S(2)}) collective-permute-start(bf16[272,512]{1,0:T(8,128)(2,1)S(1)} %shard_map.96.refs_0_), channel_id=1, source_target_pairs={{0,1},{1,0},{2,3},{3,2},{4,5},{5,4},{6,7},{7,6},{8,9},{9,8},{10,11... | collective-permute-start | bytes 835592 | tf_op jit(solution)/shard_map/ppermute | solution.py:329
  85.7 1.6 %collective-permute-start.23 = (bf16[272,512]{1,0:T(8,128)(2,1)S(1)}, bf16[272,512]{1,0:T(8,128)(2,1)S(1)}, u32[]{:S(2)}, u32[]{:S(2)}) collective-permute-start(bf16[272,512]{1,0:T(8,128)(2,1)S(1)} %shard_map.97.refs_1_), channel_id=1, source_target_pairs={{0,1},{1,0},{2,3},{3,2},{4,5},{5,4},{6,7},{7,6},{8,9},{9,8},{10,11... | collective-permute-start | bytes 835592 | tf_op jit(solution)/shard_map/ppermute | solution.py:329
  95.5 2.4 %collective-permute-start.24 = (bf16[8,128,384]{2,1,0:T(8,128)(2,1)S(1)}, bf16[8,128,384]{2,1,0:T(8,128)(2,1)S(1)}, u32[]{:S(2)}, u32[]{:S(2)}) collective-permute-start(bf16[8,128,384]{2,1,0:T(8,128)(2,1)S(1)} %shard_map.99.near_ref), channel_id=1, source_target_pairs={{0,1},{1,0},{2,3},{3,2},{4,5},{5,4},{6,7},{7,6},{8,9},{9,8},{10,11... | collective-permute-start | bytes 2359304 | tf_op jit(solution)/shard_map/ppermute | solution.py:329
  100.9 9.2 %collective-permute-start.25 = (bf16[128,1024]{1,0:T(8,128)(2,1)S(1)}, bf16[128,1024]{1,0:T(8,128)(2,1)S(1)}, u32[]{:S(2)}, u32[]{:S(2)}) collective-permute-start(bf16[128,1024]{1,0:T(8,128)(2,1)S(1)} %get-tuple-element.89), channel_id=1, source_target_pairs={{0,2},{2,0},{4,6},{6,4},{8,10},{10,8},{12,14},{14,12},{1,3},{3,1},... | collective-permute-start | bytes 786440 | tf_op jit(solution)/shard_map/ppermute | solution.py:326
  101.5 14.2 %collective-permute-start.27 = (bf16[128,1024]{1,0:T(8,128)(2,1)S(1)}, bf16[128,1024]{1,0:T(8,128)(2,1)S(1)}, u32[]{:S(2)}, u32[]{:S(2)}) collective-permute-start(bf16[128,1024]{1,0:T(8,128)(2,1)S(1)} %get-tuple-element.91), channel_id=1, source_target_pairs={{0,2},{2,0},{4,6},{6,4},{8,10},{10,8},{12,14},{14,12},{1,3},{3,1},... | collective-permute-start | bytes 786440 | tf_op jit(solution)/shard_map/ppermute | solution.py:326
  103.0 18.4 %collective-permute-start.29 = (bf16[128,1024]{1,0:T(8,128)(2,1)S(1)}, bf16[128,1024]{1,0:T(8,128)(2,1)S(1)}, u32[]{:S(2)}, u32[]{:S(2)}) collective-permute-start(bf16[128,1024]{1,0:T(8,128)(2,1)S(1)} %get-tuple-element.93), channel_id=1, source_target_pairs={{0,2},{2,0},{4,6},{6,4},{8,10},{10,8},{12,14},{14,12},{1,3},{3,1},... | collective-permute-start | bytes 786440 | tf_op jit(solution)/shard_map/ppermute | solution.py:326
  103.5 22.6 %collective-permute-start.31 = (bf16[128,1024]{1,0:T(8,128)(2,1)S(1)}, bf16[128,1024]{1,0:T(8,128)(2,1)S(1)}, u32[]{:S(2)}, u32[]{:S(2)}) collective-permute-start(bf16[128,1024]{1,0:T(8,128)(2,1)S(1)} %get-tuple-element.94), channel_id=1, source_target_pairs={{0,2},{2,0},{4,6},{6,4},{8,10},{10,8},{12,14},{14,12},{1,3},{3,1},... | collective-permute-start | bytes 786440 | tf_op jit(solution)/shard_map/ppermute | solution.py:326
  110.2 16.0 %collective-permute-start.26 = (bf16[128,1024]{1,0:T(8,128)(2,1)S(1)}, bf16[128,1024]{1,0:T(8,128)(2,1)S(1)}, u32[]{:S(2)}, u32[]{:S(2)}) collective-permute-start(bf16[128,1024]{1,0:T(8,128)(2,1)S(1)} %add_convert_fusion.2), channel_id=1, source_target_pairs={{0,12},{2,14},{4,8},{6,10},{8,4},{10,6},{12,0},{14,2},{1,13},{3,15... | collective-permute-start | bytes 786440 | tf_op jit(solution)/shard_map/ppermute | solution.py:326
  115.8 17.1 %collective-permute-start.28 = (bf16[128,1024]{1,0:T(8,128)(2,1)S(1)}, bf16[128,1024]{1,0:T(8,128)(2,1)S(1)}, u32[]{:S(2)}, u32[]{:S(2)}) collective-permute-start(bf16[128,1024]{1,0:T(8,128)(2,1)S(1)} %add_convert_fusion.1), channel_id=1, source_target_pairs={{0,8},{2,10},{4,12},{6,14},{8,0},{10,2},{12,4},{14,6},{1,9},{3,11}... | collective-permute-start | bytes 786440 | tf_op jit(solution)/shard_map/ppermute | solution.py:326
  121.4 12.4 %collective-permute-start.30 = (bf16[128,1024]{1,0:T(8,128)(2,1)S(1)}, bf16[128,1024]{1,0:T(8,128)(2,1)S(1)}, u32[]{:S(2)}, u32[]{:S(2)}) collective-permute-start(bf16[128,1024]{1,0:T(8,128)(2,1)S(1)} %add_convert_fusion), channel_id=1, source_target_pairs={{0,4},{2,6},{4,0},{6,2},{8,12},{10,14},{12,8},{14,10},{1,5},{3,7},... | collective-permute-start | bytes 786440 | tf_op jit(solution)/shard_map/ppermute | solution.py:326

commit v7 on v6

--- a/solution.py
+++ b/solution.py
@@ -117,7 +117,7 @@
 def projection_kernel(steps, pieces, *refs):
     mixed_ref, other_ref = refs[0], refs[1]
     weight_refs = refs[2 : 2 + len(pieces)]
-    keep_ref, send_ref, both_ref = refs[2 + len(pieces) :]
+    keep_ref, send_ref, both_ref = refs[-3:]
     count = mixed_ref.shape[0]
     half = steps // 2
     chunk = keep_ref.shape[1] // half
@@ -241,20 +241,30 @@
         back_ref[cross] = jnp.where(pick, here, 0.0).T.astype(BF16)
 
 
-def load_kernel(local, up_ref, down_ref, _, *refs):
-    to_refs, done_ref, sem_ref = refs[: 2 * local], refs[2 * local], refs[2 * local + 1]
-    copies = []
-    for n, ref in enumerate(to_refs):
-        e = n % local
-        whole_ref = up_ref if n < local else down_ref
-        copies.append(
-            pltpu.make_async_copy(whole_ref.at[2 * e : 2 * e + 2], ref, sem_ref.at[n])
-        )
+def load_kernel(from_ref, _, *refs):
+    to_refs, done_ref, sem_ref = refs[:-2], refs[-2], refs[-1]
+    copies = [
+        pltpu.make_async_copy(from_ref.at[2 * e : 2 * e + 2], ref, sem_ref.at[e])
+        for e, ref in enumerate(to_refs)
+    ]
     for copy in copies:
         copy.start()
     done_ref[...] = jnp.zeros(done_ref.shape, F32)
     for copy in copies:
         copy.wait()
+
+
+def load(weight, after_this, limit):
+    local = weight.shape[0] // 2
+    piece = jax.ShapeDtypeStruct((2, *weight.shape[1:]), BF16)
+    return pl.pallas_call(
+        load_kernel,
+        out_shape=[piece] * local + [jax.ShapeDtypeStruct((8, 128), F32)],
+        in_specs=[pl.BlockSpec(memory_space=pl.ANY)] * 2,
+        out_specs=[whole()] * (local + 1),
+        scratch_shapes=[pltpu.SemaphoreType.DMA((local,))],
+        compiler_params=vmem(limit),
+    )(weight, after_this)
 
 
 def hidden_kernel(steps, *refs):
@@ -269,16 +279,15 @@
         hidden_ref[e] = jnp.concatenate(halves).T.astype(BF16)
 
 
-def output_kernel(steps, local, near_ref, far_ref, *refs):
-    w_refs, back_refs = refs[:local], refs[local : local + steps]
-    out_refs, held_ref = refs[local + steps : local + 3 * steps], refs[-1]
+def output_kernel(steps, near_ref, far_ref, w_ref, *refs):
+    back_refs, out_refs, held_ref = refs[:steps], refs[steps : 3 * steps], refs[-1]
     part = lax.axis_index("sub")
     units = near_ref.shape[2] // 2
-    for e, w_ref in enumerate(w_refs):
+    for e in range(near_ref.shape[0]):
         total = 0.0
         for ref, who in ((near_ref, part), (far_ref, 1 - part)):
             at = pl.multiple_of(who * units, 64)
-            weight = jnp.concatenate([w_ref[b, pl.ds(at, units), :] for b in range(2)])
+            weight = jnp.concatenate([w_ref[2 * e + b, pl.ds(at, units), :] for b in range(2)])
             total += jnp.dot(ref[e], weight, preferred_element_type=F32)
         total = total.astype(BF16)
         for source in range(2 * steps):
@@ -361,16 +370,7 @@
     cross = hop(cross, 1)
 
     units = gate_up_weight.shape[3]
-    *loaded, done = pl.pallas_call(
-        functools.partial(load_kernel, local),
-        out_shape=[struct((2, 2, units, width), BF16)] * local
-        + [struct((2, *down_weight.shape[1:]), BF16)] * local
-        + [struct((8, 128), F32)],
-        in_specs=[pl.BlockSpec(memory_space=pl.ANY)] * 3,
-        out_specs=[whole()] * (2 * local + 1),
-        scratch_shapes=[pltpu.SemaphoreType.DMA((2 * local,))],
-        compiler_params=vmem(14),
-    )(gate_up_weight.swapaxes(2, 3), down_weight, query)
+    *ups, done = load(gate_up_weight.swapaxes(2, 3), query, 16)
 
     mine = {0: sent}
     for flip in range(2, steps):
@@ -422,7 +422,8 @@
     across = hop(shard, 1)
     column[1] = tie(column[1], across)
     crossing = {0: across, 1: hop(column[1], 1)}
-    column[2] = tie(hop(shard, 4), crossing[1])
+    beside = swap(column[1])
+    column[2] = tie(hop(shard, 4), beside)
     for flip in range(3, steps):
         low = flip & -flip
         column[flip] = hop(column[flip - low] if flip > low else shard, 2 * low)
@@ -445,7 +446,7 @@
             out_specs=[whole()] * (3 if own else 2),
             scratch_shapes=[pltpu.VMEM((count, width), BF16), pltpu.VMEM((experts, count), F32)],
             compiler_params=vmem(6),
-        )(block, crossed, swap(block), swap(crossed), small, router)
+        )(block, crossed, beside if flip == 1 else swap(block), swap(crossed), small, router)
         picked.append(results[0])
         backs.append(results[1])
         if own:
@@ -459,15 +460,15 @@
         in_specs=[whole()] * (steps + local),
         out_specs=whole(),
         compiler_params=vmem(6),
-    )(*picked, *loaded[:local])
+    )(*picked, *ups)
     share = pl.pallas_call(
-        functools.partial(output_kernel, steps, local),
+        functools.partial(output_kernel, steps),
         out_shape=[struct((count, 2 * lanes), BF16)] * sources,
-        in_specs=[whole()] * (2 + local + steps),
+        in_specs=[whole()] * (3 + steps),
         out_specs=[whole()] * sources,
         scratch_shapes=[pltpu.VMEM((sources, slots, 2 * lanes), BF16)],
         compiler_params=vmem(8),
-    )(hidden, swap(hidden), *loaded[local:], *backs)
+    )(hidden, swap(hidden), down_weight, *backs)
 
     terms = [share[0]]
     for flip in range(steps - 1, -1, -1):

time: 135 us -> 135 us (level)
  waiting for transfers between devices: 70.9 us -> 77.2 us
  Pallas kernels: 35.4 us -> 31.8 us
  starting transfers between devices: 27.9 us -> 25.5 us
    ppermute x19, waiting for transfers between devices: 65.3 us -> 71.6 us  [hop(): return lax.ppermute(x, 'dev', [(i, i ^ flip) for i in range(devices)])]
    pallas_call x2, Pallas kernels: 14.9 us -> 11.3 us  [the longest x1 8.33 us: load(): pl.pallas_call(load_kernel, out_shape=[piece] * local + [jax.ShapeDtypeSt...]
    ppermute x19, starting transfers between devices: 22.8 us -> 20.8 us  [hop(): return lax.ppermute(x, 'dev', [(i, i ^ flip) for i in range(devices)])]
  transfers between devices with their start and end apart: 32 -> 32, of which waited for: 18 -> 17; matrix products, arithmetic and copies ran while one was open for 0% -> 0% of each run, Pallas kernels for 14% -> 11%
where the time goes in v7:
time: 135 us
  waiting for transfers between devices  77.2 us (57%)
  Pallas kernels  31.8 us (24%)
  starting transfers between devices  25.5 us (19%)
    ppermute x19, waiting for transfers between devices, hop(): return lax.ppermute(x, 'dev', [(i, i ^ flip) for i in range(devices)])  71.6 us
    ppermute x19, starting transfers between devices, hop(): return lax.ppermute(x, 'dev', [(i, i ^ flip) for i in range(devices)])  20.8 us
    pallas_call x1, Pallas kernels, load(): pl.pallas_call(load_kernel, out_shape=[piece] * local + [jax.ShapeDtypeSt...  8.33 us
    pallas_call x1, Pallas kernels, gathered_body(): pl.pallas_call(functools.partial(hidden_kernel, steps), out_shape=struct(...  6.91 us
    ppermute x10, waiting for transfers between devices, swap(): return lax.ppermute(x, 'sub', [(0, 1), (1, 0)])  5.61 us
    pallas_call x4, Pallas kernels, gathered_body(): pl.pallas_call(functools.partial(select_kernel, local, topk, own), out_sh...  5.3 us
    pallas_call x1, Pallas kernels, gathered_body(): pl.pallas_call(attention_kernel, out_shape=struct((count, local_width), B...  3.1 us
    ppermute x2, starting transfers between devices, gathered_body(): theirs = lax.ppermute(mine[flip], 'groups', [(0, 1), (1, 0)])  3.04 us
  transfers between devices with their start and end apart: 32, of which 17 were waited for; matrix products, arithmetic and copies ran while one was open for 0% of the time, Pallas kernels for 11%

profile of v7, /device:TPU:0, one launch (start us, length us, event | category | flops | bytes accessed | tf_op | source)
XLA Modules:
  0.0 135.0 jit_solution(18019873813662179682)
XLA Ops:
  0.0 2.7 %shard_map.82 = (bf16[128,1024]{1,0:T(8,128)(2,1)S(1)}, bf16[256,1024]{1,0:T(8,128)(2,1)S(1)}, bf16[128,512]{1,0:T(8,128)(2,1)S(1)}, bf16[320,1024]{1,0:T(8,128)...) custom-call(bf16[128,2048]{1,0:T(8,128)(2,1)} %tokens_ref.1, bf16[3,128,1024]{2,1,0:T(8,128)(2,1)} %bitcast.9, ...), custom_call_target="tpu_custom_call" | custom-call | tf_op jit(solution)/shard_map/pallas_call | solution.py:342
  2.7 3.0 %collective-permute-start = (bf16[320,1024]{1,0:T(8,128)(2,1)}, bf16[320,1024]{1,0:T(8,128)(2,1)S(1)}, u32[]{:S(2)}, u32[]{:S(2)}) collective-permute-start(bf16[320,1024]{1,0:T(8,128)(2,1)} %get-tuple-element.44), channel_id=1, source_target_pairs={{0,2},{2,0},{4,6},{6,4},{8,10},{10,8},{12,14},{14,12},{1,3},{3,1},... | collective-permute-start | bytes 1966088 | tf_op jit(solution)/shard_map/ppermute | solution.py:335
  5.7 2.6 %collective-permute-start.3 = (bf16[128,1024]{1,0:T(8,128)(2,1)S(1)}, bf16[128,1024]{1,0:T(8,128)(2,1)S(1)}, u32[]{:S(2)}, u32[]{:S(2)}) collective-permute-start(bf16[128,1024]{1,0:T(8,128)(2,1)S(1)} %get-tuple-element.47), channel_id=1, source_target_pairs={{0,8},{2,10},{4,12},{6,14},{8,0},{10,2},{12,4},{14,6},{1,9},{3,11}... | collective-permute-start | bytes 786440 | tf_op jit(solution)/shard_map/ppermute | solution.py:335
  8.3 0.7 collective-permute-start.1
  8.9 0.0 copy-start
  9.0 0.0 copy-start.1
  9.0 0.0 copy-start.2
  9.0 8.3 %shard_map.85 = (bf16[2,2,192,2048]{3,2,1,0:T(8,128)(2,1)S(1)}, bf16[2,2,192,2048]{3,2,1,0:T(8,128)(2,1)S(1)}, bf16[2,2,192,2048]{3,2,1,0:T(8,128)(2,1)S(1)}, bf...) custom-call(bf16[16,2,192,2048]{3,2,1,0:T(8,128)(2,1)} %bitcast.8, ...), custom_call_target="tpu_custom_call" | custom-call | tf_op jit(solution)/shard_map/pallas_call | solution.py:260
  17.3 3.8 %collective-permute-done.3.refs_0_ = bf16[128,1024]{1,0:T(8,128)(2,1)S(1)} collective-permute-done((bf16[128,1024]{1,0:T(8,128)(2,1)S(1)}, bf16[128,1024]{1,0:T(8,128)(2,1)S(1)}, u32[]{:S(2)}, u32[]{:S(2)}) %collective-permute-start.3) | collective-permute-done | bytes 262176 | tf_op jit(solution)/shard_map/ppermute | solution.py:335
  21.1 2.0 %collective-permute-start.4 = (bf16[256,1024]{1,0:T(8,128)(2,1)S(1)}, bf16[256,1024]{1,0:T(8,128)(2,1)S(1)}, u32[]{:S(2)}, u32[]{:S(2)}) collective-permute-start(bf16[256,1024]{1,0:T(8,128)(2,1)S(1)} %shard_map.87.refs_2_), channel_id=1, source_target_pairs={{0,4},{2,6},{4,0},{6,2},{8,12},{10,14},{12,8},{14,10},{1,5},{3,7},... | collective-permute-start | bytes 1572872 | tf_op jit(solution)/shard_map/ppermute | solution.py:335
  23.2 1.5 %collective-permute-start.5 = (bf16[128,1024]{1,0:T(8,128)(2,1)S(1)}, bf16[128,1024]{1,0:T(8,128)(2,1)S(1)}, u32[]{:S(2)}, u32[]{:S(2)}) collective-permute-start(bf16[128,1024]{1,0:T(8,128)(2,1)S(1)} %shard_map.86.refs_1_.refs_4_), channel_id=1, source_target_pairs={{0,16},{16,0},{1,17},{17,1},{2,18},{18,2},{3,19},{19,3},{4,20},{20... | collective-permute-start | bytes 786440 | tf_op jit(solution)/shard_map/ppermute | solution.py:396
  24.7 6.4 %collective-permute-done.cross_ref = bf16[320,1024]{1,0:T(8,128)(2,1)S(1)} collective-permute-done((bf16[320,1024]{1,0:T(8,128)(2,1)}, bf16[320,1024]{1,0:T(8,128)(2,1)S(1)}, u32[]{:S(2)}, u32[]{:S(2)}) %collective-permute-start) | collective-permute-done | bytes 655392 | tf_op jit(solution)/shard_map/ppermute | solution.py:335
  31.2 3.1 %shard_map.84.refs_1_.refs_0_ = bf16[128,1024]{1,0:T(8,128)(2,1)S(1)} custom-call(bf16[128,1024]{1,0:T(8,128)(2,1)S(1)} %get-tuple-element.42._.query_ref, bf16[256,1024]{1,0:T(8,128)(2,1)S(1)} %get-tuple-element.43.own_ref, bf16[320,1024]{1,0:T(8,128)(2,1)S(1)} %collective-permute-done.cross_ref, bf16[256,1024]{1,0:T(8,128)(2,1)S(1)} %collective-permute-done.1.next_ref, ...), custom_call_target="tpu_custom_call" | custom-call | tf_op jit(solution)/shard_map/pallas_call | solution.py:385
  34.3 2.4 %collective-permute-start.2 = (bf16[128,1024]{1,0:T(8,128)(2,1)S(1)}, bf16[128,1024]{1,0:T(8,128)(2,1)S(1)}, u32[]{:S(2)}, u32[]{:S(2)}) collective-permute-start(bf16[128,1024]{1,0:T(8,128)(2,1)S(1)} %shard_map.84.refs_1_.refs_0_), channel_id=1, source_target_pairs={{0,2},{2,0},{4,6},{6,4},{8,10},{10,8},{12,14},{14,12},{1,3},{3,1},... | collective-permute-start | bytes 786440 | tf_op jit(solution)/shard_map/ppermute | solution.py:335
  36.7 0.0 collective-permute-done.6.refs_0_
  36.7 1.5 %collective-permute-start.7 = (bf16[128,1024]{1,0:T(8,128)(2,1)S(1)}, bf16[128,1024]{1,0:T(8,128)(2,1)S(1)}, u32[]{:S(2)}, u32[]{:S(2)}) collective-permute-start(bf16[128,1024]{1,0:T(8,128)(2,1)S(1)} %shard_map.88.refs_6_), channel_id=1, source_target_pairs={{0,16},{16,0},{1,17},{17,1},{2,18},{18,2},{3,19},{19,3},{4,20},{20... | collective-permute-start | bytes 786440 | tf_op jit(solution)/shard_map/ppermute | solution.py:396
  38.2 6.4 %collective-permute-done.4.refs_3_ = bf16[256,1024]{1,0:T(8,128)(2,1)S(1)} collective-permute-done((bf16[256,1024]{1,0:T(8,128)(2,1)S(1)}, bf16[256,1024]{1,0:T(8,128)(2,1)S(1)}, u32[]{:S(2)}, u32[]{:S(2)}) %collective-permute-start.4) | collective-permute-done | bytes 524320 | tf_op jit(solution)/shard_map/ppermute | solution.py:335
  44.6 0.0 collective-permute-done.2.refs_1_
  44.6 0.0 collective-permute-done.7.refs_7_
  44.6 1.4 %shard_map.89 = (f32[256,512]{1,0:T(8,128)S(1)}, f32[256,512]{1,0:T(8,128)S(1)}) custom-call(bf16[128,1024]{1,0:T(8,128)(2,1)S(1)} %shard_map.84.refs_1_.refs_0_, bf16[128,1024]{1,0:T(8,128)(2,1)S(1)} %collective-permute-done.2.refs_1_, bf16[256,1024]{1,0:T(8,128)(2,1)S(1)} %shard_map.87.refs_2_, bf16[256,1024]{1,0:T(8,128)(2,1)S(1)} %collective-permute-done.4.refs_3_, ...), custom_call_target="tpu_custom_call" | custom-call | tf_op jit(solution)/shard_map/pallas_call | solution.py:402
  46.1 0.1 collective-permute-start.8
  46.1 1.9 %collective-permute-done.8.got_ref = f32[256,512]{1,0:T(8,128)S(1)} collective-permute-done((f32[256,512]{1,0:T(8,128)S(1)}, f32[256,512]{1,0:T(8,128)S(1)}, u32[]{:S(2)}, u32[]{:S(2)}) %collective-permute-start.8) | collective-permute-done | bytes 524320 | tf_op jit(solution)/shard_map/ppermute | solution.py:338
  48.0 0.1 shard_map.90.refs_0_
  48.1 0.6 collective-permute-start.12
  48.7 0.5 collective-permute-start.9
  49.3 3.4 %collective-permute-start.16 = (bf16[272,512]{1,0:T(8,128)(2,1)S(1)}, bf16[272,512]{1,0:T(8,128)(2,1)S(1)}, u32[]{:S(2)}, u32[]{:S(2)}) collective-permute-start(bf16[272,512]{1,0:T(8,128)(2,1)S(1)} %shard_map.90.refs_0_), channel_id=1, source_target_pairs={{0,8},{2,10},{4,12},{6,14},{8,0},{10,2},{12,4},{14,6},{1,9},{3,11}... | collective-permute-start | bytes 835592 | tf_op jit(solution)/shard_map/ppermute | solution.py:335
  52.6 9.1 %collective-permute-done.12.refs_0_ = bf16[272,512]{1,0:T(8,128)(2,1)S(1)} collective-permute-done((bf16[272,512]{1,0:T(8,128)(2,1)S(1)}, bf16[272,512]{1,0:T(8,128)(2,1)S(1)}, u32[]{:S(2)}, u32[]{:S(2)}) %collective-permute-start.12) | collective-permute-done | bytes 278560 | tf_op jit(solution)/shard_map/ppermute | solution.py:335
  61.8 0.0 collective-permute-start.14
  61.8 0.5 collective-permute-start.10
  62.3 0.1 collective-permute-start.11
  62.4 2.7 %collective-permute-done.16.refs_0_ = bf16[272,512]{1,0:T(8,128)(2,1)S(1)} collective-permute-done((bf16[272,512]{1,0:T(8,128)(2,1)S(1)}, bf16[272,512]{1,0:T(8,128)(2,1)S(1)}, u32[]{:S(2)}, u32[]{:S(2)}) %collective-permute-start.16) | collective-permute-done | bytes 278560 | tf_op jit(solution)/shard_map/ppermute | solution.py:335
  65.0 0.8 collective-permute-start.17
  65.8 6.0 %collective-permute-done.13.refs_1_ = bf16[272,512]{1,0:T(8,128)(2,1)S(1)} collective-permute-done((bf16[272,512]{1,0:T(8,128)(2,1)S(1)}, bf16[272,512]{1,0:T(8,128)(2,1)S(1)}, u32[]{:S(2)}, u32[]{:S(2)}) %collective-permute-start.13) | collective-permute-done | bytes 278560 | tf_op jit(solution)/shard_map/ppermute | solution.py:335
  71.8 1.3 shard_map.91
  73.2 3.7 %collective-permute-done.17.refs_1_ = bf16[272,512]{1,0:T(8,128)(2,1)S(1)} collective-permute-done((bf16[272,512]{1,0:T(8,128)(2,1)S(1)}, bf16[272,512]{1,0:T(8,128)(2,1)S(1)}, u32[]{:S(2)}, u32[]{:S(2)}) %collective-permute-start.17) | collective-permute-done | bytes 278560 | tf_op jit(solution)/shard_map/ppermute | solution.py:335
  76.9 0.3 collective-permute-start.21
  77.2 0.2 collective-permute-start.22
  77.4 1.3 shard_map.93
  78.8 1.3 shard_map.95
  80.1 5.9 %collective-permute-done.21.refs_0_ = bf16[272,512]{1,0:T(8,128)(2,1)S(1)} collective-permute-done((bf16[272,512]{1,0:T(8,128)(2,1)S(1)}, bf16[272,512]{1,0:T(8,128)(2,1)S(1)}, u32[]{:S(2)}, u32[]{:S(2)}) %collective-permute-start.21) | collective-permute-done | bytes 278560 | tf_op jit(solution)/shard_map/ppermute | solution.py:335
  86.0 1.6 %collective-permute-done.23.refs_3_ = bf16[272,512]{1,0:T(8,128)(2,1)S(1)} collective-permute-done((bf16[272,512]{1,0:T(8,128)(2,1)S(1)}, bf16[272,512]{1,0:T(8,128)(2,1)S(1)}, u32[]{:S(2)}, u32[]{:S(2)}) %collective-permute-start.23) | collective-permute-done | bytes 278560 | tf_op jit(solution)/shard_map/ppermute | solution.py:338
  87.5 1.3 shard_map.98
  88.9 0.0 slice-start
  88.9 6.9 %shard_map.99.near_ref = bf16[8,128,384]{2,1,0:T(8,128)(2,1)S(1)} custom-call(bf16[8,32,2048]{2,1,0:T(8,128)(2,1)S(1)} %get-tuple-element.55.refs_1_.refs_0_, bf16[8,32,2048]{2,1,0:T(8,128)(2,1)S(1)} %get-tuple-element.56.refs_1_, bf16[8,32,2048]{2,1,0:T(8,128)(2,1)S(1)} %get-tuple-element.57.refs_2_, bf16[8,32,2048]{2,1,0:T(8,128)(2,1)S(1)} %get-tuple-element.58.refs_3_, ...), custom_call_target="tpu_custom_call" | custom-call | tf_op jit(solution)/shard_map/pallas_call | solution.py:457
  95.8 0.2 collective-permute-start.24
  96.0 2.1 %collective-permute-done.24.far_ref = bf16[8,128,384]{2,1,0:T(8,128)(2,1)S(1)} collective-permute-done((bf16[8,128,384]{2,1,0:T(8,128)(2,1)S(1)}, bf16[8,128,384]{2,1,0:T(8,128)(2,1)S(1)}, u32[]{:S(2)}, u32[]{:S(2)}) %collective-permute-start.24) | collective-permute-done | bytes 786464 | tf_op jit(solution)/shard_map/ppermute | solution.py:338
  98.2 3.0 %shard_map.100 = (bf16[128,1024]{1,0:T(8,128)(2,1)S(1)}, bf16[128,1024]{1,0:T(8,128)(2,1)S(1)}, bf16[128,1024]{1,0:T(8,128)(2,1)S(1)}, bf16[128,1024]{1,0:T(8,12...) custom-call(bf16[8,128,384]{2,1,0:T(8,128)(2,1)S(1)} %shard_map.99.n, ...), custom_call_target="tpu_custom_call" | custom-call | tf_op jit(solution)/shard_map/pallas_call | solution.py:464
  101.1 0.4 collective-permute-start.25
  101.5 1.7 %collective-permute-start.27 = (bf16[128,1024]{1,0:T(8,128)(2,1)S(1)}, bf16[128,1024]{1,0:T(8,128)(2,1)S(1)}, u32[]{:S(2)}, u32[]{:S(2)}) collective-permute-start(bf16[128,1024]{1,0:T(8,128)(2,1)S(1)} %get-tuple-element.75), channel_id=1, source_target_pairs={{0,2},{2,0},{4,6},{6,4},{8,10},{10,8},{12,14},{14,12},{1,3},{3,1},... | collective-permute-start | bytes 786440 | tf_op jit(solution)/shard_map/ppermute | solution.py:335
  103.2 0.3 collective-permute-start.29
  103.5 1.7 %collective-permute-start.31 = (bf16[128,1024]{1,0:T(8,128)(2,1)S(1)}, bf16[128,1024]{1,0:T(8,128)(2,1)S(1)}, u32[]{:S(2)}, u32[]{:S(2)}) collective-permute-start(bf16[128,1024]{1,0:T(8,128)(2,1)S(1)} %get-tuple-element.78), channel_id=1, source_target_pairs={{0,2},{2,0},{4,6},{6,4},{8,10},{10,8},{12,14},{14,12},{1,3},{3,1},... | collective-permute-start | bytes 786440 | tf_op jit(solution)/shard_map/ppermute | solution.py:335
  105.3 5.1 %collective-permute-done.25 = bf16[128,1024]{1,0:T(8,128)(2,1)S(1)} collective-permute-done((bf16[128,1024]{1,0:T(8,128)(2,1)S(1)}, bf16[128,1024]{1,0:T(8,128)(2,1)S(1)}, u32[]{:S(2)}, u32[]{:S(2)}) %collective-permute-start.25) | collective-permute-done | bytes 262176 | tf_op jit(solution)/shard_map/ppermute | solution.py:335
  110.4 0.1 add_convert_fusion.2
  110.4 0.9 collective-permute-start.26
  111.3 4.7 %collective-permute-done.27 = bf16[128,1024]{1,0:T(8,128)(2,1)S(1)} collective-permute-done((bf16[128,1024]{1,0:T(8,128)(2,1)S(1)}, bf16[128,1024]{1,0:T(8,128)(2,1)S(1)}, u32[]{:S(2)}, u32[]{:S(2)}) %collective-permute-start.27) | collective-permute-done | bytes 262176 | tf_op jit(solution)/shard_map/ppermute | solution.py:335
  116.0 0.1 add_convert_fusion.1
  116.1 0.1 collective-permute-start.28
  116.1 5.5 %collective-permute-done.29 = bf16[128,1024]{1,0:T(8,128)(2,1)S(1)} collective-permute-done((bf16[128,1024]{1,0:T(8,128)(2,1)S(1)}, bf16[128,1024]{1,0:T(8,128)(2,1)S(1)}, u32[]{:S(2)}, u32[]{:S(2)}) %collective-permute-start.29) | collective-permute-done | bytes 262176 | tf_op jit(solution)/shard_map/ppermute | solution.py:335
  121.6 0.1 add_convert_fusion
  121.7 0.1 collective-permute-start.30
  121.7 4.7 %collective-permute-done.31.refs_4_ = bf16[128,1024]{1,0:T(8,128)(2,1)S(1)} collective-permute-done((bf16[128,1024]{1,0:T(8,128)(2,1)S(1)}, bf16[128,1024]{1,0:T(8,128)(2,1)S(1)}, u32[]{:S(2)}, u32[]{:S(2)}) %collective-permute-start.31) | collective-permute-done | bytes 262176 | tf_op jit(solution)/shard_map/ppermute | solution.py:335
  126.4 6.7 %collective-permute-done.28.refs_2_ = bf16[128,1024]{1,0:T(8,128)(2,1)S(1)} collective-permute-done((bf16[128,1024]{1,0:T(8,128)(2,1)S(1)}, bf16[128,1024]{1,0:T(8,128)(2,1)S(1)}, u32[]{:S(2)}, u32[]{:S(2)}) %collective-permute-start.28) | collective-permute-done | bytes 262176 | tf_op jit(solution)/shard_map/ppermute | solution.py:335
  133.1 1.0 collective-permute-done.30.refs_3_
  134.1 0.9 shard_map.101
  (36 shorter events, 0.1 us)
Async XLA Ops:
  2.7 28.5 %collective-permute-start = (bf16[320,1024]{1,0:T(8,128)(2,1)}, bf16[320,1024]{1,0:T(8,128)(2,1)S(1)}, u32[]{:S(2)}, u32[]{:S(2)}) collective-permute-start(bf16[320,1024]{1,0:T(8,128)(2,1)} %get-tuple-element.44), channel_id=1, source_target_pairs={{0,2},{2,0},{4,6},{6,4},{8,10},{10,8},{12,14},{14,12},{1,3},{3,1},... | collective-permute-start | bytes 1966088 | tf_op jit(solution)/shard_map/ppermute | solution.py:335
  5.7 15.4 %collective-permute-start.3 = (bf16[128,1024]{1,0:T(8,128)(2,1)S(1)}, bf16[128,1024]{1,0:T(8,128)(2,1)S(1)}, u32[]{:S(2)}, u32[]{:S(2)}) collective-permute-start(bf16[128,1024]{1,0:T(8,128)(2,1)S(1)} %get-tuple-element.47), channel_id=1, source_target_pairs={{0,8},{2,10},{4,12},{6,14},{8,0},{10,2},{12,4},{14,6},{1,9},{3,11}... | collective-permute-start | bytes 786440 | tf_op jit(solution)/shard_map/ppermute | solution.py:335
  8.3 16.5 %collective-permute-start.1 = (bf16[256,1024]{1,0:T(8,128)(2,1)S(1)}, bf16[256,1024]{1,0:T(8,128)(2,1)S(1)}, u32[]{:S(2)}, u32[]{:S(2)}) collective-permute-start(bf16[256,1024]{1,0:T(8,128)(2,1)S(1)} %get-tuple-element.43.own_ref), channel_id=1, source_target_pairs={{2,4},{6,8},{10,12},{4,2},{8,6},{12,10},{3,5},{7,9},{11,13},{5,3},... | collective-permute-start | bytes 1572872 | tf_op jit(solution)/shard_map/ppermute | solution.py:369
  8.9 14.2 %copy-start = (bf16[2048,64]{0,1:T(8,128)(2,1)S(1)}, bf16[2048,64]{0,1:T(8,128)(2,1)}, u32[]{:S(2)}) copy-start(bf16[2048,64]{0,1:T(8,128)(2,1)} %param.12) | copy-start | bytes 786436
  9.0 14.2 %copy-start.1 = (f32[4,2048]{1,0:T(4,128)S(1)}, f32[4,2048]{1,0:T(4,128)}, u32[]{:S(2)}) copy-start(f32[4,2048]{1,0:T(4,128)} %mod_ref.1) | copy-start | bytes 98308
  9.0 14.2 %copy-start.2 = (s32[128,4]{0,1:T(4,128)S(1)}, s32[128,4]{0,1:T(4,128)}, u32[]{:S(2)}) copy-start(s32[128,4]{0,1:T(4,128)} %param.13) | copy-start | bytes 6148
  21.1 15.6 %collective-permute-start.6 = (bf16[128,1024]{1,0:T(8,128)(2,1)S(1)}, bf16[128,1024]{1,0:T(8,128)(2,1)S(1)}, u32[]{:S(2)}, u32[]{:S(2)}) collective-permute-start(bf16[128,1024]{1,0:T(8,128)(2,1)S(1)} %shard_map.86.refs_1_.refs_4_), channel_id=1, source_target_pairs={{0,4},{2,6},{4,0},{6,2},{8,12},{10,14},{12,8},{14,10},{1,5},{3,7},... | collective-permute-start | bytes 786440 | tf_op jit(solution)/shard_map/ppermute | solution.py:335
  21.1 23.5 %collective-permute-start.4 = (bf16[256,1024]{1,0:T(8,128)(2,1)S(1)}, bf16[256,1024]{1,0:T(8,128)(2,1)S(1)}, u32[]{:S(2)}, u32[]{:S(2)}) collective-permute-start(bf16[256,1024]{1,0:T(8,128)(2,1)S(1)} %shard_map.87.refs_2_), channel_id=1, source_target_pairs={{0,4},{2,6},{4,0},{6,2},{8,12},{10,14},{12,8},{14,10},{1,5},{3,7},... | collective-permute-start | bytes 1572872 | tf_op jit(solution)/shard_map/ppermute | solution.py:335
  23.2 15.0 %collective-permute-start.5 = (bf16[128,1024]{1,0:T(8,128)(2,1)S(1)}, bf16[128,1024]{1,0:T(8,128)(2,1)S(1)}, u32[]{:S(2)}, u32[]{:S(2)}) collective-permute-start(bf16[128,1024]{1,0:T(8,128)(2,1)S(1)} %shard_map.86.refs_1_.refs_4_), channel_id=1, source_target_pairs={{0,16},{16,0},{1,17},{17,1},{2,18},{18,2},{3,19},{19,3},{4,20},{20... | collective-permute-start | bytes 786440 | tf_op jit(solution)/shard_map/ppermute | solution.py:396
  34.3 10.3 %collective-permute-start.2 = (bf16[128,1024]{1,0:T(8,128)(2,1)S(1)}, bf16[128,1024]{1,0:T(8,128)(2,1)S(1)}, u32[]{:S(2)}, u32[]{:S(2)}) collective-permute-start(bf16[128,1024]{1,0:T(8,128)(2,1)S(1)} %shard_map.84.refs_1_.refs_0_), channel_id=1, source_target_pairs={{0,2},{2,0},{4,6},{6,4},{8,10},{10,8},{12,14},{14,12},{1,3},{3,1},... | collective-permute-start | bytes 786440 | tf_op jit(solution)/shard_map/ppermute | solution.py:335
  36.7 7.9 %collective-permute-start.7 = (bf16[128,1024]{1,0:T(8,128)(2,1)S(1)}, bf16[128,1024]{1,0:T(8,128)(2,1)S(1)}, u32[]{:S(2)}, u32[]{:S(2)}) collective-permute-start(bf16[128,1024]{1,0:T(8,128)(2,1)S(1)} %shard_map.88.refs_6_), channel_id=1, source_target_pairs={{0,16},{16,0},{1,17},{17,1},{2,18},{18,2},{3,19},{19,3},{4,20},{20... | collective-permute-start | bytes 786440 | tf_op jit(solution)/shard_map/ppermute | solution.py:396
  46.1 2.0 %collective-permute-start.8 = (f32[256,512]{1,0:T(8,128)S(1)}, f32[256,512]{1,0:T(8,128)S(1)}, u32[]{:S(2)}, u32[]{:S(2)}) collective-permute-start(f32[256,512]{1,0:T(8,128)S(1)} %get-tuple-element.50), channel_id=1, source_target_pairs={{0,1},{1,0},{2,3},{3,2},{4,5},{5,4},{6,7},{7,6},{8,9},{9,8},{10,11... | collective-permute-start | bytes 1572872 | tf_op jit(solution)/shard_map/ppermute | solution.py:338
  48.1 13.6 %collective-permute-start.12 = (bf16[272,512]{1,0:T(8,128)(2,1)S(1)}, bf16[272,512]{1,0:T(8,128)(2,1)S(1)}, u32[]{:S(2)}, u32[]{:S(2)}) collective-permute-start(bf16[272,512]{1,0:T(8,128)(2,1)S(1)} %shard_map.90.refs_0_), channel_id=1, source_target_pairs={{0,4},{2,6},{4,0},{6,2},{8,12},{10,14},{12,8},{14,10},{1,5},{3,7},... | collective-permute-start | bytes 835592 | tf_op jit(solution)/shard_map/ppermute | solution.py:335
  48.7 13.1 %collective-permute-start.9 = (bf16[272,512]{1,0:T(8,128)(2,1)S(1)}, bf16[272,512]{1,0:T(8,128)(2,1)S(1)}, u32[]{:S(2)}, u32[]{:S(2)}) collective-permute-start(bf16[272,512]{1,0:T(8,128)(2,1)S(1)} %shard_map.90.refs_0_), channel_id=1, source_target_pairs={{0,2},{2,0},{4,6},{6,4},{8,10},{10,8},{12,14},{14,12},{1,3},{3,1},... | collective-permute-start | bytes 835592 | tf_op jit(solution)/shard_map/ppermute | solution.py:335
  49.3 15.8 %collective-permute-start.16 = (bf16[272,512]{1,0:T(8,128)(2,1)S(1)}, bf16[272,512]{1,0:T(8,128)(2,1)S(1)}, u32[]{:S(2)}, u32[]{:S(2)}) collective-permute-start(bf16[272,512]{1,0:T(8,128)(2,1)S(1)} %shard_map.90.refs_0_), channel_id=1, source_target_pairs={{0,8},{2,10},{4,12},{6,14},{8,0},{10,2},{12,4},{14,6},{1,9},{3,11}... | collective-permute-start | bytes 835592 | tf_op jit(solution)/shard_map/ppermute | solution.py:335
  61.8 3.3 %collective-permute-start.14 = (bf16[272,512]{1,0:T(8,128)(2,1)S(1)}, bf16[272,512]{1,0:T(8,128)(2,1)S(1)}, u32[]{:S(2)}, u32[]{:S(2)}) collective-permute-start(bf16[272,512]{1,0:T(8,128)(2,1)S(1)} %shard_map.92.refs_0_), channel_id=1, source_target_pairs={{0,1},{1,0},{2,3},{3,2},{4,5},{5,4},{6,7},{7,6},{8,9},{9,8},{10,11... | collective-permute-start | bytes 835592 | tf_op jit(solution)/shard_map/ppermute | solution.py:338
  61.8 4.0 %collective-permute-start.10 = (bf16[272,512]{1,0:T(8,128)(2,1)S(1)}, bf16[272,512]{1,0:T(8,128)(2,1)S(1)}, u32[]{:S(2)}, u32[]{:S(2)}) collective-permute-start(bf16[272,512]{1,0:T(8,128)(2,1)S(1)} %shard_map.90.refs_0_), channel_id=1, source_target_pairs={{0,1},{1,0},{2,3},{3,2},{4,5},{5,4},{6,7},{7,6},{8,9},{9,8},{10,11... | collective-permute-start | bytes 835592 | tf_op jit(solution)/shard_map/ppermute | solution.py:338
  62.3 9.5 %collective-permute-start.13 = (bf16[272,512]{1,0:T(8,128)(2,1)S(1)}, bf16[272,512]{1,0:T(8,128)(2,1)S(1)}, u32[]{:S(2)}, u32[]{:S(2)}) collective-permute-start(bf16[272,512]{1,0:T(8,128)(2,1)S(1)} %shard_map.92.refs_0_), channel_id=1, source_target_pairs={{0,2},{2,0},{4,6},{6,4},{8,10},{10,8},{12,14},{14,12},{1,3},{3,1},... | collective-permute-start | bytes 835592 | tf_op jit(solution)/shard_map/ppermute | solution.py:335
  62.3 9.5 %collective-permute-start.11 = (bf16[272,512]{1,0:T(8,128)(2,1)S(1)}, bf16[272,512]{1,0:T(8,128)(2,1)S(1)}, u32[]{:S(2)}, u32[]{:S(2)}) collective-permute-start(bf16[272,512]{1,0:T(8,128)(2,1)S(1)} %collective-permute-done.9.refs_1_), channel_id=1, source_target_pairs={{0,1},{1,0},{2,3},{3,2},{4,5},{5,4},{6,7},{7,6},{8,9},{9,8},{10,11... | collective-permute-start | bytes 835592 | tf_op jit(solution)/shard_map/ppermute | solution.py:338
  65.0 11.8 %collective-permute-start.17 = (bf16[272,512]{1,0:T(8,128)(2,1)S(1)}, bf16[272,512]{1,0:T(8,128)(2,1)S(1)}, u32[]{:S(2)}, u32[]{:S(2)}) collective-permute-start(bf16[272,512]{1,0:T(8,128)(2,1)S(1)} %shard_map.94.refs_0_), channel_id=1, source_target_pairs={{0,2},{2,0},{4,6},{6,4},{8,10},{10,8},{12,14},{14,12},{1,3},{3,1},... | collective-permute-start | bytes 835592 | tf_op jit(solution)/shard_map/ppermute | solution.py:335
  65.8 11.1 %collective-permute-start.20 = (bf16[272,512]{1,0:T(8,128)(2,1)S(1)}, bf16[272,512]{1,0:T(8,128)(2,1)S(1)}, u32[]{:S(2)}, u32[]{:S(2)}) collective-permute-start(bf16[272,512]{1,0:T(8,128)(2,1)S(1)} %shard_map.94.refs_0_), channel_id=1, source_target_pairs={{0,4},{2,6},{4,0},{6,2},{8,12},{10,14},{12,8},{14,10},{1,5},{3,7},... | collective-permute-start | bytes 835592 | tf_op jit(solution)/shard_map/ppermute | solution.py:335
  65.8 12.9 %collective-permute-start.18 = (bf16[272,512]{1,0:T(8,128)(2,1)S(1)}, bf16[272,512]{1,0:T(8,128)(2,1)S(1)}, u32[]{:S(2)}, u32[]{:S(2)}) collective-permute-start(bf16[272,512]{1,0:T(8,128)(2,1)S(1)} %shard_map.94.refs_0_), channel_id=1, source_target_pairs={{0,1},{1,0},{2,3},{3,2},{4,5},{5,4},{6,7},{7,6},{8,9},{9,8},{10,11... | collective-permute-start | bytes 835592 | tf_op jit(solution)/shard_map/ppermute | solution.py:338
  71.8 5.6 %collective-permute-start.15 = (bf16[272,512]{1,0:T(8,128)(2,1)S(1)}, bf16[272,512]{1,0:T(8,128)(2,1)S(1)}, u32[]{:S(2)}, u32[]{:S(2)}) collective-permute-start(bf16[272,512]{1,0:T(8,128)(2,1)S(1)} %collective-permute-done.13.refs_1_), channel_id=1, source_target_pairs={{0,1},{1,0},{2,3},{3,2},{4,5},{5,4},{6,7},{7,6},{8,9},{9,8},{10,11... | collective-permute-start | bytes 835592 | tf_op jit(solution)/shard_map/ppermute | solution.py:338
  76.9 1.9 %collective-permute-start.19 = (bf16[272,512]{1,0:T(8,128)(2,1)S(1)}, bf16[272,512]{1,0:T(8,128)(2,1)S(1)}, u32[]{:S(2)}, u32[]{:S(2)}) collective-permute-start(bf16[272,512]{1,0:T(8,128)(2,1)S(1)} %collective-permute-done.17.refs_1_), channel_id=1, source_target_pairs={{0,1},{1,0},{2,3},{3,2},{4,5},{5,4},{6,7},{7,6},{8,9},{9,8},{10,11... | collective-permute-start | bytes 835592 | tf_op jit(solution)/shard_map/ppermute | solution.py:338
  76.9 9.1 %collective-permute-start.21 = (bf16[272,512]{1,0:T(8,128)(2,1)S(1)}, bf16[272,512]{1,0:T(8,128)(2,1)S(1)}, u32[]{:S(2)}, u32[]{:S(2)}) collective-permute-start(bf16[272,512]{1,0:T(8,128)(2,1)S(1)} %shard_map.96.refs_0_), channel_id=1, source_target_pairs={{0,2},{2,0},{4,6},{6,4},{8,10},{10,8},{12,14},{14,12},{1,3},{3,1},... | collective-permute-start | bytes 835592 | tf_op jit(solution)/shard_map/ppermute | solution.py:335
  77.2 8.7 %collective-permute-start.22 = (bf16[272,512]{1,0:T(8,128)(2,1)S(1)}, bf16[272,512]{1,0:T(8,128)(2,1)S(1)}, u32[]{:S(2)}, u32[]{:S(2)}) collective-permute-start(bf16[272,512]{1,0:T(8,128)(2,1)S(1)} %shard_map.96.refs_0_), channel_id=1, source_target_pairs={{0,1},{1,0},{2,3},{3,2},{4,5},{5,4},{6,7},{7,6},{8,9},{9,8},{10,11... | collective-permute-start | bytes 835592 | tf_op jit(solution)/shard_map/ppermute | solution.py:338
  86.0 1.6 %collective-permute-start.23 = (bf16[272,512]{1,0:T(8,128)(2,1)S(1)}, bf16[272,512]{1,0:T(8,128)(2,1)S(1)}, u32[]{:S(2)}, u32[]{:S(2)}) collective-permute-start(bf16[272,512]{1,0:T(8,128)(2,1)S(1)} %shard_map.97.refs_1_), channel_id=1, source_target_pairs={{0,1},{1,0},{2,3},{3,2},{4,5},{5,4},{6,7},{7,6},{8,9},{9,8},{10,11... | collective-permute-start | bytes 835592 | tf_op jit(solution)/shard_map/ppermute | solution.py:338
  88.9 9.3 %slice-start = ((s8[12582912]{0:T(1024)(128)(4,1)}), s8[4194304]{0:T(1024)(128)(4,1)S(1)}, s32[]{:S(2)}) async-start(s8[12582912]{0:T(1024)(128)(4,1)} %bitcast.4), calls=%async_computation | async-start | bytes 8388608
  88.9 9.3 %slice-start.1 = ((s8[12582912]{0:T(1024)(128)(4,1)}), s8[4194304]{0:T(1024)(128)(4,1)S(1)}, s32[]{:S(2)}) async-start(s8[12582912]{0:T(1024)(128)(4,1)} %bitcast.4), calls=%async_computation.1 | async-start | bytes 8388608
  88.9 9.3 %slice-start.2 = ((s8[12582912]{0:T(1024)(128)(4,1)}), s8[4194304]{0:T(1024)(128)(4,1)S(1)}, s32[]{:S(2)}) async-start(s8[12582912]{0:T(1024)(128)(4,1)} %bitcast.4), calls=%async_computation.2 | async-start | bytes 8388608
  95.8 2.4 %collective-permute-start.24 = (bf16[8,128,384]{2,1,0:T(8,128)(2,1)S(1)}, bf16[8,128,384]{2,1,0:T(8,128)(2,1)S(1)}, u32[]{:S(2)}, u32[]{:S(2)}) collective-permute-start(bf16[8,128,384]{2,1,0:T(8,128)(2,1)S(1)} %shard_map.99.near_ref), channel_id=1, source_target_pairs={{0,1},{1,0},{2,3},{3,2},{4,5},{5,4},{6,7},{7,6},{8,9},{9,8},{10,11... | collective-permute-start | bytes 2359304 | tf_op jit(solution)/shard_map/ppermute | solution.py:338
  101.1 9.2 %collective-permute-start.25 = (bf16[128,1024]{1,0:T(8,128)(2,1)S(1)}, bf16[128,1024]{1,0:T(8,128)(2,1)S(1)}, u32[]{:S(2)}, u32[]{:S(2)}) collective-permute-start(bf16[128,1024]{1,0:T(8,128)(2,1)S(1)} %get-tuple-element.73), channel_id=1, source_target_pairs={{0,2},{2,0},{4,6},{6,4},{8,10},{10,8},{12,14},{14,12},{1,3},{3,1},... | collective-permute-start | bytes 786440 | tf_op jit(solution)/shard_map/ppermute | solution.py:335
  101.5 14.5 %collective-permute-start.27 = (bf16[128,1024]{1,0:T(8,128)(2,1)S(1)}, bf16[128,1024]{1,0:T(8,128)(2,1)S(1)}, u32[]{:S(2)}, u32[]{:S(2)}) collective-permute-start(bf16[128,1024]{1,0:T(8,128)(2,1)S(1)} %get-tuple-element.75), channel_id=1, source_target_pairs={{0,2},{2,0},{4,6},{6,4},{8,10},{10,8},{12,14},{14,12},{1,3},{3,1},... | collective-permute-start | bytes 786440 | tf_op jit(solution)/shard_map/ppermute | solution.py:335
  103.2 18.4 %collective-permute-start.29 = (bf16[128,1024]{1,0:T(8,128)(2,1)S(1)}, bf16[128,1024]{1,0:T(8,128)(2,1)S(1)}, u32[]{:S(2)}, u32[]{:S(2)}) collective-permute-start(bf16[128,1024]{1,0:T(8,128)(2,1)S(1)} %get-tuple-element.77), channel_id=1, source_target_pairs={{0,2},{2,0},{4,6},{6,4},{8,10},{10,8},{12,14},{14,12},{1,3},{3,1},... | collective-permute-start | bytes 786440 | tf_op jit(solution)/shard_map/ppermute | solution.py:335
  103.5 22.9 %collective-permute-start.31 = (bf16[128,1024]{1,0:T(8,128)(2,1)S(1)}, bf16[128,1024]{1,0:T(8,128)(2,1)S(1)}, u32[]{:S(2)}, u32[]{:S(2)}) collective-permute-start(bf16[128,1024]{1,0:T(8,128)(2,1)S(1)} %get-tuple-element.78), channel_id=1, source_target_pairs={{0,2},{2,0},{4,6},{6,4},{8,10},{10,8},{12,14},{14,12},{1,3},{3,1},... | collective-permute-start | bytes 786440 | tf_op jit(solution)/shard_map/ppermute | solution.py:335
  110.4 16.0 %collective-permute-start.26 = (bf16[128,1024]{1,0:T(8,128)(2,1)S(1)}, bf16[128,1024]{1,0:T(8,128)(2,1)S(1)}, u32[]{:S(2)}, u32[]{:S(2)}) collective-permute-start(bf16[128,1024]{1,0:T(8,128)(2,1)S(1)} %add_convert_fusion.2), channel_id=1, source_target_pairs={{0,12},{2,14},{4,8},{6,10},{8,4},{10,6},{12,0},{14,2},{1,13},{3,15... | collective-permute-start | bytes 786440 | tf_op jit(solution)/shard_map/ppermute | solution.py:335
  116.1 17.0 %collective-permute-start.28 = (bf16[128,1024]{1,0:T(8,128)(2,1)S(1)}, bf16[128,1024]{1,0:T(8,128)(2,1)S(1)}, u32[]{:S(2)}, u32[]{:S(2)}) collective-permute-start(bf16[128,1024]{1,0:T(8,128)(2,1)S(1)} %add_convert_fusion.1), channel_id=1, source_target_pairs={{0,8},{2,10},{4,12},{6,14},{8,0},{10,2},{12,4},{14,6},{1,9},{3,11}... | collective-permute-start | bytes 786440 | tf_op jit(solution)/shard_map/ppermute | solution.py:335
  121.7 12.4 %collective-permute-start.30 = (bf16[128,1024]{1,0:T(8,128)(2,1)S(1)}, bf16[128,1024]{1,0:T(8,128)(2,1)S(1)}, u32[]{:S(2)}, u32[]{:S(2)}) collective-permute-start(bf16[128,1024]{1,0:T(8,128)(2,1)S(1)} %add_convert_fusion), channel_id=1, source_target_pairs={{0,4},{2,6},{4,0},{6,2},{8,12},{10,14},{12,8},{14,10},{1,5},{3,7},... | collective-permute-start | bytes 786440 | tf_op jit(solution)/shard_map/ppermute | solution.py:335

commit v8 on v7

--- a/solution.py
+++ b/solution.py
@@ -280,7 +280,7 @@
 
 
 def output_kernel(steps, near_ref, far_ref, w_ref, *refs):
-    back_refs, out_refs, held_ref = refs[:steps], refs[steps : 3 * steps], refs[-1]
+    back_refs, out_refs, held_ref = refs[:steps], refs[steps:-1], refs[-1]
     part = lax.axis_index("sub")
     units = near_ref.shape[2] // 2
     for e in range(near_ref.shape[0]):
@@ -295,17 +295,28 @@
                 source * SLOTS : (source + 1) * SLOTS
             ]
     for source in range(2 * steps):
-        out_refs[source][...] = jnp.dot(
+        routed = jnp.dot(
             back_refs[source // 2][source % 2], held_ref[source], preferred_element_type=F32
         ).astype(BF16)
-
-
-def final_kernel(state_ref, mod_ref, *refs):
-    routed = sum(ref[...].astype(F32) for ref in refs[:-1])
-    lanes = state_ref.shape[1]
+        if source < 2:
+            out_refs[source][...] = routed
+        else:
+            half = routed.shape[0] // 2
+            out_refs[2 * source - 2][...] = routed[:half]
+            out_refs[2 * source - 1][...] = routed[half:]
+
+
+def final_kernel(tops, state_ref, mod_ref, *refs):
+    out_ref = refs[-1]
+    count, lanes = state_ref.shape
     at = pl.multiple_of(lax.axis_index("sub") * lanes, 128)
     lift = 1.0 + mod_ref[3:4, pl.ds(at, lanes)]
-    refs[-1][...] = (state_ref[...].astype(F32) + lift * routed).astype(BF16)
+    for h, terms in enumerate((refs[2 : 2 + tops], refs[2 + tops : -1])):
+        rows = slice(h * count // 2, (h + 1) * count // 2)
+        routed = refs[0][rows].astype(F32) + refs[1][rows].astype(F32)
+        for ref in terms:
+            routed += ref[...].astype(F32)
+        out_ref[rows] = (state_ref[rows].astype(F32) + lift * routed).astype(BF16)
 
 
 def gathered_body(
@@ -463,27 +474,41 @@
     )(*picked, *ups)
     share = pl.pallas_call(
         functools.partial(output_kernel, steps),
-        out_shape=[struct((count, 2 * lanes), BF16)] * sources,
+        out_shape=[struct((count, 2 * lanes), BF16)] * 2
+        + [struct((count // 2, 2 * lanes), BF16)] * (2 * sources - 4),
         in_specs=[whole()] * (3 + steps),
-        out_specs=[whole()] * sources,
+        out_specs=[whole()] * (2 * sources - 2),
         scratch_shapes=[pltpu.VMEM((sources, slots, 2 * lanes), BF16)],
         compiler_params=vmem(8),
     )(hidden, swap(hidden), down_weight, *backs)
 
-    terms = [share[0]]
-    for flip in range(steps - 1, -1, -1):
-        crossed = hop(share[2 * flip + 1], 1)
-        if flip:
-            crossed = (share[2 * flip].astype(F32) + crossed.astype(F32)).astype(BF16)
-            crossed = hop(crossed, 2 * flip)
-        terms.append(crossed)
+    def added(x, y):
+        return (x.astype(F32) + y.astype(F32)).astype(BF16)
+
+    parts = {j: list(share[4 * j - 2 : 4 * j + 2]) for j in range(1, steps)}
+    crossed = {
+        (j, h): hop(parts[j][2 + h], 1) for j in range(steps - 1, 0, -1) for h in range(2)
+    }
+    across = hop(share[1], 1)
+    merged = {}
+    tops, bottoms = [], []
+    for j in range(steps - 1, 0, -1):
+        tops.append(hop(added(parts[j][0], crossed[j, 0]), 2 * j))
+        bottom = added(parts[j][1], crossed[j, 1])
+        for extra in merged.get(j, []):
+            bottom = added(bottom, extra)
+        low = j & -j
+        if j == low:
+            bottoms.append(hop(bottom, 2 * j))
+        else:
+            merged.setdefault(j - low, []).append(hop(bottom, 2 * low))
     return pl.pallas_call(
-        final_kernel,
+        functools.partial(final_kernel, len(tops)),
         out_shape=struct((count, 2 * lanes), BF16),
-        in_specs=[whole()] * (2 + len(terms)),
+        in_specs=[whole()] * (4 + len(tops) + len(bottoms)),
         out_specs=whole(),
         compiler_params=vmem(8),
-    )(state, small, *terms)
+    )(state, small, share[0], across, *tops, *bottoms)
 
 
 def extended(cells, sides, width):

time: 135 us -> 137 us (1.015)
  starting transfers between devices: 25.5 us -> 30.3 us
  waiting for transfers between devices: 77.2 us -> 74 us
    ppermute x19 -> x25, starting transfers between devices: 20.8 us -> 25.5 us  [hop(): return lax.ppermute(x, 'dev', [(i, i ^ flip) for i in range(devices)])]
    ppermute x19 -> x25, waiting for transfers between devices: 71.6 us -> 68.4 us  [hop(): return lax.ppermute(x, 'dev', [(i, i ^ flip) for i in range(devices)])]
  transfers between devices with their start and end apart: 32 -> 38, of which waited for: 17 -> 19; matrix products, arithmetic and copies ran while one was open for 0% -> 0% of each run, Pallas kernels for 11% -> 11%
where the time goes in v8:
time: 137 us
  waiting for transfers between devices  74 us (54%)
  Pallas kernels  31.8 us (23%)
  starting transfers between devices  30.3 us (22%)
    ppermute x25, waiting for transfers between devices, hop(): return lax.ppermute(x, 'dev', [(i, i ^ flip) for i in range(devices)])  68.4 us
    ppermute x25, starting transfers between devices, hop(): return lax.ppermute(x, 'dev', [(i, i ^ flip) for i in range(devices)])  25.5 us
    pallas_call x1, Pallas kernels, load(): pl.pallas_call(load_kernel, out_shape=[piece] * local + [jax.ShapeDtypeSt...  8.33 us
    pallas_call x1, Pallas kernels, gathered_body(): pl.pallas_call(functools.partial(hidden_kernel, steps), out_shape=struct(...  6.92 us
    ppermute x10, waiting for transfers between devices, swap(): return lax.ppermute(x, 'sub', [(0, 1), (1, 0)])  5.61 us
    pallas_call x4, Pallas kernels, gathered_body(): pl.pallas_call(functools.partial(select_kernel, local, topk, own), out_sh...  5.29 us
    pallas_call x1, Pallas kernels, gathered_body(): pl.pallas_call(attention_kernel, out_shape=struct((count, local_width), B...  3.1 us
    ppermute x2, starting transfers between devices, gathered_body(): theirs = lax.ppermute(mine[flip], 'groups', [(0, 1), (1, 0)])  3.04 us
  transfers between devices with their start and end apart: 38, of which 19 were waited for; matrix products, arithmetic and copies ran while one was open for 0% of the time, Pallas kernels for 11%

profile of v8, /device:TPU:0, one launch (start us, length us, event | category | flops | bytes accessed | tf_op | source)
XLA Modules:
  0.0 136.6 jit_solution(14674261568681115168)
XLA Ops:
  0.0 2.7 %shard_map.82 = (bf16[128,1024]{1,0:T(8,128)(2,1)S(1)}, bf16[256,1024]{1,0:T(8,128)(2,1)S(1)}, bf16[128,512]{1,0:T(8,128)(2,1)S(1)}, bf16[320,1024]{1,0:T(8,128)...) custom-call(bf16[128,2048]{1,0:T(8,128)(2,1)} %tokens_ref.1, bf16[3,128,1024]{2,1,0:T(8,128)(2,1)} %bitcast.9, ...), custom_call_target="tpu_custom_call" | custom-call | tf_op jit(solution)/shard_map/pallas_call | solution.py:353
  2.7 3.0 %collective-permute-start = (bf16[320,1024]{1,0:T(8,128)(2,1)}, bf16[320,1024]{1,0:T(8,128)(2,1)S(1)}, u32[]{:S(2)}, u32[]{:S(2)}) collective-permute-start(bf16[320,1024]{1,0:T(8,128)(2,1)} %get-tuple-element.50), channel_id=1, source_target_pairs={{0,2},{2,0},{4,6},{6,4},{8,10},{10,8},{12,14},{14,12},{1,3},{3,1},... | collective-permute-start | bytes 1966088 | tf_op jit(solution)/shard_map/ppermute | solution.py:346
  5.7 2.6 %collective-permute-start.3 = (bf16[128,1024]{1,0:T(8,128)(2,1)S(1)}, bf16[128,1024]{1,0:T(8,128)(2,1)S(1)}, u32[]{:S(2)}, u32[]{:S(2)}) collective-permute-start(bf16[128,1024]{1,0:T(8,128)(2,1)S(1)} %get-tuple-element.53), channel_id=1, source_target_pairs={{0,8},{2,10},{4,12},{6,14},{8,0},{10,2},{12,4},{14,6},{1,9},{3,11}... | collective-permute-start | bytes 786440 | tf_op jit(solution)/shard_map/ppermute | solution.py:346
  8.3 0.7 collective-permute-start.1
  9.0 0.0 copy-start
  9.0 0.0 copy-start.1
  9.0 0.0 copy-start.2
  9.0 8.3 %shard_map.85 = (bf16[2,2,192,2048]{3,2,1,0:T(8,128)(2,1)S(1)}, bf16[2,2,192,2048]{3,2,1,0:T(8,128)(2,1)S(1)}, bf16[2,2,192,2048]{3,2,1,0:T(8,128)(2,1)S(1)}, bf...) custom-call(bf16[16,2,192,2048]{3,2,1,0:T(8,128)(2,1)} %bitcast.8, ...), custom_call_target="tpu_custom_call" | custom-call | tf_op jit(solution)/shard_map/pallas_call | solution.py:260
  17.3 3.8 %collective-permute-done.3.refs_0_ = bf16[128,1024]{1,0:T(8,128)(2,1)S(1)} collective-permute-done((bf16[128,1024]{1,0:T(8,128)(2,1)S(1)}, bf16[128,1024]{1,0:T(8,128)(2,1)S(1)}, u32[]{:S(2)}, u32[]{:S(2)}) %collective-permute-start.3) | collective-permute-done | bytes 262176 | tf_op jit(solution)/shard_map/ppermute | solution.py:346
  21.1 2.0 %collective-permute-start.4 = (bf16[256,1024]{1,0:T(8,128)(2,1)S(1)}, bf16[256,1024]{1,0:T(8,128)(2,1)S(1)}, u32[]{:S(2)}, u32[]{:S(2)}) collective-permute-start(bf16[256,1024]{1,0:T(8,128)(2,1)S(1)} %shard_map.87.refs_2_), channel_id=1, source_target_pairs={{0,4},{2,6},{4,0},{6,2},{8,12},{10,14},{12,8},{14,10},{1,5},{3,7},... | collective-permute-start | bytes 1572872 | tf_op jit(solution)/shard_map/ppermute | solution.py:346
  23.2 1.5 %collective-permute-start.5 = (bf16[128,1024]{1,0:T(8,128)(2,1)S(1)}, bf16[128,1024]{1,0:T(8,128)(2,1)S(1)}, u32[]{:S(2)}, u32[]{:S(2)}) collective-permute-start(bf16[128,1024]{1,0:T(8,128)(2,1)S(1)} %shard_map.86.refs_1_.refs_4_), channel_id=1, source_target_pairs={{0,16},{16,0},{1,17},{17,1},{2,18},{18,2},{3,19},{19,3},{4,20},{20... | collective-permute-start | bytes 786440 | tf_op jit(solution)/shard_map/ppermute | solution.py:407
  24.8 0.0 collective-permute-done.1.next_ref
  24.8 6.4 %collective-permute-done.cross_ref = bf16[320,1024]{1,0:T(8,128)(2,1)S(1)} collective-permute-done((bf16[320,1024]{1,0:T(8,128)(2,1)}, bf16[320,1024]{1,0:T(8,128)(2,1)S(1)}, u32[]{:S(2)}, u32[]{:S(2)}) %collective-permute-start) | collective-permute-done | bytes 655392 | tf_op jit(solution)/shard_map/ppermute | solution.py:346
  31.2 3.1 %shard_map.84.refs_1_.refs_0_ = bf16[128,1024]{1,0:T(8,128)(2,1)S(1)} custom-call(bf16[128,1024]{1,0:T(8,128)(2,1)S(1)} %get-tuple-element.48._.query_ref, bf16[256,1024]{1,0:T(8,128)(2,1)S(1)} %get-tuple-element.49.own_ref, bf16[320,1024]{1,0:T(8,128)(2,1)S(1)} %collective-permute-done.cross_ref, bf16[256,1024]{1,0:T(8,128)(2,1)S(1)} %collective-permute-done.1.next_ref, ...), custom_call_target="tpu_custom_call" | custom-call | tf_op jit(solution)/shard_map/pallas_call | solution.py:396
  34.3 2.4 %collective-permute-start.2 = (bf16[128,1024]{1,0:T(8,128)(2,1)S(1)}, bf16[128,1024]{1,0:T(8,128)(2,1)S(1)}, u32[]{:S(2)}, u32[]{:S(2)}) collective-permute-start(bf16[128,1024]{1,0:T(8,128)(2,1)S(1)} %shard_map.84.refs_1_.refs_0_), channel_id=1, source_target_pairs={{0,2},{2,0},{4,6},{6,4},{8,10},{10,8},{12,14},{14,12},{1,3},{3,1},... | collective-permute-start | bytes 786440 | tf_op jit(solution)/shard_map/ppermute | solution.py:346
  36.7 1.5 %collective-permute-start.7 = (bf16[128,1024]{1,0:T(8,128)(2,1)S(1)}, bf16[128,1024]{1,0:T(8,128)(2,1)S(1)}, u32[]{:S(2)}, u32[]{:S(2)}) collective-permute-start(bf16[128,1024]{1,0:T(8,128)(2,1)S(1)} %shard_map.88.refs_6_), channel_id=1, source_target_pairs={{0,16},{16,0},{1,17},{17,1},{2,18},{18,2},{3,19},{19,3},{4,20},{20... | collective-permute-start | bytes 786440 | tf_op jit(solution)/shard_map/ppermute | solution.py:407
  38.2 6.4 %collective-permute-done.4.refs_3_ = bf16[256,1024]{1,0:T(8,128)(2,1)S(1)} collective-permute-done((bf16[256,1024]{1,0:T(8,128)(2,1)S(1)}, bf16[256,1024]{1,0:T(8,128)(2,1)S(1)}, u32[]{:S(2)}, u32[]{:S(2)}) %collective-permute-start.4) | collective-permute-done | bytes 524320 | tf_op jit(solution)/shard_map/ppermute | solution.py:346
  44.6 1.4 %shard_map.89 = (f32[256,512]{1,0:T(8,128)S(1)}, f32[256,512]{1,0:T(8,128)S(1)}) custom-call(bf16[128,1024]{1,0:T(8,128)(2,1)S(1)} %shard_map.84.refs_1_.refs_0_, bf16[128,1024]{1,0:T(8,128)(2,1)S(1)} %collective-permute-done.2.refs_1_, bf16[256,1024]{1,0:T(8,128)(2,1)S(1)} %shard_map.87.refs_2_, bf16[256,1024]{1,0:T(8,128)(2,1)S(1)} %collective-permute-done.4.refs_3_, ...), custom_call_target="tpu_custom_call" | custom-call | tf_op jit(solution)/shard_map/pallas_call | solution.py:413
  46.1 0.1 collective-permute-start.8
  46.2 1.9 %collective-permute-done.8.got_ref = f32[256,512]{1,0:T(8,128)S(1)} collective-permute-done((f32[256,512]{1,0:T(8,128)S(1)}, f32[256,512]{1,0:T(8,128)S(1)}, u32[]{:S(2)}, u32[]{:S(2)}) %collective-permute-start.8) | collective-permute-done | bytes 524320 | tf_op jit(solution)/shard_map/ppermute | solution.py:349
  48.1 0.1 shard_map.90.refs_0_
  48.2 0.6 collective-permute-start.12
  48.7 0.5 collective-permute-start.9
  49.3 3.4 %collective-permute-start.16 = (bf16[272,512]{1,0:T(8,128)(2,1)S(1)}, bf16[272,512]{1,0:T(8,128)(2,1)S(1)}, u32[]{:S(2)}, u32[]{:S(2)}) collective-permute-start(bf16[272,512]{1,0:T(8,128)(2,1)S(1)} %shard_map.90.refs_0_), channel_id=1, source_target_pairs={{0,8},{2,10},{4,12},{6,14},{8,0},{10,2},{12,4},{14,6},{1,9},{3,11}... | collective-permute-start | bytes 835592 | tf_op jit(solution)/shard_map/ppermute | solution.py:346
  52.6 9.2 %collective-permute-done.12.refs_0_ = bf16[272,512]{1,0:T(8,128)(2,1)S(1)} collective-permute-done((bf16[272,512]{1,0:T(8,128)(2,1)S(1)}, bf16[272,512]{1,0:T(8,128)(2,1)S(1)}, u32[]{:S(2)}, u32[]{:S(2)}) %collective-permute-start.12) | collective-permute-done | bytes 278560 | tf_op jit(solution)/shard_map/ppermute | solution.py:346
  61.8 0.5 collective-permute-start.10
  62.3 0.1 collective-permute-start.11
  62.4 2.7 %collective-permute-done.16.refs_0_ = bf16[272,512]{1,0:T(8,128)(2,1)S(1)} collective-permute-done((bf16[272,512]{1,0:T(8,128)(2,1)S(1)}, bf16[272,512]{1,0:T(8,128)(2,1)S(1)}, u32[]{:S(2)}, u32[]{:S(2)}) %collective-permute-start.16) | collective-permute-done | bytes 278560 | tf_op jit(solution)/shard_map/ppermute | solution.py:346
  65.1 0.8 collective-permute-start.17
  65.8 6.0 %collective-permute-done.13.refs_1_ = bf16[272,512]{1,0:T(8,128)(2,1)S(1)} collective-permute-done((bf16[272,512]{1,0:T(8,128)(2,1)S(1)}, bf16[272,512]{1,0:T(8,128)(2,1)S(1)}, u32[]{:S(2)}, u32[]{:S(2)}) %collective-permute-start.13) | collective-permute-done | bytes 278560 | tf_op jit(solution)/shard_map/ppermute | solution.py:346
  71.8 1.3 shard_map.91
  73.2 3.7 %collective-permute-done.17.refs_1_ = bf16[272,512]{1,0:T(8,128)(2,1)S(1)} collective-permute-done((bf16[272,512]{1,0:T(8,128)(2,1)S(1)}, bf16[272,512]{1,0:T(8,128)(2,1)S(1)}, u32[]{:S(2)}, u32[]{:S(2)}) %collective-permute-start.17) | collective-permute-done | bytes 278560 | tf_op jit(solution)/shard_map/ppermute | solution.py:346
  76.9 0.3 collective-permute-start.21
  77.3 0.2 collective-permute-start.22
  77.4 1.3 shard_map.93
  78.8 1.3 shard_map.95
  80.1 5.9 %collective-permute-done.21.refs_0_ = bf16[272,512]{1,0:T(8,128)(2,1)S(1)} collective-permute-done((bf16[272,512]{1,0:T(8,128)(2,1)S(1)}, bf16[272,512]{1,0:T(8,128)(2,1)S(1)}, u32[]{:S(2)}, u32[]{:S(2)}) %collective-permute-start.21) | collective-permute-done | bytes 278560 | tf_op jit(solution)/shard_map/ppermute | solution.py:346
  86.0 1.6 %collective-permute-done.23.refs_3_ = bf16[272,512]{1,0:T(8,128)(2,1)S(1)} collective-permute-done((bf16[272,512]{1,0:T(8,128)(2,1)S(1)}, bf16[272,512]{1,0:T(8,128)(2,1)S(1)}, u32[]{:S(2)}, u32[]{:S(2)}) %collective-permute-start.23) | collective-permute-done | bytes 278560 | tf_op jit(solution)/shard_map/ppermute | solution.py:349
  87.6 1.3 shard_map.98
  88.9 0.0 slice-start
  88.9 6.9 %shard_map.99.near_ref = bf16[8,128,384]{2,1,0:T(8,128)(2,1)S(1)} custom-call(bf16[8,32,2048]{2,1,0:T(8,128)(2,1)S(1)} %get-tuple-element.61.refs_1_.refs_0_, bf16[8,32,2048]{2,1,0:T(8,128)(2,1)S(1)} %get-tuple-element.62.refs_1_, bf16[8,32,2048]{2,1,0:T(8,128)(2,1)S(1)} %get-tuple-element.63.refs_2_, bf16[8,32,2048]{2,1,0:T(8,128)(2,1)S(1)} %get-tuple-element.64.refs_3_, ...), custom_call_target="tpu_custom_call" | custom-call | tf_op jit(solution)/shard_map/pallas_call | solution.py:468
  95.8 0.2 collective-permute-start.24
  96.0 2.1 %collective-permute-done.24.far_ref = bf16[8,128,384]{2,1,0:T(8,128)(2,1)S(1)} collective-permute-done((bf16[8,128,384]{2,1,0:T(8,128)(2,1)S(1)}, bf16[8,128,384]{2,1,0:T(8,128)(2,1)S(1)}, u32[]{:S(2)}, u32[]{:S(2)}) %collective-permute-start.24) | collective-permute-done | bytes 786464 | tf_op jit(solution)/shard_map/ppermute | solution.py:349
  98.2 3.0 %shard_map.100 = (bf16[128,1024]{1,0:T(8,128)(2,1)S(1)}, bf16[128,1024]{1,0:T(8,128)(2,1)S(1)}, bf16[64,1024]{1,0:T(8,128)(2,1)S(1)}, bf16[64,1024]{1,0:T(8,128)...) custom-call(bf16[8,128,384]{2,1,0:T(8,128)(2,1)S(1)} %shard_map.99.n, ...), custom_call_target="tpu_custom_call" | custom-call | tf_op jit(solution)/shard_map/pallas_call | solution.py:475
  101.2 0.4 collective-permute-start.26
  101.6 1.7 %collective-permute-start.28 = (bf16[64,1024]{1,0:T(8,128)(2,1)S(1)}, bf16[64,1024]{1,0:T(8,128)(2,1)S(1)}, u32[]{:S(2)}, u32[]{:S(2)}) collective-permute-start(bf16[64,1024]{1,0:T(8,128)(2,1)S(1)} %get-tuple-element.82), channel_id=1, source_target_pairs={{0,2},{2,0},{4,6},{6,4},{8,10},{10,8},{12,14},{14,12},{1,3},{3,1},... | collective-permute-start | bytes 393224 | tf_op jit(solution)/shard_map/ppermute | solution.py:346
  103.3 0.3 collective-permute-start.30
  103.6 1.7 %collective-permute-start.32 = (bf16[64,1024]{1,0:T(8,128)(2,1)S(1)}, bf16[64,1024]{1,0:T(8,128)(2,1)S(1)}, u32[]{:S(2)}, u32[]{:S(2)}) collective-permute-start(bf16[64,1024]{1,0:T(8,128)(2,1)S(1)} %get-tuple-element.86), channel_id=1, source_target_pairs={{0,2},{2,0},{4,6},{6,4},{8,10},{10,8},{12,14},{14,12},{1,3},{3,1},... | collective-permute-start | bytes 393224 | tf_op jit(solution)/shard_map/ppermute | solution.py:346
  105.3 0.3 collective-permute-start.33
  105.6 2.0 %collective-permute-done.26 = bf16[64,1024]{1,0:T(8,128)(2,1)S(1)} collective-permute-done((bf16[64,1024]{1,0:T(8,128)(2,1)S(1)}, bf16[64,1024]{1,0:T(8,128)(2,1)S(1)}, u32[]{:S(2)}, u32[]{:S(2)}) %collective-permute-start.26) | collective-permute-done | bytes 131104 | tf_op jit(solution)/shard_map/ppermute | solution.py:346
  107.6 0.3 collective-permute-start.36
  107.9 2.5 %collective-permute-done.28 = bf16[64,1024]{1,0:T(8,128)(2,1)S(1)} collective-permute-done((bf16[64,1024]{1,0:T(8,128)(2,1)S(1)}, bf16[64,1024]{1,0:T(8,128)(2,1)S(1)}, u32[]{:S(2)}, u32[]{:S(2)}) %collective-permute-start.28) | collective-permute-done | bytes 131104 | tf_op jit(solution)/shard_map/ppermute | solution.py:346
  110.4 0.3 collective-permute-start.25
  110.7 2.5 %collective-permute-done.30 = bf16[64,1024]{1,0:T(8,128)(2,1)S(1)} collective-permute-done((bf16[64,1024]{1,0:T(8,128)(2,1)S(1)}, bf16[64,1024]{1,0:T(8,128)(2,1)S(1)}, u32[]{:S(2)}, u32[]{:S(2)}) %collective-permute-start.30) | collective-permute-done | bytes 131104 | tf_op jit(solution)/shard_map/ppermute | solution.py:346
  113.2 0.8 collective-permute-start.27
  114.0 4.8 %collective-permute-done.33 = bf16[64,1024]{1,0:T(8,128)(2,1)S(1)} collective-permute-done((bf16[64,1024]{1,0:T(8,128)(2,1)S(1)}, bf16[64,1024]{1,0:T(8,128)(2,1)S(1)}, u32[]{:S(2)}, u32[]{:S(2)}) %collective-permute-start.33) | collective-permute-done | bytes 131104 | tf_op jit(solution)/shard_map/ppermute | solution.py:346
  118.9 2.8 %collective-permute-done.36 = bf16[64,1024]{1,0:T(8,128)(2,1)S(1)} collective-permute-done((bf16[64,1024]{1,0:T(8,128)(2,1)S(1)}, bf16[64,1024]{1,0:T(8,128)(2,1)S(1)}, u32[]{:S(2)}, u32[]{:S(2)}) %collective-permute-start.36) | collective-permute-done | bytes 131104 | tf_op jit(solution)/shard_map/ppermute | solution.py:346
  121.7 2.1 %collective-permute-start.31 = (bf16[64,1024]{1,0:T(8,128)(2,1)S(1)}, bf16[64,1024]{1,0:T(8,128)(2,1)S(1)}, u32[]{:S(2)}, u32[]{:S(2)}) collective-permute-start(bf16[64,1024]{1,0:T(8,128)(2,1)S(1)} %add_convert_fusion.4), channel_id=1, source_target_pairs={{0,4},{2,6},{4,0},{6,2},{8,12},{10,14},{12,8},{14,10},{1,5},{3,7},... | collective-permute-start | bytes 393224 | tf_op jit(solution)/shard_map/ppermute | solution.py:346
  123.8 4.8 %collective-permute-done.34 = bf16[64,1024]{1,0:T(8,128)(2,1)S(1)} collective-permute-done((bf16[64,1024]{1,0:T(8,128)(2,1)S(1)}, bf16[64,1024]{1,0:T(8,128)(2,1)S(1)}, u32[]{:S(2)}, u32[]{:S(2)}) %collective-permute-start.34) | collective-permute-done | bytes 131104 | tf_op jit(solution)/shard_map/ppermute | solution.py:346
  128.6 0.1 add_convert_fusion.1
  128.6 2.0 %collective-permute-start.35 = (bf16[64,1024]{1,0:T(8,128)(2,1)S(1)}, bf16[64,1024]{1,0:T(8,128)(2,1)S(1)}, u32[]{:S(2)}, u32[]{:S(2)}) collective-permute-start(bf16[64,1024]{1,0:T(8,128)(2,1)S(1)} %add_convert_fusion.1), channel_id=1, source_target_pairs={{0,8},{2,10},{4,12},{6,14},{8,0},{10,2},{12,4},{14,6},{1,9},{3,11}... | collective-permute-start | bytes 393224 | tf_op jit(solution)/shard_map/ppermute | solution.py:346
  130.6 2.2 %collective-permute-done.31.refs_4_ = bf16[64,1024]{1,0:T(8,128)(2,1)S(1)} collective-permute-done((bf16[64,1024]{1,0:T(8,128)(2,1)S(1)}, bf16[64,1024]{1,0:T(8,128)(2,1)S(1)}, u32[]{:S(2)}, u32[]{:S(2)}) %collective-permute-start.31) | collective-permute-done | bytes 131104 | tf_op jit(solution)/shard_map/ppermute | solution.py:346
  132.8 2.9 %collective-permute-done.37.refs_6_ = bf16[64,1024]{1,0:T(8,128)(2,1)S(1)} collective-permute-done((bf16[64,1024]{1,0:T(8,128)(2,1)S(1)}, bf16[64,1024]{1,0:T(8,128)(2,1)S(1)}, u32[]{:S(2)}, u32[]{:S(2)}) %collective-permute-start.37) | collective-permute-done | bytes 131104 | tf_op jit(solution)/shard_map/ppermute | solution.py:346
  135.7 0.9 shard_map.101
  (51 shorter events, 0.3 us)
Async XLA Ops:
  2.7 28.5 %collective-permute-start = (bf16[320,1024]{1,0:T(8,128)(2,1)}, bf16[320,1024]{1,0:T(8,128)(2,1)S(1)}, u32[]{:S(2)}, u32[]{:S(2)}) collective-permute-start(bf16[320,1024]{1,0:T(8,128)(2,1)} %get-tuple-element.50), channel_id=1, source_target_pairs={{0,2},{2,0},{4,6},{6,4},{8,10},{10,8},{12,14},{14,12},{1,3},{3,1},... | collective-permute-start | bytes 1966088 | tf_op jit(solution)/shard_map/ppermute | solution.py:346
  5.7 15.4 %collective-permute-start.3 = (bf16[128,1024]{1,0:T(8,128)(2,1)S(1)}, bf16[128,1024]{1,0:T(8,128)(2,1)S(1)}, u32[]{:S(2)}, u32[]{:S(2)}) collective-permute-start(bf16[128,1024]{1,0:T(8,128)(2,1)S(1)} %get-tuple-element.53), channel_id=1, source_target_pairs={{0,8},{2,10},{4,12},{6,14},{8,0},{10,2},{12,4},{14,6},{1,9},{3,11}... | collective-permute-start | bytes 786440 | tf_op jit(solution)/shard_map/ppermute | solution.py:346
  8.3 16.5 %collective-permute-start.1 = (bf16[256,1024]{1,0:T(8,128)(2,1)S(1)}, bf16[256,1024]{1,0:T(8,128)(2,1)S(1)}, u32[]{:S(2)}, u32[]{:S(2)}) collective-permute-start(bf16[256,1024]{1,0:T(8,128)(2,1)S(1)} %get-tuple-element.49.own_ref), channel_id=1, source_target_pairs={{2,4},{6,8},{10,12},{4,2},{8,6},{12,10},{3,5},{7,9},{11,13},{5,3},... | collective-permute-start | bytes 1572872 | tf_op jit(solution)/shard_map/ppermute | solution.py:380
  9.0 14.2 %copy-start = (bf16[2048,64]{0,1:T(8,128)(2,1)S(1)}, bf16[2048,64]{0,1:T(8,128)(2,1)}, u32[]{:S(2)}) copy-start(bf16[2048,64]{0,1:T(8,128)(2,1)} %param.12) | copy-start | bytes 786436
  9.0 14.2 %copy-start.1 = (f32[4,2048]{1,0:T(4,128)S(1)}, f32[4,2048]{1,0:T(4,128)}, u32[]{:S(2)}) copy-start(f32[4,2048]{1,0:T(4,128)} %mod_ref.1) | copy-start | bytes 98308
  9.0 14.2 %copy-start.2 = (s32[128,4]{0,1:T(4,128)S(1)}, s32[128,4]{0,1:T(4,128)}, u32[]{:S(2)}) copy-start(s32[128,4]{0,1:T(4,128)} %param.13) | copy-start | bytes 6148
  21.1 15.6 %collective-permute-start.6 = (bf16[128,1024]{1,0:T(8,128)(2,1)S(1)}, bf16[128,1024]{1,0:T(8,128)(2,1)S(1)}, u32[]{:S(2)}, u32[]{:S(2)}) collective-permute-start(bf16[128,1024]{1,0:T(8,128)(2,1)S(1)} %shard_map.86.refs_1_.refs_4_), channel_id=1, source_target_pairs={{0,4},{2,6},{4,0},{6,2},{8,12},{10,14},{12,8},{14,10},{1,5},{3,7},... | collective-permute-start | bytes 786440 | tf_op jit(solution)/shard_map/ppermute | solution.py:346
  21.1 23.5 %collective-permute-start.4 = (bf16[256,1024]{1,0:T(8,128)(2,1)S(1)}, bf16[256,1024]{1,0:T(8,128)(2,1)S(1)}, u32[]{:S(2)}, u32[]{:S(2)}) collective-permute-start(bf16[256,1024]{1,0:T(8,128)(2,1)S(1)} %shard_map.87.refs_2_), channel_id=1, source_target_pairs={{0,4},{2,6},{4,0},{6,2},{8,12},{10,14},{12,8},{14,10},{1,5},{3,7},... | collective-permute-start | bytes 1572872 | tf_op jit(solution)/shard_map/ppermute | solution.py:346
  23.2 15.0 %collective-permute-start.5 = (bf16[128,1024]{1,0:T(8,128)(2,1)S(1)}, bf16[128,1024]{1,0:T(8,128)(2,1)S(1)}, u32[]{:S(2)}, u32[]{:S(2)}) collective-permute-start(bf16[128,1024]{1,0:T(8,128)(2,1)S(1)} %shard_map.86.refs_1_.refs_4_), channel_id=1, source_target_pairs={{0,16},{16,0},{1,17},{17,1},{2,18},{18,2},{3,19},{19,3},{4,20},{20... | collective-permute-start | bytes 786440 | tf_op jit(solution)/shard_map/ppermute | solution.py:407
  34.3 10.3 %collective-permute-start.2 = (bf16[128,1024]{1,0:T(8,128)(2,1)S(1)}, bf16[128,1024]{1,0:T(8,128)(2,1)S(1)}, u32[]{:S(2)}, u32[]{:S(2)}) collective-permute-start(bf16[128,1024]{1,0:T(8,128)(2,1)S(1)} %shard_map.84.refs_1_.refs_0_), channel_id=1, source_target_pairs={{0,2},{2,0},{4,6},{6,4},{8,10},{10,8},{12,14},{14,12},{1,3},{3,1},... | collective-permute-start | bytes 786440 | tf_op jit(solution)/shard_map/ppermute | solution.py:346
  36.7 7.9 %collective-permute-start.7 = (bf16[128,1024]{1,0:T(8,128)(2,1)S(1)}, bf16[128,1024]{1,0:T(8,128)(2,1)S(1)}, u32[]{:S(2)}, u32[]{:S(2)}) collective-permute-start(bf16[128,1024]{1,0:T(8,128)(2,1)S(1)} %shard_map.88.refs_6_), channel_id=1, source_target_pairs={{0,16},{16,0},{1,17},{17,1},{2,18},{18,2},{3,19},{19,3},{4,20},{20... | collective-permute-start | bytes 786440 | tf_op jit(solution)/shard_map/ppermute | solution.py:407
  46.1 2.0 %collective-permute-start.8 = (f32[256,512]{1,0:T(8,128)S(1)}, f32[256,512]{1,0:T(8,128)S(1)}, u32[]{:S(2)}, u32[]{:S(2)}) collective-permute-start(f32[256,512]{1,0:T(8,128)S(1)} %get-tuple-element.56), channel_id=1, source_target_pairs={{0,1},{1,0},{2,3},{3,2},{4,5},{5,4},{6,7},{7,6},{8,9},{9,8},{10,11... | collective-permute-start | bytes 1572872 | tf_op jit(solution)/shard_map/ppermute | solution.py:349
  48.2 13.6 %collective-permute-start.12 = (bf16[272,512]{1,0:T(8,128)(2,1)S(1)}, bf16[272,512]{1,0:T(8,128)(2,1)S(1)}, u32[]{:S(2)}, u32[]{:S(2)}) collective-permute-start(bf16[272,512]{1,0:T(8,128)(2,1)S(1)} %shard_map.90.refs_0_), channel_id=1, source_target_pairs={{0,4},{2,6},{4,0},{6,2},{8,12},{10,14},{12,8},{14,10},{1,5},{3,7},... | collective-permute-start | bytes 835592 | tf_op jit(solution)/shard_map/ppermute | solution.py:346
  48.7 13.1 %collective-permute-start.9 = (bf16[272,512]{1,0:T(8,128)(2,1)S(1)}, bf16[272,512]{1,0:T(8,128)(2,1)S(1)}, u32[]{:S(2)}, u32[]{:S(2)}) collective-permute-start(bf16[272,512]{1,0:T(8,128)(2,1)S(1)} %shard_map.90.refs_0_), channel_id=1, source_target_pairs={{0,2},{2,0},{4,6},{6,4},{8,10},{10,8},{12,14},{14,12},{1,3},{3,1},... | collective-permute-start | bytes 835592 | tf_op jit(solution)/shard_map/ppermute | solution.py:346
  49.3 15.8 %collective-permute-start.16 = (bf16[272,512]{1,0:T(8,128)(2,1)S(1)}, bf16[272,512]{1,0:T(8,128)(2,1)S(1)}, u32[]{:S(2)}, u32[]{:S(2)}) collective-permute-start(bf16[272,512]{1,0:T(8,128)(2,1)S(1)} %shard_map.90.refs_0_), channel_id=1, source_target_pairs={{0,8},{2,10},{4,12},{6,14},{8,0},{10,2},{12,4},{14,6},{1,9},{3,11}... | collective-permute-start | bytes 835592 | tf_op jit(solution)/shard_map/ppermute | solution.py:346
  61.8 3.3 %collective-permute-start.14 = (bf16[272,512]{1,0:T(8,128)(2,1)S(1)}, bf16[272,512]{1,0:T(8,128)(2,1)S(1)}, u32[]{:S(2)}, u32[]{:S(2)}) collective-permute-start(bf16[272,512]{1,0:T(8,128)(2,1)S(1)} %shard_map.92.refs_0_), channel_id=1, source_target_pairs={{0,1},{1,0},{2,3},{3,2},{4,5},{5,4},{6,7},{7,6},{8,9},{9,8},{10,11... | collective-permute-start | bytes 835592 | tf_op jit(solution)/shard_map/ppermute | solution.py:349
  61.8 4.0 %collective-permute-start.10 = (bf16[272,512]{1,0:T(8,128)(2,1)S(1)}, bf16[272,512]{1,0:T(8,128)(2,1)S(1)}, u32[]{:S(2)}, u32[]{:S(2)}) collective-permute-start(bf16[272,512]{1,0:T(8,128)(2,1)S(1)} %shard_map.90.refs_0_), channel_id=1, source_target_pairs={{0,1},{1,0},{2,3},{3,2},{4,5},{5,4},{6,7},{7,6},{8,9},{9,8},{10,11... | collective-permute-start | bytes 835592 | tf_op jit(solution)/shard_map/ppermute | solution.py:349
  62.3 9.5 %collective-permute-start.13 = (bf16[272,512]{1,0:T(8,128)(2,1)S(1)}, bf16[272,512]{1,0:T(8,128)(2,1)S(1)}, u32[]{:S(2)}, u32[]{:S(2)}) collective-permute-start(bf16[272,512]{1,0:T(8,128)(2,1)S(1)} %shard_map.92.refs_0_), channel_id=1, source_target_pairs={{0,2},{2,0},{4,6},{6,4},{8,10},{10,8},{12,14},{14,12},{1,3},{3,1},... | collective-permute-start | bytes 835592 | tf_op jit(solution)/shard_map/ppermute | solution.py:346
  62.3 9.5 %collective-permute-start.11 = (bf16[272,512]{1,0:T(8,128)(2,1)S(1)}, bf16[272,512]{1,0:T(8,128)(2,1)S(1)}, u32[]{:S(2)}, u32[]{:S(2)}) collective-permute-start(bf16[272,512]{1,0:T(8,128)(2,1)S(1)} %collective-permute-done.9.refs_1_), channel_id=1, source_target_pairs={{0,1},{1,0},{2,3},{3,2},{4,5},{5,4},{6,7},{7,6},{8,9},{9,8},{10,11... | collective-permute-start | bytes 835592 | tf_op jit(solution)/shard_map/ppermute | solution.py:349
  65.1 11.9 %collective-permute-start.17 = (bf16[272,512]{1,0:T(8,128)(2,1)S(1)}, bf16[272,512]{1,0:T(8,128)(2,1)S(1)}, u32[]{:S(2)}, u32[]{:S(2)}) collective-permute-start(bf16[272,512]{1,0:T(8,128)(2,1)S(1)} %shard_map.94.refs_0_), channel_id=1, source_target_pairs={{0,2},{2,0},{4,6},{6,4},{8,10},{10,8},{12,14},{14,12},{1,3},{3,1},... | collective-permute-start | bytes 835592 | tf_op jit(solution)/shard_map/ppermute | solution.py:346
  65.8 11.1 %collective-permute-start.20 = (bf16[272,512]{1,0:T(8,128)(2,1)S(1)}, bf16[272,512]{1,0:T(8,128)(2,1)S(1)}, u32[]{:S(2)}, u32[]{:S(2)}) collective-permute-start(bf16[272,512]{1,0:T(8,128)(2,1)S(1)} %shard_map.94.refs_0_), channel_id=1, source_target_pairs={{0,4},{2,6},{4,0},{6,2},{8,12},{10,14},{12,8},{14,10},{1,5},{3,7},... | collective-permute-start | bytes 835592 | tf_op jit(solution)/shard_map/ppermute | solution.py:346
  65.8 12.9 %collective-permute-start.18 = (bf16[272,512]{1,0:T(8,128)(2,1)S(1)}, bf16[272,512]{1,0:T(8,128)(2,1)S(1)}, u32[]{:S(2)}, u32[]{:S(2)}) collective-permute-start(bf16[272,512]{1,0:T(8,128)(2,1)S(1)} %shard_map.94.refs_0_), channel_id=1, source_target_pairs={{0,1},{1,0},{2,3},{3,2},{4,5},{5,4},{6,7},{7,6},{8,9},{9,8},{10,11... | collective-permute-start | bytes 835592 | tf_op jit(solution)/shard_map/ppermute | solution.py:349
  71.8 5.6 %collective-permute-start.15 = (bf16[272,512]{1,0:T(8,128)(2,1)S(1)}, bf16[272,512]{1,0:T(8,128)(2,1)S(1)}, u32[]{:S(2)}, u32[]{:S(2)}) collective-permute-start(bf16[272,512]{1,0:T(8,128)(2,1)S(1)} %collective-permute-done.13.refs_1_), channel_id=1, source_target_pairs={{0,1},{1,0},{2,3},{3,2},{4,5},{5,4},{6,7},{7,6},{8,9},{9,8},{10,11... | collective-permute-start | bytes 835592 | tf_op jit(solution)/shard_map/ppermute | solution.py:349
  76.9 1.9 %collective-permute-start.19 = (bf16[272,512]{1,0:T(8,128)(2,1)S(1)}, bf16[272,512]{1,0:T(8,128)(2,1)S(1)}, u32[]{:S(2)}, u32[]{:S(2)}) collective-permute-start(bf16[272,512]{1,0:T(8,128)(2,1)S(1)} %collective-permute-done.17.refs_1_), channel_id=1, source_target_pairs={{0,1},{1,0},{2,3},{3,2},{4,5},{5,4},{6,7},{7,6},{8,9},{9,8},{10,11... | collective-permute-start | bytes 835592 | tf_op jit(solution)/shard_map/ppermute | solution.py:349
  76.9 9.1 %collective-permute-start.21 = (bf16[272,512]{1,0:T(8,128)(2,1)S(1)}, bf16[272,512]{1,0:T(8,128)(2,1)S(1)}, u32[]{:S(2)}, u32[]{:S(2)}) collective-permute-start(bf16[272,512]{1,0:T(8,128)(2,1)S(1)} %shard_map.96.refs_0_), channel_id=1, source_target_pairs={{0,2},{2,0},{4,6},{6,4},{8,10},{10,8},{12,14},{14,12},{1,3},{3,1},... | collective-permute-start | bytes 835592 | tf_op jit(solution)/shard_map/ppermute | solution.py:346
  77.3 8.7 %collective-permute-start.22 = (bf16[272,512]{1,0:T(8,128)(2,1)S(1)}, bf16[272,512]{1,0:T(8,128)(2,1)S(1)}, u32[]{:S(2)}, u32[]{:S(2)}) collective-permute-start(bf16[272,512]{1,0:T(8,128)(2,1)S(1)} %shard_map.96.refs_0_), channel_id=1, source_target_pairs={{0,1},{1,0},{2,3},{3,2},{4,5},{5,4},{6,7},{7,6},{8,9},{9,8},{10,11... | collective-permute-start | bytes 835592 | tf_op jit(solution)/shard_map/ppermute | solution.py:349
  86.0 1.6 %collective-permute-start.23 = (bf16[272,512]{1,0:T(8,128)(2,1)S(1)}, bf16[272,512]{1,0:T(8,128)(2,1)S(1)}, u32[]{:S(2)}, u32[]{:S(2)}) collective-permute-start(bf16[272,512]{1,0:T(8,128)(2,1)S(1)} %shard_map.97.refs_1_), channel_id=1, source_target_pairs={{0,1},{1,0},{2,3},{3,2},{4,5},{5,4},{6,7},{7,6},{8,9},{9,8},{10,11... | collective-permute-start | bytes 835592 | tf_op jit(solution)/shard_map/ppermute | solution.py:349
  88.9 9.3 %slice-start = ((s8[12582912]{0:T(1024)(128)(4,1)}), s8[4194304]{0:T(1024)(128)(4,1)S(1)}, s32[]{:S(2)}) async-start(s8[12582912]{0:T(1024)(128)(4,1)} %bitcast.4), calls=%async_computation | async-start | bytes 8388608
  88.9 9.3 %slice-start.1 = ((s8[12582912]{0:T(1024)(128)(4,1)}), s8[4194304]{0:T(1024)(128)(4,1)S(1)}, s32[]{:S(2)}) async-start(s8[12582912]{0:T(1024)(128)(4,1)} %bitcast.4), calls=%async_computation.1 | async-start | bytes 8388608
  88.9 9.3 %slice-start.2 = ((s8[12582912]{0:T(1024)(128)(4,1)}), s8[4194304]{0:T(1024)(128)(4,1)S(1)}, s32[]{:S(2)}) async-start(s8[12582912]{0:T(1024)(128)(4,1)} %bitcast.4), calls=%async_computation.2 | async-start | bytes 8388608
  95.8 2.4 %collective-permute-start.24 = (bf16[8,128,384]{2,1,0:T(8,128)(2,1)S(1)}, bf16[8,128,384]{2,1,0:T(8,128)(2,1)S(1)}, u32[]{:S(2)}, u32[]{:S(2)}) collective-permute-start(bf16[8,128,384]{2,1,0:T(8,128)(2,1)S(1)} %shard_map.99.near_ref), channel_id=1, source_target_pairs={{0,1},{1,0},{2,3},{3,2},{4,5},{5,4},{6,7},{7,6},{8,9},{9,8},{10,11... | collective-permute-start | bytes 2359304 | tf_op jit(solution)/shard_map/ppermute | solution.py:349
  101.2 6.4 %collective-permute-start.26 = (bf16[64,1024]{1,0:T(8,128)(2,1)S(1)}, bf16[64,1024]{1,0:T(8,128)(2,1)S(1)}, u32[]{:S(2)}, u32[]{:S(2)}) collective-permute-start(bf16[64,1024]{1,0:T(8,128)(2,1)S(1)} %get-tuple-element.80), channel_id=1, source_target_pairs={{0,2},{2,0},{4,6},{6,4},{8,10},{10,8},{12,14},{14,12},{1,3},{3,1},... | collective-permute-start | bytes 393224 | tf_op jit(solution)/shard_map/ppermute | solution.py:346
  101.6 8.8 %collective-permute-start.28 = (bf16[64,1024]{1,0:T(8,128)(2,1)S(1)}, bf16[64,1024]{1,0:T(8,128)(2,1)S(1)}, u32[]{:S(2)}, u32[]{:S(2)}) collective-permute-start(bf16[64,1024]{1,0:T(8,128)(2,1)S(1)} %get-tuple-element.82), channel_id=1, source_target_pairs={{0,2},{2,0},{4,6},{6,4},{8,10},{10,8},{12,14},{14,12},{1,3},{3,1},... | collective-permute-start | bytes 393224 | tf_op jit(solution)/shard_map/ppermute | solution.py:346
  103.3 9.9 %collective-permute-start.30 = (bf16[64,1024]{1,0:T(8,128)(2,1)S(1)}, bf16[64,1024]{1,0:T(8,128)(2,1)S(1)}, u32[]{:S(2)}, u32[]{:S(2)}) collective-permute-start(bf16[64,1024]{1,0:T(8,128)(2,1)S(1)} %get-tuple-element.84), channel_id=1, source_target_pairs={{0,2},{2,0},{4,6},{6,4},{8,10},{10,8},{12,14},{14,12},{1,3},{3,1},... | collective-permute-start | bytes 393224 | tf_op jit(solution)/shard_map/ppermute | solution.py:346
  103.6 18.1 %collective-permute-start.32 = (bf16[64,1024]{1,0:T(8,128)(2,1)S(1)}, bf16[64,1024]{1,0:T(8,128)(2,1)S(1)}, u32[]{:S(2)}, u32[]{:S(2)}) collective-permute-start(bf16[64,1024]{1,0:T(8,128)(2,1)S(1)} %get-tuple-element.86), channel_id=1, source_target_pairs={{0,2},{2,0},{4,6},{6,4},{8,10},{10,8},{12,14},{14,12},{1,3},{3,1},... | collective-permute-start | bytes 393224 | tf_op jit(solution)/shard_map/ppermute | solution.py:346
  105.3 13.5 %collective-permute-start.33 = (bf16[64,1024]{1,0:T(8,128)(2,1)S(1)}, bf16[64,1024]{1,0:T(8,128)(2,1)S(1)}, u32[]{:S(2)}, u32[]{:S(2)}) collective-permute-start(bf16[64,1024]{1,0:T(8,128)(2,1)S(1)} %get-tuple-element.88), channel_id=1, source_target_pairs={{0,2},{2,0},{4,6},{6,4},{8,10},{10,8},{12,14},{14,12},{1,3},{3,1},... | collective-permute-start | bytes 393224 | tf_op jit(solution)/shard_map/ppermute | solution.py:346
  107.6 14.0 %collective-permute-start.36 = (bf16[64,1024]{1,0:T(8,128)(2,1)S(1)}, bf16[64,1024]{1,0:T(8,128)(2,1)S(1)}, u32[]{:S(2)}, u32[]{:S(2)}) collective-permute-start(bf16[64,1024]{1,0:T(8,128)(2,1)S(1)} %get-tuple-element.90), channel_id=1, source_target_pairs={{0,2},{2,0},{4,6},{6,4},{8,10},{10,8},{12,14},{14,12},{1,3},{3,1},... | collective-permute-start | bytes 393224 | tf_op jit(solution)/shard_map/ppermute | solution.py:346
  110.4 25.3 %collective-permute-start.25 = (bf16[128,1024]{1,0:T(8,128)(2,1)S(1)}, bf16[128,1024]{1,0:T(8,128)(2,1)S(1)}, u32[]{:S(2)}, u32[]{:S(2)}) collective-permute-start(bf16[128,1024]{1,0:T(8,128)(2,1)S(1)} %get-tuple-element.78), channel_id=1, source_target_pairs={{0,2},{2,0},{4,6},{6,4},{8,10},{10,8},{12,14},{14,12},{1,3},{3,1},... | collective-permute-start | bytes 786440 | tf_op jit(solution)/shard_map/ppermute | solution.py:346
  113.2 15.4 %collective-permute-start.27 = (bf16[64,1024]{1,0:T(8,128)(2,1)S(1)}, bf16[64,1024]{1,0:T(8,128)(2,1)S(1)}, u32[]{:S(2)}, u32[]{:S(2)}) collective-permute-start(bf16[64,1024]{1,0:T(8,128)(2,1)S(1)} %add_convert_fusion.6), channel_id=1, source_target_pairs={{0,12},{2,14},{4,8},{6,10},{8,4},{10,6},{12,0},{14,2},{1,13},{3,15... | collective-permute-start | bytes 393224 | tf_op jit(solution)/shard_map/ppermute | solution.py:346
  118.8 11.8 %collective-permute-start.29 = (bf16[64,1024]{1,0:T(8,128)(2,1)S(1)}, bf16[64,1024]{1,0:T(8,128)(2,1)S(1)}, u32[]{:S(2)}, u32[]{:S(2)}) collective-permute-start(bf16[64,1024]{1,0:T(8,128)(2,1)S(1)} %add_convert_fusion.5), channel_id=1, source_target_pairs={{0,8},{2,10},{4,12},{6,14},{8,0},{10,2},{12,4},{14,6},{1,9},{3,11}... | collective-permute-start | bytes 393224 | tf_op jit(solution)/shard_map/ppermute | solution.py:346
  121.6 6.9 %collective-permute-start.34 = (bf16[64,1024]{1,0:T(8,128)(2,1)S(1)}, bf16[64,1024]{1,0:T(8,128)(2,1)S(1)}, u32[]{:S(2)}, u32[]{:S(2)}) collective-permute-start(bf16[64,1024]{1,0:T(8,128)(2,1)S(1)} %add_convert_fusion.2), channel_id=1, source_target_pairs={{0,4},{2,6},{4,0},{6,2},{8,12},{10,14},{12,8},{14,10},{1,5},{3,7},... | collective-permute-start | bytes 393224 | tf_op jit(solution)/shard_map/ppermute | solution.py:346
  121.7 11.1 %collective-permute-start.31 = (bf16[64,1024]{1,0:T(8,128)(2,1)S(1)}, bf16[64,1024]{1,0:T(8,128)(2,1)S(1)}, u32[]{:S(2)}, u32[]{:S(2)}) collective-permute-start(bf16[64,1024]{1,0:T(8,128)(2,1)S(1)} %add_convert_fusion.4), channel_id=1, source_target_pairs={{0,4},{2,6},{4,0},{6,2},{8,12},{10,14},{12,8},{14,10},{1,5},{3,7},... | collective-permute-start | bytes 393224 | tf_op jit(solution)/shard_map/ppermute | solution.py:346
  128.6 7.1 %collective-permute-start.37 = (bf16[64,1024]{1,0:T(8,128)(2,1)S(1)}, bf16[64,1024]{1,0:T(8,128)(2,1)S(1)}, u32[]{:S(2)}, u32[]{:S(2)}) collective-permute-start(bf16[64,1024]{1,0:T(8,128)(2,1)S(1)} %add_convert_fusion), channel_id=1, source_target_pairs={{0,4},{2,6},{4,0},{6,2},{8,12},{10,14},{12,8},{14,10},{1,5},{3,7},... | collective-permute-start | bytes 393224 | tf_op jit(solution)/shard_map/ppermute | solution.py:346
  128.6 7.1 %collective-permute-start.35 = (bf16[64,1024]{1,0:T(8,128)(2,1)S(1)}, bf16[64,1024]{1,0:T(8,128)(2,1)S(1)}, u32[]{:S(2)}, u32[]{:S(2)}) collective-permute-start(bf16[64,1024]{1,0:T(8,128)(2,1)S(1)} %add_convert_fusion.1), channel_id=1, source_target_pairs={{0,8},{2,10},{4,12},{6,14},{8,0},{10,2},{12,4},{14,6},{1,9},{3,11}... | collective-permute-start | bytes 393224 | tf_op jit(solution)/shard_map/ppermute | solution.py:346

commit v9 on v7

--- a/solution.py
+++ b/solution.py
@@ -30,8 +30,9 @@
 
 
 def cut_kernel(split, tokens_ref, qkv_ref, weight_ref, *refs):
-    query_ref, pair_ref, near_ref, cross_ref, sent_ref, own_ref, sem_ref = refs
-    count, lanes = near_ref.shape
+    pair_ref, cross_ref, sent_ref, sem_ref = refs
+    count = pair_ref.shape[0] // 2
+    lanes = tokens_ref.shape[1] // 4
     chunk = tokens_ref.shape[1] // lax.axis_size("dev")
     side = lax.axis_index("dev") % 2
     part = lax.axis_index("sub")
@@ -52,17 +53,27 @@
                     cross_ref.at[2 * count :, left : left + chunk],
                 )
             )
+    rows = sent_ref.shape[0]
+    at = pl.multiple_of(lax.axis_index("groups") * rows if split else 0, TILE)
+    moves.append((weight_ref.at[pl.ds(at, rows)], sent_ref))
+    copies = [pltpu.make_async_copy(*move, sem_ref.at[n]) for n, move in enumerate(moves)]
+    for copy in copies:
+        copy.start()
+    for copy in copies:
+        copy.wait()
+
+
+def rest_kernel(tokens_ref, qkv_ref, weight_ref, _, query_ref, near_ref, own_ref, sem_ref):
+    lanes = near_ref.shape[1]
+    chunk = tokens_ref.shape[1] // lax.axis_size("dev")
+    side = lax.axis_index("dev") % 2
+    part = lax.axis_index("sub")
+    moves = [(qkv_ref.at[0], query_ref), (weight_ref, own_ref)]
+    for i in range(lanes // chunk):
         at = pl.multiple_of(part * 2 * lanes + (2 * i + side) * chunk, 128)
         moves.append(
             (tokens_ref.at[:, pl.ds(at, chunk)], near_ref.at[:, i * chunk : (i + 1) * chunk])
         )
-    rows = sent_ref.shape[0]
-    at = pl.multiple_of(lax.axis_index("groups") * rows if split else 0, TILE)
-    moves += [
-        (weight_ref.at[pl.ds(at, rows)], sent_ref),
-        (qkv_ref.at[0], query_ref),
-        (weight_ref, own_ref),
-    ]
     copies = [pltpu.make_async_copy(*move, sem_ref.at[n]) for n, move in enumerate(moves)]
     for copy in copies:
         copy.start()
@@ -114,13 +125,13 @@
         mixed_ref[:, lanes] = out.astype(BF16)
 
 
-def projection_kernel(steps, pieces, *refs):
+def projection_kernel(steps, pieces, wanted, *refs):
     mixed_ref, other_ref = refs[0], refs[1]
     weight_refs = refs[2 : 2 + len(pieces)]
-    keep_ref, send_ref, both_ref = refs[-3:]
+    out_ref = refs[2 + len(pieces)]
     count = mixed_ref.shape[0]
     half = steps // 2
-    chunk = keep_ref.shape[1] // half
+    chunk = out_ref.shape[1] // half
     z = lax.axis_index("dev") // 2
     part = lax.axis_index("sub")
     group = lax.axis_index("groups")
@@ -131,16 +142,16 @@
         lane = (target % half) * chunk
         if side is not None:
             lane += (group if side == 0 else 1 - group) * rows
-        lane = pl.multiple_of(lane, 128)
-        for block, ref in enumerate((mixed_ref, other_ref)):
-            both_ref[away, block * count : (block + 1) * count, pl.ds(lane, rows)] = (
-                lax.dot_general(ref[...], w_ref[...], NT, preferred_element_type=F32)
-            )
-    keep_ref[...] = both_ref[0]
-    send_ref[...] = both_ref[1]
-
-
-def state_kernel(keep_ref, got_ref, near_ref, cross_ref, ids_ref, mod_ref, out_ref):
+
+        @pl.when(away == wanted)
+        def _(lane=pl.multiple_of(lane, 128), rows=rows, w_ref=w_ref):
+            for block, ref in enumerate((mixed_ref, other_ref)):
+                out_ref[block * count : (block + 1) * count, pl.ds(lane, rows)] = (
+                    lax.dot_general(ref[...], w_ref[...], NT, preferred_element_type=F32)
+                )
+
+
+def state_kernel(keep_ref, got_ref, near_ref, cross_ref, ids_ref, mod_ref, out_ref, again_ref):
     count, lanes = near_ref.shape
     half = count // 2
     chunk = mod_ref.shape[1] // lax.axis_size("dev")
@@ -160,6 +171,7 @@
             proj = keep_ref[rows, cols] + got_ref[rows, cols]
             out_ref[rows, cols] = (token.astype(F32) + lift * proj).astype(BF16)
     out_ref[2 * count :, :] = ids_ref[...]
+    again_ref[...] = out_ref[...]
 
 
 def tie_kernel(*refs):
@@ -267,10 +279,10 @@
     )(weight, after_this)
 
 
-def hidden_kernel(steps, *refs):
+def hidden_kernel(steps, low, *refs):
     rows_refs, w_refs, hidden_ref = refs[:steps], refs[steps:-1], refs[-1]
     for e, w_ref in enumerate(w_refs):
-        rows = jnp.concatenate([ref[e] for ref in rows_refs])
+        rows = jnp.concatenate([ref[low + e] for ref in rows_refs])
         halves = []
         for b in range(2):
             gate = lax.dot_general(w_ref[b, 0], rows, NT, preferred_element_type=F32)
@@ -279,25 +291,32 @@
         hidden_ref[e] = jnp.concatenate(halves).T.astype(BF16)
 
 
-def output_kernel(steps, near_ref, far_ref, w_ref, *refs):
-    back_refs, out_refs, held_ref = refs[:steps], refs[steps : 3 * steps], refs[-1]
+def output_kernel(low, near_ref, far_ref, w_ref, held_ref):
     part = lax.axis_index("sub")
     units = near_ref.shape[2] // 2
     for e in range(near_ref.shape[0]):
         total = 0.0
         for ref, who in ((near_ref, part), (far_ref, 1 - part)):
             at = pl.multiple_of(who * units, 64)
-            weight = jnp.concatenate([w_ref[2 * e + b, pl.ds(at, units), :] for b in range(2)])
+            weight = jnp.concatenate(
+                [w_ref[2 * (low + e) + b, pl.ds(at, units), :] for b in range(2)]
+            )
             total += jnp.dot(ref[e], weight, preferred_element_type=F32)
         total = total.astype(BF16)
-        for source in range(2 * steps):
+        for source in range(held_ref.shape[0]):
             held_ref[source, e * SLOTS : (e + 1) * SLOTS, :] = total[
                 source * SLOTS : (source + 1) * SLOTS
             ]
+
+
+def share_kernel(steps, low, before, near_ref, far_ref, w_ref, *refs):
+    held_refs, back_refs = refs[:before], refs[before : before + steps]
+    out_refs, held_ref = refs[before + steps : -1], refs[-1]
+    output_kernel(low, near_ref, far_ref, w_ref, held_ref)
     for source in range(2 * steps):
-        out_refs[source][...] = jnp.dot(
-            back_refs[source // 2][source % 2], held_ref[source], preferred_element_type=F32
-        ).astype(BF16)
+        back = back_refs[source // 2][source % 2]
+        rows = jnp.concatenate([ref[source] for ref in (*held_refs, held_ref)])
+        out_refs[source][...] = jnp.dot(back, rows, preferred_element_type=F32).astype(BF16)
 
 
 def final_kernel(state_ref, mod_ref, *refs):
@@ -339,21 +358,32 @@
 
     split = groups == 2
     held = out_weight.shape[0] // (2 if split else 1)
-    query, pair, near, cross, sent, own_weight = pl.pallas_call(
+    anywhere = pl.BlockSpec(memory_space=pl.ANY)
+    stacked = query_key_value.transpose(1, 0, 2)
+    pair, cross, sent = pl.pallas_call(
         functools.partial(cut_kernel, split),
         out_shape=[
-            struct((count, local_width), BF16),
             struct((2 * count, local_width), BF16),
-            struct((count, lanes), BF16),
             struct((2 * count + count // 2, local_width), BF16),
             struct((held, local_width), BF16),
+        ],
+        in_specs=[anywhere] * 3,
+        out_specs=[whole()] * 3,
+        scratch_shapes=[pltpu.SemaphoreType.DMA((5 + 2 * (lanes // chunk),))],
+        compiler_params=vmem(53),
+    )(tokens, stacked, out_weight)
+    query, near, own_weight = pl.pallas_call(
+        rest_kernel,
+        out_shape=[
+            struct((count, local_width), BF16),
+            struct((count, lanes), BF16),
             struct(out_weight.shape, BF16),
         ],
-        in_specs=[pl.BlockSpec(memory_space=pl.ANY)] * 3,
-        out_specs=[whole()] * 6,
-        scratch_shapes=[pltpu.SemaphoreType.DMA((7 + 3 * (lanes // chunk),))],
-        compiler_params=vmem(52),
-    )(tokens, query_key_value.transpose(1, 0, 2), out_weight)
+        in_specs=[anywhere] * 4,
+        out_specs=[whole()] * 3,
+        scratch_shapes=[pltpu.SemaphoreType.DMA((2 + lanes // chunk,))],
+        compiler_params=vmem(53),
+    )(tokens, stacked, out_weight, sent)
     ids, small, router = pl.pallas_call(
         small_kernel,
         out_shape=[
@@ -399,19 +429,22 @@
         else:
             pieces.append((flip, None))
             weights.append(mine[flip])
-    keep, send = pl.pallas_call(
-        functools.partial(projection_kernel, steps, tuple(pieces)),
-        out_shape=[struct((2 * count, lanes), F32)] * 2,
-        in_specs=[whole()] * (2 + len(weights)),
+    other = hop(mixed, 1)
+    send, keep = (
+        pl.pallas_call(
+            functools.partial(projection_kernel, steps, tuple(pieces), wanted),
+            out_shape=struct((2 * count, lanes), F32),
+            in_specs=[whole()] * (2 + len(weights)),
+            out_specs=whole(),
+            compiler_params=vmem(6),
+        )(mixed, other, *weights)
+        for wanted in (1, 0)
+    )
+    shard, again = pl.pallas_call(
+        state_kernel,
+        out_shape=[struct((2 * count + TILE, lanes), BF16)] * 2,
+        in_specs=[whole()] * 6,
         out_specs=[whole()] * 2,
-        scratch_shapes=[pltpu.VMEM((2, 2 * count, lanes), F32)],
-        compiler_params=vmem(6),
-    )(mixed, hop(mixed, 1), *weights)
-    shard = pl.pallas_call(
-        state_kernel,
-        out_shape=struct((2 * count + TILE, lanes), BF16),
-        in_specs=[whole()] * 6,
-        out_specs=whole(),
         compiler_params=vmem(6),
     )(keep, swap(send), near, cross, ids, small)
 
@@ -423,7 +456,8 @@
     column[1] = tie(column[1], across)
     crossing = {0: across, 1: hop(column[1], 1)}
     beside = swap(column[1])
-    column[2] = tie(hop(shard, 4), beside)
+    swapped = swap(shard)
+    column[2] = tie(hop(tie(again, swapped), 4), beside)
     for flip in range(3, steps):
         low = flip & -flip
         column[flip] = hop(column[flip - low] if flip > low else shard, 2 * low)
@@ -446,7 +480,7 @@
             out_specs=[whole()] * (3 if own else 2),
             scratch_shapes=[pltpu.VMEM((count, width), BF16), pltpu.VMEM((experts, count), F32)],
             compiler_params=vmem(6),
-        )(block, crossed, beside if flip == 1 else swap(block), swap(crossed), small, router)
+        )(block, crossed, beside if flip == 1 else swapped if own else swap(block), swap(crossed), small, router)
         picked.append(results[0])
         backs.append(results[1])
         if own:
@@ -454,21 +488,38 @@
 
     sources = 2 * steps
     room = sources * SLOTS
-    hidden = pl.pallas_call(
-        functools.partial(hidden_kernel, steps),
-        out_shape=struct((local, room, 2 * units), BF16),
-        in_specs=[whole()] * (steps + local),
-        out_specs=whole(),
-        compiler_params=vmem(6),
-    )(*picked, *ups)
+    first = local // 2
+    groups_of = [(0, first), (first, local)] if first else [(0, local)]
+    hidden = []
+    for low, high in groups_of:
+        own = pl.pallas_call(
+            functools.partial(hidden_kernel, steps, low),
+            out_shape=struct((high - low, room, 2 * units), BF16),
+            in_specs=[whole()] * (steps + high - low),
+            out_specs=whole(),
+            compiler_params=vmem(6),
+        )(*picked, *ups[low:high])
+        hidden.append((own, swap(own)))
+    held = []
+    for (low, high), (own, other) in zip(groups_of[:-1], hidden[:-1]):
+        held.append(
+            pl.pallas_call(
+                functools.partial(output_kernel, low),
+                out_shape=struct((sources, (high - low) * SLOTS, 2 * lanes), BF16),
+                in_specs=[whole()] * 3,
+                out_specs=whole(),
+                compiler_params=vmem(6),
+            )(own, other, down_weight)
+        )
+    low, high = groups_of[-1]
     share = pl.pallas_call(
-        functools.partial(output_kernel, steps),
+        functools.partial(share_kernel, steps, low, len(held)),
         out_shape=[struct((count, 2 * lanes), BF16)] * sources,
-        in_specs=[whole()] * (3 + steps),
+        in_specs=[whole()] * (3 + len(held) + steps),
         out_specs=[whole()] * sources,
-        scratch_shapes=[pltpu.VMEM((sources, slots, 2 * lanes), BF16)],
+        scratch_shapes=[pltpu.VMEM((sources, (high - low) * SLOTS, 2 * lanes), BF16)],
         compiler_params=vmem(8),
-    )(hidden, swap(hidden), down_weight, *backs)
+    )(*hidden[-1], down_weight, *held, *backs)
 
     terms = [share[0]]
     for flip in range(steps - 1, -1, -1):

time: 135 us -> 134 us (level)
  waiting for transfers between devices: 77.2 us -> 73 us
  Pallas kernels: 31.8 us -> 34.6 us
    ppermute x10 -> x11, waiting for transfers between devices: 5.61 us -> 2.62 us  [swap(): return lax.ppermute(x, 'sub', [(0, 1), (1, 0)])]
    pallas_call x5 -> x9, Pallas kernels: 14.1 us -> 16.9 us  [the longest x2 7.02 us: gathered_body(): pl.pallas_call(functools.partial(hidden_kernel, steps, low), out_shape=st...]
  transfers between devices with their start and end apart: 32 -> 33, of which waited for: 17 -> 17; matrix products, arithmetic and copies ran while one was open for 0% -> 0% of each run, Pallas kernels for 11% -> 18%
where the time goes in v9:
time: 134 us
  waiting for transfers between devices  73 us (54%)
  Pallas kernels  34.6 us (26%)
  starting transfers between devices  25.5 us (19%)
    ppermute x19, waiting for transfers between devices, hop(): return lax.ppermute(x, 'dev', [(i, i ^ flip) for i in range(devices)])  70.4 us
    ppermute x19, starting transfers between devices, hop(): return lax.ppermute(x, 'dev', [(i, i ^ flip) for i in range(devices)])  20.2 us
    pallas_call x1, Pallas kernels, load(): pl.pallas_call(load_kernel, out_shape=[piece] * local + [jax.ShapeDtypeSt...  8.36 us
    pallas_call x2, Pallas kernels, gathered_body(): pl.pallas_call(functools.partial(hidden_kernel, steps, low), out_shape=st...  7.02 us
    pallas_call x4, Pallas kernels, gathered_body(): pl.pallas_call(functools.partial(select_kernel, local, topk, own), out_sh...  5.31 us
    pallas_call x1, Pallas kernels, gathered_body(): pl.pallas_call(attention_kernel, out_shape=struct((count, local_width), B...  3.11 us
    ppermute x2, starting transfers between devices, gathered_body(): theirs = lax.ppermute(mine[flip], 'groups', [(0, 1), (1, 0)])  3.1 us
  transfers between devices with their start and end apart: 33, of which 17 were waited for; matrix products, arithmetic and copies ran while one was open for 0% of the time, Pallas kernels for 18%

profile of v9, /device:TPU:0, one launch (start us, length us, event | category | flops | bytes accessed | tf_op | source)
XLA Modules:
  0.0 133.7 jit_solution(9052765391378178129)
XLA Ops:
  0.0 2.3 %shard_map.82 = (bf16[256,1024]{1,0:T(8,128)(2,1)S(1)}, bf16[320,1024]{1,0:T(8,128)(2,1)}, bf16[128,1024]{1,0:T(8,128)(2,1)S(1)}) custom-call(bf16[128,2048]{1,0:T(8,128)(2,1)} %tokens_ref.3, bf16[3,128,1024]{2,1,0:T(8,128)(2,1)} %bitcast.9, bf16[256,1024]{1,0:T(8,128)(2,1)} %weight_ref.3), custom_call_target="tpu_custom_call" | custom-call | tf_op jit(solution)/shard_map/pallas_call | solution.py:363
  2.3 3.0 %collective-permute-start = (bf16[320,1024]{1,0:T(8,128)(2,1)}, bf16[320,1024]{1,0:T(8,128)(2,1)S(1)}, u32[]{:S(2)}, u32[]{:S(2)}) collective-permute-start(bf16[320,1024]{1,0:T(8,128)(2,1)} %get-tuple-element.45), channel_id=1, source_target_pairs={{0,2},{2,0},{4,6},{6,4},{8,10},{10,8},{12,14},{14,12},{1,3},{3,1},... | collective-permute-start | bytes 1966088 | tf_op jit(solution)/shard_map/ppermute | solution.py:354
  5.3 2.6 %collective-permute-start.3 = (bf16[128,1024]{1,0:T(8,128)(2,1)S(1)}, bf16[128,1024]{1,0:T(8,128)(2,1)S(1)}, u32[]{:S(2)}, u32[]{:S(2)}) collective-permute-start(bf16[128,1024]{1,0:T(8,128)(2,1)S(1)} %get-tuple-element.42._), channel_id=1, source_target_pairs={{0,8},{2,10},{4,12},{6,14},{8,0},{10,2},{12,4},{14,6},{1,9},{3,11}... | collective-permute-start | bytes 786440 | tf_op jit(solution)/shard_map/ppermute | solution.py:354
  7.9 0.7 collective-permute-start.1
  8.6 2.0 %shard_map.83 = (bf16[128,1024]{1,0:T(8,128)(2,1)S(1)}, bf16[128,512]{1,0:T(8,128)(2,1)S(1)}, bf16[256,1024]{1,0:T(8,128)(2,1)}) custom-call(bf16[128,2048]{1,0:T(8,128)(2,1)} %tokens_ref.3, bf16[3,128,1024]{2,1,0:T(8,128)(2,1)} %bitcast.10, bf16[256,1024]{1,0:T(8,128)(2,1)} %weight_ref.3, bf16[128,1024]{1,0:T(8,128)(2,1)S(1)} %get-tuple-element.42._), custom_call_target="tpu_custom_call" | custom-call | tf_op jit(solution)/shard_map/pallas_call | solution.py:375
  10.6 8.4 %shard_map.86 = (bf16[2,2,192,2048]{3,2,1,0:T(8,128)(2,1)S(1)}, bf16[2,2,192,2048]{3,2,1,0:T(8,128)(2,1)S(1)}, bf16[2,2,192,2048]{3,2,1,0:T(8,128)(2,1)S(1)}, bf...) custom-call(bf16[16,2,192,2048]{3,2,1,0:T(8,128)(2,1)} %bitcast.8, ...), custom_call_target="tpu_custom_call" | custom-call | tf_op jit(solution)/shard_map/pallas_call | solution.py:272
  18.9 1.8 %collective-permute-done.3.refs_0_ = bf16[128,1024]{1,0:T(8,128)(2,1)S(1)} collective-permute-done((bf16[128,1024]{1,0:T(8,128)(2,1)S(1)}, bf16[128,1024]{1,0:T(8,128)(2,1)S(1)}, u32[]{:S(2)}, u32[]{:S(2)}) %collective-permute-start.3) | collective-permute-done | bytes 262176 | tf_op jit(solution)/shard_map/ppermute | solution.py:354
  20.8 1.5 %collective-permute-start.6 = (bf16[128,1024]{1,0:T(8,128)(2,1)S(1)}, bf16[128,1024]{1,0:T(8,128)(2,1)S(1)}, u32[]{:S(2)}, u32[]{:S(2)}) collective-permute-start(bf16[128,1024]{1,0:T(8,128)(2,1)S(1)} %shard_map.87.refs_1_.refs_4_), channel_id=1, source_target_pairs={{0,4},{2,6},{4,0},{6,2},{8,12},{10,14},{12,8},{14,10},{1,5},{3,7},... | collective-permute-start | bytes 786440 | tf_op jit(solution)/shard_map/ppermute | solution.py:354
  22.2 0.6 collective-permute-start.4
  22.8 1.6 %collective-permute-start.5 = (bf16[128,1024]{1,0:T(8,128)(2,1)S(1)}, bf16[128,1024]{1,0:T(8,128)(2,1)S(1)}, u32[]{:S(2)}, u32[]{:S(2)}) collective-permute-start(bf16[128,1024]{1,0:T(8,128)(2,1)S(1)} %shard_map.87.refs_1_.refs_4_), channel_id=1, source_target_pairs={{0,16},{16,0},{1,17},{17,1},{2,18},{18,2},{3,19},{19,3},{4,20},{20... | collective-permute-start | bytes 786440 | tf_op jit(solution)/shard_map/ppermute | solution.py:426
  24.4 6.4 %collective-permute-done.cross_ref = bf16[320,1024]{1,0:T(8,128)(2,1)S(1)} collective-permute-done((bf16[320,1024]{1,0:T(8,128)(2,1)}, bf16[320,1024]{1,0:T(8,128)(2,1)S(1)}, u32[]{:S(2)}, u32[]{:S(2)}) %collective-permute-start) | collective-permute-done | bytes 655392 | tf_op jit(solution)/shard_map/ppermute | solution.py:354
  30.8 3.1 %shard_map.85.refs_1_.refs_0_ = bf16[128,1024]{1,0:T(8,128)(2,1)S(1)} custom-call(bf16[128,1024]{1,0:T(8,128)(2,1)S(1)} %get-tuple-element.43._.query_ref, bf16[256,1024]{1,0:T(8,128)(2,1)S(1)} %get-tuple-element.44.own_ref, bf16[320,1024]{1,0:T(8,128)(2,1)S(1)} %collective-permute-done.cross_ref, bf16[256,1024]{1,0:T(8,128)(2,1)S(1)} %collective-permute-done.1.next_ref, ...), custom_call_target="tpu_custom_call" | custom-call | tf_op jit(solution)/shard_map/pallas_call | solution.py:415
  33.9 2.4 %collective-permute-start.2 = (bf16[128,1024]{1,0:T(8,128)(2,1)S(1)}, bf16[128,1024]{1,0:T(8,128)(2,1)S(1)}, u32[]{:S(2)}, u32[]{:S(2)}) collective-permute-start(bf16[128,1024]{1,0:T(8,128)(2,1)S(1)} %shard_map.85.refs_1_.refs_0_), channel_id=1, source_target_pairs={{0,2},{2,0},{4,6},{6,4},{8,10},{10,8},{12,14},{14,12},{1,3},{3,1},... | collective-permute-start | bytes 786440 | tf_op jit(solution)/shard_map/ppermute | solution.py:354
  36.4 1.5 %collective-permute-start.7 = (bf16[128,1024]{1,0:T(8,128)(2,1)S(1)}, bf16[128,1024]{1,0:T(8,128)(2,1)S(1)}, u32[]{:S(2)}, u32[]{:S(2)}) collective-permute-start(bf16[128,1024]{1,0:T(8,128)(2,1)S(1)} %shard_map.89.refs_6_), channel_id=1, source_target_pairs={{0,16},{16,0},{1,17},{17,1},{2,18},{18,2},{3,19},{19,3},{4,20},{20... | collective-permute-start | bytes 786440 | tf_op jit(solution)/shard_map/ppermute | solution.py:426
  37.9 6.4 %collective-permute-done.4.refs_3_ = bf16[256,1024]{1,0:T(8,128)(2,1)S(1)} collective-permute-done((bf16[256,1024]{1,0:T(8,128)(2,1)S(1)}, bf16[256,1024]{1,0:T(8,128)(2,1)S(1)}, u32[]{:S(2)}, u32[]{:S(2)}) %collective-permute-start.4) | collective-permute-done | bytes 524320 | tf_op jit(solution)/shard_map/ppermute | solution.py:354
  44.3 1.2 shard_map.91
  45.5 0.1 collective-permute-start.8
  45.6 1.2 shard_map.90.keep_ref
  46.8 0.7 collective-permute-done.8.got_ref
  47.5 0.1 shard_map.92
  47.6 0.2 collective-permute-start.10
  47.8 0.6 collective-permute-start.12
  48.4 0.5 collective-permute-start.9
  48.9 0.3 collective-permute-done.10.refs_2_.refs_1_
  49.2 2.8 %collective-permute-start.16 = (bf16[272,512]{1,0:T(8,128)(2,1)S(1)}, bf16[272,512]{1,0:T(8,128)(2,1)S(1)}, u32[]{:S(2)}, u32[]{:S(2)}) collective-permute-start(bf16[272,512]{1,0:T(8,128)(2,1)S(1)} %shard_map.96), channel_id=1, source_target_pairs={{0,8},{2,10},{4,12},{6,14},{8,0},{10,2},{12,4},{14,6},{1,9},{3,11}... | collective-permute-start | bytes 835592 | tf_op jit(solution)/shard_map/ppermute | solution.py:354
  52.0 9.5 %collective-permute-done.12.refs_0_ = bf16[272,512]{1,0:T(8,128)(2,1)S(1)} collective-permute-done((bf16[272,512]{1,0:T(8,128)(2,1)S(1)}, bf16[272,512]{1,0:T(8,128)(2,1)S(1)}, u32[]{:S(2)}, u32[]{:S(2)}) %collective-permute-start.12) | collective-permute-done | bytes 278560 | tf_op jit(solution)/shard_map/ppermute | solution.py:354
  61.5 0.1 collective-permute-start.13
  61.5 0.4 collective-permute-start.11
  62.0 2.9 %collective-permute-done.16.refs_0_ = bf16[272,512]{1,0:T(8,128)(2,1)S(1)} collective-permute-done((bf16[272,512]{1,0:T(8,128)(2,1)S(1)}, bf16[272,512]{1,0:T(8,128)(2,1)S(1)}, u32[]{:S(2)}, u32[]{:S(2)}) %collective-permute-start.16) | collective-permute-done | bytes 278560 | tf_op jit(solution)/shard_map/ppermute | solution.py:354
  64.9 0.9 collective-permute-start.17
  65.7 5.3 %collective-permute-done.13.refs_1_ = bf16[272,512]{1,0:T(8,128)(2,1)S(1)} collective-permute-done((bf16[272,512]{1,0:T(8,128)(2,1)S(1)}, bf16[272,512]{1,0:T(8,128)(2,1)S(1)}, u32[]{:S(2)}, u32[]{:S(2)}) %collective-permute-start.13) | collective-permute-done | bytes 278560 | tf_op jit(solution)/shard_map/ppermute | solution.py:354
  71.0 1.3 %shard_map.93 = (bf16[8,32,2048]{2,1,0:T(8,128)(2,1)S(1)}, bf16[2,128,128]{2,1,0:T(8,128)(2,1)S(1)}, bf16[128,1024]{1,0:T(8,128)(2,1)S(1)}) custom-call(bf16[272,512]{1,0:T(8,128)(2,1)S(1)} %get-tuple-element.51.refs_0_, bf16[272,512]{1,0:T(8,128)(2,1)S(1)} %collective-permute-done.9.refs_1_, bf16[272,512]{1,0:T(8,128)(2,1)S(1)} %collective-permute-done.10.refs_2_.refs_1_, ...), custom_call_target="tpu_custom_call" | custom-call | tf_op jit(solution)/shard_map/pallas_call | solution.py:472
  72.3 4.2 %collective-permute-done.17.refs_1_ = bf16[272,512]{1,0:T(8,128)(2,1)S(1)} collective-permute-done((bf16[272,512]{1,0:T(8,128)(2,1)S(1)}, bf16[272,512]{1,0:T(8,128)(2,1)S(1)}, u32[]{:S(2)}, u32[]{:S(2)}) %collective-permute-start.17) | collective-permute-done | bytes 278560 | tf_op jit(solution)/shard_map/ppermute | solution.py:354
  76.5 0.3 collective-permute-start.21
  76.8 0.2 collective-permute-start.22
  77.0 1.3 shard_map.95
  78.4 1.3 shard_map.98
  79.7 5.9 %collective-permute-done.21.refs_0_ = bf16[272,512]{1,0:T(8,128)(2,1)S(1)} collective-permute-done((bf16[272,512]{1,0:T(8,128)(2,1)S(1)}, bf16[272,512]{1,0:T(8,128)(2,1)S(1)}, u32[]{:S(2)}, u32[]{:S(2)}) %collective-permute-start.21) | collective-permute-done | bytes 278560 | tf_op jit(solution)/shard_map/ppermute | solution.py:354
  85.6 1.6 %collective-permute-done.23.refs_3_ = bf16[272,512]{1,0:T(8,128)(2,1)S(1)} collective-permute-done((bf16[272,512]{1,0:T(8,128)(2,1)S(1)}, bf16[272,512]{1,0:T(8,128)(2,1)S(1)}, u32[]{:S(2)}, u32[]{:S(2)}) %collective-permute-start.23) | collective-permute-done | bytes 278560 | tf_op jit(solution)/shard_map/ppermute | solution.py:357
  87.1 1.3 shard_map.101
  88.5 3.5 %shard_map.103.near_ref = bf16[4,128,384]{2,1,0:T(8,128)(2,1)S(1)} custom-call(bf16[8,32,2048]{2,1,0:T(8,128)(2,1)S(1)} %get-tuple-element.54.refs_1_.refs_0_, bf16[8,32,2048]{2,1,0:T(8,128)(2,1)S(1)} %get-tuple-element.55.refs_1_, bf16[8,32,2048]{2,1,0:T(8,128)(2,1)S(1)} %get-tuple-element.57.refs_2_, bf16[8,32,2048]{2,1,0:T(8,128)(2,1)S(1)} %get-tuple-element.58.refs_3_, ...), custom_call_target="tpu_custom_call" | custom-call | tf_op jit(solution)/shard_map/pallas_call | solution.py:495
  92.0 0.2 collective-permute-start.25
  92.2 3.5 %shard_map.102.near_ref = bf16[4,128,384]{2,1,0:T(8,128)(2,1)S(1)} custom-call(bf16[8,32,2048]{2,1,0:T(8,128)(2,1)S(1)} %get-tuple-element.54.refs_1_.refs_0_, bf16[8,32,2048]{2,1,0:T(8,128)(2,1)S(1)} %get-tuple-element.55.refs_1_, bf16[8,32,2048]{2,1,0:T(8,128)(2,1)S(1)} %get-tuple-element.57.refs_2_, bf16[8,32,2048]{2,1,0:T(8,128)(2,1)S(1)} %get-tuple-element.58.refs_3_, ...), custom_call_target="tpu_custom_call" | custom-call | tf_op jit(solution)/shard_map/pallas_call | solution.py:495
  95.7 0.4 collective-permute-start.24
  96.2 1.3 shard_map.104.refs_0_
  97.5 0.0 collective-permute-done.24.far_ref
  97.5 1.9 %shard_map.105 = (bf16[128,1024]{1,0:T(8,128)(2,1)S(1)}, bf16[128,1024]{1,0:T(8,128)(2,1)S(1)}, bf16[128,1024]{1,0:T(8,128)(2,1)S(1)}, bf16[128,1024]{1,0:T(8,12...) custom-call(bf16[4,128,384]{2,1,0:T(8,128)(2,1)S(1)} %shard_map.102., ...), custom_call_target="tpu_custom_call" | custom-call | tf_op jit(solution)/shard_map/pallas_call | solution.py:515
  99.4 0.4 collective-permute-start.26
  99.8 1.7 %collective-permute-start.28 = (bf16[128,1024]{1,0:T(8,128)(2,1)S(1)}, bf16[128,1024]{1,0:T(8,128)(2,1)S(1)}, u32[]{:S(2)}, u32[]{:S(2)}) collective-permute-start(bf16[128,1024]{1,0:T(8,128)(2,1)S(1)} %get-tuple-element.75), channel_id=1, source_target_pairs={{0,2},{2,0},{4,6},{6,4},{8,10},{10,8},{12,14},{14,12},{1,3},{3,1},... | collective-permute-start | bytes 786440 | tf_op jit(solution)/shard_map/ppermute | solution.py:354
  101.5 0.3 collective-permute-start.30
  101.8 1.7 %collective-permute-start.32 = (bf16[128,1024]{1,0:T(8,128)(2,1)S(1)}, bf16[128,1024]{1,0:T(8,128)(2,1)S(1)}, u32[]{:S(2)}, u32[]{:S(2)}) collective-permute-start(bf16[128,1024]{1,0:T(8,128)(2,1)S(1)} %get-tuple-element.78), channel_id=1, source_target_pairs={{0,2},{2,0},{4,6},{6,4},{8,10},{10,8},{12,14},{14,12},{1,3},{3,1},... | collective-permute-start | bytes 786440 | tf_op jit(solution)/shard_map/ppermute | solution.py:354
  103.5 5.1 %collective-permute-done.26 = bf16[128,1024]{1,0:T(8,128)(2,1)S(1)} collective-permute-done((bf16[128,1024]{1,0:T(8,128)(2,1)S(1)}, bf16[128,1024]{1,0:T(8,128)(2,1)S(1)}, u32[]{:S(2)}, u32[]{:S(2)}) %collective-permute-start.26) | collective-permute-done | bytes 262176 | tf_op jit(solution)/shard_map/ppermute | solution.py:354
  108.6 0.1 add_convert_fusion.2
  108.7 0.7 collective-permute-start.27
  109.4 4.8 %collective-permute-done.28 = bf16[128,1024]{1,0:T(8,128)(2,1)S(1)} collective-permute-done((bf16[128,1024]{1,0:T(8,128)(2,1)S(1)}, bf16[128,1024]{1,0:T(8,128)(2,1)S(1)}, u32[]{:S(2)}, u32[]{:S(2)}) %collective-permute-start.28) | collective-permute-done | bytes 262176 | tf_op jit(solution)/shard_map/ppermute | solution.py:354
  114.2 0.1 add_convert_fusion.1
  114.3 0.1 collective-permute-start.29
  114.4 5.5 %collective-permute-done.30 = bf16[128,1024]{1,0:T(8,128)(2,1)S(1)} collective-permute-done((bf16[128,1024]{1,0:T(8,128)(2,1)S(1)}, bf16[128,1024]{1,0:T(8,128)(2,1)S(1)}, u32[]{:S(2)}, u32[]{:S(2)}) %collective-permute-start.30) | collective-permute-done | bytes 262176 | tf_op jit(solution)/shard_map/ppermute | solution.py:354
  119.8 0.1 add_convert_fusion
  119.9 0.1 collective-permute-start.31
  120.0 4.9 %collective-permute-done.32.refs_4_ = bf16[128,1024]{1,0:T(8,128)(2,1)S(1)} collective-permute-done((bf16[128,1024]{1,0:T(8,128)(2,1)S(1)}, bf16[128,1024]{1,0:T(8,128)(2,1)S(1)}, u32[]{:S(2)}, u32[]{:S(2)}) %collective-permute-start.32) | collective-permute-done | bytes 262176 | tf_op jit(solution)/shard_map/ppermute | solution.py:354
  124.9 7.0 %collective-permute-done.29.refs_2_ = bf16[128,1024]{1,0:T(8,128)(2,1)S(1)} collective-permute-done((bf16[128,1024]{1,0:T(8,128)(2,1)S(1)}, bf16[128,1024]{1,0:T(8,128)(2,1)S(1)}, u32[]{:S(2)}, u32[]{:S(2)}) %collective-permute-start.29) | collective-permute-done | bytes 262176 | tf_op jit(solution)/shard_map/ppermute | solution.py:354
  131.9 0.9 collective-permute-done.31.refs_3_
  132.8 0.9 shard_map.106
  (45 shorter events, 0.1 us)
Async XLA Ops:
  2.3 28.5 %collective-permute-start = (bf16[320,1024]{1,0:T(8,128)(2,1)}, bf16[320,1024]{1,0:T(8,128)(2,1)S(1)}, u32[]{:S(2)}, u32[]{:S(2)}) collective-permute-start(bf16[320,1024]{1,0:T(8,128)(2,1)} %get-tuple-element.45), channel_id=1, source_target_pairs={{0,2},{2,0},{4,6},{6,4},{8,10},{10,8},{12,14},{14,12},{1,3},{3,1},... | collective-permute-start | bytes 1966088 | tf_op jit(solution)/shard_map/ppermute | solution.py:354
  5.3 15.5 %collective-permute-start.3 = (bf16[128,1024]{1,0:T(8,128)(2,1)S(1)}, bf16[128,1024]{1,0:T(8,128)(2,1)S(1)}, u32[]{:S(2)}, u32[]{:S(2)}) collective-permute-start(bf16[128,1024]{1,0:T(8,128)(2,1)S(1)} %get-tuple-element.42._), channel_id=1, source_target_pairs={{0,8},{2,10},{4,12},{6,14},{8,0},{10,2},{12,4},{14,6},{1,9},{3,11}... | collective-permute-start | bytes 786440 | tf_op jit(solution)/shard_map/ppermute | solution.py:354
  7.9 16.6 %collective-permute-start.1 = (bf16[256,1024]{1,0:T(8,128)(2,1)S(1)}, bf16[256,1024]{1,0:T(8,128)(2,1)S(1)}, u32[]{:S(2)}, u32[]{:S(2)}) collective-permute-start(bf16[256,1024]{1,0:T(8,128)(2,1)S(1)} %get-tuple-element.44.own_ref), channel_id=1, source_target_pairs={{2,4},{6,8},{10,12},{4,2},{8,6},{12,10},{3,5},{7,9},{11,13},{5,3},... | collective-permute-start | bytes 1572872 | tf_op jit(solution)/shard_map/ppermute | solution.py:399
  10.5 11.7 %copy-start = (bf16[256,1024]{1,0:T(8,128)(2,1)S(1)}, bf16[256,1024]{1,0:T(8,128)(2,1)}, u32[]{:S(2)}) copy-start(bf16[256,1024]{1,0:T(8,128)(2,1)} %get-tuple-element.47.refs_0_) | copy-start | bytes 1572868
  10.5 12.3 %copy-start.1 = (bf16[2048,64]{0,1:T(8,128)(2,1)S(1)}, bf16[2048,64]{0,1:T(8,128)(2,1)}, u32[]{:S(2)}) copy-start(bf16[2048,64]{0,1:T(8,128)(2,1)} %param.12) | copy-start | bytes 786436
  10.5 12.3 %copy-start.2 = (f32[4,2048]{1,0:T(4,128)S(1)}, f32[4,2048]{1,0:T(4,128)}, u32[]{:S(2)}) copy-start(f32[4,2048]{1,0:T(4,128)} %mod_ref.1) | copy-start | bytes 98308
  10.6 12.3 %copy-start.3 = (s32[128,4]{0,1:T(4,128)S(1)}, s32[128,4]{0,1:T(4,128)}, u32[]{:S(2)}) copy-start(s32[128,4]{0,1:T(4,128)} %param.13) | copy-start | bytes 6148
  20.8 15.6 %collective-permute-start.6 = (bf16[128,1024]{1,0:T(8,128)(2,1)S(1)}, bf16[128,1024]{1,0:T(8,128)(2,1)S(1)}, u32[]{:S(2)}, u32[]{:S(2)}) collective-permute-start(bf16[128,1024]{1,0:T(8,128)(2,1)S(1)} %shard_map.87.refs_1_.refs_4_), channel_id=1, source_target_pairs={{0,4},{2,6},{4,0},{6,2},{8,12},{10,14},{12,8},{14,10},{1,5},{3,7},... | collective-permute-start | bytes 786440 | tf_op jit(solution)/shard_map/ppermute | solution.py:354
  22.2 22.0 %collective-permute-start.4 = (bf16[256,1024]{1,0:T(8,128)(2,1)S(1)}, bf16[256,1024]{1,0:T(8,128)(2,1)S(1)}, u32[]{:S(2)}, u32[]{:S(2)}) collective-permute-start(bf16[256,1024]{1,0:T(8,128)(2,1)S(1)} %shard_map.88.refs_2_), channel_id=1, source_target_pairs={{0,4},{2,6},{4,0},{6,2},{8,12},{10,14},{12,8},{14,10},{1,5},{3,7},... | collective-permute-start | bytes 1572872 | tf_op jit(solution)/shard_map/ppermute | solution.py:354
  22.8 15.1 %collective-permute-start.5 = (bf16[128,1024]{1,0:T(8,128)(2,1)S(1)}, bf16[128,1024]{1,0:T(8,128)(2,1)S(1)}, u32[]{:S(2)}, u32[]{:S(2)}) collective-permute-start(bf16[128,1024]{1,0:T(8,128)(2,1)S(1)} %shard_map.87.refs_1_.refs_4_), channel_id=1, source_target_pairs={{0,16},{16,0},{1,17},{17,1},{2,18},{18,2},{3,19},{19,3},{4,20},{20... | collective-permute-start | bytes 786440 | tf_op jit(solution)/shard_map/ppermute | solution.py:426
  33.9 10.3 %collective-permute-start.2 = (bf16[128,1024]{1,0:T(8,128)(2,1)S(1)}, bf16[128,1024]{1,0:T(8,128)(2,1)S(1)}, u32[]{:S(2)}, u32[]{:S(2)}) collective-permute-start(bf16[128,1024]{1,0:T(8,128)(2,1)S(1)} %shard_map.85.refs_1_.refs_0_), channel_id=1, source_target_pairs={{0,2},{2,0},{4,6},{6,4},{8,10},{10,8},{12,14},{14,12},{1,3},{3,1},... | collective-permute-start | bytes 786440 | tf_op jit(solution)/shard_map/ppermute | solution.py:354
  36.4 7.9 %collective-permute-start.7 = (bf16[128,1024]{1,0:T(8,128)(2,1)S(1)}, bf16[128,1024]{1,0:T(8,128)(2,1)S(1)}, u32[]{:S(2)}, u32[]{:S(2)}) collective-permute-start(bf16[128,1024]{1,0:T(8,128)(2,1)S(1)} %shard_map.89.refs_6_), channel_id=1, source_target_pairs={{0,16},{16,0},{1,17},{17,1},{2,18},{18,2},{3,19},{19,3},{4,20},{20... | collective-permute-start | bytes 786440 | tf_op jit(solution)/shard_map/ppermute | solution.py:426
  45.5 2.0 %collective-permute-start.8 = (f32[256,512]{1,0:T(8,128)S(1)}, f32[256,512]{1,0:T(8,128)S(1)}, u32[]{:S(2)}, u32[]{:S(2)}) collective-permute-start(f32[256,512]{1,0:T(8,128)S(1)} %shard_map.91), channel_id=1, source_target_pairs={{0,1},{1,0},{2,3},{3,2},{4,5},{5,4},{6,7},{7,6},{8,9},{9,8},{10,11... | collective-permute-start | bytes 1572872 | tf_op jit(solution)/shard_map/ppermute | solution.py:357
  47.6 1.6 %collective-permute-start.10 = (bf16[272,512]{1,0:T(8,128)(2,1)S(1)}, bf16[272,512]{1,0:T(8,128)(2,1)S(1)}, u32[]{:S(2)}, u32[]{:S(2)}) collective-permute-start(bf16[272,512]{1,0:T(8,128)(2,1)S(1)} %get-tuple-element.51.refs_0_), channel_id=1, source_target_pairs={{0,1},{1,0},{2,3},{3,2},{4,5},{5,4},{6,7},{7,6},{8,9},{9,8},{10,11... | collective-permute-start | bytes 835592 | tf_op jit(solution)/shard_map/ppermute | solution.py:357
  47.8 13.6 %collective-permute-start.12 = (bf16[272,512]{1,0:T(8,128)(2,1)S(1)}, bf16[272,512]{1,0:T(8,128)(2,1)S(1)}, u32[]{:S(2)}, u32[]{:S(2)}) collective-permute-start(bf16[272,512]{1,0:T(8,128)(2,1)S(1)} %get-tuple-element.51.refs_0_), channel_id=1, source_target_pairs={{0,4},{2,6},{4,0},{6,2},{8,12},{10,14},{12,8},{14,10},{1,5},{3,7},... | collective-permute-start | bytes 835592 | tf_op jit(solution)/shard_map/ppermute | solution.py:354
  48.4 13.1 %collective-permute-start.9 = (bf16[272,512]{1,0:T(8,128)(2,1)S(1)}, bf16[272,512]{1,0:T(8,128)(2,1)S(1)}, u32[]{:S(2)}, u32[]{:S(2)}) collective-permute-start(bf16[272,512]{1,0:T(8,128)(2,1)S(1)} %get-tuple-element.51.refs_0_), channel_id=1, source_target_pairs={{0,2},{2,0},{4,6},{6,4},{8,10},{10,8},{12,14},{14,12},{1,3},{3,1},... | collective-permute-start | bytes 835592 | tf_op jit(solution)/shard_map/ppermute | solution.py:354
  49.2 15.6 %collective-permute-start.16 = (bf16[272,512]{1,0:T(8,128)(2,1)S(1)}, bf16[272,512]{1,0:T(8,128)(2,1)S(1)}, u32[]{:S(2)}, u32[]{:S(2)}) collective-permute-start(bf16[272,512]{1,0:T(8,128)(2,1)S(1)} %shard_map.96), channel_id=1, source_target_pairs={{0,8},{2,10},{4,12},{6,14},{8,0},{10,2},{12,4},{14,6},{1,9},{3,11}... | collective-permute-start | bytes 835592 | tf_op jit(solution)/shard_map/ppermute | solution.py:354
  61.5 3.4 %collective-permute-start.14 = (bf16[272,512]{1,0:T(8,128)(2,1)S(1)}, bf16[272,512]{1,0:T(8,128)(2,1)S(1)}, u32[]{:S(2)}, u32[]{:S(2)}) collective-permute-start(bf16[272,512]{1,0:T(8,128)(2,1)S(1)} %shard_map.94.refs_0_), channel_id=1, source_target_pairs={{0,1},{1,0},{2,3},{3,2},{4,5},{5,4},{6,7},{7,6},{8,9},{9,8},{10,11... | collective-permute-start | bytes 835592 | tf_op jit(solution)/shard_map/ppermute | solution.py:357
  61.5 9.5 %collective-permute-start.13 = (bf16[272,512]{1,0:T(8,128)(2,1)S(1)}, bf16[272,512]{1,0:T(8,128)(2,1)S(1)}, u32[]{:S(2)}, u32[]{:S(2)}) collective-permute-start(bf16[272,512]{1,0:T(8,128)(2,1)S(1)} %shard_map.94.refs_0_), channel_id=1, source_target_pairs={{0,2},{2,0},{4,6},{6,4},{8,10},{10,8},{12,14},{14,12},{1,3},{3,1},... | collective-permute-start | bytes 835592 | tf_op jit(solution)/shard_map/ppermute | solution.py:354
  61.5 9.5 %collective-permute-start.11 = (bf16[272,512]{1,0:T(8,128)(2,1)S(1)}, bf16[272,512]{1,0:T(8,128)(2,1)S(1)}, u32[]{:S(2)}, u32[]{:S(2)}) collective-permute-start(bf16[272,512]{1,0:T(8,128)(2,1)S(1)} %collective-permute-done.9.refs_1_), channel_id=1, source_target_pairs={{0,1},{1,0},{2,3},{3,2},{4,5},{5,4},{6,7},{7,6},{8,9},{9,8},{10,11... | collective-permute-start | bytes 835592 | tf_op jit(solution)/shard_map/ppermute | solution.py:357
  64.9 11.6 %collective-permute-start.17 = (bf16[272,512]{1,0:T(8,128)(2,1)S(1)}, bf16[272,512]{1,0:T(8,128)(2,1)S(1)}, u32[]{:S(2)}, u32[]{:S(2)}) collective-permute-start(bf16[272,512]{1,0:T(8,128)(2,1)S(1)} %shard_map.97.refs_0_), channel_id=1, source_target_pairs={{0,2},{2,0},{4,6},{6,4},{8,10},{10,8},{12,14},{14,12},{1,3},{3,1},... | collective-permute-start | bytes 835592 | tf_op jit(solution)/shard_map/ppermute | solution.py:354
  65.7 10.8 %collective-permute-start.20 = (bf16[272,512]{1,0:T(8,128)(2,1)S(1)}, bf16[272,512]{1,0:T(8,128)(2,1)S(1)}, u32[]{:S(2)}, u32[]{:S(2)}) collective-permute-start(bf16[272,512]{1,0:T(8,128)(2,1)S(1)} %shard_map.97.refs_0_), channel_id=1, source_target_pairs={{0,4},{2,6},{4,0},{6,2},{8,12},{10,14},{12,8},{14,10},{1,5},{3,7},... | collective-permute-start | bytes 835592 | tf_op jit(solution)/shard_map/ppermute | solution.py:354
  65.7 12.6 %collective-permute-start.18 = (bf16[272,512]{1,0:T(8,128)(2,1)S(1)}, bf16[272,512]{1,0:T(8,128)(2,1)S(1)}, u32[]{:S(2)}, u32[]{:S(2)}) collective-permute-start(bf16[272,512]{1,0:T(8,128)(2,1)S(1)} %shard_map.97.refs_0_), channel_id=1, source_target_pairs={{0,1},{1,0},{2,3},{3,2},{4,5},{5,4},{6,7},{7,6},{8,9},{9,8},{10,11... | collective-permute-start | bytes 835592 | tf_op jit(solution)/shard_map/ppermute | solution.py:357
  71.0 6.0 %collective-permute-start.15 = (bf16[272,512]{1,0:T(8,128)(2,1)S(1)}, bf16[272,512]{1,0:T(8,128)(2,1)S(1)}, u32[]{:S(2)}, u32[]{:S(2)}) collective-permute-start(bf16[272,512]{1,0:T(8,128)(2,1)S(1)} %collective-permute-done.13.refs_1_), channel_id=1, source_target_pairs={{0,1},{1,0},{2,3},{3,2},{4,5},{5,4},{6,7},{7,6},{8,9},{9,8},{10,11... | collective-permute-start | bytes 835592 | tf_op jit(solution)/shard_map/ppermute | solution.py:357
  76.5 1.9 %collective-permute-start.19 = (bf16[272,512]{1,0:T(8,128)(2,1)S(1)}, bf16[272,512]{1,0:T(8,128)(2,1)S(1)}, u32[]{:S(2)}, u32[]{:S(2)}) collective-permute-start(bf16[272,512]{1,0:T(8,128)(2,1)S(1)} %collective-permute-done.17.refs_1_), channel_id=1, source_target_pairs={{0,1},{1,0},{2,3},{3,2},{4,5},{5,4},{6,7},{7,6},{8,9},{9,8},{10,11... | collective-permute-start | bytes 835592 | tf_op jit(solution)/shard_map/ppermute | solution.py:357
  76.5 9.1 %collective-permute-start.21 = (bf16[272,512]{1,0:T(8,128)(2,1)S(1)}, bf16[272,512]{1,0:T(8,128)(2,1)S(1)}, u32[]{:S(2)}, u32[]{:S(2)}) collective-permute-start(bf16[272,512]{1,0:T(8,128)(2,1)S(1)} %shard_map.99.refs_0_), channel_id=1, source_target_pairs={{0,2},{2,0},{4,6},{6,4},{8,10},{10,8},{12,14},{14,12},{1,3},{3,1},... | collective-permute-start | bytes 835592 | tf_op jit(solution)/shard_map/ppermute | solution.py:354
  76.8 8.7 %collective-permute-start.22 = (bf16[272,512]{1,0:T(8,128)(2,1)S(1)}, bf16[272,512]{1,0:T(8,128)(2,1)S(1)}, u32[]{:S(2)}, u32[]{:S(2)}) collective-permute-start(bf16[272,512]{1,0:T(8,128)(2,1)S(1)} %shard_map.99.refs_0_), channel_id=1, source_target_pairs={{0,1},{1,0},{2,3},{3,2},{4,5},{5,4},{6,7},{7,6},{8,9},{9,8},{10,11... | collective-permute-start | bytes 835592 | tf_op jit(solution)/shard_map/ppermute | solution.py:357
  85.6 1.6 %collective-permute-start.23 = (bf16[272,512]{1,0:T(8,128)(2,1)S(1)}, bf16[272,512]{1,0:T(8,128)(2,1)S(1)}, u32[]{:S(2)}, u32[]{:S(2)}) collective-permute-start(bf16[272,512]{1,0:T(8,128)(2,1)S(1)} %shard_map.100.refs_1_), channel_id=1, source_target_pairs={{0,1},{1,0},{2,3},{3,2},{4,5},{5,4},{6,7},{7,6},{8,9},{9,8},{10,11... | collective-permute-start | bytes 835592 | tf_op jit(solution)/shard_map/ppermute | solution.py:357
  88.5 7.7 %slice-start = ((s8[12582912]{0:T(1024)(128)(4,1)}), s8[4194304]{0:T(1024)(128)(4,1)S(1)}, s32[]{:S(2)}) async-start(s8[12582912]{0:T(1024)(128)(4,1)} %bitcast.4), calls=%async_computation | async-start | bytes 8388608
  88.5 7.7 %slice-start.1 = ((s8[12582912]{0:T(1024)(128)(4,1)}), s8[4194304]{0:T(1024)(128)(4,1)S(1)}, s32[]{:S(2)}) async-start(s8[12582912]{0:T(1024)(128)(4,1)} %bitcast.4), calls=%async_computation.1 | async-start | bytes 8388608
  92.0 4.2 %collective-permute-start.25 = (bf16[4,128,384]{2,1,0:T(8,128)(2,1)S(1)}, bf16[4,128,384]{2,1,0:T(8,128)(2,1)S(1)}, u32[]{:S(2)}, u32[]{:S(2)}) collective-permute-start(bf16[4,128,384]{2,1,0:T(8,128)(2,1)S(1)} %shard_map.103.near_ref), channel_id=1, source_target_pairs={{0,1},{1,0},{2,3},{3,2},{4,5},{5,4},{6,7},{7,6},{8,9},{9,8},{10,11... | collective-permute-start | bytes 1179656 | tf_op jit(solution)/shard_map/ppermute | solution.py:357
  92.2 4.0 %slice-start.2 = ((s8[12582912]{0:T(1024)(128)(4,1)}), s8[4194304]{0:T(1024)(128)(4,1)S(1)}, s32[]{:S(2)}) async-start(s8[12582912]{0:T(1024)(128)(4,1)} %bitcast.4), calls=%async_computation.2 | async-start | bytes 8388608
  95.7 1.8 %collective-permute-start.24 = (bf16[4,128,384]{2,1,0:T(8,128)(2,1)S(1)}, bf16[4,128,384]{2,1,0:T(8,128)(2,1)S(1)}, u32[]{:S(2)}, u32[]{:S(2)}) collective-permute-start(bf16[4,128,384]{2,1,0:T(8,128)(2,1)S(1)} %shard_map.102.near_ref), channel_id=1, source_target_pairs={{0,1},{1,0},{2,3},{3,2},{4,5},{5,4},{6,7},{7,6},{8,9},{9,8},{10,11... | collective-permute-start | bytes 1179656 | tf_op jit(solution)/shard_map/ppermute | solution.py:357
  99.4 9.2 %collective-permute-start.26 = (bf16[128,1024]{1,0:T(8,128)(2,1)S(1)}, bf16[128,1024]{1,0:T(8,128)(2,1)S(1)}, u32[]{:S(2)}, u32[]{:S(2)}) collective-permute-start(bf16[128,1024]{1,0:T(8,128)(2,1)S(1)} %get-tuple-element.73), channel_id=1, source_target_pairs={{0,2},{2,0},{4,6},{6,4},{8,10},{10,8},{12,14},{14,12},{1,3},{3,1},... | collective-permute-start | bytes 786440 | tf_op jit(solution)/shard_map/ppermute | solution.py:354
  99.8 14.5 %collective-permute-start.28 = (bf16[128,1024]{1,0:T(8,128)(2,1)S(1)}, bf16[128,1024]{1,0:T(8,128)(2,1)S(1)}, u32[]{:S(2)}, u32[]{:S(2)}) collective-permute-start(bf16[128,1024]{1,0:T(8,128)(2,1)S(1)} %get-tuple-element.75), channel_id=1, source_target_pairs={{0,2},{2,0},{4,6},{6,4},{8,10},{10,8},{12,14},{14,12},{1,3},{3,1},... | collective-permute-start | bytes 786440 | tf_op jit(solution)/shard_map/ppermute | solution.py:354
  101.5 18.3 %collective-permute-start.30 = (bf16[128,1024]{1,0:T(8,128)(2,1)S(1)}, bf16[128,1024]{1,0:T(8,128)(2,1)S(1)}, u32[]{:S(2)}, u32[]{:S(2)}) collective-permute-start(bf16[128,1024]{1,0:T(8,128)(2,1)S(1)} %get-tuple-element.77), channel_id=1, source_target_pairs={{0,2},{2,0},{4,6},{6,4},{8,10},{10,8},{12,14},{14,12},{1,3},{3,1},... | collective-permute-start | bytes 786440 | tf_op jit(solution)/shard_map/ppermute | solution.py:354
  101.8 23.1 %collective-permute-start.32 = (bf16[128,1024]{1,0:T(8,128)(2,1)S(1)}, bf16[128,1024]{1,0:T(8,128)(2,1)S(1)}, u32[]{:S(2)}, u32[]{:S(2)}) collective-permute-start(bf16[128,1024]{1,0:T(8,128)(2,1)S(1)} %get-tuple-element.78), channel_id=1, source_target_pairs={{0,2},{2,0},{4,6},{6,4},{8,10},{10,8},{12,14},{14,12},{1,3},{3,1},... | collective-permute-start | bytes 786440 | tf_op jit(solution)/shard_map/ppermute | solution.py:354
  108.7 16.2 %collective-permute-start.27 = (bf16[128,1024]{1,0:T(8,128)(2,1)S(1)}, bf16[128,1024]{1,0:T(8,128)(2,1)S(1)}, u32[]{:S(2)}, u32[]{:S(2)}) collective-permute-start(bf16[128,1024]{1,0:T(8,128)(2,1)S(1)} %add_convert_fusion.2), channel_id=1, source_target_pairs={{0,12},{2,14},{4,8},{6,10},{8,4},{10,6},{12,0},{14,2},{1,13},{3,15... | collective-permute-start | bytes 786440 | tf_op jit(solution)/shard_map/ppermute | solution.py:354
  114.3 17.6 %collective-permute-start.29 = (bf16[128,1024]{1,0:T(8,128)(2,1)S(1)}, bf16[128,1024]{1,0:T(8,128)(2,1)S(1)}, u32[]{:S(2)}, u32[]{:S(2)}) collective-permute-start(bf16[128,1024]{1,0:T(8,128)(2,1)S(1)} %add_convert_fusion.1), channel_id=1, source_target_pairs={{0,8},{2,10},{4,12},{6,14},{8,0},{10,2},{12,4},{14,6},{1,9},{3,11}... | collective-permute-start | bytes 786440 | tf_op jit(solution)/shard_map/ppermute | solution.py:354
  119.9 12.9 %collective-permute-start.31 = (bf16[128,1024]{1,0:T(8,128)(2,1)S(1)}, bf16[128,1024]{1,0:T(8,128)(2,1)S(1)}, u32[]{:S(2)}, u32[]{:S(2)}) collective-permute-start(bf16[128,1024]{1,0:T(8,128)(2,1)S(1)} %add_convert_fusion), channel_id=1, source_target_pairs={{0,4},{2,6},{4,0},{6,2},{8,12},{10,14},{12,8},{14,10},{1,5},{3,7},... | collective-permute-start | bytes 786440 | tf_op jit(solution)/shard_map/ppermute | solution.py:354

commit v10 on v9

--- a/solution.py
+++ b/solution.py
@@ -316,15 +316,27 @@
     for source in range(2 * steps):
         back = back_refs[source // 2][source % 2]
         rows = jnp.concatenate([ref[source] for ref in (*held_refs, held_ref)])
-        out_refs[source][...] = jnp.dot(back, rows, preferred_element_type=F32).astype(BF16)
-
-
-def final_kernel(state_ref, mod_ref, *refs):
-    routed = sum(ref[...].astype(F32) for ref in refs[:-1])
-    lanes = state_ref.shape[1]
+        routed = jnp.dot(back, rows, preferred_element_type=F32).astype(BF16)
+        if source < 2 * steps - 2:
+            out_refs[source][...] = routed
+        else:
+            half = routed.shape[0] // 2
+            at = 2 * source - (2 * steps - 2)
+            out_refs[at][...] = routed[:half]
+            out_refs[at + 1][...] = routed[half:]
+
+
+def final_kernel(state_ref, mod_ref, top_ref, bottom_ref, *refs):
+    out_ref = refs[-1]
+    count, lanes = state_ref.shape
     at = pl.multiple_of(lax.axis_index("sub") * lanes, 128)
     lift = 1.0 + mod_ref[3:4, pl.ds(at, lanes)]
-    refs[-1][...] = (state_ref[...].astype(F32) + lift * routed).astype(BF16)
+    for h, last_ref in enumerate((top_ref, bottom_ref)):
+        rows = slice(h * count // 2, (h + 1) * count // 2)
+        routed = last_ref[...].astype(F32)
+        for ref in refs[:-1]:
+            routed += ref[rows].astype(F32)
+        out_ref[rows] = (state_ref[rows].astype(F32) + lift * routed).astype(BF16)
 
 
 def gathered_body(
@@ -514,27 +526,32 @@
     low, high = groups_of[-1]
     share = pl.pallas_call(
         functools.partial(share_kernel, steps, low, len(held)),
-        out_shape=[struct((count, 2 * lanes), BF16)] * sources,
+        out_shape=[struct((count, 2 * lanes), BF16)] * (sources - 2)
+        + [struct((count // 2, 2 * lanes), BF16)] * 4,
         in_specs=[whole()] * (3 + len(held) + steps),
-        out_specs=[whole()] * sources,
+        out_specs=[whole()] * (sources + 2),
         scratch_shapes=[pltpu.VMEM((sources, (high - low) * SLOTS, 2 * lanes), BF16)],
         compiler_params=vmem(8),
     )(*hidden[-1], down_weight, *held, *backs)
 
-    terms = [share[0]]
-    for flip in range(steps - 1, -1, -1):
-        crossed = hop(share[2 * flip + 1], 1)
-        if flip:
-            crossed = (share[2 * flip].astype(F32) + crossed.astype(F32)).astype(BF16)
-            crossed = hop(crossed, 2 * flip)
-        terms.append(crossed)
+    def forwarded(mine, theirs, flip):
+        total = mine.astype(F32) + hop(theirs, 1).astype(F32)
+        return hop(total.astype(BF16), 2 * flip)
+
+    ends = share[-4:]
+    halves = [forwarded(ends[h], ends[2 + h], steps - 1) for h in range(2)]
+    terms = [
+        forwarded(share[2 * flip], share[2 * flip + 1], flip)
+        for flip in range(steps - 2, 0, -1)
+    ]
+    terms += [share[0], hop(share[1], 1)]
     return pl.pallas_call(
         final_kernel,
         out_shape=struct((count, 2 * lanes), BF16),
-        in_specs=[whole()] * (2 + len(terms)),
+        in_specs=[whole()] * (4 + len(terms)),
         out_specs=whole(),
         compiler_params=vmem(8),
-    )(state, small, *terms)
+    )(state, small, *halves, *terms)
 
 
 def extended(cells, sides, width):

time: 134 us -> 134 us (level)
    ppermute x19 -> x21, waiting for transfers between devices: 70.4 us -> 69.1 us  [hop(): return lax.ppermute(x, 'dev', [(i, i ^ flip) for i in range(devices)])]
    ppermute x19 -> x21, starting transfers between devices: 20.2 us -> 21.4 us  [hop(): return lax.ppermute(x, 'dev', [(i, i ^ flip) for i in range(devices)])]
  transfers between devices with their start and end apart: 33 -> 35, of which waited for: 17 -> 17; matrix products, arithmetic and copies ran while one was open for 0% -> 0% of each run, Pallas kernels for 18% -> 18%
where the time goes in v10:
time: 134 us
  waiting for transfers between devices  71.7 us (54%)
  Pallas kernels  34.9 us (26%)
  starting transfers between devices  26.7 us (20%)
    ppermute x21, waiting for transfers between devices, hop(): return lax.ppermute(x, 'dev', [(i, i ^ flip) for i in range(devices)])  69.1 us
    ppermute x21, starting transfers between devices, hop(): return lax.ppermute(x, 'dev', [(i, i ^ flip) for i in range(devices)])  21.4 us
    pallas_call x1, Pallas kernels, load(): pl.pallas_call(load_kernel, out_shape=[piece] * local + [jax.ShapeDtypeSt...  8.36 us
    pallas_call x2, Pallas kernels, gathered_body(): pl.pallas_call(functools.partial(hidden_kernel, steps, low), out_shape=st...  7.02 us
    pallas_call x4, Pallas kernels, gathered_body(): pl.pallas_call(functools.partial(select_kernel, local, topk, own), out_sh...  5.3 us
    ppermute x2, starting transfers between devices, gathered_body(): theirs = lax.ppermute(mine[flip], 'groups', [(0, 1), (1, 0)])  3.1 us
    pallas_call x1, Pallas kernels, gathered_body(): pl.pallas_call(attention_kernel, out_shape=struct((count, local_width), B...  3.1 us
  transfers between devices with their start and end apart: 35, of which 17 were waited for; matrix products, arithmetic and copies ran while one was open for 0% of the time, Pallas kernels for 18%

profile of v10, /device:TPU:0, one launch (start us, length us, event | category | flops | bytes accessed | tf_op | source)
XLA Modules:
  0.0 133.8 jit_solution(7561677742268919298)
XLA Ops:
  0.0 2.3 %shard_map.82 = (bf16[256,1024]{1,0:T(8,128)(2,1)S(1)}, bf16[320,1024]{1,0:T(8,128)(2,1)}, bf16[128,1024]{1,0:T(8,128)(2,1)S(1)}) custom-call(bf16[128,2048]{1,0:T(8,128)(2,1)} %tokens_ref.3, bf16[3,128,1024]{2,1,0:T(8,128)(2,1)} %bitcast.9, bf16[256,1024]{1,0:T(8,128)(2,1)} %weight_ref.3), custom_call_target="tpu_custom_call" | custom-call | tf_op jit(solution)/shard_map/pallas_call | solution.py:375
  2.3 3.0 %collective-permute-start = (bf16[320,1024]{1,0:T(8,128)(2,1)}, bf16[320,1024]{1,0:T(8,128)(2,1)S(1)}, u32[]{:S(2)}, u32[]{:S(2)}) collective-permute-start(bf16[320,1024]{1,0:T(8,128)(2,1)} %get-tuple-element.47), channel_id=1, source_target_pairs={{0,2},{2,0},{4,6},{6,4},{8,10},{10,8},{12,14},{14,12},{1,3},{3,1},... | collective-permute-start | bytes 1966088 | tf_op jit(solution)/shard_map/ppermute | solution.py:366
  5.3 2.6 %collective-permute-start.3 = (bf16[128,1024]{1,0:T(8,128)(2,1)S(1)}, bf16[128,1024]{1,0:T(8,128)(2,1)S(1)}, u32[]{:S(2)}, u32[]{:S(2)}) collective-permute-start(bf16[128,1024]{1,0:T(8,128)(2,1)S(1)} %get-tuple-element.44._), channel_id=1, source_target_pairs={{0,8},{2,10},{4,12},{6,14},{8,0},{10,2},{12,4},{14,6},{1,9},{3,11}... | collective-permute-start | bytes 786440 | tf_op jit(solution)/shard_map/ppermute | solution.py:366
  7.9 0.7 collective-permute-start.1
  8.6 2.0 %shard_map.83 = (bf16[128,1024]{1,0:T(8,128)(2,1)S(1)}, bf16[128,512]{1,0:T(8,128)(2,1)S(1)}, bf16[256,1024]{1,0:T(8,128)(2,1)}) custom-call(bf16[128,2048]{1,0:T(8,128)(2,1)} %tokens_ref.3, bf16[3,128,1024]{2,1,0:T(8,128)(2,1)} %bitcast.10, bf16[256,1024]{1,0:T(8,128)(2,1)} %weight_ref.3, bf16[128,1024]{1,0:T(8,128)(2,1)S(1)} %get-tuple-element.44._), custom_call_target="tpu_custom_call" | custom-call | tf_op jit(solution)/shard_map/pallas_call | solution.py:387
  10.6 8.4 %shard_map.86 = (bf16[2,2,192,2048]{3,2,1,0:T(8,128)(2,1)S(1)}, bf16[2,2,192,2048]{3,2,1,0:T(8,128)(2,1)S(1)}, bf16[2,2,192,2048]{3,2,1,0:T(8,128)(2,1)S(1)}, bf...) custom-call(bf16[16,2,192,2048]{3,2,1,0:T(8,128)(2,1)} %bitcast.8, ...), custom_call_target="tpu_custom_call" | custom-call | tf_op jit(solution)/shard_map/pallas_call | solution.py:272
  19.0 1.8 %collective-permute-done.3.refs_0_ = bf16[128,1024]{1,0:T(8,128)(2,1)S(1)} collective-permute-done((bf16[128,1024]{1,0:T(8,128)(2,1)S(1)}, bf16[128,1024]{1,0:T(8,128)(2,1)S(1)}, u32[]{:S(2)}, u32[]{:S(2)}) %collective-permute-start.3) | collective-permute-done | bytes 262176 | tf_op jit(solution)/shard_map/ppermute | solution.py:366
  20.8 1.5 %collective-permute-start.6 = (bf16[128,1024]{1,0:T(8,128)(2,1)S(1)}, bf16[128,1024]{1,0:T(8,128)(2,1)S(1)}, u32[]{:S(2)}, u32[]{:S(2)}) collective-permute-start(bf16[128,1024]{1,0:T(8,128)(2,1)S(1)} %shard_map.87.refs_1_.refs_4_), channel_id=1, source_target_pairs={{0,4},{2,6},{4,0},{6,2},{8,12},{10,14},{12,8},{14,10},{1,5},{3,7},... | collective-permute-start | bytes 786440 | tf_op jit(solution)/shard_map/ppermute | solution.py:366
  22.3 0.5 collective-permute-start.4
  22.8 1.6 %collective-permute-start.5 = (bf16[128,1024]{1,0:T(8,128)(2,1)S(1)}, bf16[128,1024]{1,0:T(8,128)(2,1)S(1)}, u32[]{:S(2)}, u32[]{:S(2)}) collective-permute-start(bf16[128,1024]{1,0:T(8,128)(2,1)S(1)} %shard_map.87.refs_1_.refs_4_), channel_id=1, source_target_pairs={{0,16},{16,0},{1,17},{17,1},{2,18},{18,2},{3,19},{19,3},{4,20},{20... | collective-permute-start | bytes 786440 | tf_op jit(solution)/shard_map/ppermute | solution.py:438
  24.4 6.4 %collective-permute-done.cross_ref = bf16[320,1024]{1,0:T(8,128)(2,1)S(1)} collective-permute-done((bf16[320,1024]{1,0:T(8,128)(2,1)}, bf16[320,1024]{1,0:T(8,128)(2,1)S(1)}, u32[]{:S(2)}, u32[]{:S(2)}) %collective-permute-start) | collective-permute-done | bytes 655392 | tf_op jit(solution)/shard_map/ppermute | solution.py:366
  30.8 3.1 %shard_map.85.refs_1_.refs_0_ = bf16[128,1024]{1,0:T(8,128)(2,1)S(1)} custom-call(bf16[128,1024]{1,0:T(8,128)(2,1)S(1)} %get-tuple-element.45._.query_ref, bf16[256,1024]{1,0:T(8,128)(2,1)S(1)} %get-tuple-element.46.own_ref, bf16[320,1024]{1,0:T(8,128)(2,1)S(1)} %collective-permute-done.cross_ref, bf16[256,1024]{1,0:T(8,128)(2,1)S(1)} %collective-permute-done.1.next_ref, ...), custom_call_target="tpu_custom_call" | custom-call | tf_op jit(solution)/shard_map/pallas_call | solution.py:427
  33.9 2.4 %collective-permute-start.2 = (bf16[128,1024]{1,0:T(8,128)(2,1)S(1)}, bf16[128,1024]{1,0:T(8,128)(2,1)S(1)}, u32[]{:S(2)}, u32[]{:S(2)}) collective-permute-start(bf16[128,1024]{1,0:T(8,128)(2,1)S(1)} %shard_map.85.refs_1_.refs_0_), channel_id=1, source_target_pairs={{0,2},{2,0},{4,6},{6,4},{8,10},{10,8},{12,14},{14,12},{1,3},{3,1},... | collective-permute-start | bytes 786440 | tf_op jit(solution)/shard_map/ppermute | solution.py:366
  36.4 1.5 %collective-permute-start.7 = (bf16[128,1024]{1,0:T(8,128)(2,1)S(1)}, bf16[128,1024]{1,0:T(8,128)(2,1)S(1)}, u32[]{:S(2)}, u32[]{:S(2)}) collective-permute-start(bf16[128,1024]{1,0:T(8,128)(2,1)S(1)} %shard_map.89.refs_6_), channel_id=1, source_target_pairs={{0,16},{16,0},{1,17},{17,1},{2,18},{18,2},{3,19},{19,3},{4,20},{20... | collective-permute-start | bytes 786440 | tf_op jit(solution)/shard_map/ppermute | solution.py:438
  37.9 6.4 %collective-permute-done.4.refs_3_ = bf16[256,1024]{1,0:T(8,128)(2,1)S(1)} collective-permute-done((bf16[256,1024]{1,0:T(8,128)(2,1)S(1)}, bf16[256,1024]{1,0:T(8,128)(2,1)S(1)}, u32[]{:S(2)}, u32[]{:S(2)}) %collective-permute-start.4) | collective-permute-done | bytes 524320 | tf_op jit(solution)/shard_map/ppermute | solution.py:366
  44.3 1.2 shard_map.91
  45.5 0.1 collective-permute-start.8
  45.6 1.2 shard_map.90.keep_ref
  46.8 0.7 collective-permute-done.8.got_ref
  47.5 0.1 shard_map.92
  47.6 0.2 collective-permute-start.10
  47.8 0.6 collective-permute-start.12
  48.4 0.5 collective-permute-start.9
  48.9 0.3 collective-permute-done.10.refs_2_.refs_1_
  49.2 2.8 %collective-permute-start.16 = (bf16[272,512]{1,0:T(8,128)(2,1)S(1)}, bf16[272,512]{1,0:T(8,128)(2,1)S(1)}, u32[]{:S(2)}, u32[]{:S(2)}) collective-permute-start(bf16[272,512]{1,0:T(8,128)(2,1)S(1)} %shard_map.96), channel_id=1, source_target_pairs={{0,8},{2,10},{4,12},{6,14},{8,0},{10,2},{12,4},{14,6},{1,9},{3,11}... | collective-permute-start | bytes 835592 | tf_op jit(solution)/shard_map/ppermute | solution.py:366
  52.0 9.5 %collective-permute-done.12.refs_0_ = bf16[272,512]{1,0:T(8,128)(2,1)S(1)} collective-permute-done((bf16[272,512]{1,0:T(8,128)(2,1)S(1)}, bf16[272,512]{1,0:T(8,128)(2,1)S(1)}, u32[]{:S(2)}, u32[]{:S(2)}) %collective-permute-start.12) | collective-permute-done | bytes 278560 | tf_op jit(solution)/shard_map/ppermute | solution.py:366
  61.4 0.1 collective-permute-start.13
  61.5 0.4 collective-permute-start.11
  62.0 2.9 %collective-permute-done.16.refs_0_ = bf16[272,512]{1,0:T(8,128)(2,1)S(1)} collective-permute-done((bf16[272,512]{1,0:T(8,128)(2,1)S(1)}, bf16[272,512]{1,0:T(8,128)(2,1)S(1)}, u32[]{:S(2)}, u32[]{:S(2)}) %collective-permute-start.16) | collective-permute-done | bytes 278560 | tf_op jit(solution)/shard_map/ppermute | solution.py:366
  64.8 0.9 collective-permute-start.17
  65.7 5.2 %collective-permute-done.13.refs_1_ = bf16[272,512]{1,0:T(8,128)(2,1)S(1)} collective-permute-done((bf16[272,512]{1,0:T(8,128)(2,1)S(1)}, bf16[272,512]{1,0:T(8,128)(2,1)S(1)}, u32[]{:S(2)}, u32[]{:S(2)}) %collective-permute-start.13) | collective-permute-done | bytes 278560 | tf_op jit(solution)/shard_map/ppermute | solution.py:366
  71.0 1.3 %shard_map.93 = (bf16[8,32,2048]{2,1,0:T(8,128)(2,1)S(1)}, bf16[2,128,128]{2,1,0:T(8,128)(2,1)S(1)}, bf16[128,1024]{1,0:T(8,128)(2,1)S(1)}) custom-call(bf16[272,512]{1,0:T(8,128)(2,1)S(1)} %get-tuple-element.53.refs_0_, bf16[272,512]{1,0:T(8,128)(2,1)S(1)} %collective-permute-done.9.refs_1_, bf16[272,512]{1,0:T(8,128)(2,1)S(1)} %collective-permute-done.10.refs_2_.refs_1_, ...), custom_call_target="tpu_custom_call" | custom-call | tf_op jit(solution)/shard_map/pallas_call | solution.py:484
  72.3 4.2 %collective-permute-done.17.refs_1_ = bf16[272,512]{1,0:T(8,128)(2,1)S(1)} collective-permute-done((bf16[272,512]{1,0:T(8,128)(2,1)S(1)}, bf16[272,512]{1,0:T(8,128)(2,1)S(1)}, u32[]{:S(2)}, u32[]{:S(2)}) %collective-permute-start.17) | collective-permute-done | bytes 278560 | tf_op jit(solution)/shard_map/ppermute | solution.py:366
  76.5 0.3 collective-permute-start.21
  76.8 0.2 collective-permute-start.22
  77.0 1.3 shard_map.95
  78.4 1.3 shard_map.98
  79.7 5.9 %collective-permute-done.21.refs_0_ = bf16[272,512]{1,0:T(8,128)(2,1)S(1)} collective-permute-done((bf16[272,512]{1,0:T(8,128)(2,1)S(1)}, bf16[272,512]{1,0:T(8,128)(2,1)S(1)}, u32[]{:S(2)}, u32[]{:S(2)}) %collective-permute-start.21) | collective-permute-done | bytes 278560 | tf_op jit(solution)/shard_map/ppermute | solution.py:366
  85.6 1.6 %collective-permute-done.23.refs_3_ = bf16[272,512]{1,0:T(8,128)(2,1)S(1)} collective-permute-done((bf16[272,512]{1,0:T(8,128)(2,1)S(1)}, bf16[272,512]{1,0:T(8,128)(2,1)S(1)}, u32[]{:S(2)}, u32[]{:S(2)}) %collective-permute-start.23) | collective-permute-done | bytes 278560 | tf_op jit(solution)/shard_map/ppermute | solution.py:369
  87.1 1.3 shard_map.101
  88.5 3.5 %shard_map.103.near_ref = bf16[4,128,384]{2,1,0:T(8,128)(2,1)S(1)} custom-call(bf16[8,32,2048]{2,1,0:T(8,128)(2,1)S(1)} %get-tuple-element.56.refs_1_.refs_0_, bf16[8,32,2048]{2,1,0:T(8,128)(2,1)S(1)} %get-tuple-element.57.refs_1_, bf16[8,32,2048]{2,1,0:T(8,128)(2,1)S(1)} %get-tuple-element.59.refs_2_, bf16[8,32,2048]{2,1,0:T(8,128)(2,1)S(1)} %get-tuple-element.60.refs_3_, ...), custom_call_target="tpu_custom_call" | custom-call | tf_op jit(solution)/shard_map/pallas_call | solution.py:507
  92.0 0.2 collective-permute-start.25
  92.2 3.5 %shard_map.102.near_ref = bf16[4,128,384]{2,1,0:T(8,128)(2,1)S(1)} custom-call(bf16[8,32,2048]{2,1,0:T(8,128)(2,1)S(1)} %get-tuple-element.56.refs_1_.refs_0_, bf16[8,32,2048]{2,1,0:T(8,128)(2,1)S(1)} %get-tuple-element.57.refs_1_, bf16[8,32,2048]{2,1,0:T(8,128)(2,1)S(1)} %get-tuple-element.59.refs_2_, bf16[8,32,2048]{2,1,0:T(8,128)(2,1)S(1)} %get-tuple-element.60.refs_3_, ...), custom_call_target="tpu_custom_call" | custom-call | tf_op jit(solution)/shard_map/pallas_call | solution.py:507
  95.7 0.4 collective-permute-start.24
  96.2 1.3 shard_map.104.refs_0_
  97.4 0.1 collective-permute-done.24.far_ref
  97.5 2.1 %shard_map.105 = (bf16[128,1024]{1,0:T(8,128)(2,1)S(1)}, bf16[128,1024]{1,0:T(8,128)(2,1)S(1)}, bf16[128,1024]{1,0:T(8,128)(2,1)S(1)}, bf16[128,1024]{1,0:T(8,12...) custom-call(bf16[4,128,384]{2,1,0:T(8,128)(2,1)S(1)} %shard_map.102., ...), custom_call_target="tpu_custom_call" | custom-call | tf_op jit(solution)/shard_map/pallas_call | solution.py:527
  99.6 0.3 collective-permute-start.26
  100.0 1.7 %collective-permute-start.30 = (bf16[128,1024]{1,0:T(8,128)(2,1)S(1)}, bf16[128,1024]{1,0:T(8,128)(2,1)S(1)}, u32[]{:S(2)}, u32[]{:S(2)}) collective-permute-start(bf16[128,1024]{1,0:T(8,128)(2,1)S(1)} %get-tuple-element.78), channel_id=1, source_target_pairs={{0,2},{2,0},{4,6},{6,4},{8,10},{10,8},{12,14},{14,12},{1,3},{3,1},... | collective-permute-start | bytes 786440 | tf_op jit(solution)/shard_map/ppermute | solution.py:366
  101.7 0.3 collective-permute-start.28
  102.0 1.7 %collective-permute-start.32 = (bf16[128,1024]{1,0:T(8,128)(2,1)S(1)}, bf16[128,1024]{1,0:T(8,128)(2,1)S(1)}, u32[]{:S(2)}, u32[]{:S(2)}) collective-permute-start(bf16[128,1024]{1,0:T(8,128)(2,1)S(1)} %get-tuple-element.80), channel_id=1, source_target_pairs={{0,2},{2,0},{4,6},{6,4},{8,10},{10,8},{12,14},{14,12},{1,3},{3,1},... | collective-permute-start | bytes 786440 | tf_op jit(solution)/shard_map/ppermute | solution.py:366
  103.8 0.3 collective-permute-start.34
  104.0 2.0 %collective-permute-done.26 = bf16[64,1024]{1,0:T(8,128)(2,1)S(1)} collective-permute-done((bf16[64,1024]{1,0:T(8,128)(2,1)S(1)}, bf16[64,1024]{1,0:T(8,128)(2,1)S(1)}, u32[]{:S(2)}, u32[]{:S(2)}) %collective-permute-start.26) | collective-permute-done | bytes 131104 | tf_op jit(solution)/shard_map/ppermute | solution.py:366
  106.1 0.8 collective-permute-start.27
  106.9 4.8 %collective-permute-done.30 = bf16[128,1024]{1,0:T(8,128)(2,1)S(1)} collective-permute-done((bf16[128,1024]{1,0:T(8,128)(2,1)S(1)}, bf16[128,1024]{1,0:T(8,128)(2,1)S(1)}, u32[]{:S(2)}, u32[]{:S(2)}) %collective-permute-start.30) | collective-permute-done | bytes 262176 | tf_op jit(solution)/shard_map/ppermute | solution.py:366
  111.6 0.1 add_convert_fusion.1
  111.7 0.1 collective-permute-start.31
  111.8 8.3 %collective-permute-done.32 = bf16[128,1024]{1,0:T(8,128)(2,1)S(1)} collective-permute-done((bf16[128,1024]{1,0:T(8,128)(2,1)S(1)}, bf16[128,1024]{1,0:T(8,128)(2,1)S(1)}, u32[]{:S(2)}, u32[]{:S(2)}) %collective-permute-start.32) | collective-permute-done | bytes 262176 | tf_op jit(solution)/shard_map/ppermute | solution.py:366
  120.1 0.1 add_convert_fusion
  120.1 0.1 collective-permute-start.33
  120.3 0.8 collective-permute-start.29
  121.1 8.3 %collective-permute-done.29.bottom_ref = bf16[64,1024]{1,0:T(8,128)(2,1)S(1)} collective-permute-done((bf16[64,1024]{1,0:T(8,128)(2,1)S(1)}, bf16[64,1024]{1,0:T(8,128)(2,1)S(1)}, u32[]{:S(2)}, u32[]{:S(2)}) %collective-permute-start.29) | collective-permute-done | bytes 131104 | tf_op jit(solution)/shard_map/ppermute | solution.py:366
  129.4 3.5 %collective-permute-done.33.refs_1_ = bf16[128,1024]{1,0:T(8,128)(2,1)S(1)} collective-permute-done((bf16[128,1024]{1,0:T(8,128)(2,1)S(1)}, bf16[128,1024]{1,0:T(8,128)(2,1)S(1)}, u32[]{:S(2)}, u32[]{:S(2)}) %collective-permute-start.33) | collective-permute-done | bytes 262176 | tf_op jit(solution)/shard_map/ppermute | solution.py:366
  132.9 0.9 shard_map.106
  (50 shorter events, 0.2 us)
Async XLA Ops:
  2.3 28.5 %collective-permute-start = (bf16[320,1024]{1,0:T(8,128)(2,1)}, bf16[320,1024]{1,0:T(8,128)(2,1)S(1)}, u32[]{:S(2)}, u32[]{:S(2)}) collective-permute-start(bf16[320,1024]{1,0:T(8,128)(2,1)} %get-tuple-element.47), channel_id=1, source_target_pairs={{0,2},{2,0},{4,6},{6,4},{8,10},{10,8},{12,14},{14,12},{1,3},{3,1},... | collective-permute-start | bytes 1966088 | tf_op jit(solution)/shard_map/ppermute | solution.py:366
  5.3 15.5 %collective-permute-start.3 = (bf16[128,1024]{1,0:T(8,128)(2,1)S(1)}, bf16[128,1024]{1,0:T(8,128)(2,1)S(1)}, u32[]{:S(2)}, u32[]{:S(2)}) collective-permute-start(bf16[128,1024]{1,0:T(8,128)(2,1)S(1)} %get-tuple-element.44._), channel_id=1, source_target_pairs={{0,8},{2,10},{4,12},{6,14},{8,0},{10,2},{12,4},{14,6},{1,9},{3,11}... | collective-permute-start | bytes 786440 | tf_op jit(solution)/shard_map/ppermute | solution.py:366
  7.9 16.6 %collective-permute-start.1 = (bf16[256,1024]{1,0:T(8,128)(2,1)S(1)}, bf16[256,1024]{1,0:T(8,128)(2,1)S(1)}, u32[]{:S(2)}, u32[]{:S(2)}) collective-permute-start(bf16[256,1024]{1,0:T(8,128)(2,1)S(1)} %get-tuple-element.46.own_ref), channel_id=1, source_target_pairs={{2,4},{6,8},{10,12},{4,2},{8,6},{12,10},{3,5},{7,9},{11,13},{5,3},... | collective-permute-start | bytes 1572872 | tf_op jit(solution)/shard_map/ppermute | solution.py:411
  10.5 11.7 %copy-start = (bf16[256,1024]{1,0:T(8,128)(2,1)S(1)}, bf16[256,1024]{1,0:T(8,128)(2,1)}, u32[]{:S(2)}) copy-start(bf16[256,1024]{1,0:T(8,128)(2,1)} %get-tuple-element.49.refs_0_) | copy-start | bytes 1572868
  10.6 12.2 %copy-start.1 = (bf16[2048,64]{0,1:T(8,128)(2,1)S(1)}, bf16[2048,64]{0,1:T(8,128)(2,1)}, u32[]{:S(2)}) copy-start(bf16[2048,64]{0,1:T(8,128)(2,1)} %param.12) | copy-start | bytes 786436
  10.6 12.2 %copy-start.2 = (f32[4,2048]{1,0:T(4,128)S(1)}, f32[4,2048]{1,0:T(4,128)}, u32[]{:S(2)}) copy-start(f32[4,2048]{1,0:T(4,128)} %mod_ref.1) | copy-start | bytes 98308
  10.6 12.2 %copy-start.3 = (s32[128,4]{0,1:T(4,128)S(1)}, s32[128,4]{0,1:T(4,128)}, u32[]{:S(2)}) copy-start(s32[128,4]{0,1:T(4,128)} %param.13) | copy-start | bytes 6148
  20.8 15.6 %collective-permute-start.6 = (bf16[128,1024]{1,0:T(8,128)(2,1)S(1)}, bf16[128,1024]{1,0:T(8,128)(2,1)S(1)}, u32[]{:S(2)}, u32[]{:S(2)}) collective-permute-start(bf16[128,1024]{1,0:T(8,128)(2,1)S(1)} %shard_map.87.refs_1_.refs_4_), channel_id=1, source_target_pairs={{0,4},{2,6},{4,0},{6,2},{8,12},{10,14},{12,8},{14,10},{1,5},{3,7},... | collective-permute-start | bytes 786440 | tf_op jit(solution)/shard_map/ppermute | solution.py:366
  22.3 22.0 %collective-permute-start.4 = (bf16[256,1024]{1,0:T(8,128)(2,1)S(1)}, bf16[256,1024]{1,0:T(8,128)(2,1)S(1)}, u32[]{:S(2)}, u32[]{:S(2)}) collective-permute-start(bf16[256,1024]{1,0:T(8,128)(2,1)S(1)} %shard_map.88.refs_2_), channel_id=1, source_target_pairs={{0,4},{2,6},{4,0},{6,2},{8,12},{10,14},{12,8},{14,10},{1,5},{3,7},... | collective-permute-start | bytes 1572872 | tf_op jit(solution)/shard_map/ppermute | solution.py:366
  22.8 15.1 %collective-permute-start.5 = (bf16[128,1024]{1,0:T(8,128)(2,1)S(1)}, bf16[128,1024]{1,0:T(8,128)(2,1)S(1)}, u32[]{:S(2)}, u32[]{:S(2)}) collective-permute-start(bf16[128,1024]{1,0:T(8,128)(2,1)S(1)} %shard_map.87.refs_1_.refs_4_), channel_id=1, source_target_pairs={{0,16},{16,0},{1,17},{17,1},{2,18},{18,2},{3,19},{19,3},{4,20},{20... | collective-permute-start | bytes 786440 | tf_op jit(solution)/shard_map/ppermute | solution.py:438
  33.9 10.3 %collective-permute-start.2 = (bf16[128,1024]{1,0:T(8,128)(2,1)S(1)}, bf16[128,1024]{1,0:T(8,128)(2,1)S(1)}, u32[]{:S(2)}, u32[]{:S(2)}) collective-permute-start(bf16[128,1024]{1,0:T(8,128)(2,1)S(1)} %shard_map.85.refs_1_.refs_0_), channel_id=1, source_target_pairs={{0,2},{2,0},{4,6},{6,4},{8,10},{10,8},{12,14},{14,12},{1,3},{3,1},... | collective-permute-start | bytes 786440 | tf_op jit(solution)/shard_map/ppermute | solution.py:366
  36.4 7.9 %collective-permute-start.7 = (bf16[128,1024]{1,0:T(8,128)(2,1)S(1)}, bf16[128,1024]{1,0:T(8,128)(2,1)S(1)}, u32[]{:S(2)}, u32[]{:S(2)}) collective-permute-start(bf16[128,1024]{1,0:T(8,128)(2,1)S(1)} %shard_map.89.refs_6_), channel_id=1, source_target_pairs={{0,16},{16,0},{1,17},{17,1},{2,18},{18,2},{3,19},{19,3},{4,20},{20... | collective-permute-start | bytes 786440 | tf_op jit(solution)/shard_map/ppermute | solution.py:438
  45.5 2.0 %collective-permute-start.8 = (f32[256,512]{1,0:T(8,128)S(1)}, f32[256,512]{1,0:T(8,128)S(1)}, u32[]{:S(2)}, u32[]{:S(2)}) collective-permute-start(f32[256,512]{1,0:T(8,128)S(1)} %shard_map.91), channel_id=1, source_target_pairs={{0,1},{1,0},{2,3},{3,2},{4,5},{5,4},{6,7},{7,6},{8,9},{9,8},{10,11... | collective-permute-start | bytes 1572872 | tf_op jit(solution)/shard_map/ppermute | solution.py:369
  47.6 1.6 %collective-permute-start.10 = (bf16[272,512]{1,0:T(8,128)(2,1)S(1)}, bf16[272,512]{1,0:T(8,128)(2,1)S(1)}, u32[]{:S(2)}, u32[]{:S(2)}) collective-permute-start(bf16[272,512]{1,0:T(8,128)(2,1)S(1)} %get-tuple-element.53.refs_0_), channel_id=1, source_target_pairs={{0,1},{1,0},{2,3},{3,2},{4,5},{5,4},{6,7},{7,6},{8,9},{9,8},{10,11... | collective-permute-start | bytes 835592 | tf_op jit(solution)/shard_map/ppermute | solution.py:369
  47.8 13.6 %collective-permute-start.12 = (bf16[272,512]{1,0:T(8,128)(2,1)S(1)}, bf16[272,512]{1,0:T(8,128)(2,1)S(1)}, u32[]{:S(2)}, u32[]{:S(2)}) collective-permute-start(bf16[272,512]{1,0:T(8,128)(2,1)S(1)} %get-tuple-element.53.refs_0_), channel_id=1, source_target_pairs={{0,4},{2,6},{4,0},{6,2},{8,12},{10,14},{12,8},{14,10},{1,5},{3,7},... | collective-permute-start | bytes 835592 | tf_op jit(solution)/shard_map/ppermute | solution.py:366
  48.4 13.0 %collective-permute-start.9 = (bf16[272,512]{1,0:T(8,128)(2,1)S(1)}, bf16[272,512]{1,0:T(8,128)(2,1)S(1)}, u32[]{:S(2)}, u32[]{:S(2)}) collective-permute-start(bf16[272,512]{1,0:T(8,128)(2,1)S(1)} %get-tuple-element.53.refs_0_), channel_id=1, source_target_pairs={{0,2},{2,0},{4,6},{6,4},{8,10},{10,8},{12,14},{14,12},{1,3},{3,1},... | collective-permute-start | bytes 835592 | tf_op jit(solution)/shard_map/ppermute | solution.py:366
  49.2 15.6 %collective-permute-start.16 = (bf16[272,512]{1,0:T(8,128)(2,1)S(1)}, bf16[272,512]{1,0:T(8,128)(2,1)S(1)}, u32[]{:S(2)}, u32[]{:S(2)}) collective-permute-start(bf16[272,512]{1,0:T(8,128)(2,1)S(1)} %shard_map.96), channel_id=1, source_target_pairs={{0,8},{2,10},{4,12},{6,14},{8,0},{10,2},{12,4},{14,6},{1,9},{3,11}... | collective-permute-start | bytes 835592 | tf_op jit(solution)/shard_map/ppermute | solution.py:366
  61.4 3.4 %collective-permute-start.14 = (bf16[272,512]{1,0:T(8,128)(2,1)S(1)}, bf16[272,512]{1,0:T(8,128)(2,1)S(1)}, u32[]{:S(2)}, u32[]{:S(2)}) collective-permute-start(bf16[272,512]{1,0:T(8,128)(2,1)S(1)} %shard_map.94.refs_0_), channel_id=1, source_target_pairs={{0,1},{1,0},{2,3},{3,2},{4,5},{5,4},{6,7},{7,6},{8,9},{9,8},{10,11... | collective-permute-start | bytes 835592 | tf_op jit(solution)/shard_map/ppermute | solution.py:369
  61.4 9.5 %collective-permute-start.13 = (bf16[272,512]{1,0:T(8,128)(2,1)S(1)}, bf16[272,512]{1,0:T(8,128)(2,1)S(1)}, u32[]{:S(2)}, u32[]{:S(2)}) collective-permute-start(bf16[272,512]{1,0:T(8,128)(2,1)S(1)} %shard_map.94.refs_0_), channel_id=1, source_target_pairs={{0,2},{2,0},{4,6},{6,4},{8,10},{10,8},{12,14},{14,12},{1,3},{3,1},... | collective-permute-start | bytes 835592 | tf_op jit(solution)/shard_map/ppermute | solution.py:366
  61.5 9.5 %collective-permute-start.11 = (bf16[272,512]{1,0:T(8,128)(2,1)S(1)}, bf16[272,512]{1,0:T(8,128)(2,1)S(1)}, u32[]{:S(2)}, u32[]{:S(2)}) collective-permute-start(bf16[272,512]{1,0:T(8,128)(2,1)S(1)} %collective-permute-done.9.refs_1_), channel_id=1, source_target_pairs={{0,1},{1,0},{2,3},{3,2},{4,5},{5,4},{6,7},{7,6},{8,9},{9,8},{10,11... | collective-permute-start | bytes 835592 | tf_op jit(solution)/shard_map/ppermute | solution.py:369
  64.8 11.6 %collective-permute-start.17 = (bf16[272,512]{1,0:T(8,128)(2,1)S(1)}, bf16[272,512]{1,0:T(8,128)(2,1)S(1)}, u32[]{:S(2)}, u32[]{:S(2)}) collective-permute-start(bf16[272,512]{1,0:T(8,128)(2,1)S(1)} %shard_map.97.refs_0_), channel_id=1, source_target_pairs={{0,2},{2,0},{4,6},{6,4},{8,10},{10,8},{12,14},{14,12},{1,3},{3,1},... | collective-permute-start | bytes 835592 | tf_op jit(solution)/shard_map/ppermute | solution.py:366
  65.7 10.8 %collective-permute-start.20 = (bf16[272,512]{1,0:T(8,128)(2,1)S(1)}, bf16[272,512]{1,0:T(8,128)(2,1)S(1)}, u32[]{:S(2)}, u32[]{:S(2)}) collective-permute-start(bf16[272,512]{1,0:T(8,128)(2,1)S(1)} %shard_map.97.refs_0_), channel_id=1, source_target_pairs={{0,4},{2,6},{4,0},{6,2},{8,12},{10,14},{12,8},{14,10},{1,5},{3,7},... | collective-permute-start | bytes 835592 | tf_op jit(solution)/shard_map/ppermute | solution.py:366
  65.7 12.6 %collective-permute-start.18 = (bf16[272,512]{1,0:T(8,128)(2,1)S(1)}, bf16[272,512]{1,0:T(8,128)(2,1)S(1)}, u32[]{:S(2)}, u32[]{:S(2)}) collective-permute-start(bf16[272,512]{1,0:T(8,128)(2,1)S(1)} %shard_map.97.refs_0_), channel_id=1, source_target_pairs={{0,1},{1,0},{2,3},{3,2},{4,5},{5,4},{6,7},{7,6},{8,9},{9,8},{10,11... | collective-permute-start | bytes 835592 | tf_op jit(solution)/shard_map/ppermute | solution.py:369
  71.0 6.0 %collective-permute-start.15 = (bf16[272,512]{1,0:T(8,128)(2,1)S(1)}, bf16[272,512]{1,0:T(8,128)(2,1)S(1)}, u32[]{:S(2)}, u32[]{:S(2)}) collective-permute-start(bf16[272,512]{1,0:T(8,128)(2,1)S(1)} %collective-permute-done.13.refs_1_), channel_id=1, source_target_pairs={{0,1},{1,0},{2,3},{3,2},{4,5},{5,4},{6,7},{7,6},{8,9},{9,8},{10,11... | collective-permute-start | bytes 835592 | tf_op jit(solution)/shard_map/ppermute | solution.py:369
  76.5 1.9 %collective-permute-start.19 = (bf16[272,512]{1,0:T(8,128)(2,1)S(1)}, bf16[272,512]{1,0:T(8,128)(2,1)S(1)}, u32[]{:S(2)}, u32[]{:S(2)}) collective-permute-start(bf16[272,512]{1,0:T(8,128)(2,1)S(1)} %collective-permute-done.17.refs_1_), channel_id=1, source_target_pairs={{0,1},{1,0},{2,3},{3,2},{4,5},{5,4},{6,7},{7,6},{8,9},{9,8},{10,11... | collective-permute-start | bytes 835592 | tf_op jit(solution)/shard_map/ppermute | solution.py:369
  76.5 9.1 %collective-permute-start.21 = (bf16[272,512]{1,0:T(8,128)(2,1)S(1)}, bf16[272,512]{1,0:T(8,128)(2,1)S(1)}, u32[]{:S(2)}, u32[]{:S(2)}) collective-permute-start(bf16[272,512]{1,0:T(8,128)(2,1)S(1)} %shard_map.99.refs_0_), channel_id=1, source_target_pairs={{0,2},{2,0},{4,6},{6,4},{8,10},{10,8},{12,14},{14,12},{1,3},{3,1},... | collective-permute-start | bytes 835592 | tf_op jit(solution)/shard_map/ppermute | solution.py:366
  76.8 8.7 %collective-permute-start.22 = (bf16[272,512]{1,0:T(8,128)(2,1)S(1)}, bf16[272,512]{1,0:T(8,128)(2,1)S(1)}, u32[]{:S(2)}, u32[]{:S(2)}) collective-permute-start(bf16[272,512]{1,0:T(8,128)(2,1)S(1)} %shard_map.99.refs_0_), channel_id=1, source_target_pairs={{0,1},{1,0},{2,3},{3,2},{4,5},{5,4},{6,7},{7,6},{8,9},{9,8},{10,11... | collective-permute-start | bytes 835592 | tf_op jit(solution)/shard_map/ppermute | solution.py:369
  85.6 1.6 %collective-permute-start.23 = (bf16[272,512]{1,0:T(8,128)(2,1)S(1)}, bf16[272,512]{1,0:T(8,128)(2,1)S(1)}, u32[]{:S(2)}, u32[]{:S(2)}) collective-permute-start(bf16[272,512]{1,0:T(8,128)(2,1)S(1)} %shard_map.100.refs_1_), channel_id=1, source_target_pairs={{0,1},{1,0},{2,3},{3,2},{4,5},{5,4},{6,7},{7,6},{8,9},{9,8},{10,11... | collective-permute-start | bytes 835592 | tf_op jit(solution)/shard_map/ppermute | solution.py:369
  88.4 7.7 %slice-start = ((s8[12582912]{0:T(1024)(128)(4,1)}), s8[4194304]{0:T(1024)(128)(4,1)S(1)}, s32[]{:S(2)}) async-start(s8[12582912]{0:T(1024)(128)(4,1)} %bitcast.4), calls=%async_computation | async-start | bytes 8388608
  88.5 7.7 %slice-start.1 = ((s8[12582912]{0:T(1024)(128)(4,1)}), s8[4194304]{0:T(1024)(128)(4,1)S(1)}, s32[]{:S(2)}) async-start(s8[12582912]{0:T(1024)(128)(4,1)} %bitcast.4), calls=%async_computation.1 | async-start | bytes 8388608
  92.0 4.2 %collective-permute-start.25 = (bf16[4,128,384]{2,1,0:T(8,128)(2,1)S(1)}, bf16[4,128,384]{2,1,0:T(8,128)(2,1)S(1)}, u32[]{:S(2)}, u32[]{:S(2)}) collective-permute-start(bf16[4,128,384]{2,1,0:T(8,128)(2,1)S(1)} %shard_map.103.near_ref), channel_id=1, source_target_pairs={{0,1},{1,0},{2,3},{3,2},{4,5},{5,4},{6,7},{7,6},{8,9},{9,8},{10,11... | collective-permute-start | bytes 1179656 | tf_op jit(solution)/shard_map/ppermute | solution.py:369
  92.2 4.0 %slice-start.2 = ((s8[12582912]{0:T(1024)(128)(4,1)}), s8[4194304]{0:T(1024)(128)(4,1)S(1)}, s32[]{:S(2)}) async-start(s8[12582912]{0:T(1024)(128)(4,1)} %bitcast.4), calls=%async_computation.2 | async-start | bytes 8388608
  95.7 1.8 %collective-permute-start.24 = (bf16[4,128,384]{2,1,0:T(8,128)(2,1)S(1)}, bf16[4,128,384]{2,1,0:T(8,128)(2,1)S(1)}, u32[]{:S(2)}, u32[]{:S(2)}) collective-permute-start(bf16[4,128,384]{2,1,0:T(8,128)(2,1)S(1)} %shard_map.102.near_ref), channel_id=1, source_target_pairs={{0,1},{1,0},{2,3},{3,2},{4,5},{5,4},{6,7},{7,6},{8,9},{9,8},{10,11... | collective-permute-start | bytes 1179656 | tf_op jit(solution)/shard_map/ppermute | solution.py:369
  99.6 6.4 %collective-permute-start.26 = (bf16[64,1024]{1,0:T(8,128)(2,1)S(1)}, bf16[64,1024]{1,0:T(8,128)(2,1)S(1)}, u32[]{:S(2)}, u32[]{:S(2)}) collective-permute-start(bf16[64,1024]{1,0:T(8,128)(2,1)S(1)} %get-tuple-element.74), channel_id=1, source_target_pairs={{0,2},{2,0},{4,6},{6,4},{8,10},{10,8},{12,14},{14,12},{1,3},{3,1},... | collective-permute-start | bytes 393224 | tf_op jit(solution)/shard_map/ppermute | solution.py:366
  100.0 11.6 %collective-permute-start.30 = (bf16[128,1024]{1,0:T(8,128)(2,1)S(1)}, bf16[128,1024]{1,0:T(8,128)(2,1)S(1)}, u32[]{:S(2)}, u32[]{:S(2)}) collective-permute-start(bf16[128,1024]{1,0:T(8,128)(2,1)S(1)} %get-tuple-element.78), channel_id=1, source_target_pairs={{0,2},{2,0},{4,6},{6,4},{8,10},{10,8},{12,14},{14,12},{1,3},{3,1},... | collective-permute-start | bytes 786440 | tf_op jit(solution)/shard_map/ppermute | solution.py:366
  101.7 18.5 %collective-permute-start.28 = (bf16[64,1024]{1,0:T(8,128)(2,1)S(1)}, bf16[64,1024]{1,0:T(8,128)(2,1)S(1)}, u32[]{:S(2)}, u32[]{:S(2)}) collective-permute-start(bf16[64,1024]{1,0:T(8,128)(2,1)S(1)} %get-tuple-element.76), channel_id=1, source_target_pairs={{0,2},{2,0},{4,6},{6,4},{8,10},{10,8},{12,14},{14,12},{1,3},{3,1},... | collective-permute-start | bytes 393224 | tf_op jit(solution)/shard_map/ppermute | solution.py:366
  102.0 18.0 %collective-permute-start.32 = (bf16[128,1024]{1,0:T(8,128)(2,1)S(1)}, bf16[128,1024]{1,0:T(8,128)(2,1)S(1)}, u32[]{:S(2)}, u32[]{:S(2)}) collective-permute-start(bf16[128,1024]{1,0:T(8,128)(2,1)S(1)} %get-tuple-element.80), channel_id=1, source_target_pairs={{0,2},{2,0},{4,6},{6,4},{8,10},{10,8},{12,14},{14,12},{1,3},{3,1},... | collective-permute-start | bytes 786440 | tf_op jit(solution)/shard_map/ppermute | solution.py:366
  103.8 25.6 %collective-permute-start.34 = (bf16[128,1024]{1,0:T(8,128)(2,1)S(1)}, bf16[128,1024]{1,0:T(8,128)(2,1)S(1)}, u32[]{:S(2)}, u32[]{:S(2)}) collective-permute-start(bf16[128,1024]{1,0:T(8,128)(2,1)S(1)} %get-tuple-element.82), channel_id=1, source_target_pairs={{0,2},{2,0},{4,6},{6,4},{8,10},{10,8},{12,14},{14,12},{1,3},{3,1},... | collective-permute-start | bytes 786440 | tf_op jit(solution)/shard_map/ppermute | solution.py:366
  106.1 15.0 %collective-permute-start.27 = (bf16[64,1024]{1,0:T(8,128)(2,1)S(1)}, bf16[64,1024]{1,0:T(8,128)(2,1)S(1)}, u32[]{:S(2)}, u32[]{:S(2)}) collective-permute-start(bf16[64,1024]{1,0:T(8,128)(2,1)S(1)} %add_convert_fusion.3), channel_id=1, source_target_pairs={{0,12},{2,14},{4,8},{6,10},{8,4},{10,6},{12,0},{14,2},{1,13},{3,15... | collective-permute-start | bytes 393224 | tf_op jit(solution)/shard_map/ppermute | solution.py:366
  111.7 17.7 %collective-permute-start.31 = (bf16[128,1024]{1,0:T(8,128)(2,1)S(1)}, bf16[128,1024]{1,0:T(8,128)(2,1)S(1)}, u32[]{:S(2)}, u32[]{:S(2)}) collective-permute-start(bf16[128,1024]{1,0:T(8,128)(2,1)S(1)} %add_convert_fusion.1), channel_id=1, source_target_pairs={{0,8},{2,10},{4,12},{6,14},{8,0},{10,2},{12,4},{14,6},{1,9},{3,11}... | collective-permute-start | bytes 786440 | tf_op jit(solution)/shard_map/ppermute | solution.py:366
  120.1 12.8 %collective-permute-start.33 = (bf16[128,1024]{1,0:T(8,128)(2,1)S(1)}, bf16[128,1024]{1,0:T(8,128)(2,1)S(1)}, u32[]{:S(2)}, u32[]{:S(2)}) collective-permute-start(bf16[128,1024]{1,0:T(8,128)(2,1)S(1)} %add_convert_fusion), channel_id=1, source_target_pairs={{0,4},{2,6},{4,0},{6,2},{8,12},{10,14},{12,8},{14,10},{1,5},{3,7},... | collective-permute-start | bytes 786440 | tf_op jit(solution)/shard_map/ppermute | solution.py:366
  120.3 9.1 %collective-permute-start.29 = (bf16[64,1024]{1,0:T(8,128)(2,1)S(1)}, bf16[64,1024]{1,0:T(8,128)(2,1)S(1)}, u32[]{:S(2)}, u32[]{:S(2)}) collective-permute-start(bf16[64,1024]{1,0:T(8,128)(2,1)S(1)} %add_convert_fusion.2), channel_id=1, source_target_pairs={{0,12},{2,14},{4,8},{6,10},{8,4},{10,6},{12,0},{14,2},{1,13},{3,15... | collective-permute-start | bytes 393224 | tf_op jit(solution)/shard_map/ppermute | solution.py:366

commit v11 on v10

--- a/solution.py
+++ b/solution.py
@@ -534,17 +534,17 @@
         compiler_params=vmem(8),
     )(*hidden[-1], down_weight, *held, *backs)
 
-    def forwarded(mine, theirs, flip):
-        total = mine.astype(F32) + hop(theirs, 1).astype(F32)
+    def forwarded(mine, crossed, flip):
+        total = mine.astype(F32) + crossed.astype(F32)
         return hop(total.astype(BF16), 2 * flip)
 
     ends = share[-4:]
-    halves = [forwarded(ends[h], ends[2 + h], steps - 1) for h in range(2)]
-    terms = [
-        forwarded(share[2 * flip], share[2 * flip + 1], flip)
-        for flip in range(steps - 2, 0, -1)
-    ]
-    terms += [share[0], hop(share[1], 1)]
+    top = hop(ends[2], 1)
+    crossed = {flip: hop(share[2 * flip + 1], 1) for flip in range(steps - 2, 0, -1)}
+    bottom = hop(tie(ends[3], top), 1)
+    halves = [forwarded(ends[0], top, steps - 1), forwarded(ends[1], bottom, steps - 1)]
+    terms = [forwarded(share[2 * flip], crossed[flip], flip) for flip in crossed]
+    terms += [share[0], hop(tie(share[1], crossed[steps - 2]), 1)]
     return pl.pallas_call(
         final_kernel,
         out_shape=struct((count, 2 * lanes), BF16),

time: 134 us -> 134 us (level)
  transfers between devices with their start and end apart: 35 -> 35, of which waited for: 17 -> 18; matrix products, arithmetic and copies ran while one was open for 0% -> 0% of each run, Pallas kernels for 18% -> 18%
where the time goes in v11:
time: 134 us; the launch traced here: 133 us
  waiting for transfers between devices  71.6 us (53%)
  Pallas kernels  34.9 us (26%)
  starting transfers between devices  26.4 us (20%)
    ppermute x21, waiting for transfers between devices, hop(): return lax.ppermute(x, 'dev', [(i, i ^ flip) for i in range(devices)])  68.9 us
    ppermute x21, starting transfers between devices, hop(): return lax.ppermute(x, 'dev', [(i, i ^ flip) for i in range(devices)])  21.1 us
    pallas_call x1, Pallas kernels, load(): pl.pallas_call(load_kernel, out_shape=[piece] * local + [jax.ShapeDtypeSt...  8.36 us
    pallas_call x2, Pallas kernels, gathered_body(): pl.pallas_call(functools.partial(hidden_kernel, steps, low), out_shape=st...  7.02 us
    pallas_call x4, Pallas kernels, gathered_body(): pl.pallas_call(functools.partial(select_kernel, local, topk, own), out_sh...  5.3 us
    ppermute x2, starting transfers between devices, gathered_body(): theirs = lax.ppermute(mine[flip], 'groups', [(0, 1), (1, 0)])  3.1 us
    pallas_call x1, Pallas kernels, gathered_body(): pl.pallas_call(attention_kernel, out_shape=struct((count, local_width), B...  3.1 us
  transfers between devices with their start and end apart: 35, of which 18 were waited for; matrix products, arithmetic and copies ran while one was open for 0% of the time, Pallas kernels for 18%

profile of v11, /device:TPU:0, one launch (start us, length us, event | category | flops | bytes accessed | tf_op | source)
XLA Modules:
  0.0 133.4 jit_solution(12690292231982627074)
XLA Ops:
  0.0 2.3 %shard_map.82 = (bf16[256,1024]{1,0:T(8,128)(2,1)S(1)}, bf16[320,1024]{1,0:T(8,128)(2,1)}, bf16[128,1024]{1,0:T(8,128)(2,1)S(1)}) custom-call(bf16[128,2048]{1,0:T(8,128)(2,1)} %tokens_ref.3, bf16[3,128,1024]{2,1,0:T(8,128)(2,1)} %bitcast.9, bf16[256,1024]{1,0:T(8,128)(2,1)} %weight_ref.3), custom_call_target="tpu_custom_call" | custom-call | tf_op jit(solution)/shard_map/pallas_call | solution.py:375
  2.3 3.0 %collective-permute-start = (bf16[320,1024]{1,0:T(8,128)(2,1)}, bf16[320,1024]{1,0:T(8,128)(2,1)S(1)}, u32[]{:S(2)}, u32[]{:S(2)}) collective-permute-start(bf16[320,1024]{1,0:T(8,128)(2,1)} %get-tuple-element.47), channel_id=1, source_target_pairs={{0,2},{2,0},{4,6},{6,4},{8,10},{10,8},{12,14},{14,12},{1,3},{3,1},... | collective-permute-start | bytes 1966088 | tf_op jit(solution)/shard_map/ppermute | solution.py:366
  5.3 2.6 %collective-permute-start.3 = (bf16[128,1024]{1,0:T(8,128)(2,1)S(1)}, bf16[128,1024]{1,0:T(8,128)(2,1)S(1)}, u32[]{:S(2)}, u32[]{:S(2)}) collective-permute-start(bf16[128,1024]{1,0:T(8,128)(2,1)S(1)} %get-tuple-element.44._), channel_id=1, source_target_pairs={{0,8},{2,10},{4,12},{6,14},{8,0},{10,2},{12,4},{14,6},{1,9},{3,11}... | collective-permute-start | bytes 786440 | tf_op jit(solution)/shard_map/ppermute | solution.py:366
  7.9 0.7 collective-permute-start.1
  8.6 2.0 %shard_map.83 = (bf16[128,1024]{1,0:T(8,128)(2,1)S(1)}, bf16[128,512]{1,0:T(8,128)(2,1)S(1)}, bf16[256,1024]{1,0:T(8,128)(2,1)}) custom-call(bf16[128,2048]{1,0:T(8,128)(2,1)} %tokens_ref.3, bf16[3,128,1024]{2,1,0:T(8,128)(2,1)} %bitcast.10, bf16[256,1024]{1,0:T(8,128)(2,1)} %weight_ref.3, bf16[128,1024]{1,0:T(8,128)(2,1)S(1)} %get-tuple-element.44._), custom_call_target="tpu_custom_call" | custom-call | tf_op jit(solution)/shard_map/pallas_call | solution.py:387
  10.6 8.4 %shard_map.86 = (bf16[2,2,192,2048]{3,2,1,0:T(8,128)(2,1)S(1)}, bf16[2,2,192,2048]{3,2,1,0:T(8,128)(2,1)S(1)}, bf16[2,2,192,2048]{3,2,1,0:T(8,128)(2,1)S(1)}, bf...) custom-call(bf16[16,2,192,2048]{3,2,1,0:T(8,128)(2,1)} %bitcast.8, ...), custom_call_target="tpu_custom_call" | custom-call | tf_op jit(solution)/shard_map/pallas_call | solution.py:272
  19.0 1.8 %collective-permute-done.3.refs_0_ = bf16[128,1024]{1,0:T(8,128)(2,1)S(1)} collective-permute-done((bf16[128,1024]{1,0:T(8,128)(2,1)S(1)}, bf16[128,1024]{1,0:T(8,128)(2,1)S(1)}, u32[]{:S(2)}, u32[]{:S(2)}) %collective-permute-start.3) | collective-permute-done | bytes 262176 | tf_op jit(solution)/shard_map/ppermute | solution.py:366
  20.8 1.5 %collective-permute-start.6 = (bf16[128,1024]{1,0:T(8,128)(2,1)S(1)}, bf16[128,1024]{1,0:T(8,128)(2,1)S(1)}, u32[]{:S(2)}, u32[]{:S(2)}) collective-permute-start(bf16[128,1024]{1,0:T(8,128)(2,1)S(1)} %shard_map.87.refs_1_.refs_4_), channel_id=1, source_target_pairs={{0,4},{2,6},{4,0},{6,2},{8,12},{10,14},{12,8},{14,10},{1,5},{3,7},... | collective-permute-start | bytes 786440 | tf_op jit(solution)/shard_map/ppermute | solution.py:366
  22.3 0.5 collective-permute-start.4
  22.8 1.6 %collective-permute-start.5 = (bf16[128,1024]{1,0:T(8,128)(2,1)S(1)}, bf16[128,1024]{1,0:T(8,128)(2,1)S(1)}, u32[]{:S(2)}, u32[]{:S(2)}) collective-permute-start(bf16[128,1024]{1,0:T(8,128)(2,1)S(1)} %shard_map.87.refs_1_.refs_4_), channel_id=1, source_target_pairs={{0,16},{16,0},{1,17},{17,1},{2,18},{18,2},{3,19},{19,3},{4,20},{20... | collective-permute-start | bytes 786440 | tf_op jit(solution)/shard_map/ppermute | solution.py:438
  24.4 6.4 %collective-permute-done.cross_ref = bf16[320,1024]{1,0:T(8,128)(2,1)S(1)} collective-permute-done((bf16[320,1024]{1,0:T(8,128)(2,1)}, bf16[320,1024]{1,0:T(8,128)(2,1)S(1)}, u32[]{:S(2)}, u32[]{:S(2)}) %collective-permute-start) | collective-permute-done | bytes 655392 | tf_op jit(solution)/shard_map/ppermute | solution.py:366
  30.8 3.1 %shard_map.85.refs_1_.refs_0_ = bf16[128,1024]{1,0:T(8,128)(2,1)S(1)} custom-call(bf16[128,1024]{1,0:T(8,128)(2,1)S(1)} %get-tuple-element.45._.query_ref, bf16[256,1024]{1,0:T(8,128)(2,1)S(1)} %get-tuple-element.46.own_ref, bf16[320,1024]{1,0:T(8,128)(2,1)S(1)} %collective-permute-done.cross_ref, bf16[256,1024]{1,0:T(8,128)(2,1)S(1)} %collective-permute-done.1.next_ref, ...), custom_call_target="tpu_custom_call" | custom-call | tf_op jit(solution)/shard_map/pallas_call | solution.py:427
  33.9 2.4 %collective-permute-start.2 = (bf16[128,1024]{1,0:T(8,128)(2,1)S(1)}, bf16[128,1024]{1,0:T(8,128)(2,1)S(1)}, u32[]{:S(2)}, u32[]{:S(2)}) collective-permute-start(bf16[128,1024]{1,0:T(8,128)(2,1)S(1)} %shard_map.85.refs_1_.refs_0_), channel_id=1, source_target_pairs={{0,2},{2,0},{4,6},{6,4},{8,10},{10,8},{12,14},{14,12},{1,3},{3,1},... | collective-permute-start | bytes 786440 | tf_op jit(solution)/shard_map/ppermute | solution.py:366
  36.4 1.5 %collective-permute-start.7 = (bf16[128,1024]{1,0:T(8,128)(2,1)S(1)}, bf16[128,1024]{1,0:T(8,128)(2,1)S(1)}, u32[]{:S(2)}, u32[]{:S(2)}) collective-permute-start(bf16[128,1024]{1,0:T(8,128)(2,1)S(1)} %shard_map.89.refs_6_), channel_id=1, source_target_pairs={{0,16},{16,0},{1,17},{17,1},{2,18},{18,2},{3,19},{19,3},{4,20},{20... | collective-permute-start | bytes 786440 | tf_op jit(solution)/shard_map/ppermute | solution.py:438
  37.9 6.4 %collective-permute-done.4.refs_3_ = bf16[256,1024]{1,0:T(8,128)(2,1)S(1)} collective-permute-done((bf16[256,1024]{1,0:T(8,128)(2,1)S(1)}, bf16[256,1024]{1,0:T(8,128)(2,1)S(1)}, u32[]{:S(2)}, u32[]{:S(2)}) %collective-permute-start.4) | collective-permute-done | bytes 524320 | tf_op jit(solution)/shard_map/ppermute | solution.py:366
  44.3 1.2 shard_map.91
  45.5 0.1 collective-permute-start.8
  45.6 1.2 shard_map.90.keep_ref
  46.8 0.7 collective-permute-done.8.got_ref
  47.5 0.1 shard_map.92
  47.6 0.2 collective-permute-start.10
  47.8 0.6 collective-permute-start.12
  48.4 0.5 collective-permute-start.9
  48.9 0.3 collective-permute-done.10.refs_2_.refs_1_
  49.2 2.8 %collective-permute-start.16 = (bf16[272,512]{1,0:T(8,128)(2,1)S(1)}, bf16[272,512]{1,0:T(8,128)(2,1)S(1)}, u32[]{:S(2)}, u32[]{:S(2)}) collective-permute-start(bf16[272,512]{1,0:T(8,128)(2,1)S(1)} %shard_map.96), channel_id=1, source_target_pairs={{0,8},{2,10},{4,12},{6,14},{8,0},{10,2},{12,4},{14,6},{1,9},{3,11}... | collective-permute-start | bytes 835592 | tf_op jit(solution)/shard_map/ppermute | solution.py:366
  52.0 9.5 %collective-permute-done.12.refs_0_ = bf16[272,512]{1,0:T(8,128)(2,1)S(1)} collective-permute-done((bf16[272,512]{1,0:T(8,128)(2,1)S(1)}, bf16[272,512]{1,0:T(8,128)(2,1)S(1)}, u32[]{:S(2)}, u32[]{:S(2)}) %collective-permute-start.12) | collective-permute-done | bytes 278560 | tf_op jit(solution)/shard_map/ppermute | solution.py:366
  61.4 0.1 collective-permute-start.13
  61.5 0.4 collective-permute-start.11
  62.0 2.9 %collective-permute-done.16.refs_0_ = bf16[272,512]{1,0:T(8,128)(2,1)S(1)} collective-permute-done((bf16[272,512]{1,0:T(8,128)(2,1)S(1)}, bf16[272,512]{1,0:T(8,128)(2,1)S(1)}, u32[]{:S(2)}, u32[]{:S(2)}) %collective-permute-start.16) | collective-permute-done | bytes 278560 | tf_op jit(solution)/shard_map/ppermute | solution.py:366
  64.8 0.9 collective-permute-start.17
  65.7 5.2 %collective-permute-done.13.refs_1_ = bf16[272,512]{1,0:T(8,128)(2,1)S(1)} collective-permute-done((bf16[272,512]{1,0:T(8,128)(2,1)S(1)}, bf16[272,512]{1,0:T(8,128)(2,1)S(1)}, u32[]{:S(2)}, u32[]{:S(2)}) %collective-permute-start.13) | collective-permute-done | bytes 278560 | tf_op jit(solution)/shard_map/ppermute | solution.py:366
  71.0 1.3 %shard_map.93 = (bf16[8,32,2048]{2,1,0:T(8,128)(2,1)S(1)}, bf16[2,128,128]{2,1,0:T(8,128)(2,1)S(1)}, bf16[128,1024]{1,0:T(8,128)(2,1)S(1)}) custom-call(bf16[272,512]{1,0:T(8,128)(2,1)S(1)} %get-tuple-element.53.refs_0_, bf16[272,512]{1,0:T(8,128)(2,1)S(1)} %collective-permute-done.9.refs_1_, bf16[272,512]{1,0:T(8,128)(2,1)S(1)} %collective-permute-done.10.refs_2_.refs_1_, ...), custom_call_target="tpu_custom_call" | custom-call | tf_op jit(solution)/shard_map/pallas_call | solution.py:484
  72.3 4.2 %collective-permute-done.17.refs_1_ = bf16[272,512]{1,0:T(8,128)(2,1)S(1)} collective-permute-done((bf16[272,512]{1,0:T(8,128)(2,1)S(1)}, bf16[272,512]{1,0:T(8,128)(2,1)S(1)}, u32[]{:S(2)}, u32[]{:S(2)}) %collective-permute-start.17) | collective-permute-done | bytes 278560 | tf_op jit(solution)/shard_map/ppermute | solution.py:366
  76.5 0.3 collective-permute-start.21
  76.8 0.2 collective-permute-start.22
  77.0 1.3 shard_map.95
  78.4 1.3 shard_map.98
  79.7 5.9 %collective-permute-done.21.refs_0_ = bf16[272,512]{1,0:T(8,128)(2,1)S(1)} collective-permute-done((bf16[272,512]{1,0:T(8,128)(2,1)S(1)}, bf16[272,512]{1,0:T(8,128)(2,1)S(1)}, u32[]{:S(2)}, u32[]{:S(2)}) %collective-permute-start.21) | collective-permute-done | bytes 278560 | tf_op jit(solution)/shard_map/ppermute | solution.py:366
  85.6 1.6 %collective-permute-done.23.refs_3_ = bf16[272,512]{1,0:T(8,128)(2,1)S(1)} collective-permute-done((bf16[272,512]{1,0:T(8,128)(2,1)S(1)}, bf16[272,512]{1,0:T(8,128)(2,1)S(1)}, u32[]{:S(2)}, u32[]{:S(2)}) %collective-permute-start.23) | collective-permute-done | bytes 278560 | tf_op jit(solution)/shard_map/ppermute | solution.py:369
  87.1 1.3 shard_map.101
  88.5 3.5 %shard_map.103.near_ref = bf16[4,128,384]{2,1,0:T(8,128)(2,1)S(1)} custom-call(bf16[8,32,2048]{2,1,0:T(8,128)(2,1)S(1)} %get-tuple-element.56.refs_1_.refs_0_, bf16[8,32,2048]{2,1,0:T(8,128)(2,1)S(1)} %get-tuple-element.57.refs_1_, bf16[8,32,2048]{2,1,0:T(8,128)(2,1)S(1)} %get-tuple-element.59.refs_2_, bf16[8,32,2048]{2,1,0:T(8,128)(2,1)S(1)} %get-tuple-element.60.refs_3_, ...), custom_call_target="tpu_custom_call" | custom-call | tf_op jit(solution)/shard_map/pallas_call | solution.py:507
  92.0 0.2 collective-permute-start.25
  92.2 3.5 %shard_map.102.near_ref = bf16[4,128,384]{2,1,0:T(8,128)(2,1)S(1)} custom-call(bf16[8,32,2048]{2,1,0:T(8,128)(2,1)S(1)} %get-tuple-element.56.refs_1_.refs_0_, bf16[8,32,2048]{2,1,0:T(8,128)(2,1)S(1)} %get-tuple-element.57.refs_1_, bf16[8,32,2048]{2,1,0:T(8,128)(2,1)S(1)} %get-tuple-element.59.refs_2_, bf16[8,32,2048]{2,1,0:T(8,128)(2,1)S(1)} %get-tuple-element.60.refs_3_, ...), custom_call_target="tpu_custom_call" | custom-call | tf_op jit(solution)/shard_map/pallas_call | solution.py:507
  95.7 0.4 collective-permute-start.24
  96.2 1.3 shard_map.104.refs_0_
  97.4 0.1 collective-permute-done.24.far_ref
  97.5 2.1 %shard_map.105 = (bf16[128,1024]{1,0:T(8,128)(2,1)S(1)}, bf16[128,1024]{1,0:T(8,128)(2,1)S(1)}, bf16[128,1024]{1,0:T(8,128)(2,1)S(1)}, bf16[128,1024]{1,0:T(8,12...) custom-call(bf16[4,128,384]{2,1,0:T(8,128)(2,1)S(1)} %shard_map.102., ...), custom_call_target="tpu_custom_call" | custom-call | tf_op jit(solution)/shard_map/pallas_call | solution.py:527
  99.6 0.3 collective-permute-start.26
  100.0 1.7 %collective-permute-start.30 = (bf16[128,1024]{1,0:T(8,128)(2,1)S(1)}, bf16[128,1024]{1,0:T(8,128)(2,1)S(1)}, u32[]{:S(2)}, u32[]{:S(2)}) collective-permute-start(bf16[128,1024]{1,0:T(8,128)(2,1)S(1)} %get-tuple-element.78), channel_id=1, source_target_pairs={{0,2},{2,0},{4,6},{6,4},{8,10},{10,8},{12,14},{14,12},{1,3},{3,1},... | collective-permute-start | bytes 786440 | tf_op jit(solution)/shard_map/ppermute | solution.py:366
  101.7 0.3 collective-permute-start.32
  102.0 4.0 %collective-permute-done.26.refs_1_ = bf16[64,1024]{1,0:T(8,128)(2,1)S(1)} collective-permute-done((bf16[64,1024]{1,0:T(8,128)(2,1)S(1)}, bf16[64,1024]{1,0:T(8,128)(2,1)S(1)}, u32[]{:S(2)}, u32[]{:S(2)}) %collective-permute-start.26) | collective-permute-done | bytes 131104 | tf_op jit(solution)/shard_map/ppermute | solution.py:366
  106.1 0.8 collective-permute-start.27
  106.9 1.4 %collective-permute-start.28 = (bf16[64,1024]{1,0:T(8,128)(2,1)S(1)}, bf16[64,1024]{1,0:T(8,128)(2,1)S(1)}, u32[]{:S(2)}, u32[]{:S(2)}) collective-permute-start(bf16[64,1024]{1,0:T(8,128)(2,1)S(1)} %shard_map.106), channel_id=1, source_target_pairs={{0,2},{2,0},{4,6},{6,4},{8,10},{10,8},{12,14},{14,12},{1,3},{3,1},... | collective-permute-start | bytes 393224 | tf_op jit(solution)/shard_map/ppermute | solution.py:366
  108.3 3.3 %collective-permute-done.30.refs_1_ = bf16[128,1024]{1,0:T(8,128)(2,1)S(1)} collective-permute-done((bf16[128,1024]{1,0:T(8,128)(2,1)S(1)}, bf16[128,1024]{1,0:T(8,128)(2,1)S(1)}, u32[]{:S(2)}, u32[]{:S(2)}) %collective-permute-start.30) | collective-permute-done | bytes 262176 | tf_op jit(solution)/shard_map/ppermute | solution.py:366
  111.6 0.1 add_convert_fusion.1
  111.7 0.1 collective-permute-start.31
  111.8 0.4 collective-permute-start.34
  112.2 5.1 %collective-permute-done.32 = bf16[128,1024]{1,0:T(8,128)(2,1)S(1)} collective-permute-done((bf16[128,1024]{1,0:T(8,128)(2,1)S(1)}, bf16[128,1024]{1,0:T(8,128)(2,1)S(1)}, u32[]{:S(2)}, u32[]{:S(2)}) %collective-permute-start.32) | collective-permute-done | bytes 262176 | tf_op jit(solution)/shard_map/ppermute | solution.py:366
  117.3 0.1 collective-permute-start.33
  117.4 2.7 %collective-permute-done.28 = bf16[64,1024]{1,0:T(8,128)(2,1)S(1)} collective-permute-done((bf16[64,1024]{1,0:T(8,128)(2,1)S(1)}, bf16[64,1024]{1,0:T(8,128)(2,1)S(1)}, u32[]{:S(2)}, u32[]{:S(2)}) %collective-permute-start.28) | collective-permute-done | bytes 131104 | tf_op jit(solution)/shard_map/ppermute | solution.py:366
  120.1 0.8 collective-permute-start.29
  120.9 6.6 %collective-permute-done.29.bottom_ref = bf16[64,1024]{1,0:T(8,128)(2,1)S(1)} collective-permute-done((bf16[64,1024]{1,0:T(8,128)(2,1)S(1)}, bf16[64,1024]{1,0:T(8,128)(2,1)S(1)}, u32[]{:S(2)}, u32[]{:S(2)}) %collective-permute-start.29) | collective-permute-done | bytes 131104 | tf_op jit(solution)/shard_map/ppermute | solution.py:366
  127.5 5.0 %collective-permute-done.33.refs_1_ = bf16[128,1024]{1,0:T(8,128)(2,1)S(1)} collective-permute-done((bf16[128,1024]{1,0:T(8,128)(2,1)S(1)}, bf16[128,1024]{1,0:T(8,128)(2,1)S(1)}, u32[]{:S(2)}, u32[]{:S(2)}) %collective-permute-start.33) | collective-permute-done | bytes 262176 | tf_op jit(solution)/shard_map/ppermute | solution.py:366
  132.5 0.9 shard_map.108
  (52 shorter events, 0.3 us)
Async XLA Ops:
  2.3 28.5 %collective-permute-start = (bf16[320,1024]{1,0:T(8,128)(2,1)}, bf16[320,1024]{1,0:T(8,128)(2,1)S(1)}, u32[]{:S(2)}, u32[]{:S(2)}) collective-permute-start(bf16[320,1024]{1,0:T(8,128)(2,1)} %get-tuple-element.47), channel_id=1, source_target_pairs={{0,2},{2,0},{4,6},{6,4},{8,10},{10,8},{12,14},{14,12},{1,3},{3,1},... | collective-permute-start | bytes 1966088 | tf_op jit(solution)/shard_map/ppermute | solution.py:366
  5.3 15.5 %collective-permute-start.3 = (bf16[128,1024]{1,0:T(8,128)(2,1)S(1)}, bf16[128,1024]{1,0:T(8,128)(2,1)S(1)}, u32[]{:S(2)}, u32[]{:S(2)}) collective-permute-start(bf16[128,1024]{1,0:T(8,128)(2,1)S(1)} %get-tuple-element.44._), channel_id=1, source_target_pairs={{0,8},{2,10},{4,12},{6,14},{8,0},{10,2},{12,4},{14,6},{1,9},{3,11}... | collective-permute-start | bytes 786440 | tf_op jit(solution)/shard_map/ppermute | solution.py:366
  7.9 16.6 %collective-permute-start.1 = (bf16[256,1024]{1,0:T(8,128)(2,1)S(1)}, bf16[256,1024]{1,0:T(8,128)(2,1)S(1)}, u32[]{:S(2)}, u32[]{:S(2)}) collective-permute-start(bf16[256,1024]{1,0:T(8,128)(2,1)S(1)} %get-tuple-element.46.own_ref), channel_id=1, source_target_pairs={{2,4},{6,8},{10,12},{4,2},{8,6},{12,10},{3,5},{7,9},{11,13},{5,3},... | collective-permute-start | bytes 1572872 | tf_op jit(solution)/shard_map/ppermute | solution.py:411
  10.5 11.7 %copy-start = (bf16[256,1024]{1,0:T(8,128)(2,1)S(1)}, bf16[256,1024]{1,0:T(8,128)(2,1)}, u32[]{:S(2)}) copy-start(bf16[256,1024]{1,0:T(8,128)(2,1)} %get-tuple-element.49.refs_0_) | copy-start | bytes 1572868
  10.6 12.2 %copy-start.1 = (bf16[2048,64]{0,1:T(8,128)(2,1)S(1)}, bf16[2048,64]{0,1:T(8,128)(2,1)}, u32[]{:S(2)}) copy-start(bf16[2048,64]{0,1:T(8,128)(2,1)} %param.12) | copy-start | bytes 786436
  10.6 12.2 %copy-start.2 = (f32[4,2048]{1,0:T(4,128)S(1)}, f32[4,2048]{1,0:T(4,128)}, u32[]{:S(2)}) copy-start(f32[4,2048]{1,0:T(4,128)} %mod_ref.1) | copy-start | bytes 98308
  10.6 12.2 %copy-start.3 = (s32[128,4]{0,1:T(4,128)S(1)}, s32[128,4]{0,1:T(4,128)}, u32[]{:S(2)}) copy-start(s32[128,4]{0,1:T(4,128)} %param.13) | copy-start | bytes 6148
  20.8 15.6 %collective-permute-start.6 = (bf16[128,1024]{1,0:T(8,128)(2,1)S(1)}, bf16[128,1024]{1,0:T(8,128)(2,1)S(1)}, u32[]{:S(2)}, u32[]{:S(2)}) collective-permute-start(bf16[128,1024]{1,0:T(8,128)(2,1)S(1)} %shard_map.87.refs_1_.refs_4_), channel_id=1, source_target_pairs={{0,4},{2,6},{4,0},{6,2},{8,12},{10,14},{12,8},{14,10},{1,5},{3,7},... | collective-permute-start | bytes 786440 | tf_op jit(solution)/shard_map/ppermute | solution.py:366
  22.3 22.0 %collective-permute-start.4 = (bf16[256,1024]{1,0:T(8,128)(2,1)S(1)}, bf16[256,1024]{1,0:T(8,128)(2,1)S(1)}, u32[]{:S(2)}, u32[]{:S(2)}) collective-permute-start(bf16[256,1024]{1,0:T(8,128)(2,1)S(1)} %shard_map.88.refs_2_), channel_id=1, source_target_pairs={{0,4},{2,6},{4,0},{6,2},{8,12},{10,14},{12,8},{14,10},{1,5},{3,7},... | collective-permute-start | bytes 1572872 | tf_op jit(solution)/shard_map/ppermute | solution.py:366
  22.8 15.1 %collective-permute-start.5 = (bf16[128,1024]{1,0:T(8,128)(2,1)S(1)}, bf16[128,1024]{1,0:T(8,128)(2,1)S(1)}, u32[]{:S(2)}, u32[]{:S(2)}) collective-permute-start(bf16[128,1024]{1,0:T(8,128)(2,1)S(1)} %shard_map.87.refs_1_.refs_4_), channel_id=1, source_target_pairs={{0,16},{16,0},{1,17},{17,1},{2,18},{18,2},{3,19},{19,3},{4,20},{20... | collective-permute-start | bytes 786440 | tf_op jit(solution)/shard_map/ppermute | solution.py:438
  33.9 10.3 %collective-permute-start.2 = (bf16[128,1024]{1,0:T(8,128)(2,1)S(1)}, bf16[128,1024]{1,0:T(8,128)(2,1)S(1)}, u32[]{:S(2)}, u32[]{:S(2)}) collective-permute-start(bf16[128,1024]{1,0:T(8,128)(2,1)S(1)} %shard_map.85.refs_1_.refs_0_), channel_id=1, source_target_pairs={{0,2},{2,0},{4,6},{6,4},{8,10},{10,8},{12,14},{14,12},{1,3},{3,1},... | collective-permute-start | bytes 786440 | tf_op jit(solution)/shard_map/ppermute | solution.py:366
  36.4 7.9 %collective-permute-start.7 = (bf16[128,1024]{1,0:T(8,128)(2,1)S(1)}, bf16[128,1024]{1,0:T(8,128)(2,1)S(1)}, u32[]{:S(2)}, u32[]{:S(2)}) collective-permute-start(bf16[128,1024]{1,0:T(8,128)(2,1)S(1)} %shard_map.89.refs_6_), channel_id=1, source_target_pairs={{0,16},{16,0},{1,17},{17,1},{2,18},{18,2},{3,19},{19,3},{4,20},{20... | collective-permute-start | bytes 786440 | tf_op jit(solution)/shard_map/ppermute | solution.py:438
  45.5 2.0 %collective-permute-start.8 = (f32[256,512]{1,0:T(8,128)S(1)}, f32[256,512]{1,0:T(8,128)S(1)}, u32[]{:S(2)}, u32[]{:S(2)}) collective-permute-start(f32[256,512]{1,0:T(8,128)S(1)} %shard_map.91), channel_id=1, source_target_pairs={{0,1},{1,0},{2,3},{3,2},{4,5},{5,4},{6,7},{7,6},{8,9},{9,8},{10,11... | collective-permute-start | bytes 1572872 | tf_op jit(solution)/shard_map/ppermute | solution.py:369
  47.6 1.6 %collective-permute-start.10 = (bf16[272,512]{1,0:T(8,128)(2,1)S(1)}, bf16[272,512]{1,0:T(8,128)(2,1)S(1)}, u32[]{:S(2)}, u32[]{:S(2)}) collective-permute-start(bf16[272,512]{1,0:T(8,128)(2,1)S(1)} %get-tuple-element.53.refs_0_), channel_id=1, source_target_pairs={{0,1},{1,0},{2,3},{3,2},{4,5},{5,4},{6,7},{7,6},{8,9},{9,8},{10,11... | collective-permute-start | bytes 835592 | tf_op jit(solution)/shard_map/ppermute | solution.py:369
  47.8 13.6 %collective-permute-start.12 = (bf16[272,512]{1,0:T(8,128)(2,1)S(1)}, bf16[272,512]{1,0:T(8,128)(2,1)S(1)}, u32[]{:S(2)}, u32[]{:S(2)}) collective-permute-start(bf16[272,512]{1,0:T(8,128)(2,1)S(1)} %get-tuple-element.53.refs_0_), channel_id=1, source_target_pairs={{0,4},{2,6},{4,0},{6,2},{8,12},{10,14},{12,8},{14,10},{1,5},{3,7},... | collective-permute-start | bytes 835592 | tf_op jit(solution)/shard_map/ppermute | solution.py:366
  48.4 13.0 %collective-permute-start.9 = (bf16[272,512]{1,0:T(8,128)(2,1)S(1)}, bf16[272,512]{1,0:T(8,128)(2,1)S(1)}, u32[]{:S(2)}, u32[]{:S(2)}) collective-permute-start(bf16[272,512]{1,0:T(8,128)(2,1)S(1)} %get-tuple-element.53.refs_0_), channel_id=1, source_target_pairs={{0,2},{2,0},{4,6},{6,4},{8,10},{10,8},{12,14},{14,12},{1,3},{3,1},... | collective-permute-start | bytes 835592 | tf_op jit(solution)/shard_map/ppermute | solution.py:366
  49.2 15.6 %collective-permute-start.16 = (bf16[272,512]{1,0:T(8,128)(2,1)S(1)}, bf16[272,512]{1,0:T(8,128)(2,1)S(1)}, u32[]{:S(2)}, u32[]{:S(2)}) collective-permute-start(bf16[272,512]{1,0:T(8,128)(2,1)S(1)} %shard_map.96), channel_id=1, source_target_pairs={{0,8},{2,10},{4,12},{6,14},{8,0},{10,2},{12,4},{14,6},{1,9},{3,11}... | collective-permute-start | bytes 835592 | tf_op jit(solution)/shard_map/ppermute | solution.py:366
  61.4 3.4 %collective-permute-start.14 = (bf16[272,512]{1,0:T(8,128)(2,1)S(1)}, bf16[272,512]{1,0:T(8,128)(2,1)S(1)}, u32[]{:S(2)}, u32[]{:S(2)}) collective-permute-start(bf16[272,512]{1,0:T(8,128)(2,1)S(1)} %shard_map.94.refs_0_), channel_id=1, source_target_pairs={{0,1},{1,0},{2,3},{3,2},{4,5},{5,4},{6,7},{7,6},{8,9},{9,8},{10,11... | collective-permute-start | bytes 835592 | tf_op jit(solution)/shard_map/ppermute | solution.py:369
  61.4 9.5 %collective-permute-start.13 = (bf16[272,512]{1,0:T(8,128)(2,1)S(1)}, bf16[272,512]{1,0:T(8,128)(2,1)S(1)}, u32[]{:S(2)}, u32[]{:S(2)}) collective-permute-start(bf16[272,512]{1,0:T(8,128)(2,1)S(1)} %shard_map.94.refs_0_), channel_id=1, source_target_pairs={{0,2},{2,0},{4,6},{6,4},{8,10},{10,8},{12,14},{14,12},{1,3},{3,1},... | collective-permute-start | bytes 835592 | tf_op jit(solution)/shard_map/ppermute | solution.py:366
  61.5 9.5 %collective-permute-start.11 = (bf16[272,512]{1,0:T(8,128)(2,1)S(1)}, bf16[272,512]{1,0:T(8,128)(2,1)S(1)}, u32[]{:S(2)}, u32[]{:S(2)}) collective-permute-start(bf16[272,512]{1,0:T(8,128)(2,1)S(1)} %collective-permute-done.9.refs_1_), channel_id=1, source_target_pairs={{0,1},{1,0},{2,3},{3,2},{4,5},{5,4},{6,7},{7,6},{8,9},{9,8},{10,11... | collective-permute-start | bytes 835592 | tf_op jit(solution)/shard_map/ppermute | solution.py:369
  64.8 11.6 %collective-permute-start.17 = (bf16[272,512]{1,0:T(8,128)(2,1)S(1)}, bf16[272,512]{1,0:T(8,128)(2,1)S(1)}, u32[]{:S(2)}, u32[]{:S(2)}) collective-permute-start(bf16[272,512]{1,0:T(8,128)(2,1)S(1)} %shard_map.97.refs_0_), channel_id=1, source_target_pairs={{0,2},{2,0},{4,6},{6,4},{8,10},{10,8},{12,14},{14,12},{1,3},{3,1},... | collective-permute-start | bytes 835592 | tf_op jit(solution)/shard_map/ppermute | solution.py:366
  65.7 10.8 %collective-permute-start.20 = (bf16[272,512]{1,0:T(8,128)(2,1)S(1)}, bf16[272,512]{1,0:T(8,128)(2,1)S(1)}, u32[]{:S(2)}, u32[]{:S(2)}) collective-permute-start(bf16[272,512]{1,0:T(8,128)(2,1)S(1)} %shard_map.97.refs_0_), channel_id=1, source_target_pairs={{0,4},{2,6},{4,0},{6,2},{8,12},{10,14},{12,8},{14,10},{1,5},{3,7},... | collective-permute-start | bytes 835592 | tf_op jit(solution)/shard_map/ppermute | solution.py:366
  65.7 12.6 %collective-permute-start.18 = (bf16[272,512]{1,0:T(8,128)(2,1)S(1)}, bf16[272,512]{1,0:T(8,128)(2,1)S(1)}, u32[]{:S(2)}, u32[]{:S(2)}) collective-permute-start(bf16[272,512]{1,0:T(8,128)(2,1)S(1)} %shard_map.97.refs_0_), channel_id=1, source_target_pairs={{0,1},{1,0},{2,3},{3,2},{4,5},{5,4},{6,7},{7,6},{8,9},{9,8},{10,11... | collective-permute-start | bytes 835592 | tf_op jit(solution)/shard_map/ppermute | solution.py:369
  71.0 6.0 %collective-permute-start.15 = (bf16[272,512]{1,0:T(8,128)(2,1)S(1)}, bf16[272,512]{1,0:T(8,128)(2,1)S(1)}, u32[]{:S(2)}, u32[]{:S(2)}) collective-permute-start(bf16[272,512]{1,0:T(8,128)(2,1)S(1)} %collective-permute-done.13.refs_1_), channel_id=1, source_target_pairs={{0,1},{1,0},{2,3},{3,2},{4,5},{5,4},{6,7},{7,6},{8,9},{9,8},{10,11... | collective-permute-start | bytes 835592 | tf_op jit(solution)/shard_map/ppermute | solution.py:369
  76.5 1.9 %collective-permute-start.19 = (bf16[272,512]{1,0:T(8,128)(2,1)S(1)}, bf16[272,512]{1,0:T(8,128)(2,1)S(1)}, u32[]{:S(2)}, u32[]{:S(2)}) collective-permute-start(bf16[272,512]{1,0:T(8,128)(2,1)S(1)} %collective-permute-done.17.refs_1_), channel_id=1, source_target_pairs={{0,1},{1,0},{2,3},{3,2},{4,5},{5,4},{6,7},{7,6},{8,9},{9,8},{10,11... | collective-permute-start | bytes 835592 | tf_op jit(solution)/shard_map/ppermute | solution.py:369
  76.5 9.1 %collective-permute-start.21 = (bf16[272,512]{1,0:T(8,128)(2,1)S(1)}, bf16[272,512]{1,0:T(8,128)(2,1)S(1)}, u32[]{:S(2)}, u32[]{:S(2)}) collective-permute-start(bf16[272,512]{1,0:T(8,128)(2,1)S(1)} %shard_map.99.refs_0_), channel_id=1, source_target_pairs={{0,2},{2,0},{4,6},{6,4},{8,10},{10,8},{12,14},{14,12},{1,3},{3,1},... | collective-permute-start | bytes 835592 | tf_op jit(solution)/shard_map/ppermute | solution.py:366
  76.8 8.7 %collective-permute-start.22 = (bf16[272,512]{1,0:T(8,128)(2,1)S(1)}, bf16[272,512]{1,0:T(8,128)(2,1)S(1)}, u32[]{:S(2)}, u32[]{:S(2)}) collective-permute-start(bf16[272,512]{1,0:T(8,128)(2,1)S(1)} %shard_map.99.refs_0_), channel_id=1, source_target_pairs={{0,1},{1,0},{2,3},{3,2},{4,5},{5,4},{6,7},{7,6},{8,9},{9,8},{10,11... | collective-permute-start | bytes 835592 | tf_op jit(solution)/shard_map/ppermute | solution.py:369
  85.6 1.6 %collective-permute-start.23 = (bf16[272,512]{1,0:T(8,128)(2,1)S(1)}, bf16[272,512]{1,0:T(8,128)(2,1)S(1)}, u32[]{:S(2)}, u32[]{:S(2)}) collective-permute-start(bf16[272,512]{1,0:T(8,128)(2,1)S(1)} %shard_map.100.refs_1_), channel_id=1, source_target_pairs={{0,1},{1,0},{2,3},{3,2},{4,5},{5,4},{6,7},{7,6},{8,9},{9,8},{10,11... | collective-permute-start | bytes 835592 | tf_op jit(solution)/shard_map/ppermute | solution.py:369
  88.4 7.7 %slice-start = ((s8[12582912]{0:T(1024)(128)(4,1)}), s8[4194304]{0:T(1024)(128)(4,1)S(1)}, s32[]{:S(2)}) async-start(s8[12582912]{0:T(1024)(128)(4,1)} %bitcast.4), calls=%async_computation | async-start | bytes 8388608
  88.5 7.7 %slice-start.1 = ((s8[12582912]{0:T(1024)(128)(4,1)}), s8[4194304]{0:T(1024)(128)(4,1)S(1)}, s32[]{:S(2)}) async-start(s8[12582912]{0:T(1024)(128)(4,1)} %bitcast.4), calls=%async_computation.1 | async-start | bytes 8388608
  92.0 4.2 %collective-permute-start.25 = (bf16[4,128,384]{2,1,0:T(8,128)(2,1)S(1)}, bf16[4,128,384]{2,1,0:T(8,128)(2,1)S(1)}, u32[]{:S(2)}, u32[]{:S(2)}) collective-permute-start(bf16[4,128,384]{2,1,0:T(8,128)(2,1)S(1)} %shard_map.103.near_ref), channel_id=1, source_target_pairs={{0,1},{1,0},{2,3},{3,2},{4,5},{5,4},{6,7},{7,6},{8,9},{9,8},{10,11... | collective-permute-start | bytes 1179656 | tf_op jit(solution)/shard_map/ppermute | solution.py:369
  92.2 4.0 %slice-start.2 = ((s8[12582912]{0:T(1024)(128)(4,1)}), s8[4194304]{0:T(1024)(128)(4,1)S(1)}, s32[]{:S(2)}) async-start(s8[12582912]{0:T(1024)(128)(4,1)} %bitcast.4), calls=%async_computation.2 | async-start | bytes 8388608
  95.7 1.8 %collective-permute-start.24 = (bf16[4,128,384]{2,1,0:T(8,128)(2,1)S(1)}, bf16[4,128,384]{2,1,0:T(8,128)(2,1)S(1)}, u32[]{:S(2)}, u32[]{:S(2)}) collective-permute-start(bf16[4,128,384]{2,1,0:T(8,128)(2,1)S(1)} %shard_map.102.near_ref), channel_id=1, source_target_pairs={{0,1},{1,0},{2,3},{3,2},{4,5},{5,4},{6,7},{7,6},{8,9},{9,8},{10,11... | collective-permute-start | bytes 1179656 | tf_op jit(solution)/shard_map/ppermute | solution.py:369
  99.6 6.4 %collective-permute-start.26 = (bf16[64,1024]{1,0:T(8,128)(2,1)S(1)}, bf16[64,1024]{1,0:T(8,128)(2,1)S(1)}, u32[]{:S(2)}, u32[]{:S(2)}) collective-permute-start(bf16[64,1024]{1,0:T(8,128)(2,1)S(1)} %get-tuple-element.74), channel_id=1, source_target_pairs={{0,2},{2,0},{4,6},{6,4},{8,10},{10,8},{12,14},{14,12},{1,3},{3,1},... | collective-permute-start | bytes 393224 | tf_op jit(solution)/shard_map/ppermute | solution.py:366
  100.0 11.6 %collective-permute-start.30 = (bf16[128,1024]{1,0:T(8,128)(2,1)S(1)}, bf16[128,1024]{1,0:T(8,128)(2,1)S(1)}, u32[]{:S(2)}, u32[]{:S(2)}) collective-permute-start(bf16[128,1024]{1,0:T(8,128)(2,1)S(1)} %get-tuple-element.78), channel_id=1, source_target_pairs={{0,2},{2,0},{4,6},{6,4},{8,10},{10,8},{12,14},{14,12},{1,3},{3,1},... | collective-permute-start | bytes 786440 | tf_op jit(solution)/shard_map/ppermute | solution.py:366
  101.7 15.5 %collective-permute-start.32 = (bf16[128,1024]{1,0:T(8,128)(2,1)S(1)}, bf16[128,1024]{1,0:T(8,128)(2,1)S(1)}, u32[]{:S(2)}, u32[]{:S(2)}) collective-permute-start(bf16[128,1024]{1,0:T(8,128)(2,1)S(1)} %get-tuple-element.80), channel_id=1, source_target_pairs={{0,2},{2,0},{4,6},{6,4},{8,10},{10,8},{12,14},{14,12},{1,3},{3,1},... | collective-permute-start | bytes 786440 | tf_op jit(solution)/shard_map/ppermute | solution.py:366
  106.1 14.8 %collective-permute-start.27 = (bf16[64,1024]{1,0:T(8,128)(2,1)S(1)}, bf16[64,1024]{1,0:T(8,128)(2,1)S(1)}, u32[]{:S(2)}, u32[]{:S(2)}) collective-permute-start(bf16[64,1024]{1,0:T(8,128)(2,1)S(1)} %add_convert_fusion.3), channel_id=1, source_target_pairs={{0,12},{2,14},{4,8},{6,10},{8,4},{10,6},{12,0},{14,2},{1,13},{3,15... | collective-permute-start | bytes 393224 | tf_op jit(solution)/shard_map/ppermute | solution.py:366
  106.9 13.2 %collective-permute-start.28 = (bf16[64,1024]{1,0:T(8,128)(2,1)S(1)}, bf16[64,1024]{1,0:T(8,128)(2,1)S(1)}, u32[]{:S(2)}, u32[]{:S(2)}) collective-permute-start(bf16[64,1024]{1,0:T(8,128)(2,1)S(1)} %shard_map.106), channel_id=1, source_target_pairs={{0,2},{2,0},{4,6},{6,4},{8,10},{10,8},{12,14},{14,12},{1,3},{3,1},... | collective-permute-start | bytes 393224 | tf_op jit(solution)/shard_map/ppermute | solution.py:366
  111.7 15.8 %collective-permute-start.31 = (bf16[128,1024]{1,0:T(8,128)(2,1)S(1)}, bf16[128,1024]{1,0:T(8,128)(2,1)S(1)}, u32[]{:S(2)}, u32[]{:S(2)}) collective-permute-start(bf16[128,1024]{1,0:T(8,128)(2,1)S(1)} %add_convert_fusion.1), channel_id=1, source_target_pairs={{0,8},{2,10},{4,12},{6,14},{8,0},{10,2},{12,4},{14,6},{1,9},{3,11}... | collective-permute-start | bytes 786440 | tf_op jit(solution)/shard_map/ppermute | solution.py:366
  111.8 15.7 %collective-permute-start.34 = (bf16[128,1024]{1,0:T(8,128)(2,1)S(1)}, bf16[128,1024]{1,0:T(8,128)(2,1)S(1)}, u32[]{:S(2)}, u32[]{:S(2)}) collective-permute-start(bf16[128,1024]{1,0:T(8,128)(2,1)S(1)} %shard_map.107), channel_id=1, source_target_pairs={{0,2},{2,0},{4,6},{6,4},{8,10},{10,8},{12,14},{14,12},{1,3},{3,1},... | collective-permute-start | bytes 786440 | tf_op jit(solution)/shard_map/ppermute | solution.py:366
  117.3 15.2 %collective-permute-start.33 = (bf16[128,1024]{1,0:T(8,128)(2,1)S(1)}, bf16[128,1024]{1,0:T(8,128)(2,1)S(1)}, u32[]{:S(2)}, u32[]{:S(2)}) collective-permute-start(bf16[128,1024]{1,0:T(8,128)(2,1)S(1)} %add_convert_fusion), channel_id=1, source_target_pairs={{0,4},{2,6},{4,0},{6,2},{8,12},{10,14},{12,8},{14,10},{1,5},{3,7},... | collective-permute-start | bytes 786440 | tf_op jit(solution)/shard_map/ppermute | solution.py:366
  120.1 7.4 %collective-permute-start.29 = (bf16[64,1024]{1,0:T(8,128)(2,1)S(1)}, bf16[64,1024]{1,0:T(8,128)(2,1)S(1)}, u32[]{:S(2)}, u32[]{:S(2)}) collective-permute-start(bf16[64,1024]{1,0:T(8,128)(2,1)S(1)} %add_convert_fusion.2), channel_id=1, source_target_pairs={{0,12},{2,14},{4,8},{6,10},{8,4},{10,6},{12,0},{14,2},{1,13},{3,15... | collective-permute-start | bytes 393224 | tf_op jit(solution)/shard_map/ppermute | solution.py:366

commit v12 on v11

--- a/solution.py
+++ b/solution.py
@@ -190,13 +190,14 @@
     )(array, *others)
 
 
-def select_kernel(local, topk, own, *refs):
-    shard_refs, (mod_ref, router_ref) = refs[:4], refs[4:6]
-    rows_ref, back_ref = refs[6:8]
-    state_ref = refs[8] if own else None
+def select_kernel(local, topk, own, cut, *refs):
+    shard_refs, refs = refs[: 4 * cut], refs[4 * cut :]
+    mod_ref, router_ref, rows_ref, back_ref = refs[:4]
+    state_ref = refs[4] if own else None
     full_ref, gate_ref = refs[-2:]
     count, width = full_ref.shape
     lanes = shard_refs[0].shape[1]
+    tail = (3 - cut) * count
     device = lax.axis_index("dev")
     side = device % 2
     part = lax.axis_index("sub")
@@ -212,8 +213,9 @@
     for cross in range(2):
         for far_half in range(2):
             for far_side in range(2):
-                ref = shard_refs[2 * far_half + far_side]
                 top = (cross ^ far_side) * count
+                ref = shard_refs[cut * (2 * far_half + far_side) + (top if cut == 2 else 0) // count]
+                top = 0 if cut == 2 else top
                 half = part if far_half == 0 else 1 - part
                 parity = side if far_side == 0 else 1 - side
                 for i in range(lanes // chunk):
@@ -226,7 +228,7 @@
         scale = lax.rsqrt(jnp.mean(state * state, 1, keepdims=True) + EPS)
         normed = state * scale * (1.0 + mod_ref[2:3, :]) + mod_ref[1:2, :]
         normed = normed.astype(BF16)
-        ids = shard_refs[cross][2 * count : 2 * count + TILE, :]
+        ids = shard_refs[cut * cross + cut - 1][tail : tail + TILE, :]
         ids = ids.astype(F32)[0:1, :].astype(jnp.int32)
         named = [ids[:, k * count : (k + 1) * count] for k in range(topk)]
         hot = sum((mine == n).astype(F32) for n in named)
@@ -474,25 +476,32 @@
         low = flip & -flip
         column[flip] = hop(column[flip - low] if flip > low else shard, 2 * low)
     for flip in range(steps):
+        own = flip == 0
         if flip == steps - 1:
-            column[flip] = tie(column[flip], picked[0])
-        block = column[flip]
-        crossed = crossing[flip] if flip in crossing else hop(block, 1)
-        if flip == steps - 1:
-            crossed = tie(crossed, *picked[1:])
-        own = flip == 0
+            low = flip & -flip
+            before = column[flip - low]
+            cut = [hop(before[:count], 2 * low), hop(before[count:], 2 * low)]
+            cut[0] = tie(cut[0], picked[0])
+            over = [hop(piece, 1) for piece in cut]
+            over[1] = tie(over[1], *picked[1:])
+            blocks = cut + over + [swap(piece) for piece in cut + over]
+        else:
+            block = column[flip]
+            crossed = crossing[flip] if flip in crossing else hop(block, 1)
+            near_half = beside if flip == 1 else swapped if own else swap(block)
+            blocks = [block, crossed, near_half, swap(crossed)]
         results = pl.pallas_call(
-            functools.partial(select_kernel, local, topk, own),
+            functools.partial(select_kernel, local, topk, own, len(blocks) // 4),
             out_shape=[
                 struct((local, 2 * SLOTS, width), BF16),
                 struct((2, count, slots), BF16),
             ]
             + ([struct((count, 2 * lanes), BF16)] if own else []),
-            in_specs=[whole()] * 6,
+            in_specs=[whole()] * (2 + len(blocks)),
             out_specs=[whole()] * (3 if own else 2),
             scratch_shapes=[pltpu.VMEM((count, width), BF16), pltpu.VMEM((experts, count), F32)],
             compiler_params=vmem(6),
-        )(block, crossed, beside if flip == 1 else swapped if own else swap(block), swap(crossed), small, router)
+        )(*blocks, small, router)
         picked.append(results[0])
         backs.append(results[1])
         if own:

time: 134 us -> 135 us (level)
  starting transfers between devices: 26.4 us -> 28.8 us
    ppermute x21 -> x23, starting transfers between devices: 21.1 us -> 22.9 us  [hop(): return lax.ppermute(x, 'dev', [(i, i ^ flip) for i in range(devices)])]
    ppermute x21 -> x23, waiting for transfers between devices: 68.9 us -> 68.3 us  [hop(): return lax.ppermute(x, 'dev', [(i, i ^ flip) for i in range(devices)])]
  transfers between devices with their start and end apart: 35 -> 39, of which waited for: 18 -> 18; matrix products, arithmetic and copies ran while one was open for 0% -> 0% of each run, Pallas kernels for 18% -> 17%
where the time goes in v12:
time: 135 us
  waiting for transfers between devices  70.7 us (52%)
  Pallas kernels  34.8 us (26%)
  starting transfers between devices  28.8 us (21%)
    ppermute x23, waiting for transfers between devices, hop(): return lax.ppermute(x, 'dev', [(i, i ^ flip) for i in range(devices)])  68.3 us
    ppermute x23, starting transfers between devices, hop(): return lax.ppermute(x, 'dev', [(i, i ^ flip) for i in range(devices)])  22.9 us
    pallas_call x1, Pallas kernels, load(): pl.pallas_call(load_kernel, out_shape=[piece] * local + [jax.ShapeDtypeSt...  8.36 us
    pallas_call x2, Pallas kernels, gathered_body(): pl.pallas_call(functools.partial(hidden_kernel, steps, low), out_shape=st...  7.02 us
    pallas_call x4, Pallas kernels, gathered_body(): pl.pallas_call(functools.partial(select_kernel, local, topk, own, len(blo...  5.31 us
    pallas_call x1, Pallas kernels, gathered_body(): pl.pallas_call(attention_kernel, out_shape=struct((count, local_width), B...  3.11 us
    ppermute x2, starting transfers between devices, gathered_body(): theirs = lax.ppermute(mine[flip], 'groups', [(0, 1), (1, 0)])  3.1 us
  transfers between devices with their start and end apart: 39, of which 18 were waited for; matrix products, arithmetic and copies ran while one was open for 0% of the time, Pallas kernels for 17%

profile of v12, /device:TPU:0, one launch (start us, length us, event | category | flops | bytes accessed | tf_op | source)
XLA Modules:
  0.0 135.0 jit_solution(5011006429755259710)
XLA Ops:
  0.0 2.3 %shard_map.82 = (bf16[256,1024]{1,0:T(8,128)(2,1)S(1)}, bf16[320,1024]{1,0:T(8,128)(2,1)}, bf16[128,1024]{1,0:T(8,128)(2,1)S(1)}) custom-call(bf16[128,2048]{1,0:T(8,128)(2,1)} %tokens_ref.3, bf16[3,128,1024]{2,1,0:T(8,128)(2,1)} %bitcast.9, bf16[256,1024]{1,0:T(8,128)(2,1)} %weight_ref.3), custom_call_target="tpu_custom_call" | custom-call | tf_op jit(solution)/shard_map/pallas_call | solution.py:377
  2.3 3.0 %collective-permute-start = (bf16[320,1024]{1,0:T(8,128)(2,1)}, bf16[320,1024]{1,0:T(8,128)(2,1)S(1)}, u32[]{:S(2)}, u32[]{:S(2)}) collective-permute-start(bf16[320,1024]{1,0:T(8,128)(2,1)} %get-tuple-element.47), channel_id=1, source_target_pairs={{0,2},{2,0},{4,6},{6,4},{8,10},{10,8},{12,14},{14,12},{1,3},{3,1},... | collective-permute-start | bytes 1966088 | tf_op jit(solution)/shard_map/ppermute | solution.py:368
  5.3 2.6 %collective-permute-start.3 = (bf16[128,1024]{1,0:T(8,128)(2,1)S(1)}, bf16[128,1024]{1,0:T(8,128)(2,1)S(1)}, u32[]{:S(2)}, u32[]{:S(2)}) collective-permute-start(bf16[128,1024]{1,0:T(8,128)(2,1)S(1)} %get-tuple-element.44._), channel_id=1, source_target_pairs={{0,8},{2,10},{4,12},{6,14},{8,0},{10,2},{12,4},{14,6},{1,9},{3,11}... | collective-permute-start | bytes 786440 | tf_op jit(solution)/shard_map/ppermute | solution.py:368
  7.9 0.7 collective-permute-start.1
  8.6 2.0 %shard_map.83 = (bf16[128,1024]{1,0:T(8,128)(2,1)S(1)}, bf16[128,512]{1,0:T(8,128)(2,1)S(1)}, bf16[256,1024]{1,0:T(8,128)(2,1)}) custom-call(bf16[128,2048]{1,0:T(8,128)(2,1)} %tokens_ref.3, bf16[3,128,1024]{2,1,0:T(8,128)(2,1)} %bitcast.10, bf16[256,1024]{1,0:T(8,128)(2,1)} %weight_ref.3, bf16[128,1024]{1,0:T(8,128)(2,1)S(1)} %get-tuple-element.44._), custom_call_target="tpu_custom_call" | custom-call | tf_op jit(solution)/shard_map/pallas_call | solution.py:389
  10.6 8.4 %shard_map.86 = (bf16[2,2,192,2048]{3,2,1,0:T(8,128)(2,1)S(1)}, bf16[2,2,192,2048]{3,2,1,0:T(8,128)(2,1)S(1)}, bf16[2,2,192,2048]{3,2,1,0:T(8,128)(2,1)S(1)}, bf...) custom-call(bf16[16,2,192,2048]{3,2,1,0:T(8,128)(2,1)} %bitcast.8, ...), custom_call_target="tpu_custom_call" | custom-call | tf_op jit(solution)/shard_map/pallas_call | solution.py:274
  18.9 1.8 %collective-permute-done.3.refs_0_ = bf16[128,1024]{1,0:T(8,128)(2,1)S(1)} collective-permute-done((bf16[128,1024]{1,0:T(8,128)(2,1)S(1)}, bf16[128,1024]{1,0:T(8,128)(2,1)S(1)}, u32[]{:S(2)}, u32[]{:S(2)}) %collective-permute-start.3) | collective-permute-done | bytes 262176 | tf_op jit(solution)/shard_map/ppermute | solution.py:368
  20.8 1.5 %collective-permute-start.6 = (bf16[128,1024]{1,0:T(8,128)(2,1)S(1)}, bf16[128,1024]{1,0:T(8,128)(2,1)S(1)}, u32[]{:S(2)}, u32[]{:S(2)}) collective-permute-start(bf16[128,1024]{1,0:T(8,128)(2,1)S(1)} %shard_map.87.refs_1_.refs_4_), channel_id=1, source_target_pairs={{0,4},{2,6},{4,0},{6,2},{8,12},{10,14},{12,8},{14,10},{1,5},{3,7},... | collective-permute-start | bytes 786440 | tf_op jit(solution)/shard_map/ppermute | solution.py:368
  22.2 0.6 collective-permute-start.4
  22.8 1.6 %collective-permute-start.5 = (bf16[128,1024]{1,0:T(8,128)(2,1)S(1)}, bf16[128,1024]{1,0:T(8,128)(2,1)S(1)}, u32[]{:S(2)}, u32[]{:S(2)}) collective-permute-start(bf16[128,1024]{1,0:T(8,128)(2,1)S(1)} %shard_map.87.refs_1_.refs_4_), channel_id=1, source_target_pairs={{0,16},{16,0},{1,17},{17,1},{2,18},{18,2},{3,19},{19,3},{4,20},{20... | collective-permute-start | bytes 786440 | tf_op jit(solution)/shard_map/ppermute | solution.py:440
  24.4 6.4 %collective-permute-done.cross_ref = bf16[320,1024]{1,0:T(8,128)(2,1)S(1)} collective-permute-done((bf16[320,1024]{1,0:T(8,128)(2,1)}, bf16[320,1024]{1,0:T(8,128)(2,1)S(1)}, u32[]{:S(2)}, u32[]{:S(2)}) %collective-permute-start) | collective-permute-done | bytes 655392 | tf_op jit(solution)/shard_map/ppermute | solution.py:368
  30.8 3.1 %shard_map.85.refs_1_.refs_0_ = bf16[128,1024]{1,0:T(8,128)(2,1)S(1)} custom-call(bf16[128,1024]{1,0:T(8,128)(2,1)S(1)} %get-tuple-element.45._.query_ref, bf16[256,1024]{1,0:T(8,128)(2,1)S(1)} %get-tuple-element.46.own_ref, bf16[320,1024]{1,0:T(8,128)(2,1)S(1)} %collective-permute-done.cross_ref, bf16[256,1024]{1,0:T(8,128)(2,1)S(1)} %collective-permute-done.1.next_ref, ...), custom_call_target="tpu_custom_call" | custom-call | tf_op jit(solution)/shard_map/pallas_call | solution.py:429
  33.9 2.4 %collective-permute-start.2 = (bf16[128,1024]{1,0:T(8,128)(2,1)S(1)}, bf16[128,1024]{1,0:T(8,128)(2,1)S(1)}, u32[]{:S(2)}, u32[]{:S(2)}) collective-permute-start(bf16[128,1024]{1,0:T(8,128)(2,1)S(1)} %shard_map.85.refs_1_.refs_0_), channel_id=1, source_target_pairs={{0,2},{2,0},{4,6},{6,4},{8,10},{10,8},{12,14},{14,12},{1,3},{3,1},... | collective-permute-start | bytes 786440 | tf_op jit(solution)/shard_map/ppermute | solution.py:368
  36.4 1.5 %collective-permute-start.7 = (bf16[128,1024]{1,0:T(8,128)(2,1)S(1)}, bf16[128,1024]{1,0:T(8,128)(2,1)S(1)}, u32[]{:S(2)}, u32[]{:S(2)}) collective-permute-start(bf16[128,1024]{1,0:T(8,128)(2,1)S(1)} %shard_map.89.refs_6_), channel_id=1, source_target_pairs={{0,16},{16,0},{1,17},{17,1},{2,18},{18,2},{3,19},{19,3},{4,20},{20... | collective-permute-start | bytes 786440 | tf_op jit(solution)/shard_map/ppermute | solution.py:440
  37.9 6.4 %collective-permute-done.4.refs_3_ = bf16[256,1024]{1,0:T(8,128)(2,1)S(1)} collective-permute-done((bf16[256,1024]{1,0:T(8,128)(2,1)S(1)}, bf16[256,1024]{1,0:T(8,128)(2,1)S(1)}, u32[]{:S(2)}, u32[]{:S(2)}) %collective-permute-start.4) | collective-permute-done | bytes 524320 | tf_op jit(solution)/shard_map/ppermute | solution.py:368
  44.3 1.2 shard_map.91
  45.5 0.1 collective-permute-start.8
  45.6 1.2 shard_map.90.keep_ref
  46.8 0.7 collective-permute-done.8.got_ref
  47.5 0.1 shard_map.92
  47.6 0.2 collective-permute-start.10
  47.8 0.6 collective-permute-start.12
  48.4 0.5 collective-permute-start.9
  48.9 0.3 collective-permute-done.10.refs_2_.refs_1_
  49.2 2.8 %collective-permute-start.16 = (bf16[272,512]{1,0:T(8,128)(2,1)S(1)}, bf16[272,512]{1,0:T(8,128)(2,1)S(1)}, u32[]{:S(2)}, u32[]{:S(2)}) collective-permute-start(bf16[272,512]{1,0:T(8,128)(2,1)S(1)} %shard_map.96), channel_id=1, source_target_pairs={{0,8},{2,10},{4,12},{6,14},{8,0},{10,2},{12,4},{14,6},{1,9},{3,11}... | collective-permute-start | bytes 835592 | tf_op jit(solution)/shard_map/ppermute | solution.py:368
  52.0 9.5 %collective-permute-done.12.refs_0_ = bf16[272,512]{1,0:T(8,128)(2,1)S(1)} collective-permute-done((bf16[272,512]{1,0:T(8,128)(2,1)S(1)}, bf16[272,512]{1,0:T(8,128)(2,1)S(1)}, u32[]{:S(2)}, u32[]{:S(2)}) %collective-permute-start.12) | collective-permute-done | bytes 278560 | tf_op jit(solution)/shard_map/ppermute | solution.py:368
  61.5 3.3 %collective-permute-done.16.refs_0_ = bf16[272,512]{1,0:T(8,128)(2,1)S(1)} collective-permute-done((bf16[272,512]{1,0:T(8,128)(2,1)S(1)}, bf16[272,512]{1,0:T(8,128)(2,1)S(1)}, u32[]{:S(2)}, u32[]{:S(2)}) %collective-permute-start.16) | collective-permute-done | bytes 278560 | tf_op jit(solution)/shard_map/ppermute | solution.py:368
  64.9 0.8 collective-permute-start.17
  65.7 0.1 collective-permute-start.21
  65.8 5.2 %collective-permute-done.13.refs_1_ = bf16[272,512]{1,0:T(8,128)(2,1)S(1)} collective-permute-done((bf16[272,512]{1,0:T(8,128)(2,1)S(1)}, bf16[272,512]{1,0:T(8,128)(2,1)S(1)}, u32[]{:S(2)}, u32[]{:S(2)}) %collective-permute-start.13) | collective-permute-done | bytes 278560 | tf_op jit(solution)/shard_map/ppermute | solution.py:368
  71.0 0.5 collective-permute-start.18
  71.5 5.0 %collective-permute-done.17.refs_1_ = bf16[272,512]{1,0:T(8,128)(2,1)S(1)} collective-permute-done((bf16[272,512]{1,0:T(8,128)(2,1)S(1)}, bf16[272,512]{1,0:T(8,128)(2,1)S(1)}, u32[]{:S(2)}, u32[]{:S(2)}) %collective-permute-start.17) | collective-permute-done | bytes 278560 | tf_op jit(solution)/shard_map/ppermute | solution.py:368
  76.6 0.3 collective-permute-start.23
  77.0 1.3 shard_map.93
  78.3 4.2 %collective-permute-done.20.refs_0_ = bf16[128,512]{1,0:T(8,128)(2,1)S(1)} collective-permute-done((bf16[128,512]{1,0:T(8,128)(2,1)S(1)}, bf16[128,512]{1,0:T(8,128)(2,1)S(1)}, u32[]{:S(2)}, u32[]{:S(2)}) %collective-permute-start.20) | collective-permute-done | bytes 131104 | tf_op jit(solution)/shard_map/ppermute | solution.py:368
  82.5 0.3 collective-permute-start.22
  82.8 1.3 shard_map.95
  84.1 1.3 shard_map.98
  85.5 0.6 collective-permute-start.27
  86.1 0.1 collective-permute-start.24
  86.1 1.5 %collective-permute-done.22.refs_2_ = bf16[128,512]{1,0:T(8,128)(2,1)S(1)} collective-permute-done((bf16[128,512]{1,0:T(8,128)(2,1)S(1)}, bf16[128,512]{1,0:T(8,128)(2,1)S(1)}, u32[]{:S(2)}, u32[]{:S(2)}) %collective-permute-start.22) | collective-permute-done | bytes 131104 | tf_op jit(solution)/shard_map/ppermute | solution.py:368
  87.6 1.3 collective-permute-done.26.refs_6_
  89.0 1.3 shard_map.101
  90.3 3.5 %shard_map.103.near_ref = bf16[4,128,384]{2,1,0:T(8,128)(2,1)S(1)} custom-call(bf16[8,32,2048]{2,1,0:T(8,128)(2,1)S(1)} %get-tuple-element.56.refs_1_.refs_0_, bf16[8,32,2048]{2,1,0:T(8,128)(2,1)S(1)} %get-tuple-element.57.refs_1_, bf16[8,32,2048]{2,1,0:T(8,128)(2,1)S(1)} %get-tuple-element.59.refs_2_, bf16[8,32,2048]{2,1,0:T(8,128)(2,1)S(1)} %get-tuple-element.60.refs_3_, ...), custom_call_target="tpu_custom_call" | custom-call | tf_op jit(solution)/shard_map/pallas_call | solution.py:516
  93.8 0.2 collective-permute-start.29
  94.0 3.5 %shard_map.102.near_ref = bf16[4,128,384]{2,1,0:T(8,128)(2,1)S(1)} custom-call(bf16[8,32,2048]{2,1,0:T(8,128)(2,1)S(1)} %get-tuple-element.56.refs_1_.refs_0_, bf16[8,32,2048]{2,1,0:T(8,128)(2,1)S(1)} %get-tuple-element.57.refs_1_, bf16[8,32,2048]{2,1,0:T(8,128)(2,1)S(1)} %get-tuple-element.59.refs_2_, bf16[8,32,2048]{2,1,0:T(8,128)(2,1)S(1)} %get-tuple-element.60.refs_3_, ...), custom_call_target="tpu_custom_call" | custom-call | tf_op jit(solution)/shard_map/pallas_call | solution.py:516
  97.6 0.4 collective-permute-start.28
  98.0 1.5 %shard_map.104.refs_0_ = bf16[8,64,1024]{2,1,0:T(8,128)(2,1)S(1)} custom-call(bf16[4,128,384]{2,1,0:T(8,128)(2,1)S(1)} %shard_map.103.near_ref, bf16[4,128,384]{2,1,0:T(8,128)(2,1)S(1)} %collective-permute-done.29.far_ref, bf16[16,384,1024]{2,1,0:T(8,128)(2,1)S(1)} %bitcast.5), custom_call_target="tpu_custom_call" | custom-call | tf_op jit(solution)/shard_map/pallas_call | solution.py:527
  99.5 1.9 %shard_map.105 = (bf16[128,1024]{1,0:T(8,128)(2,1)S(1)}, bf16[128,1024]{1,0:T(8,128)(2,1)S(1)}, bf16[128,1024]{1,0:T(8,128)(2,1)S(1)}, bf16[128,1024]{1,0:T(8,12...) custom-call(bf16[4,128,384]{2,1,0:T(8,128)(2,1)S(1)} %shard_map.102., ...), custom_call_target="tpu_custom_call" | custom-call | tf_op jit(solution)/shard_map/pallas_call | solution.py:536
  101.4 0.5 collective-permute-start.30
  101.9 1.6 %collective-permute-start.34 = (bf16[128,1024]{1,0:T(8,128)(2,1)S(1)}, bf16[128,1024]{1,0:T(8,128)(2,1)S(1)}, u32[]{:S(2)}, u32[]{:S(2)}) collective-permute-start(bf16[128,1024]{1,0:T(8,128)(2,1)S(1)} %get-tuple-element.78), channel_id=1, source_target_pairs={{0,2},{2,0},{4,6},{6,4},{8,10},{10,8},{12,14},{14,12},{1,3},{3,1},... | collective-permute-start | bytes 786440 | tf_op jit(solution)/shard_map/ppermute | solution.py:368
  103.5 0.4 collective-permute-start.36
  103.9 3.9 %collective-permute-done.30.refs_1_ = bf16[64,1024]{1,0:T(8,128)(2,1)S(1)} collective-permute-done((bf16[64,1024]{1,0:T(8,128)(2,1)S(1)}, bf16[64,1024]{1,0:T(8,128)(2,1)S(1)}, u32[]{:S(2)}, u32[]{:S(2)}) %collective-permute-start.30) | collective-permute-done | bytes 131104 | tf_op jit(solution)/shard_map/ppermute | solution.py:368
  107.8 0.8 collective-permute-start.31
  108.6 1.5 %collective-permute-start.32 = (bf16[64,1024]{1,0:T(8,128)(2,1)S(1)}, bf16[64,1024]{1,0:T(8,128)(2,1)S(1)}, u32[]{:S(2)}, u32[]{:S(2)}) collective-permute-start(bf16[64,1024]{1,0:T(8,128)(2,1)S(1)} %shard_map.106), channel_id=1, source_target_pairs={{0,2},{2,0},{4,6},{6,4},{8,10},{10,8},{12,14},{14,12},{1,3},{3,1},... | collective-permute-start | bytes 393224 | tf_op jit(solution)/shard_map/ppermute | solution.py:368
  110.1 3.3 %collective-permute-done.34.refs_1_ = bf16[128,1024]{1,0:T(8,128)(2,1)S(1)} collective-permute-done((bf16[128,1024]{1,0:T(8,128)(2,1)S(1)}, bf16[128,1024]{1,0:T(8,128)(2,1)S(1)}, u32[]{:S(2)}, u32[]{:S(2)}) %collective-permute-start.34) | collective-permute-done | bytes 262176 | tf_op jit(solution)/shard_map/ppermute | solution.py:368
  113.6 1.2 collective-permute-start.38
  114.7 4.3 %collective-permute-done.36 = bf16[128,1024]{1,0:T(8,128)(2,1)S(1)} collective-permute-done((bf16[128,1024]{1,0:T(8,128)(2,1)S(1)}, bf16[128,1024]{1,0:T(8,128)(2,1)S(1)}, u32[]{:S(2)}, u32[]{:S(2)}) %collective-permute-start.36) | collective-permute-done | bytes 262176 | tf_op jit(solution)/shard_map/ppermute | solution.py:368
  119.1 0.6 collective-permute-start.37
  119.7 2.2 %collective-permute-done.32 = bf16[64,1024]{1,0:T(8,128)(2,1)S(1)} collective-permute-done((bf16[64,1024]{1,0:T(8,128)(2,1)S(1)}, bf16[64,1024]{1,0:T(8,128)(2,1)S(1)}, u32[]{:S(2)}, u32[]{:S(2)}) %collective-permute-start.32) | collective-permute-done | bytes 131104 | tf_op jit(solution)/shard_map/ppermute | solution.py:368
  121.9 0.8 collective-permute-start.33
  122.6 7.3 %collective-permute-done.33.bottom_ref = bf16[64,1024]{1,0:T(8,128)(2,1)S(1)} collective-permute-done((bf16[64,1024]{1,0:T(8,128)(2,1)S(1)}, bf16[64,1024]{1,0:T(8,128)(2,1)S(1)}, u32[]{:S(2)}, u32[]{:S(2)}) %collective-permute-start.33) | collective-permute-done | bytes 131104 | tf_op jit(solution)/shard_map/ppermute | solution.py:368
  129.9 4.2 %collective-permute-done.37.refs_1_ = bf16[128,1024]{1,0:T(8,128)(2,1)S(1)} collective-permute-done((bf16[128,1024]{1,0:T(8,128)(2,1)S(1)}, bf16[128,1024]{1,0:T(8,128)(2,1)S(1)}, u32[]{:S(2)}, u32[]{:S(2)}) %collective-permute-start.37) | collective-permute-done | bytes 262176 | tf_op jit(solution)/shard_map/ppermute | solution.py:368
  134.1 0.9 shard_map.108
  (62 shorter events, 0.6 us)
Async XLA Ops:
  2.3 28.5 %collective-permute-start = (bf16[320,1024]{1,0:T(8,128)(2,1)}, bf16[320,1024]{1,0:T(8,128)(2,1)S(1)}, u32[]{:S(2)}, u32[]{:S(2)}) collective-permute-start(bf16[320,1024]{1,0:T(8,128)(2,1)} %get-tuple-element.47), channel_id=1, source_target_pairs={{0,2},{2,0},{4,6},{6,4},{8,10},{10,8},{12,14},{14,12},{1,3},{3,1},... | collective-permute-start | bytes 1966088 | tf_op jit(solution)/shard_map/ppermute | solution.py:368
  5.3 15.5 %collective-permute-start.3 = (bf16[128,1024]{1,0:T(8,128)(2,1)S(1)}, bf16[128,1024]{1,0:T(8,128)(2,1)S(1)}, u32[]{:S(2)}, u32[]{:S(2)}) collective-permute-start(bf16[128,1024]{1,0:T(8,128)(2,1)S(1)} %get-tuple-element.44._), channel_id=1, source_target_pairs={{0,8},{2,10},{4,12},{6,14},{8,0},{10,2},{12,4},{14,6},{1,9},{3,11}... | collective-permute-start | bytes 786440 | tf_op jit(solution)/shard_map/ppermute | solution.py:368
  7.9 16.6 %collective-permute-start.1 = (bf16[256,1024]{1,0:T(8,128)(2,1)S(1)}, bf16[256,1024]{1,0:T(8,128)(2,1)S(1)}, u32[]{:S(2)}, u32[]{:S(2)}) collective-permute-start(bf16[256,1024]{1,0:T(8,128)(2,1)S(1)} %get-tuple-element.46.own_ref), channel_id=1, source_target_pairs={{2,4},{6,8},{10,12},{4,2},{8,6},{12,10},{3,5},{7,9},{11,13},{5,3},... | collective-permute-start | bytes 1572872 | tf_op jit(solution)/shard_map/ppermute | solution.py:413
  10.5 11.7 %copy-start = (bf16[256,1024]{1,0:T(8,128)(2,1)S(1)}, bf16[256,1024]{1,0:T(8,128)(2,1)}, u32[]{:S(2)}) copy-start(bf16[256,1024]{1,0:T(8,128)(2,1)} %get-tuple-element.49.refs_0_) | copy-start | bytes 1572868
  10.5 12.3 %copy-start.1 = (bf16[2048,64]{0,1:T(8,128)(2,1)S(1)}, bf16[2048,64]{0,1:T(8,128)(2,1)}, u32[]{:S(2)}) copy-start(bf16[2048,64]{0,1:T(8,128)(2,1)} %param.12) | copy-start | bytes 786436
  10.5 12.3 %copy-start.2 = (f32[4,2048]{1,0:T(4,128)S(1)}, f32[4,2048]{1,0:T(4,128)}, u32[]{:S(2)}) copy-start(f32[4,2048]{1,0:T(4,128)} %mod_ref.1) | copy-start | bytes 98308
  10.6 12.2 %copy-start.3 = (s32[128,4]{0,1:T(4,128)S(1)}, s32[128,4]{0,1:T(4,128)}, u32[]{:S(2)}) copy-start(s32[128,4]{0,1:T(4,128)} %param.13) | copy-start | bytes 6148
  20.8 15.6 %collective-permute-start.6 = (bf16[128,1024]{1,0:T(8,128)(2,1)S(1)}, bf16[128,1024]{1,0:T(8,128)(2,1)S(1)}, u32[]{:S(2)}, u32[]{:S(2)}) collective-permute-start(bf16[128,1024]{1,0:T(8,128)(2,1)S(1)} %shard_map.87.refs_1_.refs_4_), channel_id=1, source_target_pairs={{0,4},{2,6},{4,0},{6,2},{8,12},{10,14},{12,8},{14,10},{1,5},{3,7},... | collective-permute-start | bytes 786440 | tf_op jit(solution)/shard_map/ppermute | solution.py:368
  22.2 22.0 %collective-permute-start.4 = (bf16[256,1024]{1,0:T(8,128)(2,1)S(1)}, bf16[256,1024]{1,0:T(8,128)(2,1)S(1)}, u32[]{:S(2)}, u32[]{:S(2)}) collective-permute-start(bf16[256,1024]{1,0:T(8,128)(2,1)S(1)} %shard_map.88.refs_2_), channel_id=1, source_target_pairs={{0,4},{2,6},{4,0},{6,2},{8,12},{10,14},{12,8},{14,10},{1,5},{3,7},... | collective-permute-start | bytes 1572872 | tf_op jit(solution)/shard_map/ppermute | solution.py:368
  22.8 15.1 %collective-permute-start.5 = (bf16[128,1024]{1,0:T(8,128)(2,1)S(1)}, bf16[128,1024]{1,0:T(8,128)(2,1)S(1)}, u32[]{:S(2)}, u32[]{:S(2)}) collective-permute-start(bf16[128,1024]{1,0:T(8,128)(2,1)S(1)} %shard_map.87.refs_1_.refs_4_), channel_id=1, source_target_pairs={{0,16},{16,0},{1,17},{17,1},{2,18},{18,2},{3,19},{19,3},{4,20},{20... | collective-permute-start | bytes 786440 | tf_op jit(solution)/shard_map/ppermute | solution.py:440
  33.9 10.3 %collective-permute-start.2 = (bf16[128,1024]{1,0:T(8,128)(2,1)S(1)}, bf16[128,1024]{1,0:T(8,128)(2,1)S(1)}, u32[]{:S(2)}, u32[]{:S(2)}) collective-permute-start(bf16[128,1024]{1,0:T(8,128)(2,1)S(1)} %shard_map.85.refs_1_.refs_0_), channel_id=1, source_target_pairs={{0,2},{2,0},{4,6},{6,4},{8,10},{10,8},{12,14},{14,12},{1,3},{3,1},... | collective-permute-start | bytes 786440 | tf_op jit(solution)/shard_map/ppermute | solution.py:368
  36.4 7.9 %collective-permute-start.7 = (bf16[128,1024]{1,0:T(8,128)(2,1)S(1)}, bf16[128,1024]{1,0:T(8,128)(2,1)S(1)}, u32[]{:S(2)}, u32[]{:S(2)}) collective-permute-start(bf16[128,1024]{1,0:T(8,128)(2,1)S(1)} %shard_map.89.refs_6_), channel_id=1, source_target_pairs={{0,16},{16,0},{1,17},{17,1},{2,18},{18,2},{3,19},{19,3},{4,20},{20... | collective-permute-start | bytes 786440 | tf_op jit(solution)/shard_map/ppermute | solution.py:440
  45.5 2.0 %collective-permute-start.8 = (f32[256,512]{1,0:T(8,128)S(1)}, f32[256,512]{1,0:T(8,128)S(1)}, u32[]{:S(2)}, u32[]{:S(2)}) collective-permute-start(f32[256,512]{1,0:T(8,128)S(1)} %shard_map.91), channel_id=1, source_target_pairs={{0,1},{1,0},{2,3},{3,2},{4,5},{5,4},{6,7},{7,6},{8,9},{9,8},{10,11... | collective-permute-start | bytes 1572872 | tf_op jit(solution)/shard_map/ppermute | solution.py:371
  47.6 1.6 %collective-permute-start.10 = (bf16[272,512]{1,0:T(8,128)(2,1)S(1)}, bf16[272,512]{1,0:T(8,128)(2,1)S(1)}, u32[]{:S(2)}, u32[]{:S(2)}) collective-permute-start(bf16[272,512]{1,0:T(8,128)(2,1)S(1)} %get-tuple-element.53.refs_0_), channel_id=1, source_target_pairs={{0,1},{1,0},{2,3},{3,2},{4,5},{5,4},{6,7},{7,6},{8,9},{9,8},{10,11... | collective-permute-start | bytes 835592 | tf_op jit(solution)/shard_map/ppermute | solution.py:371
  47.8 13.6 %collective-permute-start.12 = (bf16[272,512]{1,0:T(8,128)(2,1)S(1)}, bf16[272,512]{1,0:T(8,128)(2,1)S(1)}, u32[]{:S(2)}, u32[]{:S(2)}) collective-permute-start(bf16[272,512]{1,0:T(8,128)(2,1)S(1)} %get-tuple-element.53.refs_0_), channel_id=1, source_target_pairs={{0,4},{2,6},{4,0},{6,2},{8,12},{10,14},{12,8},{14,10},{1,5},{3,7},... | collective-permute-start | bytes 835592 | tf_op jit(solution)/shard_map/ppermute | solution.py:368
  48.4 13.1 %collective-permute-start.9 = (bf16[272,512]{1,0:T(8,128)(2,1)S(1)}, bf16[272,512]{1,0:T(8,128)(2,1)S(1)}, u32[]{:S(2)}, u32[]{:S(2)}) collective-permute-start(bf16[272,512]{1,0:T(8,128)(2,1)S(1)} %get-tuple-element.53.refs_0_), channel_id=1, source_target_pairs={{0,2},{2,0},{4,6},{6,4},{8,10},{10,8},{12,14},{14,12},{1,3},{3,1},... | collective-permute-start | bytes 835592 | tf_op jit(solution)/shard_map/ppermute | solution.py:368
  49.2 15.6 %collective-permute-start.16 = (bf16[272,512]{1,0:T(8,128)(2,1)S(1)}, bf16[272,512]{1,0:T(8,128)(2,1)S(1)}, u32[]{:S(2)}, u32[]{:S(2)}) collective-permute-start(bf16[272,512]{1,0:T(8,128)(2,1)S(1)} %shard_map.96), channel_id=1, source_target_pairs={{0,8},{2,10},{4,12},{6,14},{8,0},{10,2},{12,4},{14,6},{1,9},{3,11}... | collective-permute-start | bytes 835592 | tf_op jit(solution)/shard_map/ppermute | solution.py:368
  61.4 3.4 %collective-permute-start.14 = (bf16[272,512]{1,0:T(8,128)(2,1)S(1)}, bf16[272,512]{1,0:T(8,128)(2,1)S(1)}, u32[]{:S(2)}, u32[]{:S(2)}) collective-permute-start(bf16[272,512]{1,0:T(8,128)(2,1)S(1)} %shard_map.94.refs_0_), channel_id=1, source_target_pairs={{0,1},{1,0},{2,3},{3,2},{4,5},{5,4},{6,7},{7,6},{8,9},{9,8},{10,11... | collective-permute-start | bytes 835592 | tf_op jit(solution)/shard_map/ppermute | solution.py:371
  61.5 9.5 %collective-permute-start.13 = (bf16[272,512]{1,0:T(8,128)(2,1)S(1)}, bf16[272,512]{1,0:T(8,128)(2,1)S(1)}, u32[]{:S(2)}, u32[]{:S(2)}) collective-permute-start(bf16[272,512]{1,0:T(8,128)(2,1)S(1)} %shard_map.94.refs_0_), channel_id=1, source_target_pairs={{0,2},{2,0},{4,6},{6,4},{8,10},{10,8},{12,14},{14,12},{1,3},{3,1},... | collective-permute-start | bytes 835592 | tf_op jit(solution)/shard_map/ppermute | solution.py:368
  64.9 11.6 %collective-permute-start.17 = (bf16[272,512]{1,0:T(8,128)(2,1)S(1)}, bf16[272,512]{1,0:T(8,128)(2,1)S(1)}, u32[]{:S(2)}, u32[]{:S(2)}) collective-permute-start(bf16[272,512]{1,0:T(8,128)(2,1)S(1)} %shard_map.97.refs_0_), channel_id=1, source_target_pairs={{0,2},{2,0},{4,6},{6,4},{8,10},{10,8},{12,14},{14,12},{1,3},{3,1},... | collective-permute-start | bytes 835592 | tf_op jit(solution)/shard_map/ppermute | solution.py:368
  65.7 10.8 %collective-permute-start.11 = (bf16[272,512]{1,0:T(8,128)(2,1)S(1)}, bf16[272,512]{1,0:T(8,128)(2,1)S(1)}, u32[]{:S(2)}, u32[]{:S(2)}) collective-permute-start(bf16[272,512]{1,0:T(8,128)(2,1)S(1)} %collective-permute-done.9.refs_1_), channel_id=1, source_target_pairs={{0,1},{1,0},{2,3},{3,2},{4,5},{5,4},{6,7},{7,6},{8,9},{9,8},{10,11... | collective-permute-start | bytes 835592 | tf_op jit(solution)/shard_map/ppermute | solution.py:371
  65.7 10.9 %collective-permute-start.21 = (bf16[144,512]{1,0:T(8,128)(2,1)S(1)}, bf16[144,512]{1,0:T(8,128)(2,1)S(1)}, u32[]{:S(2)}, u32[]{:S(2)}) collective-permute-start(bf16[144,512]{1,0:T(8,128)(2,1)S(1)} %slice.9), channel_id=1, source_target_pairs={{0,4},{2,6},{4,0},{6,2},{8,12},{10,14},{12,8},{14,10},{1,5},{3,7},... | collective-permute-start | bytes 442376 | tf_op jit(solution)/shard_map/ppermute | solution.py:368
  71.0 11.8 %collective-permute-start.15 = (bf16[272,512]{1,0:T(8,128)(2,1)S(1)}, bf16[272,512]{1,0:T(8,128)(2,1)S(1)}, u32[]{:S(2)}, u32[]{:S(2)}) collective-permute-start(bf16[272,512]{1,0:T(8,128)(2,1)S(1)} %collective-permute-done.13.refs_1_), channel_id=1, source_target_pairs={{0,1},{1,0},{2,3},{3,2},{4,5},{5,4},{6,7},{7,6},{8,9},{9,8},{10,11... | collective-permute-start | bytes 835592 | tf_op jit(solution)/shard_map/ppermute | solution.py:371
  71.0 13.1 %collective-permute-start.18 = (bf16[272,512]{1,0:T(8,128)(2,1)S(1)}, bf16[272,512]{1,0:T(8,128)(2,1)S(1)}, u32[]{:S(2)}, u32[]{:S(2)}) collective-permute-start(bf16[272,512]{1,0:T(8,128)(2,1)S(1)} %shard_map.97.refs_0_), channel_id=1, source_target_pairs={{0,1},{1,0},{2,3},{3,2},{4,5},{5,4},{6,7},{7,6},{8,9},{9,8},{10,11... | collective-permute-start | bytes 835592 | tf_op jit(solution)/shard_map/ppermute | solution.py:371
  76.5 7.6 %collective-permute-start.19 = (bf16[272,512]{1,0:T(8,128)(2,1)S(1)}, bf16[272,512]{1,0:T(8,128)(2,1)S(1)}, u32[]{:S(2)}, u32[]{:S(2)}) collective-permute-start(bf16[272,512]{1,0:T(8,128)(2,1)S(1)} %collective-permute-done.17.refs_1_), channel_id=1, source_target_pairs={{0,1},{1,0},{2,3},{3,2},{4,5},{5,4},{6,7},{7,6},{8,9},{9,8},{10,11... | collective-permute-start | bytes 835592 | tf_op jit(solution)/shard_map/ppermute | solution.py:371
  76.5 6.0 %collective-permute-start.20 = (bf16[128,512]{1,0:T(8,128)(2,1)S(1)}, bf16[128,512]{1,0:T(8,128)(2,1)S(1)}, u32[]{:S(2)}, u32[]{:S(2)}) collective-permute-start(bf16[128,512]{1,0:T(8,128)(2,1)S(1)} %slice.8), channel_id=1, source_target_pairs={{0,4},{2,6},{4,0},{6,2},{8,12},{10,14},{12,8},{14,10},{1,5},{3,7},... | collective-permute-start | bytes 393224 | tf_op jit(solution)/shard_map/ppermute | solution.py:368
  76.6 8.9 %collective-permute-start.23 = (bf16[144,512]{1,0:T(8,128)(2,1)S(1)}, bf16[144,512]{1,0:T(8,128)(2,1)S(1)}, u32[]{:S(2)}, u32[]{:S(2)}) collective-permute-start(bf16[144,512]{1,0:T(8,128)(2,1)S(1)} %collective-permute-done.21.refs_1_), channel_id=1, source_target_pairs={{0,2},{2,0},{4,6},{6,4},{8,10},{10,8},{12,14},{14,12},{1,3},{3,1},... | collective-permute-start | bytes 442376 | tf_op jit(solution)/shard_map/ppermute | solution.py:368
  82.5 5.1 %collective-permute-start.22 = (bf16[128,512]{1,0:T(8,128)(2,1)S(1)}, bf16[128,512]{1,0:T(8,128)(2,1)S(1)}, u32[]{:S(2)}, u32[]{:S(2)}) collective-permute-start(bf16[128,512]{1,0:T(8,128)(2,1)S(1)} %shard_map.99.refs_0_), channel_id=1, source_target_pairs={{0,2},{2,0},{4,6},{6,4},{8,10},{10,8},{12,14},{14,12},{1,3},{3,1},... | collective-permute-start | bytes 393224 | tf_op jit(solution)/shard_map/ppermute | solution.py:368
  82.8 4.9 %collective-permute-start.25 = (bf16[144,512]{1,0:T(8,128)(2,1)S(1)}, bf16[144,512]{1,0:T(8,128)(2,1)S(1)}, u32[]{:S(2)}, u32[]{:S(2)}) collective-permute-start(bf16[144,512]{1,0:T(8,128)(2,1)S(1)} %collective-permute-done.21.refs_1_), channel_id=1, source_target_pairs={{0,1},{1,0},{2,3},{3,2},{4,5},{5,4},{6,7},{7,6},{8,9},{9,8},{10,11... | collective-permute-start | bytes 442376 | tf_op jit(solution)/shard_map/ppermute | solution.py:371
  85.5 3.5 %collective-permute-start.27 = (bf16[144,512]{1,0:T(8,128)(2,1)S(1)}, bf16[144,512]{1,0:T(8,128)(2,1)S(1)}, u32[]{:S(2)}, u32[]{:S(2)}) collective-permute-start(bf16[144,512]{1,0:T(8,128)(2,1)S(1)} %shard_map.100.refs_3_), channel_id=1, source_target_pairs={{0,1},{1,0},{2,3},{3,2},{4,5},{5,4},{6,7},{7,6},{8,9},{9,8},{10,11... | collective-permute-start | bytes 442376 | tf_op jit(solution)/shard_map/ppermute | solution.py:371
  86.1 1.6 %collective-permute-start.24 = (bf16[128,512]{1,0:T(8,128)(2,1)S(1)}, bf16[128,512]{1,0:T(8,128)(2,1)S(1)}, u32[]{:S(2)}, u32[]{:S(2)}) collective-permute-start(bf16[128,512]{1,0:T(8,128)(2,1)S(1)} %shard_map.99.refs_0_), channel_id=1, source_target_pairs={{0,1},{1,0},{2,3},{3,2},{4,5},{5,4},{6,7},{7,6},{8,9},{9,8},{10,11... | collective-permute-start | bytes 393224 | tf_op jit(solution)/shard_map/ppermute | solution.py:371
  87.6 1.3 collective-permute-start.26
  90.3 7.7 %slice-start = ((s8[12582912]{0:T(1024)(128)(4,1)}), s8[4194304]{0:T(1024)(128)(4,1)S(1)}, s32[]{:S(2)}) async-start(s8[12582912]{0:T(1024)(128)(4,1)} %bitcast.4), calls=%async_computation | async-start | bytes 8388608
  90.3 7.7 %slice-start.1 = ((s8[12582912]{0:T(1024)(128)(4,1)}), s8[4194304]{0:T(1024)(128)(4,1)S(1)}, s32[]{:S(2)}) async-start(s8[12582912]{0:T(1024)(128)(4,1)} %bitcast.4), calls=%async_computation.1 | async-start | bytes 8388608
  93.8 4.2 %collective-permute-start.29 = (bf16[4,128,384]{2,1,0:T(8,128)(2,1)S(1)}, bf16[4,128,384]{2,1,0:T(8,128)(2,1)S(1)}, u32[]{:S(2)}, u32[]{:S(2)}) collective-permute-start(bf16[4,128,384]{2,1,0:T(8,128)(2,1)S(1)} %shard_map.103.near_ref), channel_id=1, source_target_pairs={{0,1},{1,0},{2,3},{3,2},{4,5},{5,4},{6,7},{7,6},{8,9},{9,8},{10,11... | collective-permute-start | bytes 1179656 | tf_op jit(solution)/shard_map/ppermute | solution.py:371
  94.0 4.0 %slice-start.2 = ((s8[12582912]{0:T(1024)(128)(4,1)}), s8[4194304]{0:T(1024)(128)(4,1)S(1)}, s32[]{:S(2)}) async-start(s8[12582912]{0:T(1024)(128)(4,1)} %bitcast.4), calls=%async_computation.2 | async-start | bytes 8388608
  97.6 1.9 %collective-permute-start.28 = (bf16[4,128,384]{2,1,0:T(8,128)(2,1)S(1)}, bf16[4,128,384]{2,1,0:T(8,128)(2,1)S(1)}, u32[]{:S(2)}, u32[]{:S(2)}) collective-permute-start(bf16[4,128,384]{2,1,0:T(8,128)(2,1)S(1)} %shard_map.102.near_ref), channel_id=1, source_target_pairs={{0,1},{1,0},{2,3},{3,2},{4,5},{5,4},{6,7},{7,6},{8,9},{9,8},{10,11... | collective-permute-start | bytes 1179656 | tf_op jit(solution)/shard_map/ppermute | solution.py:371
  101.4 6.4 %collective-permute-start.30 = (bf16[64,1024]{1,0:T(8,128)(2,1)S(1)}, bf16[64,1024]{1,0:T(8,128)(2,1)S(1)}, u32[]{:S(2)}, u32[]{:S(2)}) collective-permute-start(bf16[64,1024]{1,0:T(8,128)(2,1)S(1)} %get-tuple-element.74), channel_id=1, source_target_pairs={{0,2},{2,0},{4,6},{6,4},{8,10},{10,8},{12,14},{14,12},{1,3},{3,1},... | collective-permute-start | bytes 393224 | tf_op jit(solution)/shard_map/ppermute | solution.py:368
  101.9 11.5 %collective-permute-start.34 = (bf16[128,1024]{1,0:T(8,128)(2,1)S(1)}, bf16[128,1024]{1,0:T(8,128)(2,1)S(1)}, u32[]{:S(2)}, u32[]{:S(2)}) collective-permute-start(bf16[128,1024]{1,0:T(8,128)(2,1)S(1)} %get-tuple-element.78), channel_id=1, source_target_pairs={{0,2},{2,0},{4,6},{6,4},{8,10},{10,8},{12,14},{14,12},{1,3},{3,1},... | collective-permute-start | bytes 786440 | tf_op jit(solution)/shard_map/ppermute | solution.py:368
  103.5 15.5 %collective-permute-start.36 = (bf16[128,1024]{1,0:T(8,128)(2,1)S(1)}, bf16[128,1024]{1,0:T(8,128)(2,1)S(1)}, u32[]{:S(2)}, u32[]{:S(2)}) collective-permute-start(bf16[128,1024]{1,0:T(8,128)(2,1)S(1)} %get-tuple-element.80), channel_id=1, source_target_pairs={{0,2},{2,0},{4,6},{6,4},{8,10},{10,8},{12,14},{14,12},{1,3},{3,1},... | collective-permute-start | bytes 786440 | tf_op jit(solution)/shard_map/ppermute | solution.py:368
  107.8 14.8 %collective-permute-start.31 = (bf16[64,1024]{1,0:T(8,128)(2,1)S(1)}, bf16[64,1024]{1,0:T(8,128)(2,1)S(1)}, u32[]{:S(2)}, u32[]{:S(2)}) collective-permute-start(bf16[64,1024]{1,0:T(8,128)(2,1)S(1)} %add_convert_fusion.3), channel_id=1, source_target_pairs={{0,12},{2,14},{4,8},{6,10},{8,4},{10,6},{12,0},{14,2},{1,13},{3,15... | collective-permute-start | bytes 393224 | tf_op jit(solution)/shard_map/ppermute | solution.py:368
  108.6 13.2 %collective-permute-start.32 = (bf16[64,1024]{1,0:T(8,128)(2,1)S(1)}, bf16[64,1024]{1,0:T(8,128)(2,1)S(1)}, u32[]{:S(2)}, u32[]{:S(2)}) collective-permute-start(bf16[64,1024]{1,0:T(8,128)(2,1)S(1)} %shard_map.106), channel_id=1, source_target_pairs={{0,2},{2,0},{4,6},{6,4},{8,10},{10,8},{12,14},{14,12},{1,3},{3,1},... | collective-permute-start | bytes 393224 | tf_op jit(solution)/shard_map/ppermute | solution.py:368
  113.5 16.4 %collective-permute-start.35 = (bf16[128,1024]{1,0:T(8,128)(2,1)S(1)}, bf16[128,1024]{1,0:T(8,128)(2,1)S(1)}, u32[]{:S(2)}, u32[]{:S(2)}) collective-permute-start(bf16[128,1024]{1,0:T(8,128)(2,1)S(1)} %add_convert_fusion.1), channel_id=1, source_target_pairs={{0,8},{2,10},{4,12},{6,14},{8,0},{10,2},{12,4},{14,6},{1,9},{3,11}... | collective-permute-start | bytes 786440 | tf_op jit(solution)/shard_map/ppermute | solution.py:368
  113.6 16.3 %collective-permute-start.38 = (bf16[128,1024]{1,0:T(8,128)(2,1)S(1)}, bf16[128,1024]{1,0:T(8,128)(2,1)S(1)}, u32[]{:S(2)}, u32[]{:S(2)}) collective-permute-start(bf16[128,1024]{1,0:T(8,128)(2,1)S(1)} %shard_map.107), channel_id=1, source_target_pairs={{0,2},{2,0},{4,6},{6,4},{8,10},{10,8},{12,14},{14,12},{1,3},{3,1},... | collective-permute-start | bytes 786440 | tf_op jit(solution)/shard_map/ppermute | solution.py:368
  119.1 15.0 %collective-permute-start.37 = (bf16[128,1024]{1,0:T(8,128)(2,1)S(1)}, bf16[128,1024]{1,0:T(8,128)(2,1)S(1)}, u32[]{:S(2)}, u32[]{:S(2)}) collective-permute-start(bf16[128,1024]{1,0:T(8,128)(2,1)S(1)} %add_convert_fusion), channel_id=1, source_target_pairs={{0,4},{2,6},{4,0},{6,2},{8,12},{10,14},{12,8},{14,10},{1,5},{3,7},... | collective-permute-start | bytes 786440 | tf_op jit(solution)/shard_map/ppermute | solution.py:368
  121.9 8.0 %collective-permute-start.33 = (bf16[64,1024]{1,0:T(8,128)(2,1)S(1)}, bf16[64,1024]{1,0:T(8,128)(2,1)S(1)}, u32[]{:S(2)}, u32[]{:S(2)}) collective-permute-start(bf16[64,1024]{1,0:T(8,128)(2,1)S(1)} %add_convert_fusion.2), channel_id=1, source_target_pairs={{0,12},{2,14},{4,8},{6,10},{8,4},{10,6},{12,0},{14,2},{1,13},{3,15... | collective-permute-start | bytes 393224 | tf_op jit(solution)/shard_map/ppermute | solution.py:368

commit v13 on v11

--- a/solution.py
+++ b/solution.py
@@ -309,21 +309,28 @@
             ]
 
 
-def share_kernel(steps, low, before, near_ref, far_ref, w_ref, *refs):
+def routed_rows(steps, which, back_refs, held_refs, out_refs):
+    for flip in range(steps):
+        source = 2 * flip + which
+        rows = jnp.concatenate([ref[source] for ref in held_refs])
+        routed = jnp.dot(back_refs[flip][which], rows, preferred_element_type=F32).astype(BF16)
+        if flip < steps - 1:
+            out_refs[flip][...] = routed
+        else:
+            half = routed.shape[0] // 2
+            out_refs[flip][...] = routed[:half]
+            out_refs[flip + 1][...] = routed[half:]
+
+
+def crossing_kernel(steps, low, before, near_ref, far_ref, w_ref, *refs):
     held_refs, back_refs = refs[:before], refs[before : before + steps]
     out_refs, held_ref = refs[before + steps : -1], refs[-1]
     output_kernel(low, near_ref, far_ref, w_ref, held_ref)
-    for source in range(2 * steps):
-        back = back_refs[source // 2][source % 2]
-        rows = jnp.concatenate([ref[source] for ref in (*held_refs, held_ref)])
-        routed = jnp.dot(back, rows, preferred_element_type=F32).astype(BF16)
-        if source < 2 * steps - 2:
-            out_refs[source][...] = routed
-        else:
-            half = routed.shape[0] // 2
-            at = 2 * source - (2 * steps - 2)
-            out_refs[at][...] = routed[:half]
-            out_refs[at + 1][...] = routed[half:]
+    routed_rows(steps, 1, back_refs, (*held_refs, held_ref), out_refs)
+
+
+def column_kernel(steps, before, *refs):
+    routed_rows(steps, 0, refs[before : before + steps], refs[:before], refs[before + steps :])
 
 
 def final_kernel(state_ref, mod_ref, top_ref, bottom_ref, *refs):
@@ -524,27 +531,34 @@
             )(own, other, down_weight)
         )
     low, high = groups_of[-1]
-    share = pl.pallas_call(
-        functools.partial(share_kernel, steps, low, len(held)),
-        out_shape=[struct((count, 2 * lanes), BF16)] * (sources - 2)
-        + [struct((count // 2, 2 * lanes), BF16)] * 4,
+    blocks_out = [struct((count, 2 * lanes), BF16)] * (steps - 1)
+    blocks_out += [struct((count // 2, 2 * lanes), BF16)] * 2
+    *crossing_out, last = pl.pallas_call(
+        functools.partial(crossing_kernel, steps, low, len(held)),
+        out_shape=blocks_out + [struct((sources, (high - low) * SLOTS, 2 * lanes), BF16)],
         in_specs=[whole()] * (3 + len(held) + steps),
-        out_specs=[whole()] * (sources + 2),
-        scratch_shapes=[pltpu.VMEM((sources, (high - low) * SLOTS, 2 * lanes), BF16)],
+        out_specs=[whole()] * (steps + 2),
         compiler_params=vmem(8),
     )(*hidden[-1], down_weight, *held, *backs)
+    held.append(last)
+    column_out = pl.pallas_call(
+        functools.partial(column_kernel, steps, len(held)),
+        out_shape=blocks_out,
+        in_specs=[whole()] * (len(held) + steps),
+        out_specs=[whole()] * (steps + 1),
+        compiler_params=vmem(8),
+    )(*held, *backs)
 
     def forwarded(mine, crossed, flip):
         total = mine.astype(F32) + crossed.astype(F32)
         return hop(total.astype(BF16), 2 * flip)
 
-    ends = share[-4:]
-    top = hop(ends[2], 1)
-    crossed = {flip: hop(share[2 * flip + 1], 1) for flip in range(steps - 2, 0, -1)}
-    bottom = hop(tie(ends[3], top), 1)
-    halves = [forwarded(ends[0], top, steps - 1), forwarded(ends[1], bottom, steps - 1)]
-    terms = [forwarded(share[2 * flip], crossed[flip], flip) for flip in crossed]
-    terms += [share[0], hop(tie(share[1], crossed[steps - 2]), 1)]
+    top = hop(crossing_out[-2], 1)
+    crossed = {flip: hop(crossing_out[flip], 1) for flip in range(steps - 2, 0, -1)}
+    bottom = hop(tie(crossing_out[-1], top), 1)
+    halves = [forwarded(column_out[h - 2], (top, bottom)[h], steps - 1) for h in range(2)]
+    terms = [forwarded(column_out[flip], crossed[flip], flip) for flip in crossed]
+    terms += [column_out[0], hop(tie(crossing_out[0], crossed[steps - 2]), 1)]
     return pl.pallas_call(
         final_kernel,
         out_shape=struct((count, 2 * lanes), BF16),

time: 134 us -> 133 us (level)
  no operation moved by 1% of the time
where the time goes in v13:
time: 133 us
  waiting for transfers between devices  71.1 us (53%)
  Pallas kernels  35.1 us (26%)
  starting transfers between devices  26.4 us (20%)
    ppermute x21, waiting for transfers between devices, hop(): return lax.ppermute(x, 'dev', [(i, i ^ flip) for i in range(devices)])  68.5 us
    ppermute x21, starting transfers between devices, hop(): return lax.ppermute(x, 'dev', [(i, i ^ flip) for i in range(devices)])  21.1 us
    pallas_call x1, Pallas kernels, load(): pl.pallas_call(load_kernel, out_shape=[piece] * local + [jax.ShapeDtypeSt...  8.36 us
    pallas_call x2, Pallas kernels, gathered_body(): pl.pallas_call(functools.partial(hidden_kernel, steps, low), out_shape=st...  7.02 us
    pallas_call x4, Pallas kernels, gathered_body(): pl.pallas_call(functools.partial(select_kernel, local, topk, own), out_sh...  5.3 us
    ppermute x2, starting transfers between devices, gathered_body(): theirs = lax.ppermute(mine[flip], 'groups', [(0, 1), (1, 0)])  3.11 us
    pallas_call x1, Pallas kernels, gathered_body(): pl.pallas_call(attention_kernel, out_shape=struct((count, local_width), B...  3.11 us
  transfers between devices with their start and end apart: 35, of which 18 were waited for; matrix products, arithmetic and copies ran while one was open for 0% of the time, Pallas kernels for 18%

profile of v13, /device:TPU:0, one launch (start us, length us, event | category | flops | bytes accessed | tf_op | source)
XLA Modules:
  0.0 133.2 jit_solution(12049285090966425890)
XLA Ops:
  0.0 2.3 %shard_map.82 = (bf16[256,1024]{1,0:T(8,128)(2,1)S(1)}, bf16[320,1024]{1,0:T(8,128)(2,1)}, bf16[128,1024]{1,0:T(8,128)(2,1)S(1)}) custom-call(bf16[128,2048]{1,0:T(8,128)(2,1)} %tokens_ref.3, bf16[3,128,1024]{2,1,0:T(8,128)(2,1)} %bitcast.9, bf16[256,1024]{1,0:T(8,128)(2,1)} %weight_ref.3), custom_call_target="tpu_custom_call" | custom-call | tf_op jit(solution)/shard_map/pallas_call | solution.py:382
  2.3 3.0 %collective-permute-start = (bf16[320,1024]{1,0:T(8,128)(2,1)}, bf16[320,1024]{1,0:T(8,128)(2,1)S(1)}, u32[]{:S(2)}, u32[]{:S(2)}) collective-permute-start(bf16[320,1024]{1,0:T(8,128)(2,1)} %get-tuple-element.48), channel_id=1, source_target_pairs={{0,2},{2,0},{4,6},{6,4},{8,10},{10,8},{12,14},{14,12},{1,3},{3,1},... | collective-permute-start | bytes 1966088 | tf_op jit(solution)/shard_map/ppermute | solution.py:373
  5.3 2.6 %collective-permute-start.3 = (bf16[128,1024]{1,0:T(8,128)(2,1)S(1)}, bf16[128,1024]{1,0:T(8,128)(2,1)S(1)}, u32[]{:S(2)}, u32[]{:S(2)}) collective-permute-start(bf16[128,1024]{1,0:T(8,128)(2,1)S(1)} %get-tuple-element.45._), channel_id=1, source_target_pairs={{0,8},{2,10},{4,12},{6,14},{8,0},{10,2},{12,4},{14,6},{1,9},{3,11}... | collective-permute-start | bytes 786440 | tf_op jit(solution)/shard_map/ppermute | solution.py:373
  7.9 0.7 collective-permute-start.1
  8.6 2.0 %shard_map.83 = (bf16[128,1024]{1,0:T(8,128)(2,1)S(1)}, bf16[128,512]{1,0:T(8,128)(2,1)S(1)}, bf16[256,1024]{1,0:T(8,128)(2,1)}) custom-call(bf16[128,2048]{1,0:T(8,128)(2,1)} %tokens_ref.3, bf16[3,128,1024]{2,1,0:T(8,128)(2,1)} %bitcast.10, bf16[256,1024]{1,0:T(8,128)(2,1)} %weight_ref.3, bf16[128,1024]{1,0:T(8,128)(2,1)S(1)} %get-tuple-element.45._), custom_call_target="tpu_custom_call" | custom-call | tf_op jit(solution)/shard_map/pallas_call | solution.py:394
  10.6 8.4 %shard_map.86 = (bf16[2,2,192,2048]{3,2,1,0:T(8,128)(2,1)S(1)}, bf16[2,2,192,2048]{3,2,1,0:T(8,128)(2,1)S(1)}, bf16[2,2,192,2048]{3,2,1,0:T(8,128)(2,1)S(1)}, bf...) custom-call(bf16[16,2,192,2048]{3,2,1,0:T(8,128)(2,1)} %bitcast.8, ...), custom_call_target="tpu_custom_call" | custom-call | tf_op jit(solution)/shard_map/pallas_call | solution.py:272
  19.0 1.8 %collective-permute-done.3.refs_0_ = bf16[128,1024]{1,0:T(8,128)(2,1)S(1)} collective-permute-done((bf16[128,1024]{1,0:T(8,128)(2,1)S(1)}, bf16[128,1024]{1,0:T(8,128)(2,1)S(1)}, u32[]{:S(2)}, u32[]{:S(2)}) %collective-permute-start.3) | collective-permute-done | bytes 262176 | tf_op jit(solution)/shard_map/ppermute | solution.py:373
  20.8 1.5 %collective-permute-start.6 = (bf16[128,1024]{1,0:T(8,128)(2,1)S(1)}, bf16[128,1024]{1,0:T(8,128)(2,1)S(1)}, u32[]{:S(2)}, u32[]{:S(2)}) collective-permute-start(bf16[128,1024]{1,0:T(8,128)(2,1)S(1)} %shard_map.87.refs_1_.refs_4_), channel_id=1, source_target_pairs={{0,4},{2,6},{4,0},{6,2},{8,12},{10,14},{12,8},{14,10},{1,5},{3,7},... | collective-permute-start | bytes 786440 | tf_op jit(solution)/shard_map/ppermute | solution.py:373
  22.3 0.5 collective-permute-start.4
  22.8 1.6 %collective-permute-start.5 = (bf16[128,1024]{1,0:T(8,128)(2,1)S(1)}, bf16[128,1024]{1,0:T(8,128)(2,1)S(1)}, u32[]{:S(2)}, u32[]{:S(2)}) collective-permute-start(bf16[128,1024]{1,0:T(8,128)(2,1)S(1)} %shard_map.87.refs_1_.refs_4_), channel_id=1, source_target_pairs={{0,16},{16,0},{1,17},{17,1},{2,18},{18,2},{3,19},{19,3},{4,20},{20... | collective-permute-start | bytes 786440 | tf_op jit(solution)/shard_map/ppermute | solution.py:445
  24.4 6.4 %collective-permute-done.cross_ref = bf16[320,1024]{1,0:T(8,128)(2,1)S(1)} collective-permute-done((bf16[320,1024]{1,0:T(8,128)(2,1)}, bf16[320,1024]{1,0:T(8,128)(2,1)S(1)}, u32[]{:S(2)}, u32[]{:S(2)}) %collective-permute-start) | collective-permute-done | bytes 655392 | tf_op jit(solution)/shard_map/ppermute | solution.py:373
  30.8 3.1 %shard_map.85.refs_1_.refs_0_ = bf16[128,1024]{1,0:T(8,128)(2,1)S(1)} custom-call(bf16[128,1024]{1,0:T(8,128)(2,1)S(1)} %get-tuple-element.46._.query_ref, bf16[256,1024]{1,0:T(8,128)(2,1)S(1)} %get-tuple-element.47.own_ref, bf16[320,1024]{1,0:T(8,128)(2,1)S(1)} %collective-permute-done.cross_ref, bf16[256,1024]{1,0:T(8,128)(2,1)S(1)} %collective-permute-done.1.next_ref, ...), custom_call_target="tpu_custom_call" | custom-call | tf_op jit(solution)/shard_map/pallas_call | solution.py:434
  33.9 2.4 %collective-permute-start.2 = (bf16[128,1024]{1,0:T(8,128)(2,1)S(1)}, bf16[128,1024]{1,0:T(8,128)(2,1)S(1)}, u32[]{:S(2)}, u32[]{:S(2)}) collective-permute-start(bf16[128,1024]{1,0:T(8,128)(2,1)S(1)} %shard_map.85.refs_1_.refs_0_), channel_id=1, source_target_pairs={{0,2},{2,0},{4,6},{6,4},{8,10},{10,8},{12,14},{14,12},{1,3},{3,1},... | collective-permute-start | bytes 786440 | tf_op jit(solution)/shard_map/ppermute | solution.py:373
  36.4 1.5 %collective-permute-start.7 = (bf16[128,1024]{1,0:T(8,128)(2,1)S(1)}, bf16[128,1024]{1,0:T(8,128)(2,1)S(1)}, u32[]{:S(2)}, u32[]{:S(2)}) collective-permute-start(bf16[128,1024]{1,0:T(8,128)(2,1)S(1)} %shard_map.89.refs_6_), channel_id=1, source_target_pairs={{0,16},{16,0},{1,17},{17,1},{2,18},{18,2},{3,19},{19,3},{4,20},{20... | collective-permute-start | bytes 786440 | tf_op jit(solution)/shard_map/ppermute | solution.py:445
  37.9 6.4 %collective-permute-done.4.refs_3_ = bf16[256,1024]{1,0:T(8,128)(2,1)S(1)} collective-permute-done((bf16[256,1024]{1,0:T(8,128)(2,1)S(1)}, bf16[256,1024]{1,0:T(8,128)(2,1)S(1)}, u32[]{:S(2)}, u32[]{:S(2)}) %collective-permute-start.4) | collective-permute-done | bytes 524320 | tf_op jit(solution)/shard_map/ppermute | solution.py:373
  44.3 1.2 shard_map.91
  45.5 0.1 collective-permute-start.8
  45.6 1.2 shard_map.90.keep_ref
  46.8 0.7 collective-permute-done.8.got_ref
  47.5 0.1 shard_map.92
  47.6 0.2 collective-permute-start.10
  47.8 0.6 collective-permute-start.12
  48.4 0.5 collective-permute-start.9
  48.9 0.3 collective-permute-done.10.refs_2_.refs_1_
  49.2 2.7 %collective-permute-start.16 = (bf16[272,512]{1,0:T(8,128)(2,1)S(1)}, bf16[272,512]{1,0:T(8,128)(2,1)S(1)}, u32[]{:S(2)}, u32[]{:S(2)}) collective-permute-start(bf16[272,512]{1,0:T(8,128)(2,1)S(1)} %shard_map.96), channel_id=1, source_target_pairs={{0,8},{2,10},{4,12},{6,14},{8,0},{10,2},{12,4},{14,6},{1,9},{3,11}... | collective-permute-start | bytes 835592 | tf_op jit(solution)/shard_map/ppermute | solution.py:373
  52.0 9.4 %collective-permute-done.12.refs_0_ = bf16[272,512]{1,0:T(8,128)(2,1)S(1)} collective-permute-done((bf16[272,512]{1,0:T(8,128)(2,1)S(1)}, bf16[272,512]{1,0:T(8,128)(2,1)S(1)}, u32[]{:S(2)}, u32[]{:S(2)}) %collective-permute-start.12) | collective-permute-done | bytes 278560 | tf_op jit(solution)/shard_map/ppermute | solution.py:373
  61.5 0.1 collective-permute-start.13
  61.5 0.4 collective-permute-start.11
  62.0 2.9 %collective-permute-done.16.refs_0_ = bf16[272,512]{1,0:T(8,128)(2,1)S(1)} collective-permute-done((bf16[272,512]{1,0:T(8,128)(2,1)S(1)}, bf16[272,512]{1,0:T(8,128)(2,1)S(1)}, u32[]{:S(2)}, u32[]{:S(2)}) %collective-permute-start.16) | collective-permute-done | bytes 278560 | tf_op jit(solution)/shard_map/ppermute | solution.py:373
  64.9 0.9 collective-permute-start.17
  65.7 5.2 %collective-permute-done.13.refs_1_ = bf16[272,512]{1,0:T(8,128)(2,1)S(1)} collective-permute-done((bf16[272,512]{1,0:T(8,128)(2,1)S(1)}, bf16[272,512]{1,0:T(8,128)(2,1)S(1)}, u32[]{:S(2)}, u32[]{:S(2)}) %collective-permute-start.13) | collective-permute-done | bytes 278560 | tf_op jit(solution)/shard_map/ppermute | solution.py:373
  71.0 1.3 %shard_map.93 = (bf16[8,32,2048]{2,1,0:T(8,128)(2,1)S(1)}, bf16[2,128,128]{2,1,0:T(8,128)(2,1)S(1)}, bf16[128,1024]{1,0:T(8,128)(2,1)S(1)}) custom-call(bf16[272,512]{1,0:T(8,128)(2,1)S(1)} %get-tuple-element.54.refs_0_, bf16[272,512]{1,0:T(8,128)(2,1)S(1)} %collective-permute-done.9.refs_1_, bf16[272,512]{1,0:T(8,128)(2,1)S(1)} %collective-permute-done.10.refs_2_.refs_1_, ...), custom_call_target="tpu_custom_call" | custom-call | tf_op jit(solution)/shard_map/pallas_call | solution.py:491
  72.3 4.2 %collective-permute-done.17.refs_1_ = bf16[272,512]{1,0:T(8,128)(2,1)S(1)} collective-permute-done((bf16[272,512]{1,0:T(8,128)(2,1)S(1)}, bf16[272,512]{1,0:T(8,128)(2,1)S(1)}, u32[]{:S(2)}, u32[]{:S(2)}) %collective-permute-start.17) | collective-permute-done | bytes 278560 | tf_op jit(solution)/shard_map/ppermute | solution.py:373
  76.5 0.3 collective-permute-start.21
  76.8 0.2 collective-permute-start.22
  77.0 1.3 shard_map.95
  78.4 1.3 shard_map.98
  79.7 5.9 %collective-permute-done.21.refs_0_ = bf16[272,512]{1,0:T(8,128)(2,1)S(1)} collective-permute-done((bf16[272,512]{1,0:T(8,128)(2,1)S(1)}, bf16[272,512]{1,0:T(8,128)(2,1)S(1)}, u32[]{:S(2)}, u32[]{:S(2)}) %collective-permute-start.21) | collective-permute-done | bytes 278560 | tf_op jit(solution)/shard_map/ppermute | solution.py:373
  85.6 1.6 %collective-permute-done.23.refs_3_ = bf16[272,512]{1,0:T(8,128)(2,1)S(1)} collective-permute-done((bf16[272,512]{1,0:T(8,128)(2,1)S(1)}, bf16[272,512]{1,0:T(8,128)(2,1)S(1)}, u32[]{:S(2)}, u32[]{:S(2)}) %collective-permute-start.23) | collective-permute-done | bytes 278560 | tf_op jit(solution)/shard_map/ppermute | solution.py:376
  87.1 1.3 shard_map.101
  88.5 3.5 %shard_map.102.near_ref = bf16[4,128,384]{2,1,0:T(8,128)(2,1)S(1)} custom-call(bf16[8,32,2048]{2,1,0:T(8,128)(2,1)S(1)} %get-tuple-element.57.refs_1_.refs_0_, bf16[8,32,2048]{2,1,0:T(8,128)(2,1)S(1)} %get-tuple-element.58.refs_1_, bf16[8,32,2048]{2,1,0:T(8,128)(2,1)S(1)} %get-tuple-element.60.refs_2_, bf16[8,32,2048]{2,1,0:T(8,128)(2,1)S(1)} %get-tuple-element.61.refs_3_, ...), custom_call_target="tpu_custom_call" | custom-call | tf_op jit(solution)/shard_map/pallas_call | solution.py:514
  92.0 0.2 collective-permute-start.24
  92.2 3.5 %shard_map.104.near_ref = bf16[4,128,384]{2,1,0:T(8,128)(2,1)S(1)} custom-call(bf16[8,32,2048]{2,1,0:T(8,128)(2,1)S(1)} %get-tuple-element.57.refs_1_.refs_0_, bf16[8,32,2048]{2,1,0:T(8,128)(2,1)S(1)} %get-tuple-element.58.refs_1_, bf16[8,32,2048]{2,1,0:T(8,128)(2,1)S(1)} %get-tuple-element.60.refs_2_, bf16[8,32,2048]{2,1,0:T(8,128)(2,1)S(1)} %get-tuple-element.61.refs_3_, ...), custom_call_target="tpu_custom_call" | custom-call | tf_op jit(solution)/shard_map/pallas_call | solution.py:514
  95.7 0.4 collective-permute-start.25
  96.2 1.3 shard_map.103.refs_0_
  97.5 1.9 %shard_map.105 = (bf16[128,1024]{1,0:T(8,128)(2,1)S(1)}, bf16[128,1024]{1,0:T(8,128)(2,1)S(1)}, bf16[128,1024]{1,0:T(8,128)(2,1)S(1)}, bf16[64,1024]{1,0:T(8,128...) custom-call(bf16[4,128,384]{2,1,0:T(8,128)(2,1)S(1)} %shard_map.104.near_ref, ...), custom_call_target="tpu_custom_call" | custom-call | tf_op jit(solution)/shard_map/pallas_call | solution.py:536
  99.4 0.3 collective-permute-start.26
  99.7 1.8 %collective-permute-start.30 = (bf16[128,1024]{1,0:T(8,128)(2,1)S(1)}, bf16[128,1024]{1,0:T(8,128)(2,1)S(1)}, u32[]{:S(2)}, u32[]{:S(2)}) collective-permute-start(bf16[128,1024]{1,0:T(8,128)(2,1)S(1)} %get-tuple-element.80), channel_id=1, source_target_pairs={{0,2},{2,0},{4,6},{6,4},{8,10},{10,8},{12,14},{14,12},{1,3},{3,1},... | collective-permute-start | bytes 786440 | tf_op jit(solution)/shard_map/ppermute | solution.py:373
  101.5 0.4 shard_map.106
  101.9 0.3 collective-permute-start.32
  102.3 3.5 %collective-permute-done.26.refs_1_ = bf16[64,1024]{1,0:T(8,128)(2,1)S(1)} collective-permute-done((bf16[64,1024]{1,0:T(8,128)(2,1)S(1)}, bf16[64,1024]{1,0:T(8,128)(2,1)S(1)}, u32[]{:S(2)}, u32[]{:S(2)}) %collective-permute-start.26) | collective-permute-done | bytes 131104 | tf_op jit(solution)/shard_map/ppermute | solution.py:373
  105.8 0.8 collective-permute-start.27
  106.6 1.4 %collective-permute-start.28 = (bf16[64,1024]{1,0:T(8,128)(2,1)S(1)}, bf16[64,1024]{1,0:T(8,128)(2,1)S(1)}, u32[]{:S(2)}, u32[]{:S(2)}) collective-permute-start(bf16[64,1024]{1,0:T(8,128)(2,1)S(1)} %shard_map.107), channel_id=1, source_target_pairs={{0,2},{2,0},{4,6},{6,4},{8,10},{10,8},{12,14},{14,12},{1,3},{3,1},... | collective-permute-start | bytes 393224 | tf_op jit(solution)/shard_map/ppermute | solution.py:373
  108.0 3.4 %collective-permute-done.30.refs_1_ = bf16[128,1024]{1,0:T(8,128)(2,1)S(1)} collective-permute-done((bf16[128,1024]{1,0:T(8,128)(2,1)S(1)}, bf16[128,1024]{1,0:T(8,128)(2,1)S(1)}, u32[]{:S(2)}, u32[]{:S(2)}) %collective-permute-start.30) | collective-permute-done | bytes 262176 | tf_op jit(solution)/shard_map/ppermute | solution.py:373
  111.4 0.1 add_convert_fusion.1
  111.5 0.1 collective-permute-start.31
  111.6 0.3 collective-permute-start.34
  111.9 5.1 %collective-permute-done.32 = bf16[128,1024]{1,0:T(8,128)(2,1)S(1)} collective-permute-done((bf16[128,1024]{1,0:T(8,128)(2,1)S(1)}, bf16[128,1024]{1,0:T(8,128)(2,1)S(1)}, u32[]{:S(2)}, u32[]{:S(2)}) %collective-permute-start.32) | collective-permute-done | bytes 262176 | tf_op jit(solution)/shard_map/ppermute | solution.py:373
  117.1 0.1 collective-permute-start.33
  117.2 2.7 %collective-permute-done.28 = bf16[64,1024]{1,0:T(8,128)(2,1)S(1)} collective-permute-done((bf16[64,1024]{1,0:T(8,128)(2,1)S(1)}, bf16[64,1024]{1,0:T(8,128)(2,1)S(1)}, u32[]{:S(2)}, u32[]{:S(2)}) %collective-permute-start.28) | collective-permute-done | bytes 131104 | tf_op jit(solution)/shard_map/ppermute | solution.py:373
  119.9 0.8 collective-permute-start.29
  120.7 6.6 %collective-permute-done.29.bottom_ref = bf16[64,1024]{1,0:T(8,128)(2,1)S(1)} collective-permute-done((bf16[64,1024]{1,0:T(8,128)(2,1)S(1)}, bf16[64,1024]{1,0:T(8,128)(2,1)S(1)}, u32[]{:S(2)}, u32[]{:S(2)}) %collective-permute-start.29) | collective-permute-done | bytes 131104 | tf_op jit(solution)/shard_map/ppermute | solution.py:373
  127.2 5.0 %collective-permute-done.33.refs_1_ = bf16[128,1024]{1,0:T(8,128)(2,1)S(1)} collective-permute-done((bf16[128,1024]{1,0:T(8,128)(2,1)S(1)}, bf16[128,1024]{1,0:T(8,128)(2,1)S(1)}, u32[]{:S(2)}, u32[]{:S(2)}) %collective-permute-start.33) | collective-permute-done | bytes 262176 | tf_op jit(solution)/shard_map/ppermute | solution.py:373
  132.3 0.9 shard_map.109
  (53 shorter events, 0.3 us)
Async XLA Ops:
  2.3 28.5 %collective-permute-start = (bf16[320,1024]{1,0:T(8,128)(2,1)}, bf16[320,1024]{1,0:T(8,128)(2,1)S(1)}, u32[]{:S(2)}, u32[]{:S(2)}) collective-permute-start(bf16[320,1024]{1,0:T(8,128)(2,1)} %get-tuple-element.48), channel_id=1, source_target_pairs={{0,2},{2,0},{4,6},{6,4},{8,10},{10,8},{12,14},{14,12},{1,3},{3,1},... | collective-permute-start | bytes 1966088 | tf_op jit(solution)/shard_map/ppermute | solution.py:373
  5.3 15.5 %collective-permute-start.3 = (bf16[128,1024]{1,0:T(8,128)(2,1)S(1)}, bf16[128,1024]{1,0:T(8,128)(2,1)S(1)}, u32[]{:S(2)}, u32[]{:S(2)}) collective-permute-start(bf16[128,1024]{1,0:T(8,128)(2,1)S(1)} %get-tuple-element.45._), channel_id=1, source_target_pairs={{0,8},{2,10},{4,12},{6,14},{8,0},{10,2},{12,4},{14,6},{1,9},{3,11}... | collective-permute-start | bytes 786440 | tf_op jit(solution)/shard_map/ppermute | solution.py:373
  7.9 16.6 %collective-permute-start.1 = (bf16[256,1024]{1,0:T(8,128)(2,1)S(1)}, bf16[256,1024]{1,0:T(8,128)(2,1)S(1)}, u32[]{:S(2)}, u32[]{:S(2)}) collective-permute-start(bf16[256,1024]{1,0:T(8,128)(2,1)S(1)} %get-tuple-element.47.own_ref), channel_id=1, source_target_pairs={{2,4},{6,8},{10,12},{4,2},{8,6},{12,10},{3,5},{7,9},{11,13},{5,3},... | collective-permute-start | bytes 1572872 | tf_op jit(solution)/shard_map/ppermute | solution.py:418
  10.5 11.7 %copy-start = (bf16[256,1024]{1,0:T(8,128)(2,1)S(1)}, bf16[256,1024]{1,0:T(8,128)(2,1)}, u32[]{:S(2)}) copy-start(bf16[256,1024]{1,0:T(8,128)(2,1)} %get-tuple-element.50.refs_0_) | copy-start | bytes 1572868
  10.6 12.3 %copy-start.1 = (bf16[2048,64]{0,1:T(8,128)(2,1)S(1)}, bf16[2048,64]{0,1:T(8,128)(2,1)}, u32[]{:S(2)}) copy-start(bf16[2048,64]{0,1:T(8,128)(2,1)} %param.12) | copy-start | bytes 786436
  10.6 12.2 %copy-start.2 = (f32[4,2048]{1,0:T(4,128)S(1)}, f32[4,2048]{1,0:T(4,128)}, u32[]{:S(2)}) copy-start(f32[4,2048]{1,0:T(4,128)} %mod_ref.1) | copy-start | bytes 98308
  10.6 12.2 %copy-start.3 = (s32[128,4]{0,1:T(4,128)S(1)}, s32[128,4]{0,1:T(4,128)}, u32[]{:S(2)}) copy-start(s32[128,4]{0,1:T(4,128)} %param.13) | copy-start | bytes 6148
  20.8 15.6 %collective-permute-start.6 = (bf16[128,1024]{1,0:T(8,128)(2,1)S(1)}, bf16[128,1024]{1,0:T(8,128)(2,1)S(1)}, u32[]{:S(2)}, u32[]{:S(2)}) collective-permute-start(bf16[128,1024]{1,0:T(8,128)(2,1)S(1)} %shard_map.87.refs_1_.refs_4_), channel_id=1, source_target_pairs={{0,4},{2,6},{4,0},{6,2},{8,12},{10,14},{12,8},{14,10},{1,5},{3,7},... | collective-permute-start | bytes 786440 | tf_op jit(solution)/shard_map/ppermute | solution.py:373
  22.3 22.0 %collective-permute-start.4 = (bf16[256,1024]{1,0:T(8,128)(2,1)S(1)}, bf16[256,1024]{1,0:T(8,128)(2,1)S(1)}, u32[]{:S(2)}, u32[]{:S(2)}) collective-permute-start(bf16[256,1024]{1,0:T(8,128)(2,1)S(1)} %shard_map.88.refs_2_), channel_id=1, source_target_pairs={{0,4},{2,6},{4,0},{6,2},{8,12},{10,14},{12,8},{14,10},{1,5},{3,7},... | collective-permute-start | bytes 1572872 | tf_op jit(solution)/shard_map/ppermute | solution.py:373
  22.8 15.1 %collective-permute-start.5 = (bf16[128,1024]{1,0:T(8,128)(2,1)S(1)}, bf16[128,1024]{1,0:T(8,128)(2,1)S(1)}, u32[]{:S(2)}, u32[]{:S(2)}) collective-permute-start(bf16[128,1024]{1,0:T(8,128)(2,1)S(1)} %shard_map.87.refs_1_.refs_4_), channel_id=1, source_target_pairs={{0,16},{16,0},{1,17},{17,1},{2,18},{18,2},{3,19},{19,3},{4,20},{20... | collective-permute-start | bytes 786440 | tf_op jit(solution)/shard_map/ppermute | solution.py:445
  33.9 10.3 %collective-permute-start.2 = (bf16[128,1024]{1,0:T(8,128)(2,1)S(1)}, bf16[128,1024]{1,0:T(8,128)(2,1)S(1)}, u32[]{:S(2)}, u32[]{:S(2)}) collective-permute-start(bf16[128,1024]{1,0:T(8,128)(2,1)S(1)} %shard_map.85.refs_1_.refs_0_), channel_id=1, source_target_pairs={{0,2},{2,0},{4,6},{6,4},{8,10},{10,8},{12,14},{14,12},{1,3},{3,1},... | collective-permute-start | bytes 786440 | tf_op jit(solution)/shard_map/ppermute | solution.py:373
  36.4 7.9 %collective-permute-start.7 = (bf16[128,1024]{1,0:T(8,128)(2,1)S(1)}, bf16[128,1024]{1,0:T(8,128)(2,1)S(1)}, u32[]{:S(2)}, u32[]{:S(2)}) collective-permute-start(bf16[128,1024]{1,0:T(8,128)(2,1)S(1)} %shard_map.89.refs_6_), channel_id=1, source_target_pairs={{0,16},{16,0},{1,17},{17,1},{2,18},{18,2},{3,19},{19,3},{4,20},{20... | collective-permute-start | bytes 786440 | tf_op jit(solution)/shard_map/ppermute | solution.py:445
  45.5 2.0 %collective-permute-start.8 = (f32[256,512]{1,0:T(8,128)S(1)}, f32[256,512]{1,0:T(8,128)S(1)}, u32[]{:S(2)}, u32[]{:S(2)}) collective-permute-start(f32[256,512]{1,0:T(8,128)S(1)} %shard_map.91), channel_id=1, source_target_pairs={{0,1},{1,0},{2,3},{3,2},{4,5},{5,4},{6,7},{7,6},{8,9},{9,8},{10,11... | collective-permute-start | bytes 1572872 | tf_op jit(solution)/shard_map/ppermute | solution.py:376
  47.6 1.6 %collective-permute-start.10 = (bf16[272,512]{1,0:T(8,128)(2,1)S(1)}, bf16[272,512]{1,0:T(8,128)(2,1)S(1)}, u32[]{:S(2)}, u32[]{:S(2)}) collective-permute-start(bf16[272,512]{1,0:T(8,128)(2,1)S(1)} %get-tuple-element.54.refs_0_), channel_id=1, source_target_pairs={{0,1},{1,0},{2,3},{3,2},{4,5},{5,4},{6,7},{7,6},{8,9},{9,8},{10,11... | collective-permute-start | bytes 835592 | tf_op jit(solution)/shard_map/ppermute | solution.py:376
  47.8 13.6 %collective-permute-start.12 = (bf16[272,512]{1,0:T(8,128)(2,1)S(1)}, bf16[272,512]{1,0:T(8,128)(2,1)S(1)}, u32[]{:S(2)}, u32[]{:S(2)}) collective-permute-start(bf16[272,512]{1,0:T(8,128)(2,1)S(1)} %get-tuple-element.54.refs_0_), channel_id=1, source_target_pairs={{0,4},{2,6},{4,0},{6,2},{8,12},{10,14},{12,8},{14,10},{1,5},{3,7},... | collective-permute-start | bytes 835592 | tf_op jit(solution)/shard_map/ppermute | solution.py:373
  48.4 13.0 %collective-permute-start.9 = (bf16[272,512]{1,0:T(8,128)(2,1)S(1)}, bf16[272,512]{1,0:T(8,128)(2,1)S(1)}, u32[]{:S(2)}, u32[]{:S(2)}) collective-permute-start(bf16[272,512]{1,0:T(8,128)(2,1)S(1)} %get-tuple-element.54.refs_0_), channel_id=1, source_target_pairs={{0,2},{2,0},{4,6},{6,4},{8,10},{10,8},{12,14},{14,12},{1,3},{3,1},... | collective-permute-start | bytes 835592 | tf_op jit(solution)/shard_map/ppermute | solution.py:373
  49.2 15.6 %collective-permute-start.16 = (bf16[272,512]{1,0:T(8,128)(2,1)S(1)}, bf16[272,512]{1,0:T(8,128)(2,1)S(1)}, u32[]{:S(2)}, u32[]{:S(2)}) collective-permute-start(bf16[272,512]{1,0:T(8,128)(2,1)S(1)} %shard_map.96), channel_id=1, source_target_pairs={{0,8},{2,10},{4,12},{6,14},{8,0},{10,2},{12,4},{14,6},{1,9},{3,11}... | collective-permute-start | bytes 835592 | tf_op jit(solution)/shard_map/ppermute | solution.py:373
  61.5 3.4 %collective-permute-start.14 = (bf16[272,512]{1,0:T(8,128)(2,1)S(1)}, bf16[272,512]{1,0:T(8,128)(2,1)S(1)}, u32[]{:S(2)}, u32[]{:S(2)}) collective-permute-start(bf16[272,512]{1,0:T(8,128)(2,1)S(1)} %shard_map.94.refs_0_), channel_id=1, source_target_pairs={{0,1},{1,0},{2,3},{3,2},{4,5},{5,4},{6,7},{7,6},{8,9},{9,8},{10,11... | collective-permute-start | bytes 835592 | tf_op jit(solution)/shard_map/ppermute | solution.py:376
  61.5 9.5 %collective-permute-start.13 = (bf16[272,512]{1,0:T(8,128)(2,1)S(1)}, bf16[272,512]{1,0:T(8,128)(2,1)S(1)}, u32[]{:S(2)}, u32[]{:S(2)}) collective-permute-start(bf16[272,512]{1,0:T(8,128)(2,1)S(1)} %shard_map.94.refs_0_), channel_id=1, source_target_pairs={{0,2},{2,0},{4,6},{6,4},{8,10},{10,8},{12,14},{14,12},{1,3},{3,1},... | collective-permute-start | bytes 835592 | tf_op jit(solution)/shard_map/ppermute | solution.py:373
  61.5 9.5 %collective-permute-start.11 = (bf16[272,512]{1,0:T(8,128)(2,1)S(1)}, bf16[272,512]{1,0:T(8,128)(2,1)S(1)}, u32[]{:S(2)}, u32[]{:S(2)}) collective-permute-start(bf16[272,512]{1,0:T(8,128)(2,1)S(1)} %collective-permute-done.9.refs_1_), channel_id=1, source_target_pairs={{0,1},{1,0},{2,3},{3,2},{4,5},{5,4},{6,7},{7,6},{8,9},{9,8},{10,11... | collective-permute-start | bytes 835592 | tf_op jit(solution)/shard_map/ppermute | solution.py:376
  64.9 11.6 %collective-permute-start.17 = (bf16[272,512]{1,0:T(8,128)(2,1)S(1)}, bf16[272,512]{1,0:T(8,128)(2,1)S(1)}, u32[]{:S(2)}, u32[]{:S(2)}) collective-permute-start(bf16[272,512]{1,0:T(8,128)(2,1)S(1)} %shard_map.97.refs_0_), channel_id=1, source_target_pairs={{0,2},{2,0},{4,6},{6,4},{8,10},{10,8},{12,14},{14,12},{1,3},{3,1},... | collective-permute-start | bytes 835592 | tf_op jit(solution)/shard_map/ppermute | solution.py:373
  65.7 10.8 %collective-permute-start.20 = (bf16[272,512]{1,0:T(8,128)(2,1)S(1)}, bf16[272,512]{1,0:T(8,128)(2,1)S(1)}, u32[]{:S(2)}, u32[]{:S(2)}) collective-permute-start(bf16[272,512]{1,0:T(8,128)(2,1)S(1)} %shard_map.97.refs_0_), channel_id=1, source_target_pairs={{0,4},{2,6},{4,0},{6,2},{8,12},{10,14},{12,8},{14,10},{1,5},{3,7},... | collective-permute-start | bytes 835592 | tf_op jit(solution)/shard_map/ppermute | solution.py:373
  65.7 12.6 %collective-permute-start.18 = (bf16[272,512]{1,0:T(8,128)(2,1)S(1)}, bf16[272,512]{1,0:T(8,128)(2,1)S(1)}, u32[]{:S(2)}, u32[]{:S(2)}) collective-permute-start(bf16[272,512]{1,0:T(8,128)(2,1)S(1)} %shard_map.97.refs_0_), channel_id=1, source_target_pairs={{0,1},{1,0},{2,3},{3,2},{4,5},{5,4},{6,7},{7,6},{8,9},{9,8},{10,11... | collective-permute-start | bytes 835592 | tf_op jit(solution)/shard_map/ppermute | solution.py:376
  71.0 6.0 %collective-permute-start.15 = (bf16[272,512]{1,0:T(8,128)(2,1)S(1)}, bf16[272,512]{1,0:T(8,128)(2,1)S(1)}, u32[]{:S(2)}, u32[]{:S(2)}) collective-permute-start(bf16[272,512]{1,0:T(8,128)(2,1)S(1)} %collective-permute-done.13.refs_1_), channel_id=1, source_target_pairs={{0,1},{1,0},{2,3},{3,2},{4,5},{5,4},{6,7},{7,6},{8,9},{9,8},{10,11... | collective-permute-start | bytes 835592 | tf_op jit(solution)/shard_map/ppermute | solution.py:376
  76.5 1.9 %collective-permute-start.19 = (bf16[272,512]{1,0:T(8,128)(2,1)S(1)}, bf16[272,512]{1,0:T(8,128)(2,1)S(1)}, u32[]{:S(2)}, u32[]{:S(2)}) collective-permute-start(bf16[272,512]{1,0:T(8,128)(2,1)S(1)} %collective-permute-done.17.refs_1_), channel_id=1, source_target_pairs={{0,1},{1,0},{2,3},{3,2},{4,5},{5,4},{6,7},{7,6},{8,9},{9,8},{10,11... | collective-permute-start | bytes 835592 | tf_op jit(solution)/shard_map/ppermute | solution.py:376
  76.5 9.1 %collective-permute-start.21 = (bf16[272,512]{1,0:T(8,128)(2,1)S(1)}, bf16[272,512]{1,0:T(8,128)(2,1)S(1)}, u32[]{:S(2)}, u32[]{:S(2)}) collective-permute-start(bf16[272,512]{1,0:T(8,128)(2,1)S(1)} %shard_map.99.refs_0_), channel_id=1, source_target_pairs={{0,2},{2,0},{4,6},{6,4},{8,10},{10,8},{12,14},{14,12},{1,3},{3,1},... | collective-permute-start | bytes 835592 | tf_op jit(solution)/shard_map/ppermute | solution.py:373
  76.8 8.7 %collective-permute-start.22 = (bf16[272,512]{1,0:T(8,128)(2,1)S(1)}, bf16[272,512]{1,0:T(8,128)(2,1)S(1)}, u32[]{:S(2)}, u32[]{:S(2)}) collective-permute-start(bf16[272,512]{1,0:T(8,128)(2,1)S(1)} %shard_map.99.refs_0_), channel_id=1, source_target_pairs={{0,1},{1,0},{2,3},{3,2},{4,5},{5,4},{6,7},{7,6},{8,9},{9,8},{10,11... | collective-permute-start | bytes 835592 | tf_op jit(solution)/shard_map/ppermute | solution.py:376
  85.6 1.6 %collective-permute-start.23 = (bf16[272,512]{1,0:T(8,128)(2,1)S(1)}, bf16[272,512]{1,0:T(8,128)(2,1)S(1)}, u32[]{:S(2)}, u32[]{:S(2)}) collective-permute-start(bf16[272,512]{1,0:T(8,128)(2,1)S(1)} %shard_map.100.refs_1_), channel_id=1, source_target_pairs={{0,1},{1,0},{2,3},{3,2},{4,5},{5,4},{6,7},{7,6},{8,9},{9,8},{10,11... | collective-permute-start | bytes 835592 | tf_op jit(solution)/shard_map/ppermute | solution.py:376
  88.5 7.7 %slice-start = ((s8[12582912]{0:T(1024)(128)(4,1)}), s8[4194304]{0:T(1024)(128)(4,1)S(1)}, s32[]{:S(2)}) async-start(s8[12582912]{0:T(1024)(128)(4,1)} %bitcast.4), calls=%async_computation | async-start | bytes 8388608
  88.5 7.7 %slice-start.1 = ((s8[12582912]{0:T(1024)(128)(4,1)}), s8[4194304]{0:T(1024)(128)(4,1)S(1)}, s32[]{:S(2)}) async-start(s8[12582912]{0:T(1024)(128)(4,1)} %bitcast.4), calls=%async_computation.1 | async-start | bytes 8388608
  92.0 4.2 %collective-permute-start.24 = (bf16[4,128,384]{2,1,0:T(8,128)(2,1)S(1)}, bf16[4,128,384]{2,1,0:T(8,128)(2,1)S(1)}, u32[]{:S(2)}, u32[]{:S(2)}) collective-permute-start(bf16[4,128,384]{2,1,0:T(8,128)(2,1)S(1)} %shard_map.102.near_ref), channel_id=1, source_target_pairs={{0,1},{1,0},{2,3},{3,2},{4,5},{5,4},{6,7},{7,6},{8,9},{9,8},{10,11... | collective-permute-start | bytes 1179656 | tf_op jit(solution)/shard_map/ppermute | solution.py:376
  92.2 4.0 %slice-start.2 = ((s8[12582912]{0:T(1024)(128)(4,1)}), s8[4194304]{0:T(1024)(128)(4,1)S(1)}, s32[]{:S(2)}) async-start(s8[12582912]{0:T(1024)(128)(4,1)} %bitcast.4), calls=%async_computation.2 | async-start | bytes 8388608
  95.7 1.8 %collective-permute-start.25 = (bf16[4,128,384]{2,1,0:T(8,128)(2,1)S(1)}, bf16[4,128,384]{2,1,0:T(8,128)(2,1)S(1)}, u32[]{:S(2)}, u32[]{:S(2)}) collective-permute-start(bf16[4,128,384]{2,1,0:T(8,128)(2,1)S(1)} %shard_map.104.near_ref), channel_id=1, source_target_pairs={{0,1},{1,0},{2,3},{3,2},{4,5},{5,4},{6,7},{7,6},{8,9},{9,8},{10,11... | collective-permute-start | bytes 1179656 | tf_op jit(solution)/shard_map/ppermute | solution.py:376
  99.4 6.4 %collective-permute-start.26 = (bf16[64,1024]{1,0:T(8,128)(2,1)S(1)}, bf16[64,1024]{1,0:T(8,128)(2,1)S(1)}, u32[]{:S(2)}, u32[]{:S(2)}) collective-permute-start(bf16[64,1024]{1,0:T(8,128)(2,1)S(1)} %get-tuple-element.76), channel_id=1, source_target_pairs={{0,2},{2,0},{4,6},{6,4},{8,10},{10,8},{12,14},{14,12},{1,3},{3,1},... | collective-permute-start | bytes 393224 | tf_op jit(solution)/shard_map/ppermute | solution.py:373
  99.7 11.7 %collective-permute-start.30 = (bf16[128,1024]{1,0:T(8,128)(2,1)S(1)}, bf16[128,1024]{1,0:T(8,128)(2,1)S(1)}, u32[]{:S(2)}, u32[]{:S(2)}) collective-permute-start(bf16[128,1024]{1,0:T(8,128)(2,1)S(1)} %get-tuple-element.80), channel_id=1, source_target_pairs={{0,2},{2,0},{4,6},{6,4},{8,10},{10,8},{12,14},{14,12},{1,3},{3,1},... | collective-permute-start | bytes 786440 | tf_op jit(solution)/shard_map/ppermute | solution.py:373
  101.9 15.1 %collective-permute-start.32 = (bf16[128,1024]{1,0:T(8,128)(2,1)S(1)}, bf16[128,1024]{1,0:T(8,128)(2,1)S(1)}, u32[]{:S(2)}, u32[]{:S(2)}) collective-permute-start(bf16[128,1024]{1,0:T(8,128)(2,1)S(1)} %get-tuple-element.82), channel_id=1, source_target_pairs={{0,2},{2,0},{4,6},{6,4},{8,10},{10,8},{12,14},{14,12},{1,3},{3,1},... | collective-permute-start | bytes 786440 | tf_op jit(solution)/shard_map/ppermute | solution.py:373
  105.8 14.8 %collective-permute-start.27 = (bf16[64,1024]{1,0:T(8,128)(2,1)S(1)}, bf16[64,1024]{1,0:T(8,128)(2,1)S(1)}, u32[]{:S(2)}, u32[]{:S(2)}) collective-permute-start(bf16[64,1024]{1,0:T(8,128)(2,1)S(1)} %add_convert_fusion.3), channel_id=1, source_target_pairs={{0,12},{2,14},{4,8},{6,10},{8,4},{10,6},{12,0},{14,2},{1,13},{3,15... | collective-permute-start | bytes 393224 | tf_op jit(solution)/shard_map/ppermute | solution.py:373
  106.6 13.2 %collective-permute-start.28 = (bf16[64,1024]{1,0:T(8,128)(2,1)S(1)}, bf16[64,1024]{1,0:T(8,128)(2,1)S(1)}, u32[]{:S(2)}, u32[]{:S(2)}) collective-permute-start(bf16[64,1024]{1,0:T(8,128)(2,1)S(1)} %shard_map.107), channel_id=1, source_target_pairs={{0,2},{2,0},{4,6},{6,4},{8,10},{10,8},{12,14},{14,12},{1,3},{3,1},... | collective-permute-start | bytes 393224 | tf_op jit(solution)/shard_map/ppermute | solution.py:373
  111.5 15.8 %collective-permute-start.31 = (bf16[128,1024]{1,0:T(8,128)(2,1)S(1)}, bf16[128,1024]{1,0:T(8,128)(2,1)S(1)}, u32[]{:S(2)}, u32[]{:S(2)}) collective-permute-start(bf16[128,1024]{1,0:T(8,128)(2,1)S(1)} %add_convert_fusion.1), channel_id=1, source_target_pairs={{0,8},{2,10},{4,12},{6,14},{8,0},{10,2},{12,4},{14,6},{1,9},{3,11}... | collective-permute-start | bytes 786440 | tf_op jit(solution)/shard_map/ppermute | solution.py:373
  111.6 15.7 %collective-permute-start.34 = (bf16[128,1024]{1,0:T(8,128)(2,1)S(1)}, bf16[128,1024]{1,0:T(8,128)(2,1)S(1)}, u32[]{:S(2)}, u32[]{:S(2)}) collective-permute-start(bf16[128,1024]{1,0:T(8,128)(2,1)S(1)} %shard_map.108), channel_id=1, source_target_pairs={{0,2},{2,0},{4,6},{6,4},{8,10},{10,8},{12,14},{14,12},{1,3},{3,1},... | collective-permute-start | bytes 786440 | tf_op jit(solution)/shard_map/ppermute | solution.py:373
  117.1 15.2 %collective-permute-start.33 = (bf16[128,1024]{1,0:T(8,128)(2,1)S(1)}, bf16[128,1024]{1,0:T(8,128)(2,1)S(1)}, u32[]{:S(2)}, u32[]{:S(2)}) collective-permute-start(bf16[128,1024]{1,0:T(8,128)(2,1)S(1)} %add_convert_fusion), channel_id=1, source_target_pairs={{0,4},{2,6},{4,0},{6,2},{8,12},{10,14},{12,8},{14,10},{1,5},{3,7},... | collective-permute-start | bytes 786440 | tf_op jit(solution)/shard_map/ppermute | solution.py:373
  119.9 7.4 %collective-permute-start.29 = (bf16[64,1024]{1,0:T(8,128)(2,1)S(1)}, bf16[64,1024]{1,0:T(8,128)(2,1)S(1)}, u32[]{:S(2)}, u32[]{:S(2)}) collective-permute-start(bf16[64,1024]{1,0:T(8,128)(2,1)S(1)} %add_convert_fusion.2), channel_id=1, source_target_pairs={{0,12},{2,14},{4,8},{6,10},{8,4},{10,6},{12,0},{14,2},{1,13},{3,15... | collective-permute-start | bytes 393224 | tf_op jit(solution)/shard_map/ppermute | solution.py:373

commit v14 on v13

--- a/solution.py
+++ b/solution.py
@@ -507,7 +507,7 @@
 
     sources = 2 * steps
     room = sources * SLOTS
-    first = local // 2
+    first = 5 * local // 8
     groups_of = [(0, first), (first, local)] if first else [(0, local)]
     hidden = []
     for low, high in groups_of:

time: 133 us -> 134 us (level)
  waiting for transfers between devices: 71.1 us -> 67.9 us
  starting transfers between devices: 26.4 us -> 29.1 us
    ppermute x21, waiting for transfers between devices: 68.5 us -> 65.6 us  [hop(): return lax.ppermute(x, 'dev', [(i, i ^ flip) for i in range(devices)])]
    ppermute x21, starting transfers between devices: 21.1 us -> 23 us  [hop(): return lax.ppermute(x, 'dev', [(i, i ^ flip) for i in range(devices)])]
  transfers between devices with their start and end apart: 35 -> 35, of which waited for: 18 -> 16; matrix products, arithmetic and copies ran while one was open for 0% -> 0% of each run, Pallas kernels for 18% -> 18%
where the time goes in v14:
time: 134 us
  waiting for transfers between devices  67.9 us (51%)
  Pallas kernels  36.4 us (27%)
  starting transfers between devices  29.1 us (22%)
    ppermute x21, waiting for transfers between devices, hop(): return lax.ppermute(x, 'dev', [(i, i ^ flip) for i in range(devices)])  65.6 us
    ppermute x21, starting transfers between devices, hop(): return lax.ppermute(x, 'dev', [(i, i ^ flip) for i in range(devices)])  23 us
    pallas_call x1, Pallas kernels, load(): pl.pallas_call(load_kernel, out_shape=[piece] * local + [jax.ShapeDtypeSt...  8.36 us
    pallas_call x2, Pallas kernels, gathered_body(): pl.pallas_call(functools.partial(hidden_kernel, steps, low), out_shape=st...  7.01 us
    pallas_call x4, Pallas kernels, gathered_body(): pl.pallas_call(functools.partial(select_kernel, local, topk, own), out_sh...  5.3 us
    pallas_call x1, Pallas kernels, gathered_body(): pl.pallas_call(attention_kernel, out_shape=struct((count, local_width), B...  4.3 us
    ppermute x2, starting transfers between devices, gathered_body(): theirs = lax.ppermute(mine[flip], 'groups', [(0, 1), (1, 0)])  3.1 us
  transfers between devices with their start and end apart: 35, of which 16 were waited for; matrix products, arithmetic and copies ran while one was open for 0% of the time, Pallas kernels for 18%

profile of v14, /device:TPU:0, one launch (start us, length us, event | category | flops | bytes accessed | tf_op | source)
XLA Modules:
  0.0 134.0 jit_solution(7267489277398363961)
XLA Ops:
  0.0 2.5 %shard_map.82 = (bf16[256,1024]{1,0:T(8,128)(2,1)}, bf16[320,1024]{1,0:T(8,128)(2,1)}, bf16[128,1024]{1,0:T(8,128)(2,1)S(1)}) custom-call(bf16[128,2048]{1,0:T(8,128)(2,1)} %tokens_ref.3, bf16[3,128,1024]{2,1,0:T(8,128)(2,1)} %bitcast.9, bf16[256,1024]{1,0:T(8,128)(2,1)} %weight_ref.3), custom_call_target="tpu_custom_call" | custom-call | tf_op jit(solution)/shard_map/pallas_call | solution.py:382
  2.5 3.0 %collective-permute-start = (bf16[320,1024]{1,0:T(8,128)(2,1)}, bf16[320,1024]{1,0:T(8,128)(2,1)S(1)}, u32[]{:S(2)}, u32[]{:S(2)}) collective-permute-start(bf16[320,1024]{1,0:T(8,128)(2,1)} %get-tuple-element.48), channel_id=1, source_target_pairs={{0,2},{2,0},{4,6},{6,4},{8,10},{10,8},{12,14},{14,12},{1,3},{3,1},... | collective-permute-start | bytes 1966088 | tf_op jit(solution)/shard_map/ppermute | solution.py:373
  5.5 2.6 %collective-permute-start.3 = (bf16[128,1024]{1,0:T(8,128)(2,1)S(1)}, bf16[128,1024]{1,0:T(8,128)(2,1)S(1)}, u32[]{:S(2)}, u32[]{:S(2)}) collective-permute-start(bf16[128,1024]{1,0:T(8,128)(2,1)S(1)} %get-tuple-element.45._), channel_id=1, source_target_pairs={{0,8},{2,10},{4,12},{6,14},{8,0},{10,2},{12,4},{14,6},{1,9},{3,11}... | collective-permute-start | bytes 786440 | tf_op jit(solution)/shard_map/ppermute | solution.py:373
  8.1 1.5 %collective-permute-start.1 = (bf16[256,1024]{1,0:T(8,128)(2,1)}, bf16[256,1024]{1,0:T(8,128)(2,1)}, u32[]{:S(2)}, u32[]{:S(2)}) collective-permute-start(bf16[256,1024]{1,0:T(8,128)(2,1)} %get-tuple-element.47.own_ref), channel_id=1, source_target_pairs={{2,4},{6,8},{10,12},{4,2},{8,6},{12,10},{3,5},{7,9},{11,13},{5,3},... | collective-permute-start | bytes 1572872 | tf_op jit(solution)/shard_map/ppermute | solution.py:418
  9.5 2.0 %shard_map.83 = (bf16[128,1024]{1,0:T(8,128)(2,1)S(1)}, bf16[128,512]{1,0:T(8,128)(2,1)S(1)}, bf16[256,1024]{1,0:T(8,128)(2,1)}) custom-call(bf16[128,2048]{1,0:T(8,128)(2,1)} %tokens_ref.3, bf16[3,128,1024]{2,1,0:T(8,128)(2,1)} %bitcast.10, bf16[256,1024]{1,0:T(8,128)(2,1)} %weight_ref.3, bf16[128,1024]{1,0:T(8,128)(2,1)S(1)} %get-tuple-element.45._), custom_call_target="tpu_custom_call" | custom-call | tf_op jit(solution)/shard_map/pallas_call | solution.py:394
  11.6 8.4 %shard_map.86 = (bf16[2,2,192,2048]{3,2,1,0:T(8,128)(2,1)S(1)}, bf16[2,2,192,2048]{3,2,1,0:T(8,128)(2,1)S(1)}, bf16[2,2,192,2048]{3,2,1,0:T(8,128)(2,1)S(1)}, bf...) custom-call(bf16[16,2,192,2048]{3,2,1,0:T(8,128)(2,1)} %bitcast.8, ...), custom_call_target="tpu_custom_call" | custom-call | tf_op jit(solution)/shard_map/pallas_call | solution.py:272
  19.9 1.1 collective-permute-done.3.refs_0_
  21.0 1.5 %collective-permute-start.6 = (bf16[128,1024]{1,0:T(8,128)(2,1)S(1)}, bf16[128,1024]{1,0:T(8,128)(2,1)S(1)}, u32[]{:S(2)}, u32[]{:S(2)}) collective-permute-start(bf16[128,1024]{1,0:T(8,128)(2,1)S(1)} %shard_map.87.refs_1_.refs_4_), channel_id=1, source_target_pairs={{0,4},{2,6},{4,0},{6,2},{8,12},{10,14},{12,8},{14,10},{1,5},{3,7},... | collective-permute-start | bytes 786440 | tf_op jit(solution)/shard_map/ppermute | solution.py:373
  22.5 0.5 collective-permute-start.4
  23.1 1.6 %collective-permute-start.5 = (bf16[128,1024]{1,0:T(8,128)(2,1)S(1)}, bf16[128,1024]{1,0:T(8,128)(2,1)S(1)}, u32[]{:S(2)}, u32[]{:S(2)}) collective-permute-start(bf16[128,1024]{1,0:T(8,128)(2,1)S(1)} %shard_map.87.refs_1_.refs_4_), channel_id=1, source_target_pairs={{0,16},{16,0},{1,17},{17,1},{2,18},{18,2},{3,19},{19,3},{4,20},{20... | collective-permute-start | bytes 786440 | tf_op jit(solution)/shard_map/ppermute | solution.py:445
  24.6 6.4 %collective-permute-done.cross_ref = bf16[320,1024]{1,0:T(8,128)(2,1)S(1)} collective-permute-done((bf16[320,1024]{1,0:T(8,128)(2,1)}, bf16[320,1024]{1,0:T(8,128)(2,1)S(1)}, u32[]{:S(2)}, u32[]{:S(2)}) %collective-permute-start) | collective-permute-done | bytes 655392 | tf_op jit(solution)/shard_map/ppermute | solution.py:373
  31.0 4.3 %shard_map.85.refs_1_.refs_0_ = bf16[128,1024]{1,0:T(8,128)(2,1)S(1)} custom-call(bf16[128,1024]{1,0:T(8,128)(2,1)S(1)} %get-tuple-element.46._.query_ref, bf16[256,1024]{1,0:T(8,128)(2,1)} %get-tuple-element.47.own_ref, bf16[320,1024]{1,0:T(8,128)(2,1)S(1)} %collective-permute-done.cross_ref, bf16[256,1024]{1,0:T(8,128)(2,1)} %collective-permute-done.1.next_ref, ...), custom_call_target="tpu_custom_call" | custom-call | tf_op jit(solution)/shard_map/pallas_call | solution.py:434
  35.3 2.4 %collective-permute-start.2 = (bf16[128,1024]{1,0:T(8,128)(2,1)S(1)}, bf16[128,1024]{1,0:T(8,128)(2,1)S(1)}, u32[]{:S(2)}, u32[]{:S(2)}) collective-permute-start(bf16[128,1024]{1,0:T(8,128)(2,1)S(1)} %shard_map.85.refs_1_.refs_0_), channel_id=1, source_target_pairs={{0,2},{2,0},{4,6},{6,4},{8,10},{10,8},{12,14},{14,12},{1,3},{3,1},... | collective-permute-start | bytes 786440 | tf_op jit(solution)/shard_map/ppermute | solution.py:373
  37.8 1.5 %collective-permute-start.7 = (bf16[128,1024]{1,0:T(8,128)(2,1)S(1)}, bf16[128,1024]{1,0:T(8,128)(2,1)S(1)}, u32[]{:S(2)}, u32[]{:S(2)}) collective-permute-start(bf16[128,1024]{1,0:T(8,128)(2,1)S(1)} %shard_map.89.refs_6_), channel_id=1, source_target_pairs={{0,16},{16,0},{1,17},{17,1},{2,18},{18,2},{3,19},{19,3},{4,20},{20... | collective-permute-start | bytes 786440 | tf_op jit(solution)/shard_map/ppermute | solution.py:445
  39.3 5.4 %collective-permute-done.4.refs_3_ = bf16[256,1024]{1,0:T(8,128)(2,1)S(1)} collective-permute-done((bf16[256,1024]{1,0:T(8,128)(2,1)S(1)}, bf16[256,1024]{1,0:T(8,128)(2,1)S(1)}, u32[]{:S(2)}, u32[]{:S(2)}) %collective-permute-start.4) | collective-permute-done | bytes 524320 | tf_op jit(solution)/shard_map/ppermute | solution.py:373
  44.7 1.2 shard_map.91
  45.9 0.1 collective-permute-start.8
  46.0 1.2 shard_map.90.keep_ref
  47.2 0.7 collective-permute-done.8.got_ref
  47.9 0.1 shard_map.92
  48.0 0.2 collective-permute-start.10
  48.2 1.6 %collective-permute-start.12 = (bf16[272,512]{1,0:T(8,128)(2,1)S(1)}, bf16[272,512]{1,0:T(8,128)(2,1)S(1)}, u32[]{:S(2)}, u32[]{:S(2)}) collective-permute-start(bf16[272,512]{1,0:T(8,128)(2,1)S(1)} %get-tuple-element.54.refs_0_), channel_id=1, source_target_pairs={{0,4},{2,6},{4,0},{6,2},{8,12},{10,14},{12,8},{14,10},{1,5},{3,7},... | collective-permute-start | bytes 835592 | tf_op jit(solution)/shard_map/ppermute | solution.py:373
  49.8 0.5 collective-permute-start.9
  50.4 2.3 %collective-permute-start.16 = (bf16[272,512]{1,0:T(8,128)(2,1)S(1)}, bf16[272,512]{1,0:T(8,128)(2,1)S(1)}, u32[]{:S(2)}, u32[]{:S(2)}) collective-permute-start(bf16[272,512]{1,0:T(8,128)(2,1)S(1)} %shard_map.96), channel_id=1, source_target_pairs={{0,8},{2,10},{4,12},{6,14},{8,0},{10,2},{12,4},{14,6},{1,9},{3,11}... | collective-permute-start | bytes 835592 | tf_op jit(solution)/shard_map/ppermute | solution.py:373
  52.7 9.8 %collective-permute-done.12.refs_0_ = bf16[272,512]{1,0:T(8,128)(2,1)S(1)} collective-permute-done((bf16[272,512]{1,0:T(8,128)(2,1)S(1)}, bf16[272,512]{1,0:T(8,128)(2,1)S(1)}, u32[]{:S(2)}, u32[]{:S(2)}) %collective-permute-start.12) | collective-permute-done | bytes 278560 | tf_op jit(solution)/shard_map/ppermute | solution.py:373
  62.5 0.1 collective-permute-start.13
  62.6 0.4 collective-permute-start.11
  63.0 2.6 %collective-permute-done.16.refs_0_ = bf16[272,512]{1,0:T(8,128)(2,1)S(1)} collective-permute-done((bf16[272,512]{1,0:T(8,128)(2,1)S(1)}, bf16[272,512]{1,0:T(8,128)(2,1)S(1)}, u32[]{:S(2)}, u32[]{:S(2)}) %collective-permute-start.16) | collective-permute-done | bytes 278560 | tf_op jit(solution)/shard_map/ppermute | solution.py:373
  65.6 1.5 %collective-permute-start.17 = (bf16[272,512]{1,0:T(8,128)(2,1)S(1)}, bf16[272,512]{1,0:T(8,128)(2,1)S(1)}, u32[]{:S(2)}, u32[]{:S(2)}) collective-permute-start(bf16[272,512]{1,0:T(8,128)(2,1)S(1)} %shard_map.97.refs_0_), channel_id=1, source_target_pairs={{0,2},{2,0},{4,6},{6,4},{8,10},{10,8},{12,14},{14,12},{1,3},{3,1},... | collective-permute-start | bytes 835592 | tf_op jit(solution)/shard_map/ppermute | solution.py:373
  67.1 4.9 %collective-permute-done.13.refs_1_ = bf16[272,512]{1,0:T(8,128)(2,1)S(1)} collective-permute-done((bf16[272,512]{1,0:T(8,128)(2,1)S(1)}, bf16[272,512]{1,0:T(8,128)(2,1)S(1)}, u32[]{:S(2)}, u32[]{:S(2)}) %collective-permute-start.13) | collective-permute-done | bytes 278560 | tf_op jit(solution)/shard_map/ppermute | solution.py:373
  72.0 1.3 shard_map.93
  73.4 4.2 %collective-permute-done.17.refs_1_ = bf16[272,512]{1,0:T(8,128)(2,1)S(1)} collective-permute-done((bf16[272,512]{1,0:T(8,128)(2,1)S(1)}, bf16[272,512]{1,0:T(8,128)(2,1)S(1)}, u32[]{:S(2)}, u32[]{:S(2)}) %collective-permute-start.17) | collective-permute-done | bytes 278560 | tf_op jit(solution)/shard_map/ppermute | solution.py:373
  77.6 0.3 collective-permute-start.21
  77.9 0.2 collective-permute-start.22
  78.1 1.3 shard_map.95
  79.4 1.3 shard_map.98
  80.8 5.9 %collective-permute-done.21.refs_0_ = bf16[272,512]{1,0:T(8,128)(2,1)S(1)} collective-permute-done((bf16[272,512]{1,0:T(8,128)(2,1)S(1)}, bf16[272,512]{1,0:T(8,128)(2,1)S(1)}, u32[]{:S(2)}, u32[]{:S(2)}) %collective-permute-start.21) | collective-permute-done | bytes 278560 | tf_op jit(solution)/shard_map/ppermute | solution.py:373
  86.6 1.6 %collective-permute-done.23.refs_3_ = bf16[272,512]{1,0:T(8,128)(2,1)S(1)} collective-permute-done((bf16[272,512]{1,0:T(8,128)(2,1)S(1)}, bf16[272,512]{1,0:T(8,128)(2,1)S(1)}, u32[]{:S(2)}, u32[]{:S(2)}) %collective-permute-start.23) | collective-permute-done | bytes 278560 | tf_op jit(solution)/shard_map/ppermute | solution.py:376
  88.2 1.3 shard_map.101
  89.5 4.3 %shard_map.102.near_ref = bf16[5,128,384]{2,1,0:T(8,128)(2,1)S(1)} custom-call(bf16[8,32,2048]{2,1,0:T(8,128)(2,1)S(1)} %get-tuple-element.57.refs_1_.refs_0_, bf16[8,32,2048]{2,1,0:T(8,128)(2,1)S(1)} %get-tuple-element.58.refs_1_, bf16[8,32,2048]{2,1,0:T(8,128)(2,1)S(1)} %get-tuple-element.60.refs_2_, bf16[8,32,2048]{2,1,0:T(8,128)(2,1)S(1)} %get-tuple-element.61.refs_3_, ...), custom_call_target="tpu_custom_call" | custom-call | tf_op jit(solution)/shard_map/pallas_call | solution.py:514
  93.9 0.2 collective-permute-start.24
  94.1 2.7 %shard_map.104.near_ref = bf16[3,128,384]{2,1,0:T(8,128)(2,1)S(1)} custom-call(bf16[8,32,2048]{2,1,0:T(8,128)(2,1)S(1)} %get-tuple-element.57.refs_1_.refs_0_, bf16[8,32,2048]{2,1,0:T(8,128)(2,1)S(1)} %get-tuple-element.58.refs_1_, bf16[8,32,2048]{2,1,0:T(8,128)(2,1)S(1)} %get-tuple-element.60.refs_2_, bf16[8,32,2048]{2,1,0:T(8,128)(2,1)S(1)} %get-tuple-element.61.refs_3_, ...), custom_call_target="tpu_custom_call" | custom-call | tf_op jit(solution)/shard_map/pallas_call | solution.py:514
  96.8 0.4 collective-permute-start.25
  97.2 1.5 %shard_map.103.refs_0_ = bf16[8,80,1024]{2,1,0:T(8,128)(2,1)S(1)} custom-call(bf16[5,128,384]{2,1,0:T(8,128)(2,1)S(1)} %shard_map.102.near_ref, bf16[5,128,384]{2,1,0:T(8,128)(2,1)S(1)} %collective-permute-done.24.far_ref, bf16[16,384,1024]{2,1,0:T(8,128)(2,1)S(1)} %bitcast.5), custom_call_target="tpu_custom_call" | custom-call | tf_op jit(solution)/shard_map/pallas_call | solution.py:525
  98.8 1.6 %shard_map.105 = (bf16[128,1024]{1,0:T(8,128)(2,1)S(1)}, bf16[128,1024]{1,0:T(8,128)(2,1)S(1)}, bf16[128,1024]{1,0:T(8,128)(2,1)S(1)}, bf16[64,1024]{1,0:T(8,128...) custom-call(bf16[3,128,384]{2,1,0:T(8,128)(2,1)S(1)} %shard_map.104.near_ref, ...), custom_call_target="tpu_custom_call" | custom-call | tf_op jit(solution)/shard_map/pallas_call | solution.py:536
  100.4 0.4 collective-permute-start.26
  100.7 1.7 %collective-permute-start.30 = (bf16[128,1024]{1,0:T(8,128)(2,1)S(1)}, bf16[128,1024]{1,0:T(8,128)(2,1)S(1)}, u32[]{:S(2)}, u32[]{:S(2)}) collective-permute-start(bf16[128,1024]{1,0:T(8,128)(2,1)S(1)} %get-tuple-element.80), channel_id=1, source_target_pairs={{0,2},{2,0},{4,6},{6,4},{8,10},{10,8},{12,14},{14,12},{1,3},{3,1},... | collective-permute-start | bytes 786440 | tf_op jit(solution)/shard_map/ppermute | solution.py:373
  102.5 0.4 shard_map.106
  102.9 0.4 collective-permute-start.32
  103.3 3.5 %collective-permute-done.26.refs_1_ = bf16[64,1024]{1,0:T(8,128)(2,1)S(1)} collective-permute-done((bf16[64,1024]{1,0:T(8,128)(2,1)S(1)}, bf16[64,1024]{1,0:T(8,128)(2,1)S(1)}, u32[]{:S(2)}, u32[]{:S(2)}) %collective-permute-start.26) | collective-permute-done | bytes 131104 | tf_op jit(solution)/shard_map/ppermute | solution.py:373
  106.8 1.3 collective-permute-start.27
  108.2 1.0 collective-permute-start.28
  109.2 3.2 %collective-permute-done.30.refs_1_ = bf16[128,1024]{1,0:T(8,128)(2,1)S(1)} collective-permute-done((bf16[128,1024]{1,0:T(8,128)(2,1)S(1)}, bf16[128,1024]{1,0:T(8,128)(2,1)S(1)}, u32[]{:S(2)}, u32[]{:S(2)}) %collective-permute-start.30) | collective-permute-done | bytes 262176 | tf_op jit(solution)/shard_map/ppermute | solution.py:373
  112.4 0.1 add_convert_fusion.1
  112.5 0.1 collective-permute-start.31
  112.6 0.4 collective-permute-start.34
  112.9 5.1 %collective-permute-done.32 = bf16[128,1024]{1,0:T(8,128)(2,1)S(1)} collective-permute-done((bf16[128,1024]{1,0:T(8,128)(2,1)S(1)}, bf16[128,1024]{1,0:T(8,128)(2,1)S(1)}, u32[]{:S(2)}, u32[]{:S(2)}) %collective-permute-start.32) | collective-permute-done | bytes 262176 | tf_op jit(solution)/shard_map/ppermute | solution.py:373
  118.0 0.1 add_convert_fusion
  118.1 0.1 collective-permute-start.33
  118.2 2.7 %collective-permute-done.28 = bf16[64,1024]{1,0:T(8,128)(2,1)S(1)} collective-permute-done((bf16[64,1024]{1,0:T(8,128)(2,1)S(1)}, bf16[64,1024]{1,0:T(8,128)(2,1)S(1)}, u32[]{:S(2)}, u32[]{:S(2)}) %collective-permute-start.28) | collective-permute-done | bytes 131104 | tf_op jit(solution)/shard_map/ppermute | solution.py:373
  120.9 1.3 collective-permute-start.29
  122.2 5.7 %collective-permute-done.29.bottom_ref = bf16[64,1024]{1,0:T(8,128)(2,1)S(1)} collective-permute-done((bf16[64,1024]{1,0:T(8,128)(2,1)S(1)}, bf16[64,1024]{1,0:T(8,128)(2,1)S(1)}, u32[]{:S(2)}, u32[]{:S(2)}) %collective-permute-start.29) | collective-permute-done | bytes 131104 | tf_op jit(solution)/shard_map/ppermute | solution.py:373
  127.9 5.2 %collective-permute-done.33.refs_1_ = bf16[128,1024]{1,0:T(8,128)(2,1)S(1)} collective-permute-done((bf16[128,1024]{1,0:T(8,128)(2,1)S(1)}, bf16[128,1024]{1,0:T(8,128)(2,1)S(1)}, u32[]{:S(2)}, u32[]{:S(2)}) %collective-permute-start.33) | collective-permute-done | bytes 262176 | tf_op jit(solution)/shard_map/ppermute | solution.py:373
  133.1 0.9 shard_map.109
  (53 shorter events, 0.2 us)
Async XLA Ops:
  2.5 28.5 %collective-permute-start = (bf16[320,1024]{1,0:T(8,128)(2,1)}, bf16[320,1024]{1,0:T(8,128)(2,1)S(1)}, u32[]{:S(2)}, u32[]{:S(2)}) collective-permute-start(bf16[320,1024]{1,0:T(8,128)(2,1)} %get-tuple-element.48), channel_id=1, source_target_pairs={{0,2},{2,0},{4,6},{6,4},{8,10},{10,8},{12,14},{14,12},{1,3},{3,1},... | collective-permute-start | bytes 1966088 | tf_op jit(solution)/shard_map/ppermute | solution.py:373
  5.5 15.5 %collective-permute-start.3 = (bf16[128,1024]{1,0:T(8,128)(2,1)S(1)}, bf16[128,1024]{1,0:T(8,128)(2,1)S(1)}, u32[]{:S(2)}, u32[]{:S(2)}) collective-permute-start(bf16[128,1024]{1,0:T(8,128)(2,1)S(1)} %get-tuple-element.45._), channel_id=1, source_target_pairs={{0,8},{2,10},{4,12},{6,14},{8,0},{10,2},{12,4},{14,6},{1,9},{3,11}... | collective-permute-start | bytes 786440 | tf_op jit(solution)/shard_map/ppermute | solution.py:373
  8.1 16.6 %collective-permute-start.1 = (bf16[256,1024]{1,0:T(8,128)(2,1)}, bf16[256,1024]{1,0:T(8,128)(2,1)}, u32[]{:S(2)}, u32[]{:S(2)}) collective-permute-start(bf16[256,1024]{1,0:T(8,128)(2,1)} %get-tuple-element.47.own_ref), channel_id=1, source_target_pairs={{2,4},{6,8},{10,12},{4,2},{8,6},{12,10},{3,5},{7,9},{11,13},{5,3},... | collective-permute-start | bytes 1572872 | tf_op jit(solution)/shard_map/ppermute | solution.py:418
  11.5 11.0 %copy-start = (bf16[256,1024]{1,0:T(8,128)(2,1)S(1)}, bf16[256,1024]{1,0:T(8,128)(2,1)}, u32[]{:S(2)}) copy-start(bf16[256,1024]{1,0:T(8,128)(2,1)} %get-tuple-element.50.refs_0_) | copy-start | bytes 1572868
  11.5 11.5 %copy-start.1 = (bf16[2048,64]{0,1:T(8,128)(2,1)S(1)}, bf16[2048,64]{0,1:T(8,128)(2,1)}, u32[]{:S(2)}) copy-start(bf16[2048,64]{0,1:T(8,128)(2,1)} %param.12) | copy-start | bytes 786436
  11.5 11.5 %copy-start.2 = (f32[4,2048]{1,0:T(4,128)S(1)}, f32[4,2048]{1,0:T(4,128)}, u32[]{:S(2)}) copy-start(f32[4,2048]{1,0:T(4,128)} %mod_ref.1) | copy-start | bytes 98308
  11.6 11.5 %copy-start.3 = (s32[128,4]{0,1:T(4,128)S(1)}, s32[128,4]{0,1:T(4,128)}, u32[]{:S(2)}) copy-start(s32[128,4]{0,1:T(4,128)} %param.13) | copy-start | bytes 6148
  21.0 16.8 %collective-permute-start.6 = (bf16[128,1024]{1,0:T(8,128)(2,1)S(1)}, bf16[128,1024]{1,0:T(8,128)(2,1)S(1)}, u32[]{:S(2)}, u32[]{:S(2)}) collective-permute-start(bf16[128,1024]{1,0:T(8,128)(2,1)S(1)} %shard_map.87.refs_1_.refs_4_), channel_id=1, source_target_pairs={{0,4},{2,6},{4,0},{6,2},{8,12},{10,14},{12,8},{14,10},{1,5},{3,7},... | collective-permute-start | bytes 786440 | tf_op jit(solution)/shard_map/ppermute | solution.py:373
  22.5 22.2 %collective-permute-start.4 = (bf16[256,1024]{1,0:T(8,128)(2,1)S(1)}, bf16[256,1024]{1,0:T(8,128)(2,1)S(1)}, u32[]{:S(2)}, u32[]{:S(2)}) collective-permute-start(bf16[256,1024]{1,0:T(8,128)(2,1)S(1)} %shard_map.88.refs_2_), channel_id=1, source_target_pairs={{0,4},{2,6},{4,0},{6,2},{8,12},{10,14},{12,8},{14,10},{1,5},{3,7},... | collective-permute-start | bytes 1572872 | tf_op jit(solution)/shard_map/ppermute | solution.py:373
  23.1 16.3 %collective-permute-start.5 = (bf16[128,1024]{1,0:T(8,128)(2,1)S(1)}, bf16[128,1024]{1,0:T(8,128)(2,1)S(1)}, u32[]{:S(2)}, u32[]{:S(2)}) collective-permute-start(bf16[128,1024]{1,0:T(8,128)(2,1)S(1)} %shard_map.87.refs_1_.refs_4_), channel_id=1, source_target_pairs={{0,16},{16,0},{1,17},{17,1},{2,18},{18,2},{3,19},{19,3},{4,20},{20... | collective-permute-start | bytes 786440 | tf_op jit(solution)/shard_map/ppermute | solution.py:445
  35.3 9.4 %collective-permute-start.2 = (bf16[128,1024]{1,0:T(8,128)(2,1)S(1)}, bf16[128,1024]{1,0:T(8,128)(2,1)S(1)}, u32[]{:S(2)}, u32[]{:S(2)}) collective-permute-start(bf16[128,1024]{1,0:T(8,128)(2,1)S(1)} %shard_map.85.refs_1_.refs_0_), channel_id=1, source_target_pairs={{0,2},{2,0},{4,6},{6,4},{8,10},{10,8},{12,14},{14,12},{1,3},{3,1},... | collective-permute-start | bytes 786440 | tf_op jit(solution)/shard_map/ppermute | solution.py:373
  37.8 6.9 %collective-permute-start.7 = (bf16[128,1024]{1,0:T(8,128)(2,1)S(1)}, bf16[128,1024]{1,0:T(8,128)(2,1)S(1)}, u32[]{:S(2)}, u32[]{:S(2)}) collective-permute-start(bf16[128,1024]{1,0:T(8,128)(2,1)S(1)} %shard_map.89.refs_6_), channel_id=1, source_target_pairs={{0,16},{16,0},{1,17},{17,1},{2,18},{18,2},{3,19},{19,3},{4,20},{20... | collective-permute-start | bytes 786440 | tf_op jit(solution)/shard_map/ppermute | solution.py:445
  45.9 2.0 %collective-permute-start.8 = (f32[256,512]{1,0:T(8,128)S(1)}, f32[256,512]{1,0:T(8,128)S(1)}, u32[]{:S(2)}, u32[]{:S(2)}) collective-permute-start(f32[256,512]{1,0:T(8,128)S(1)} %shard_map.91), channel_id=1, source_target_pairs={{0,1},{1,0},{2,3},{3,2},{4,5},{5,4},{6,7},{7,6},{8,9},{9,8},{10,11... | collective-permute-start | bytes 1572872 | tf_op jit(solution)/shard_map/ppermute | solution.py:376
  48.0 2.3 %collective-permute-start.10 = (bf16[272,512]{1,0:T(8,128)(2,1)S(1)}, bf16[272,512]{1,0:T(8,128)(2,1)S(1)}, u32[]{:S(2)}, u32[]{:S(2)}) collective-permute-start(bf16[272,512]{1,0:T(8,128)(2,1)S(1)} %get-tuple-element.54.refs_0_), channel_id=1, source_target_pairs={{0,1},{1,0},{2,3},{3,2},{4,5},{5,4},{6,7},{7,6},{8,9},{9,8},{10,11... | collective-permute-start | bytes 835592 | tf_op jit(solution)/shard_map/ppermute | solution.py:376
  48.2 14.3 %collective-permute-start.12 = (bf16[272,512]{1,0:T(8,128)(2,1)S(1)}, bf16[272,512]{1,0:T(8,128)(2,1)S(1)}, u32[]{:S(2)}, u32[]{:S(2)}) collective-permute-start(bf16[272,512]{1,0:T(8,128)(2,1)S(1)} %get-tuple-element.54.refs_0_), channel_id=1, source_target_pairs={{0,4},{2,6},{4,0},{6,2},{8,12},{10,14},{12,8},{14,10},{1,5},{3,7},... | collective-permute-start | bytes 835592 | tf_op jit(solution)/shard_map/ppermute | solution.py:373
  49.8 12.7 %collective-permute-start.9 = (bf16[272,512]{1,0:T(8,128)(2,1)S(1)}, bf16[272,512]{1,0:T(8,128)(2,1)S(1)}, u32[]{:S(2)}, u32[]{:S(2)}) collective-permute-start(bf16[272,512]{1,0:T(8,128)(2,1)S(1)} %get-tuple-element.54.refs_0_), channel_id=1, source_target_pairs={{0,2},{2,0},{4,6},{6,4},{8,10},{10,8},{12,14},{14,12},{1,3},{3,1},... | collective-permute-start | bytes 835592 | tf_op jit(solution)/shard_map/ppermute | solution.py:373
  50.4 15.3 %collective-permute-start.16 = (bf16[272,512]{1,0:T(8,128)(2,1)S(1)}, bf16[272,512]{1,0:T(8,128)(2,1)S(1)}, u32[]{:S(2)}, u32[]{:S(2)}) collective-permute-start(bf16[272,512]{1,0:T(8,128)(2,1)S(1)} %shard_map.96), channel_id=1, source_target_pairs={{0,8},{2,10},{4,12},{6,14},{8,0},{10,2},{12,4},{14,6},{1,9},{3,11}... | collective-permute-start | bytes 835592 | tf_op jit(solution)/shard_map/ppermute | solution.py:373
  62.5 3.1 %collective-permute-start.14 = (bf16[272,512]{1,0:T(8,128)(2,1)S(1)}, bf16[272,512]{1,0:T(8,128)(2,1)S(1)}, u32[]{:S(2)}, u32[]{:S(2)}) collective-permute-start(bf16[272,512]{1,0:T(8,128)(2,1)S(1)} %shard_map.94.refs_0_), channel_id=1, source_target_pairs={{0,1},{1,0},{2,3},{3,2},{4,5},{5,4},{6,7},{7,6},{8,9},{9,8},{10,11... | collective-permute-start | bytes 835592 | tf_op jit(solution)/shard_map/ppermute | solution.py:376
  62.5 9.5 %collective-permute-start.13 = (bf16[272,512]{1,0:T(8,128)(2,1)S(1)}, bf16[272,512]{1,0:T(8,128)(2,1)S(1)}, u32[]{:S(2)}, u32[]{:S(2)}) collective-permute-start(bf16[272,512]{1,0:T(8,128)(2,1)S(1)} %shard_map.94.refs_0_), channel_id=1, source_target_pairs={{0,2},{2,0},{4,6},{6,4},{8,10},{10,8},{12,14},{14,12},{1,3},{3,1},... | collective-permute-start | bytes 835592 | tf_op jit(solution)/shard_map/ppermute | solution.py:373
  62.6 9.5 %collective-permute-start.11 = (bf16[272,512]{1,0:T(8,128)(2,1)S(1)}, bf16[272,512]{1,0:T(8,128)(2,1)S(1)}, u32[]{:S(2)}, u32[]{:S(2)}) collective-permute-start(bf16[272,512]{1,0:T(8,128)(2,1)S(1)} %collective-permute-done.9.refs_1_), channel_id=1, source_target_pairs={{0,1},{1,0},{2,3},{3,2},{4,5},{5,4},{6,7},{7,6},{8,9},{9,8},{10,11... | collective-permute-start | bytes 835592 | tf_op jit(solution)/shard_map/ppermute | solution.py:376
  65.6 11.9 %collective-permute-start.17 = (bf16[272,512]{1,0:T(8,128)(2,1)S(1)}, bf16[272,512]{1,0:T(8,128)(2,1)S(1)}, u32[]{:S(2)}, u32[]{:S(2)}) collective-permute-start(bf16[272,512]{1,0:T(8,128)(2,1)S(1)} %shard_map.97.refs_0_), channel_id=1, source_target_pairs={{0,2},{2,0},{4,6},{6,4},{8,10},{10,8},{12,14},{14,12},{1,3},{3,1},... | collective-permute-start | bytes 835592 | tf_op jit(solution)/shard_map/ppermute | solution.py:373
  67.1 10.4 %collective-permute-start.20 = (bf16[272,512]{1,0:T(8,128)(2,1)S(1)}, bf16[272,512]{1,0:T(8,128)(2,1)S(1)}, u32[]{:S(2)}, u32[]{:S(2)}) collective-permute-start(bf16[272,512]{1,0:T(8,128)(2,1)S(1)} %shard_map.97.refs_0_), channel_id=1, source_target_pairs={{0,4},{2,6},{4,0},{6,2},{8,12},{10,14},{12,8},{14,10},{1,5},{3,7},... | collective-permute-start | bytes 835592 | tf_op jit(solution)/shard_map/ppermute | solution.py:373
  67.1 12.3 %collective-permute-start.18 = (bf16[272,512]{1,0:T(8,128)(2,1)S(1)}, bf16[272,512]{1,0:T(8,128)(2,1)S(1)}, u32[]{:S(2)}, u32[]{:S(2)}) collective-permute-start(bf16[272,512]{1,0:T(8,128)(2,1)S(1)} %shard_map.97.refs_0_), channel_id=1, source_target_pairs={{0,1},{1,0},{2,3},{3,2},{4,5},{5,4},{6,7},{7,6},{8,9},{9,8},{10,11... | collective-permute-start | bytes 835592 | tf_op jit(solution)/shard_map/ppermute | solution.py:376
  72.0 6.0 %collective-permute-start.15 = (bf16[272,512]{1,0:T(8,128)(2,1)S(1)}, bf16[272,512]{1,0:T(8,128)(2,1)S(1)}, u32[]{:S(2)}, u32[]{:S(2)}) collective-permute-start(bf16[272,512]{1,0:T(8,128)(2,1)S(1)} %collective-permute-done.13.refs_1_), channel_id=1, source_target_pairs={{0,1},{1,0},{2,3},{3,2},{4,5},{5,4},{6,7},{7,6},{8,9},{9,8},{10,11... | collective-permute-start | bytes 835592 | tf_op jit(solution)/shard_map/ppermute | solution.py:376
  77.6 1.9 %collective-permute-start.19 = (bf16[272,512]{1,0:T(8,128)(2,1)S(1)}, bf16[272,512]{1,0:T(8,128)(2,1)S(1)}, u32[]{:S(2)}, u32[]{:S(2)}) collective-permute-start(bf16[272,512]{1,0:T(8,128)(2,1)S(1)} %collective-permute-done.17.refs_1_), channel_id=1, source_target_pairs={{0,1},{1,0},{2,3},{3,2},{4,5},{5,4},{6,7},{7,6},{8,9},{9,8},{10,11... | collective-permute-start | bytes 835592 | tf_op jit(solution)/shard_map/ppermute | solution.py:376
  77.6 9.1 %collective-permute-start.21 = (bf16[272,512]{1,0:T(8,128)(2,1)S(1)}, bf16[272,512]{1,0:T(8,128)(2,1)S(1)}, u32[]{:S(2)}, u32[]{:S(2)}) collective-permute-start(bf16[272,512]{1,0:T(8,128)(2,1)S(1)} %shard_map.99.refs_0_), channel_id=1, source_target_pairs={{0,2},{2,0},{4,6},{6,4},{8,10},{10,8},{12,14},{14,12},{1,3},{3,1},... | collective-permute-start | bytes 835592 | tf_op jit(solution)/shard_map/ppermute | solution.py:373
  77.9 8.7 %collective-permute-start.22 = (bf16[272,512]{1,0:T(8,128)(2,1)S(1)}, bf16[272,512]{1,0:T(8,128)(2,1)S(1)}, u32[]{:S(2)}, u32[]{:S(2)}) collective-permute-start(bf16[272,512]{1,0:T(8,128)(2,1)S(1)} %shard_map.99.refs_0_), channel_id=1, source_target_pairs={{0,1},{1,0},{2,3},{3,2},{4,5},{5,4},{6,7},{7,6},{8,9},{9,8},{10,11... | collective-permute-start | bytes 835592 | tf_op jit(solution)/shard_map/ppermute | solution.py:376
  86.6 1.6 %collective-permute-start.23 = (bf16[272,512]{1,0:T(8,128)(2,1)S(1)}, bf16[272,512]{1,0:T(8,128)(2,1)S(1)}, u32[]{:S(2)}, u32[]{:S(2)}) collective-permute-start(bf16[272,512]{1,0:T(8,128)(2,1)S(1)} %shard_map.100.refs_1_), channel_id=1, source_target_pairs={{0,1},{1,0},{2,3},{3,2},{4,5},{5,4},{6,7},{7,6},{8,9},{9,8},{10,11... | collective-permute-start | bytes 835592 | tf_op jit(solution)/shard_map/ppermute | solution.py:376
  89.5 7.7 %slice-start = ((s8[12582912]{0:T(1024)(128)(4,1)}), s8[4194304]{0:T(1024)(128)(4,1)S(1)}, s32[]{:S(2)}) async-start(s8[12582912]{0:T(1024)(128)(4,1)} %bitcast.4), calls=%async_computation | async-start | bytes 8388608
  89.5 7.7 %slice-start.1 = ((s8[12582912]{0:T(1024)(128)(4,1)}), s8[4194304]{0:T(1024)(128)(4,1)S(1)}, s32[]{:S(2)}) async-start(s8[12582912]{0:T(1024)(128)(4,1)} %bitcast.4), calls=%async_computation.1 | async-start | bytes 8388608
  93.9 3.3 %collective-permute-start.24 = (bf16[5,128,384]{2,1,0:T(8,128)(2,1)S(1)}, bf16[5,128,384]{2,1,0:T(8,128)(2,1)S(1)}, u32[]{:S(2)}, u32[]{:S(2)}) collective-permute-start(bf16[5,128,384]{2,1,0:T(8,128)(2,1)S(1)} %shard_map.102.near_ref), channel_id=1, source_target_pairs={{0,1},{1,0},{2,3},{3,2},{4,5},{5,4},{6,7},{7,6},{8,9},{9,8},{10,11... | collective-permute-start | bytes 1474568 | tf_op jit(solution)/shard_map/ppermute | solution.py:376
  94.1 3.1 %slice-start.2 = ((s8[12582912]{0:T(1024)(128)(4,1)}), s8[4194304]{0:T(1024)(128)(4,1)S(1)}, s32[]{:S(2)}) async-start(s8[12582912]{0:T(1024)(128)(4,1)} %bitcast.4), calls=%async_computation.2 | async-start | bytes 8388608
  96.8 2.0 %collective-permute-start.25 = (bf16[3,128,384]{2,1,0:T(8,128)(2,1)S(1)}, bf16[3,128,384]{2,1,0:T(8,128)(2,1)S(1)}, u32[]{:S(2)}, u32[]{:S(2)}) collective-permute-start(bf16[3,128,384]{2,1,0:T(8,128)(2,1)S(1)} %shard_map.104.near_ref), channel_id=1, source_target_pairs={{0,1},{1,0},{2,3},{3,2},{4,5},{5,4},{6,7},{7,6},{8,9},{9,8},{10,11... | collective-permute-start | bytes 884744 | tf_op jit(solution)/shard_map/ppermute | solution.py:376
  100.4 6.4 %collective-permute-start.26 = (bf16[64,1024]{1,0:T(8,128)(2,1)S(1)}, bf16[64,1024]{1,0:T(8,128)(2,1)S(1)}, u32[]{:S(2)}, u32[]{:S(2)}) collective-permute-start(bf16[64,1024]{1,0:T(8,128)(2,1)S(1)} %get-tuple-element.76), channel_id=1, source_target_pairs={{0,2},{2,0},{4,6},{6,4},{8,10},{10,8},{12,14},{14,12},{1,3},{3,1},... | collective-permute-start | bytes 393224 | tf_op jit(solution)/shard_map/ppermute | solution.py:373
  100.7 11.7 %collective-permute-start.30 = (bf16[128,1024]{1,0:T(8,128)(2,1)S(1)}, bf16[128,1024]{1,0:T(8,128)(2,1)S(1)}, u32[]{:S(2)}, u32[]{:S(2)}) collective-permute-start(bf16[128,1024]{1,0:T(8,128)(2,1)S(1)} %get-tuple-element.80), channel_id=1, source_target_pairs={{0,2},{2,0},{4,6},{6,4},{8,10},{10,8},{12,14},{14,12},{1,3},{3,1},... | collective-permute-start | bytes 786440 | tf_op jit(solution)/shard_map/ppermute | solution.py:373
  102.9 15.1 %collective-permute-start.32 = (bf16[128,1024]{1,0:T(8,128)(2,1)S(1)}, bf16[128,1024]{1,0:T(8,128)(2,1)S(1)}, u32[]{:S(2)}, u32[]{:S(2)}) collective-permute-start(bf16[128,1024]{1,0:T(8,128)(2,1)S(1)} %get-tuple-element.82), channel_id=1, source_target_pairs={{0,2},{2,0},{4,6},{6,4},{8,10},{10,8},{12,14},{14,12},{1,3},{3,1},... | collective-permute-start | bytes 786440 | tf_op jit(solution)/shard_map/ppermute | solution.py:373
  106.8 15.4 %collective-permute-start.27 = (bf16[64,1024]{1,0:T(8,128)(2,1)S(1)}, bf16[64,1024]{1,0:T(8,128)(2,1)S(1)}, u32[]{:S(2)}, u32[]{:S(2)}) collective-permute-start(bf16[64,1024]{1,0:T(8,128)(2,1)S(1)} %add_convert_fusion.3), channel_id=1, source_target_pairs={{0,12},{2,14},{4,8},{6,10},{8,4},{10,6},{12,0},{14,2},{1,13},{3,15... | collective-permute-start | bytes 393224 | tf_op jit(solution)/shard_map/ppermute | solution.py:373
  108.2 12.7 %collective-permute-start.28 = (bf16[64,1024]{1,0:T(8,128)(2,1)S(1)}, bf16[64,1024]{1,0:T(8,128)(2,1)S(1)}, u32[]{:S(2)}, u32[]{:S(2)}) collective-permute-start(bf16[64,1024]{1,0:T(8,128)(2,1)S(1)} %shard_map.107), channel_id=1, source_target_pairs={{0,2},{2,0},{4,6},{6,4},{8,10},{10,8},{12,14},{14,12},{1,3},{3,1},... | collective-permute-start | bytes 393224 | tf_op jit(solution)/shard_map/ppermute | solution.py:373
  112.5 15.4 %collective-permute-start.31 = (bf16[128,1024]{1,0:T(8,128)(2,1)S(1)}, bf16[128,1024]{1,0:T(8,128)(2,1)S(1)}, u32[]{:S(2)}, u32[]{:S(2)}) collective-permute-start(bf16[128,1024]{1,0:T(8,128)(2,1)S(1)} %add_convert_fusion.1), channel_id=1, source_target_pairs={{0,8},{2,10},{4,12},{6,14},{8,0},{10,2},{12,4},{14,6},{1,9},{3,11}... | collective-permute-start | bytes 786440 | tf_op jit(solution)/shard_map/ppermute | solution.py:373
  112.6 15.3 %collective-permute-start.34 = (bf16[128,1024]{1,0:T(8,128)(2,1)S(1)}, bf16[128,1024]{1,0:T(8,128)(2,1)S(1)}, u32[]{:S(2)}, u32[]{:S(2)}) collective-permute-start(bf16[128,1024]{1,0:T(8,128)(2,1)S(1)} %shard_map.108), channel_id=1, source_target_pairs={{0,2},{2,0},{4,6},{6,4},{8,10},{10,8},{12,14},{14,12},{1,3},{3,1},... | collective-permute-start | bytes 786440 | tf_op jit(solution)/shard_map/ppermute | solution.py:373
  118.1 15.0 %collective-permute-start.33 = (bf16[128,1024]{1,0:T(8,128)(2,1)S(1)}, bf16[128,1024]{1,0:T(8,128)(2,1)S(1)}, u32[]{:S(2)}, u32[]{:S(2)}) collective-permute-start(bf16[128,1024]{1,0:T(8,128)(2,1)S(1)} %add_convert_fusion), channel_id=1, source_target_pairs={{0,4},{2,6},{4,0},{6,2},{8,12},{10,14},{12,8},{14,10},{1,5},{3,7},... | collective-permute-start | bytes 786440 | tf_op jit(solution)/shard_map/ppermute | solution.py:373
  120.9 7.0 %collective-permute-start.29 = (bf16[64,1024]{1,0:T(8,128)(2,1)S(1)}, bf16[64,1024]{1,0:T(8,128)(2,1)S(1)}, u32[]{:S(2)}, u32[]{:S(2)}) collective-permute-start(bf16[64,1024]{1,0:T(8,128)(2,1)S(1)} %add_convert_fusion.2), channel_id=1, source_target_pairs={{0,12},{2,14},{4,8},{6,10},{8,4},{10,6},{12,0},{14,2},{1,13},{3,15... | collective-permute-start | bytes 393224 | tf_op jit(solution)/shard_map/ppermute | solution.py:373
